TPU v7x, 256 devices: a whole 4x4x8 slice. The times are simulated.
256 devices in a mesh: ctx: 32 (over y, x, core), head: 8 (over z).
Axes of the slice: x: 4, y: 4, z: 8, core: 2. Of those that a mesh axis runs over, the one named last changes fastest.
Arguments:
- query_in: bfloat16 [8192, 2048], P('ctx', 'head'), may hold values from -6 to 6
- key_in: bfloat16 [8192, 2048], P('ctx', 'head'), may hold values from -3 to 3
- value_in: bfloat16 [8192, 4096], P('ctx', 'head'), may hold values from -6 to 6
- out_gate: bfloat16 [8192, 4096], P('ctx', 'head'), may hold values from -6 to 6
- log_decay: float32 [32, 8192], P('head', 'ctx'), may hold values from -1 to 0
- beta_gate: float32 [32, 8192], P('head', 'ctx'), may hold values from 0.05 to 1
- doc_start: int32 [8192], P('ctx'), may hold values from 0 to 8064, as said below
- conv_query: float32 [4, 2048], P(None, 'head'), may hold values from -3 to 3
- conv_key: float32 [4, 2048], P(None, 'head'), may hold values from -3 to 3
- conv_value: float32 [4, 4096], P(None, 'head'), may hold values from -3 to 3
- norm_gain: float32 [128], replicated, may hold values from 0.1 to 1.9
- out_weight: bfloat16 [4096, 2048], P('head'), may hold values from -0.09375 to 0.09375
Outputs:
- mixed: bfloat16 [8192, 2048], P(('ctx', 'head'))
Inputs may be any that keep to these rules, and one draw needn't show every extreme that they name: doc_start[t] is the position of the first token of the document holding token t: it never falls, doc_start[t] <= t and doc_start[0] = 0; the sequence holds at most 8 documents, and the last one begins at 8064.
All inputs are finite; a program needn't handle non-finite values.
Results may differ from a plain program's by a relative error of at most 0.02.
Values may be sent and summed in bfloat16 or wider, within the bound.
No kernel may reach another device: no remote copies, remote signals or barrier semaphores. Data moves between devices by JAX's collectives and lax.ppermute only.
A program may use at most 128 MiB of HBM per device.

v0:
```python
import jax
import jax.numpy as jnp
from jax import lax
from jax.sharding import PartitionSpec as P

DK = 128
DV = 128
SPAN = 64


EXACT_PRECISION = lax.Precision.HIGHEST
epsilon = 1e-06


def passed_along(block, axis, distance):
    devices = range(lax.axis_size(axis))
    route = [(i - distance, i) for i in devices if i - distance in devices]
    return lax.ppermute(block, axis, route)


def prefix_2(shard, axis, join, neutral):
    place = lax.axis_index(axis)
    gathered = jax.tree.map(
        lambda a, kind: lax.all_gather(a.astype(kind), axis), shard, (jnp.bfloat16, jnp.bfloat16)
    )
    state = jax.tree.map(lambda a, e: jnp.zeros_like(a) + jnp.asarray(e, a.dtype), shard, neutral)

    def one(hop, state):
        return join(
            state,
            jax.tree.map(
                lambda a, own: lax.dynamic_index_in_dim(a, hop, 0, False).astype(own.dtype),
                gathered,
                shard,
            ),
        )

    return lax.fori_loop(0, place, one, state)


def short_conv(extended, weight, doc_start, token_position):
    tok_count = doc_start.shape[0]
    tap_total = weight.shape[0]
    source = extended.astype(jnp.float32)
    accum = jnp.zeros((tok_count, source.shape[1]), jnp.float32)
    for tap_index in range(tap_total):
        first_row = tap_total - 1 - tap_index
        shifted = lax.slice_in_dim(source, first_row, first_row + tok_count, axis=0)
        valid = (doc_start <= token_position - tap_index).astype(jnp.float32)
        accum = accum + shifted * weight[tap_index][None, :] * valid[:, None]
    return jax.nn.silu(accum)


def matmul_hi(left, right):
    return jnp.einsum("hde,hef->hdf", left, right, precision=EXACT_PRECISION)


def span_terms(q_blocks, k_blocks, v_blocks, decay_blocks, beta_blocks, starts, positions):
    span_len = q_blocks.shape[2]
    key_width = k_blocks.shape[3]
    cum_decay = jnp.cumsum(decay_blocks, axis=-1)
    first_pos = positions[:, :1]
    lower_mask = jnp.tril(jnp.ones((span_len, span_len), jnp.bool_))
    linked = (starts[:, :, None] <= positions[:, None, :]) & lower_mask[None]
    linked = jnp.broadcast_to(linked[None], cum_decay.shape[:2] + (span_len, span_len))
    log_gap = cum_decay[..., :, None] - cum_decay[..., None, :]
    fading = jnp.where(linked, jnp.exp(jnp.where(linked, log_gap, 0.0)), 0.0)
    carry_in = jnp.where((starts < first_pos)[None], jnp.exp(cum_decay), 0.0)
    eye_span = jnp.eye(span_len, dtype=jnp.float32)
    key_key = jnp.einsum("hncd,hnjd->hncj", k_blocks, k_blocks, precision=EXACT_PRECISION)
    query_key = jnp.einsum("hncd,hnjd->hncj", q_blocks, k_blocks, precision=EXACT_PRECISION)
    system = eye_span + beta_blocks[..., None] * fading * key_key * (1.0 - eye_span)
    right_side = jnp.concatenate(
        [(beta_blocks * carry_in)[..., None] * k_blocks, beta_blocks[..., None] * v_blocks], axis=-1
    )
    solved = jax.scipy.linalg.solve_triangular(system, right_side, lower=True, unit_diagonal=True)
    weights_w = solved[..., :key_width]
    values_u = solved[..., key_width:]
    scored = fading * query_key
    faded_key = fading[..., -1, :][..., None] * k_blocks
    eye_key = jnp.eye(key_width, dtype=jnp.float32)
    transition = carry_in[..., -1][..., None, None] * eye_key - jnp.einsum(
        "hncd,hnce->hnde", faded_key, weights_w, precision=EXACT_PRECISION
    )
    injection = jnp.einsum("hncd,hncv->hndv", faded_key, values_u, precision=EXACT_PRECISION)
    intra_out = jnp.einsum("hntj,hnjv->hntv", scored, values_u, precision=EXACT_PRECISION)
    effective = carry_in[..., None] * q_blocks - jnp.einsum(
        "hntj,hnjd->hntd", scored, weights_w, precision=EXACT_PRECISION
    )
    return (transition, injection, intra_out, effective)


def on_device(
    query_in,
    key_in,
    value_in,
    out_gate,
    log_decay,
    beta_gate,
    doc_start,
    conv_query,
    conv_key,
    conv_value,
    norm_gain,
    out_weight,
):
    tok_count = doc_start.shape[0]
    tap_count = conv_query.shape[0] - 1
    rim_rows = passed_along(
        (
            query_in[tok_count - tap_count :],
            key_in[tok_count - tap_count :],
            value_in[tok_count - tap_count :],
        ),
        "ctx",
        1,
    )
    token_position = lax.axis_index("ctx") * tok_count + jnp.arange(tok_count, dtype=jnp.int32)
    query_conv = short_conv(
        jnp.concatenate([rim_rows[0], query_in], axis=0), conv_query, doc_start, token_position
    )
    key_conv = short_conv(
        jnp.concatenate([rim_rows[1], key_in], axis=0), conv_key, doc_start, token_position
    )
    value_conv = short_conv(
        jnp.concatenate([rim_rows[2], value_in], axis=0), conv_value, doc_start, token_position
    )
    key_groups = key_conv.shape[1] // DK
    head_count = value_conv.shape[1] // DV
    group_ratio = head_count // key_groups
    key_conv = key_conv.reshape(tok_count, key_groups, DK)
    key_unit = key_conv * lax.rsqrt(jnp.sum(key_conv * key_conv, axis=-1, keepdims=True) + epsilon)
    query_heads = jnp.repeat(query_conv.reshape(tok_count, key_groups, DK), group_ratio, axis=1)
    key_heads = jnp.repeat(key_unit, group_ratio, axis=1)
    value_heads = value_conv.reshape(tok_count, head_count, DV)
    blocks = tok_count // SPAN

    def to_blocks(tensor):
        return tensor.reshape(blocks, SPAN, tensor.shape[1], tensor.shape[2]).transpose(2, 0, 1, 3)

    transition, injection, intra_out, effective = span_terms(
        to_blocks(query_heads),
        to_blocks(key_heads),
        to_blocks(value_heads),
        log_decay.reshape(head_count, blocks, SPAN),
        beta_gate.reshape(head_count, blocks, SPAN),
        doc_start.reshape(blocks, SPAN),
        token_position.reshape(blocks, SPAN),
    )
    eye_k = jnp.broadcast_to(jnp.eye(DK, dtype=jnp.float32), (head_count, DK, DK))
    zero_state = jnp.zeros((head_count, DK, DV), jnp.float32)

    def advance(carried, inputs):
        state_map, state_sum = carried
        step_map, step_sum = inputs
        return (
            (matmul_hi(step_map, state_map), matmul_hi(step_map, state_sum) + step_sum),
            (state_map, state_sum),
        )

    (local_map, local_sum), (before_map, before_sum) = lax.scan(
        advance,
        (eye_k, zero_state),
        (transition.transpose(1, 0, 2, 3), injection.transpose(1, 0, 2, 3)),
    )
    local_out = intra_out + jnp.einsum(
        "hntd,nhdv->hntv", effective, before_sum, precision=EXACT_PRECISION
    )
    reach_map = jnp.einsum("hntd,nhde->hnte", effective, before_map, precision=EXACT_PRECISION)

    def combine(earlier, later):
        return (matmul_hi(later[0], earlier[0]), matmul_hi(later[0], earlier[1]) + later[1])

    prefix = prefix_2((local_map, local_sum), "ctx", combine, (eye_k, zero_state))
    incoming = prefix[1]
    heads_out = local_out + jnp.einsum(
        "hnte,hev->hntv", reach_map, incoming, precision=EXACT_PRECISION
    )
    heads_out = heads_out.transpose(1, 2, 0, 3).reshape(tok_count, head_count, DV)
    gate_float = out_gate.reshape(tok_count, head_count, DV).astype(jnp.float32)
    inv_rms = lax.rsqrt(jnp.mean(heads_out * heads_out, axis=-1, keepdims=True) + epsilon)
    normed = (
        (heads_out * inv_rms * norm_gain * jax.nn.silu(gate_float))
        .reshape(tok_count, head_count * DV)
        .astype(jnp.bfloat16)
    )
    return lax.psum_scatter(
        jnp.dot(normed, out_weight, preferred_element_type=jnp.float32).astype(jnp.bfloat16),
        "head",
        scatter_dimension=0,
        tiled=True,
    )


def solution(mesh):
    placed = (
        P("ctx", "head"),
        P("ctx", "head"),
        P("ctx", "head"),
        P("ctx", "head"),
        P("head", "ctx"),
        P("head", "ctx"),
        P("ctx"),
        P(None, "head"),
        P(None, "head"),
        P(None, "head"),
        P(),
        P("head", None),
    )
    return jax.shard_map(
        on_device, mesh=mesh, in_specs=placed, out_specs=P(("ctx", "head"), None), check_vma=False
    )
```

profile of v0, /device:TPU:6, one launch (start us, length us, event | category | flops | bytes accessed | tf_op | source)
XLA Modules:
  0.0 338.9 jit_solution(8894180966464808060)
XLA Ops:
  6.5 0.8 slice.111
  7.4 1.9 collective-permute-start.1
  9.3 1.3 slice.121
  10.6 3.5 %collective-permute-start.2 = (bf16[3,512]{1,0:T(4,128)(2,1)}, bf16[3,512]{1,0:T(4,128)(2,1)}, u32[]{:S(2)}, u32[]{:S(2)}) collective-permute-start(bf16[3,512]{1,0:T(4,128)(2,1)} %slice.121), channel_id=1, source_target_pairs={{0,8},{8,16},{16,24},{24,32},{32,40},{40,48},{48,56},{56,64},{64,7... | collective-permute-start | bytes 9224 | tf_op jit(solution)/shard_map/ppermute | solution.py:18
  14.1 0.8 le.39
  14.9 1.3 compare_convert_fusion.3
  16.2 0.6 broadcast_subtract_fusion
  16.8 0.6 fusion.70
  17.5 1.4 fusion.75
  19.0 0.8 mul.396
  19.7 0.8 reshape.130
  20.5 1.5 fusion.74
  22.1 0.7 iota_compare_fusion.3
  22.8 0.9 reduce_window_sum.11
  24.0 0.8 slice_reduce_fusion
  24.8 0.9 maximum_convert_fusion.2
  25.7 0.9 divide_multiply_fusion.1
  26.8 0.3 multiply_reduce_fusion.1
  27.2 0.3 broadcast_multiply_fusion.1
  27.6 2.6 fusion.21
  30.2 80.0 %custom-call.4 = f32[4,4,1,64,64]{3,4,2,1,0:T(8,128)} custom-call(f32[4,4,1,64,64]{4,3,2,1,0:T(8,128)} %fusion.21), custom_call_target="InvertDiagBlocksLowerTriangular" | custom-call | tf_op jit(solution)/shard_map/jit(_solve_triangular)/vmap(vmap())/triangular_solve | solution.py:76
  110.2 0.7 maximum_convert_fusion
  111.0 1.1 divide_multiply_fusion
  112.1 1.0 reshape_reshape.11
  113.0 1.4 bitcast_multiply_fusion.1
  114.4 2.1 fusion.22
  116.5 3.0 convolution_bitcast_fusion
  119.5 3.0 fusion.14
  122.6 14.8 %while.30 = (s32[]{:T(128)}, f32[4,128,128]{2,1,0:T(8,128)S(1)}, f32[4,128,128]{2,1,0:T(8,128)S(1)}, f32[4,4,128,128]{3,2,0,1:T(8,128)}, f32[4,4,128,128]{3,2,0,...) while((s32[]{:T(128)}, f32[4,128,128]{2,1,0:T(8,128)S(1)}, ...), condition=%wide.region_3.4_spmd.clone, body=%wide.region_2.3_spmd.clone.sunk | while | flops 201523200 | bytes 3933815 | solution.py:161
  122.7 0.8 bitcast_dynamic-update-slice_fusion.3
  123.5 1.4 convolution_add_fusion.6
  124.9 1.4 fusion.105
  126.4 0.9 bitcast_dynamic-update-slice_fusion.3
  127.2 1.4 convolution_add_fusion.6
  128.6 1.4 fusion.105
  130.1 0.8 bitcast_dynamic-update-slice_fusion.3
  130.9 1.4 convolution_add_fusion.6
  132.3 1.4 fusion.105
  133.8 0.9 bitcast_dynamic-update-slice_fusion.3
  134.6 1.4 convolution_add_fusion.6
  136.1 1.4 fusion.105
  137.4 0.7 convert_element_type.85
  138.2 0.7 convert_element_type.86
  138.9 2.1 collective-permute-start
  141.1 2.7 collective-permute-done
  144.2 1.0 convolution_multiply_fusion.1
  145.2 0.6 fusion.43
  145.8 0.7 convolution_subtract_fusion
  146.5 1.9 fusion.77
  148.4 43.2 %all-gather.5.cloned.1.call-done = bf16[128,128,128]{2,1,0:T(8,128)(2,1)} async-done(((bf16[4,128,128]{2,1,0:T(8,128)(2,1)}), bf16[128,128,128]{2,1,0:T(8,128)(2,1)}) %all-gather.5.cloned.1.call-update) | async-done | bytes 4194320 | tf_op jit(solution)/shard_map/all_gather | solution.py:24
  191.6 53.1 %all-gather.7.cloned.1.call-done = bf16[128,128,128]{2,1,0:T(8,128)(2,1)} async-done(((bf16[4,128,128]{2,1,0:T(8,128)(2,1)}), bf16[128,128,128]{2,1,0:T(8,128)(2,1)}) %all-gather.7.cloned.1.call-update) | async-done | bytes 4194320 | tf_op jit(solution)/shard_map/all_gather | solution.py:24
  244.8 7.9 %while.29 = (s32[]{:T(128)}, f32[4,128,128]{2,1,0:T(8,128)S(1)}, s32[]{:T(128)}, bf16[32,4,128,128]{3,2,1,0:T(8,128)(2,1)}, bf16[32,4,128,128]{3,2,1,0:T(8,128)(2,1)}, /*index=5*/s32[]{:T(128)}, s32[]{:T(128)}, s32[]{:T(128)}) while((s32[]{:T(128)}, f32[4,128,128]{2,1,0:T(8,128)S(1)}, s32[]{:T(128)}, bf16[32,4,128,128]{3,2,1,0:T(8,128)(2,1)}, ...), condition=%wide.region_5.6_spmd, body=%wide.region_4.5_spmd.sunk | while | flops 100794368 | bytes 1311871 | solution.py:38
  244.8 1.3 convolution_add_fusion.5
  246.1 1.3 convolution_add_fusion.5
  247.4 1.3 convolution_add_fusion.5
  248.7 1.3 convolution_add_fusion.5
  250.1 1.3 convolution_add_fusion.5
  251.4 1.3 convolution_add_fusion.5
  252.6 1.6 fusion.62
  254.3 3.1 multiply_reduce_fusion
  257.5 1.4 copy.58
  258.9 0.3 mul.439
  259.2 2.7 convolution_convert_fusion
  262.0 70.4 %reduce-scatter.2.cloned.1.call-done = bf16[32,2048]{1,0:T(8,128)(2,1)} async-done(((bf16[256,2048]{1,0:T(8,128)(2,1)}), bf16[32,2048]{1,0:T(8,128)(2,1)}) %reduce-scatter.2.cloned.1.call-update) | async-done | bytes 131088 | tf_op jit(solution)/shard_map/reduce_scatter | solution.py:187
  (71 shorter events, 1.7 us)
Async XLA Ops:
  6.5 252.7 %copy-start = (bf16[512,2048]{1,0:T(8,128)(2,1)S(1)}, bf16[512,2048]{1,0:T(8,128)(2,1)}, u32[]{:S(2)}) copy-start(bf16[512,2048]{1,0:T(8,128)(2,1)} %param.27) | copy-start | bytes 6291460
  6.5 103.7 %copy-start.4 = (bf16[256,512]{1,0:T(8,128)(2,1)S(1)}, bf16[256,512]{1,0:T(8,128)(2,1)}, u32[]{:S(2)}) copy-start(bf16[256,512]{1,0:T(8,128)(2,1)} %param.18) | copy-start | bytes 786436
  6.5 185.1 %all-gather.5.cloned.1.call-start = ((), (), s32[]{:S(2)}) async-start(), calls=%async_computation.2 | async-start | bytes 4325376 | tf_op jit(solution)/shard_map/all_gather | solution.py:24
  7.4 17.4 %collective-permute-start.1 = (bf16[3,256]{1,0:T(4,128)(2,1)S(1)}, bf16[3,256]{1,0:T(4,128)(2,1)S(1)}, u32[]{:S(2)}, u32[]{:S(2)}) collective-permute-start(bf16[3,256]{1,0:T(4,128)(2,1)S(1)} %slice.111), channel_id=1, source_target_pairs={{0,8},{8,16},{16,24},{24,32},{32,40},{40,48},{48,56},{56,64},{64,7... | collective-permute-start | bytes 4616 | tf_op jit(solution)/shard_map/ppermute | solution.py:18
  10.6 99.6 %collective-permute-start.2 = (bf16[3,512]{1,0:T(4,128)(2,1)}, bf16[3,512]{1,0:T(4,128)(2,1)}, u32[]{:S(2)}, u32[]{:S(2)}) collective-permute-start(bf16[3,512]{1,0:T(4,128)(2,1)} %slice.121), channel_id=1, source_target_pairs={{0,8},{8,16},{16,24},{24,32},{32,40},{40,48},{48,56},{56,64},{64,7... | collective-permute-start | bytes 9224 | tf_op jit(solution)/shard_map/ppermute | solution.py:18
  113.0 6.5 %copy-start.8 = (f32[4,4]{1,0:T(4,128)S(1)}, f32[4,4]{1,0:T(4,128)}, u32[]{:S(2)}) copy-start(f32[4,4]{1,0:T(4,128)} %slice_reduce_fusion) | copy-start | bytes 196
  116.5 3.0 copy-start.1
  122.5 16.4 %copy-start.5 = (bf16[256,256]{1,0:T(8,128)(2,1)S(1)}, bf16[256,256]{1,0:T(8,128)(2,1)}, u32[]{:S(2)}) copy-start(bf16[256,256]{1,0:T(8,128)(2,1)} %param.16) | copy-start | bytes 393220
  122.5 18.5 %copy-start.9 = (f32[4,256]{1,0:T(4,128)S(1)}, f32[4,256]{1,0:T(4,128)}, u32[]{:S(2)}) copy-start(f32[4,256]{1,0:T(4,128)} %param.23) | copy-start | bytes 12292
  122.6 18.5 %copy-start.10 = (f32[128]{0:T(128)S(1)}, f32[128]{0:T(128)}, u32[]{:S(2)}) copy-start(f32[128]{0:T(128)} %param.26) | copy-start | bytes 1540
  122.6 21.3 %copy-start.6 = (f32[256]{0:T(256)S(1)}, f32[256]{0:T(256)}, u32[]{:S(2)}) copy-start(f32[256]{0:T(256)} %get-tuple-element.195) | copy-start | bytes 3076
  122.6 21.3 %copy-start.7 = (f32[256]{0:T(256)S(1)}, f32[256]{0:T(256)}, u32[]{:S(2)}) copy-start(f32[256]{0:T(256)} %get-tuple-element.196) | copy-start | bytes 3076
  138.1 106.6 %all-gather.7.cloned.1.call-start = ((), (), s32[]{:S(2)}) async-start(), calls=%async_computation.3 | async-start | bytes 4325376 | tf_op jit(solution)/shard_map/all_gather | solution.py:24
  138.9 193.5 %reduce-scatter.2.cloned.1.call-start = ((), (), s32[]{:S(2)}) async-start(), calls=%async_computation.1 | async-start | bytes 1179648 | tf_op jit(solution)/shard_map/reduce_scatter | solution.py:187
  138.9 4.9 %collective-permute-start = (bf16[3,256]{1,0:T(4,128)(2,1)S(1)}, bf16[3,256]{1,0:T(4,128)(2,1)S(1)}, u32[]{:S(2)}, u32[]{:S(2)}) collective-permute-start(bf16[3,256]{1,0:T(4,128)(2,1)S(1)} %slice.102), channel_id=1, source_target_pairs={{0,8},{8,16},{16,24},{24,32},{32,40},{40,48},{48,56},{56,64},{64,7... | collective-permute-start | bytes 4616 | tf_op jit(solution)/shard_map/ppermute | solution.py:18
  141.1 4.1 %copy-start.2 = (f32[4,4,64,256]{3,2,1,0:T(8,128)S(1)}, f32[4,4,64,256]{3,2,1,0:T(8,128)}, u32[]{:S(2)}) copy-start(f32[4,4,64,256]{3,2,1,0:T(8,128)} %copy-done.1) | copy-start | bytes 3145732
  141.1 5.4 %copy-start.3 = (f32[4,4,128,128]{3,2,0,1:T(8,128)S(1)}, f32[4,4,128,128]{3,2,0,1:T(8,128)}, u32[]{:S(2)}) copy-start(f32[4,4,128,128]{3,2,0,1:T(8,128)} %get-tuple-element.90) | copy-start | bytes 3145732
Sparse Core Ops, SparseCore 0:
  138.2 53.3 all-gather.4
  194.2 50.5 all-gather.6
  262.1 70.2 reduce-scatter.1
where the time goes:
time: 341 us; the launch traced here: 339 us
  waiting for transfers between devices  169 us (50%)
  other arithmetic  95.4 us (28%)
  matrix products  40.9 us (12%)
  between operations  13.5 us (4%)
  local copies, waits for them, and re-layouts  11.6 us (3%)
  starting transfers between devices  7.59 us (2%)
    all_gather x2, waiting for transfers between devices, prefix_2(): lax.all_gather(a.astype(kind), axis)  96.3 us
    another operation x4, other arithmetic, span_terms(): jax.scipy.linalg.solve_triangular(system, right_side, lower=True, unit_di...  81.3 us
    reduce_scatter x1, waiting for transfers between devices, on_device(): lax.psum_scatter(jnp.dot(normed, out_weight, preferred_element_type=jnp.f...  70.4 us
    dot_general x14, matrix products, matmul_hi(): return jnp.einsum('hde,hef->hdf', left, right, precision=EXACT_PRECISION)  18.6 us
    ppermute x3, starting transfers between devices, passed_along(): return lax.ppermute(block, axis, route)  7.5 us
  transfers between devices with their start and end apart: 6, of which 4 were waited for; matrix products, arithmetic and copies ran while one was open for 30% of the time, Pallas kernels for 0%

commit v1 on v0

v1 whole, which is shorter than its diff:
```python
import jax
import jax.numpy as jnp
from jax import lax
from jax.experimental import pallas as pl
from jax.experimental.pallas import tpu as pltpu
from jax.sharding import PartitionSpec as P

DK = 128
DV = 128
TOK = 256
HEADS = 4
GROUPS = 2
TAPS = 4
RIM = 16
EPS = 1e-6
F32 = jnp.float32
BF16 = jnp.bfloat16
FAR = -1e30
MIB = 1 << 20

CTX = 32
CORES = 2
CHIPS_X = 4
CHIPS_Y = 4


def core_swap():
    return [(i, i ^ 1) for i in range(CTX)]


def along_x(step):
    return [
        ((y * 4 + x) * 2 + c, (y * 4 + (x + step) % 4) * 2 + c)
        for y in range(4)
        for x in range(4)
        for c in range(2)
    ]


def along_y(step):
    return [
        ((y * 4 + x) * 2 + c, (((y + step) % 4) * 4 + x) * 2 + c)
        for y in range(4)
        for x in range(4)
        for c in range(2)
    ]


def mm(left, right):
    return jnp.dot(left, right, preferred_element_type=F32)


def mm_t(left, right):
    return lax.dot_general(left, right, (((1,), (1,)), ((), ())), preferred_element_type=F32)


def parts(value, count):
    out = []
    for _ in range(count):
        piece = value.astype(BF16)
        out.append(piece)
        value = value - piece.astype(F32)
    return out


def rows_and_columns(shape=(TOK, TOK)):
    return lax.broadcasted_iota(jnp.int32, shape, 0), lax.broadcasted_iota(jnp.int32, shape, 1)


def spread(rows_list, pattern, count):
    out = []
    for pair in range(0, len(rows_list), 2):
        chosen = rows_list[pair : pair + 2]
        wide = jnp.concatenate([jnp.broadcast_to(r, (128, TOK)) for r in chosen], axis=0)
        total = None
        for piece in parts(wide, count):
            term = mm_t(pattern, piece)
            total = term if total is None else total + term
        for k in range(len(chosen)):
            out.append(total[:, k * 128 : (k + 1) * 128])
    return out


def local_start(doc_ref):
    first = lax.axis_index("ctx") * TOK
    return jnp.maximum(doc_ref[...] - first, -TAPS).astype(F32)


def short_conv(ext_ref, x_ref, rim, w_ref, valid):
    width = x_ref.shape[1]
    own = x_ref[...].astype(F32)
    ext_ref[0:8, :width] = rim
    ext_ref[8 : 8 + TOK, :width] = own
    total = own * w_ref[0:1, :]
    for tap in range(1, TAPS):
        shifted = ext_ref[8 - tap : 8 - tap + TOK, :width]
        mask = jnp.concatenate([valid[tap - 1]] * (width // 128), axis=1)
        total = total + jnp.where(mask, shifted * w_ref[tap : tap + 1, :], 0.0)
    return total * jax.nn.sigmoid(total)


def tap_masks(start):
    token = lax.broadcasted_iota(jnp.int32, (TOK, 128), 0).astype(F32)
    return [start <= token - tap for tap in range(1, TAPS)]


def unit_keys(key_conv):
    out = []
    for g in range(GROUPS):
        k = key_conv[:, g * DK : (g + 1) * DK]
        out.append(k * lax.rsqrt(jnp.sum(k * k, axis=-1, keepdims=True) + EPS))
    return out


def fading(cum_col, cum_row, start, keep):
    gap = jnp.concatenate([cum_col, cum_col], axis=1) - cum_row
    return jnp.exp(jnp.where(keep, gap, FAR))


def linked_mask(start):
    row, col = rows_and_columns()
    begin = jnp.concatenate([start, start], axis=1)
    return (col <= row) & (begin <= col.astype(F32))


def unit_lower_inverse(a, row, col):
    apart = row ^ col
    eye = (row == col).astype(F32)
    d = jnp.where(apart < 8, a, 0.0)
    db = d.astype(BF16)
    square = mm(db, db).astype(BF16)
    t = eye - d
    t = t + mm(t.astype(BF16), square)
    fourth = mm(square, square).astype(BF16)
    t = t + mm(t.astype(BF16), fourth)
    size = 8
    while size < TOK:
        e = jnp.where((apart >= size) & (apart < 2 * size), a, 0.0).astype(BF16)
        tb = t.astype(BF16)
        t = t - mm(mm(tb, e).astype(BF16), tb)
        size *= 2
    guess = t.astype(BF16)
    high, low = parts(a, 2)
    rest = eye - guess.astype(F32) - mm(high, guess) - mm(low, guess)
    return guess.astype(F32) + mm(guess, rest.astype(BF16))


def pack_kernel(q_ref, k_ref, v_ref, out_ref):
    out_ref[:, 0:256] = q_ref[...]
    out_ref[:, 256:512] = k_ref[...]
    out_ref[:, 512:1024] = v_ref[...]


def map_kernel(
    k_ref, v_ref, rim_ref, decay_ref, beta_ref, doc_ref, wk_ref, wv_ref,
    wu_ref, kb_ref, own_ref, give_ref, ext_ref,
):
    row, col = rows_and_columns()
    lower = (col <= row).astype(BF16)
    eye = (col == row).astype(BF16)
    rim = rim_ref[...].astype(F32)[8:16]
    start = spread([local_start(doc_ref)], eye, 1)[0]
    valid = tap_masks(start)
    key_conv = short_conv(ext_ref, k_ref, rim[:, 256:512], wk_ref, valid)
    value_conv = short_conv(ext_ref, v_ref, rim[:, 512:1024], wv_ref, valid)
    keys = [k.astype(BF16) for k in unit_keys(key_conv)]
    decay = decay_ref[...]
    beta = beta_ref[...]
    cum_row = sum(mm_t(piece, lower) for piece in parts(decay, 3))
    cum_col = spread([decay[h : h + 1] for h in range(HEADS)], lower, 3)
    beta_col = spread([beta[h : h + 1] for h in range(HEADS)], eye, 2)
    keep = linked_mask(start)
    gram = [mm_t(k, k) for k in keys]
    flipped = [k.astype(F32).T for k in keys]
    core = lax.axis_index("ctx") % CORES
    for g in range(GROUPS):
        kb_ref[g] = keys[g]
    for h in range(HEADS):
        g = h // 2
        key = keys[g].astype(F32)
        fade = fading(cum_col[h], cum_row[h : h + 1], start, keep)
        beta_wide = jnp.concatenate([beta_col[h], beta_col[h]], axis=1)
        a = jnp.where(col < row, beta_wide * fade * gram[g], 0.0)
        t = unit_lower_inverse(a, row, col) * beta[h : h + 1]
        carry = jnp.where(start < 0.0, jnp.exp(cum_col[h]), 0.0)
        right = jnp.concatenate(
            [(carry * key).astype(BF16), value_conv[:, h * DV : (h + 1) * DV].astype(BF16)], axis=1
        )
        high, low = parts(t, 2)
        solved = (mm(high, right) + mm(low, right)).astype(BF16)
        wu_ref[h] = solved
        faded = (flipped[g] * fade[TOK - 1 : TOK, :]).astype(BF16)
        both = mm(faded, solved)
        r, c = rows_and_columns((DK, DK))
        diagonal = jnp.where(r == c, jnp.broadcast_to(carry[TOK - 1 : TOK, :], (DK, DK)), 0.0)
        step = jnp.concatenate([diagonal - both[:, :DK], both[:, DK:]], axis=1).astype(BF16)

        @pl.when(core == h // 2)
        def _():
            own_ref[h % 2] = step

        @pl.when(core != h // 2)
        def _():
            give_ref[h % 2] = step


def output_kernel(
    q_ref, rim_ref, decay_ref, doc_ref, wq_ref, kb_ref, wu_ref, out_ref, reach_ref, ext_ref
):
    row, col = rows_and_columns()
    lower = (col <= row).astype(BF16)
    eye = (col == row).astype(BF16)
    rim = rim_ref[...].astype(F32)[8:16]
    start = spread([local_start(doc_ref)], eye, 1)[0]
    query_conv = short_conv(ext_ref, q_ref, rim[:, 0:256], wq_ref, tap_masks(start))
    decay = decay_ref[...]
    cum_row = sum(mm_t(piece, lower) for piece in parts(decay, 3))
    cum_col = spread([decay[h : h + 1] for h in range(HEADS)], lower, 3)
    keep = linked_mask(start)
    scores = []
    for g in range(GROUPS):
        query = query_conv[:, g * DK : (g + 1) * DK].astype(BF16)
        scores.append(mm_t(query, kb_ref[g]))
    for h in range(HEADS):
        g = h // 2
        fade = fading(cum_col[h], cum_row[h : h + 1], start, keep)
        both = mm((fade * scores[g]).astype(BF16), wu_ref[h])
        carry = jnp.where(start < 0.0, jnp.exp(cum_col[h]), 0.0)
        reach = carry * query_conv[:, g * DK : (g + 1) * DK] - both[:, :DK]
        reach_ref[h] = reach.astype(BF16)
        out_ref[h] = both[:, DK:]


def joined(first, later):
    moved = mm(later[:, :DK], first)
    return jnp.concatenate([moved[:, :DK], moved[:, DK:] + later[:, DK:].astype(F32)], axis=1)


def pair_kernel(own_ref, got_ref, out_ref):
    core = lax.axis_index("ctx") % CORES
    for k in range(2):
        own = own_ref[k]
        got = got_ref[k]
        first = jnp.where(core == 0, own, got)
        later = jnp.where(core == 0, got, own)
        out_ref[k] = joined(first, later).astype(BF16)


def row_kernel(own_ref, one_ref, two_ref, three_ref, before_ref, total_ref, slots):
    x = (lax.axis_index("ctx") // CORES) % CHIPS_X
    for step, ref in enumerate((own_ref, one_ref, two_ref, three_ref)):
        slots[(x + CHIPS_X - step) % CHIPS_X] = ref[...]
    r, c = rows_and_columns((DK, DK + DV))
    start = (r == c).astype(BF16)
    for k in range(2):
        run = slots[0, k]
        before_ref[k] = jnp.where(x == 0, start, run)
        for place in range(1, CHIPS_X):
            run = joined(run, slots[place, k]).astype(BF16)
            if place < CHIPS_X - 1:
                before_ref[k] = jnp.where(x == place + 1, run, before_ref[k])
        total_ref[k] = run


def state_kernel(
    own_ref, one_ref, two_ref, three_ref, before_ref, mine_ref, other_ref, keep_ref, give_ref, slots
):
    index = lax.axis_index("ctx")
    core = index % CORES
    y = index // (CORES * CHIPS_X)
    for step, ref in enumerate((own_ref, one_ref, two_ref, three_ref)):
        slots[(y + CHIPS_Y - step) % CHIPS_Y] = ref[...]
    for k in range(2):
        state = jnp.where(y > 0, slots[0, k][:, DK:].astype(F32), 0.0)
        for place in range(1, CHIPS_Y - 1):
            block = slots[place, k]
            moved = mm(block[:, :DK], state.astype(BF16)) + block[:, DK:].astype(F32)
            state = jnp.where(place < y, moved, state)
        block = before_ref[k]
        state = mm(block[:, :DK], state.astype(BF16)) + block[:, DK:].astype(F32)
        block = jnp.where(core == 0, mine_ref[k], other_ref[k])
        after = mm(block[:, :DK], state.astype(BF16)) + block[:, DK:].astype(F32)
        keep_ref[k] = jnp.where(core == 0, state, after).astype(BF16)
        give_ref[k] = jnp.where(core == 0, after, state).astype(BF16)


def project_kernel(
    local_ref, reach_ref, mine_ref, got_ref, gate_ref, gain_ref, weight_ref, out_ref,
    weight_buf, normed_buf, sem,
):
    load = pltpu.make_async_copy(weight_ref, weight_buf, sem)
    load.start()
    core = lax.axis_index("ctx") % CORES
    for h in range(HEADS):
        state = jnp.where(core == h // 2, mine_ref[h % 2], got_ref[h % 2])
        heads = local_ref[h] + mm(reach_ref[h], state)
        inv = lax.rsqrt(jnp.mean(heads * heads, axis=-1, keepdims=True) + EPS)
        gate = gate_ref[:, h * DV : (h + 1) * DV].astype(F32)
        gate = gate * jax.nn.sigmoid(gate)
        normed_buf[:, h * DV : (h + 1) * DV] = (heads * inv * gain_ref[...] * gate).astype(BF16)
    load.wait()
    normed = normed_buf[...]
    for part in range(0, weight_buf.shape[1], 512):
        out_ref[:, part : part + 512] = mm(normed, weight_buf[:, part : part + 512]).astype(BF16)


def sum_kernel(in_ref, out_ref):
    total = in_ref[0].astype(F32)
    for k in range(1, in_ref.shape[0]):
        total = total + in_ref[k].astype(F32)
    out_ref[...] = total.astype(BF16)


VMEM = pl.BlockSpec(memory_space=pltpu.VMEM)


def call(kernel, outs, inputs, scratch=(), flops=0, moved=0, limit=32, specs=None):
    return pl.pallas_call(
        kernel,
        out_shape=[jax.ShapeDtypeStruct(s, t) for s, t in outs],
        in_specs=[VMEM] * len(inputs) if specs is None else specs,
        out_specs=[VMEM] * len(outs),
        scratch_shapes=list(scratch),
        compiler_params=pltpu.CompilerParams(vmem_limit_bytes=limit * MIB),
        cost_estimate=pl.CostEstimate(flops=flops, bytes_accessed=moved, transcendentals=0),
    )(*inputs)


def on_device(
    query_in, key_in, value_in, out_gate, log_decay, beta_gate, doc_start,
    conv_query, conv_key, conv_value, norm_gain, out_weight,
):
    doc_row = doc_start.reshape(1, TOK)
    gain_row = norm_gain.reshape(1, DV)
    last = TOK // RIM - 1
    rim = pl.pallas_call(
        pack_kernel,
        grid=(1,),
        out_shape=jax.ShapeDtypeStruct((RIM, 1024), BF16),
        in_specs=[
            pl.BlockSpec((RIM, 256), lambda i: (last, 0)),
            pl.BlockSpec((RIM, 256), lambda i: (last, 0)),
            pl.BlockSpec((RIM, 512), lambda i: (last, 0)),
        ],
        out_specs=pl.BlockSpec((RIM, 1024), lambda i: (0, 0)),
    )(query_in, key_in, value_in)
    rim = lax.ppermute(rim, "ctx", [(i, i + 1) for i in range(CTX - 1)])
    wide = (2, DK, DK + DV)
    solved, keys, own, give = call(
        map_kernel,
        [((HEADS, TOK, DK + DV), BF16), ((GROUPS, TOK, DK), BF16), (wide, BF16), (wide, BF16)],
        [key_in, value_in, rim, log_decay, beta_gate, doc_row, conv_key, conv_value],
        [pltpu.VMEM((8 + TOK, 512), F32)],
        flops=4_000_000_000, moved=2_000_000,
    )
    other = lax.ppermute(give, "ctx", core_swap())
    (pair,) = call(pair_kernel, [(wide, BF16)], [own, other], flops=20_000_000, moved=400_000)
    near = [lax.ppermute(pair, "ctx", along_x(k)) for k in (1, 2, 3)]
    local, reach = call(
        output_kernel,
        [((HEADS, TOK, DV), F32), ((HEADS, TOK, DK), BF16)],
        [query_in, rim, log_decay, doc_row, conv_query, keys, solved],
        [pltpu.VMEM((8 + TOK, 256), F32)],
        flops=2_000_000_000, moved=2_000_000,
    )
    before, total = call(
        row_kernel, [(wide, BF16), (wide, BF16)], [pair] + near,
        [pltpu.VMEM((CHIPS_X,) + wide, BF16)], flops=60_000_000, moved=800_000,
    )
    far = [lax.ppermute(total, "ctx", along_y(k)) for k in (1, 2, 3)]
    narrow = (2, DK, DV)
    mine, to_other = call(
        state_kernel, [(narrow, BF16), (narrow, BF16)], [total] + far + [before, own, other],
        [pltpu.VMEM((CHIPS_Y,) + wide, BF16)], flops=60_000_000, moved=1_000_000,
    )
    got = lax.ppermute(to_other, "ctx", core_swap())
    width = out_weight.shape[1]
    (partial,) = call(
        project_kernel,
        [((TOK, width), BF16)],
        [local, reach, mine, got, out_gate, gain_row, out_weight],
        [
            pltpu.VMEM(out_weight.shape, BF16),
            pltpu.VMEM((TOK, HEADS * DV), BF16),
            pltpu.SemaphoreType.DMA,
        ],
        flops=600_000_000, moved=4_000_000,
        specs=[VMEM] * 6 + [pl.BlockSpec(memory_space=pl.ANY)],
    )
    groups = lax.axis_size("head")
    blocks = lax.all_to_all(
        partial.reshape(groups, TOK // groups, width), "head", 0, 0
    )
    (mixed,) = call(
        sum_kernel, [((TOK // groups, width), BF16)], [blocks], flops=1_000_000, moved=1_200_000
    )
    return mixed


def solution(mesh):
    placed = (
        P("ctx", "head"),
        P("ctx", "head"),
        P("ctx", "head"),
        P("ctx", "head"),
        P("head", "ctx"),
        P("head", "ctx"),
        P("ctx"),
        P(None, "head"),
        P(None, "head"),
        P(None, "head"),
        P(),
        P("head", None),
    )
    return jax.shard_map(
        on_device, mesh=mesh, in_specs=placed, out_specs=P(("ctx", "head"), None), check_vma=False
    )
```

time: 341 us -> 94.3 us (0.28)
  the two profiles are of different devices: /device:TPU:6 before, /device:TPU:1 now
where the time goes in v1:
time: 94.3 us; the launch traced here: 93.9 us
  blocking collectives  37.2 us (39%)
  waiting for transfers between devices  20 us (21%)
  Pallas kernels  17.2 us (18%)
  starting transfers between devices  13.5 us (14%)
  local copies, waits for them, and re-layouts  6.02 us (6%)
    all_to_all x1, blocking collectives, on_device(): lax.all_to_all(partial.reshape(groups, TOK // groups, width), 'head', 0, 0)  37.2 us
    pallas_call x7, Pallas kernels, call(): pl.pallas_call(kernel, out_shape=[jax.ShapeDtypeStruct(s, t) for s, t in...  15.8 us
    ppermute x3, waiting for transfers between devices, on_device(): far = [lax.ppermute(total, 'ctx', along_y(k)) for k in (1, 2, 3)]  8.69 us
    ppermute x3, waiting for transfers between devices, on_device(): near = [lax.ppermute(pair, 'ctx', along_x(k)) for k in (1, 2, 3)]  8.6 us
    unnamed x28, local copies, waits for them, and re-layouts  6.02 us
    ppermute x1, starting transfers between devices, on_device(): rim = lax.ppermute(rim, 'ctx', [(i, i + 1) for i in range(CTX - 1)])  4.5 us
    ppermute x3, starting transfers between devices, on_device(): near = [lax.ppermute(pair, 'ctx', along_x(k)) for k in (1, 2, 3)]  4.43 us
    ppermute x3, starting transfers between devices, on_device(): far = [lax.ppermute(total, 'ctx', along_y(k)) for k in (1, 2, 3)]  3.85 us
  transfers between devices with their start and end apart: 9, of which 8 were waited for; matrix products, arithmetic and copies ran while one was open for 0% of the time, Pallas kernels for 1%

profile of v1, /device:TPU:1, one launch (start us, length us, event | category | flops | bytes accessed | tf_op | source)
XLA Modules:
  0.0 93.9 jit_solution(15951901708921475976)
XLA Ops:
  0.0 1.4 %shard_map.118 = bf16[16,1024]{1,0:T(8,128)(2,1)} custom-call(bf16[256,256]{1,0:T(8,128)(2,1)} %q_ref.3, bf16[256,256]{1,0:T(8,128)(2,1)} %k_ref.3, bf16[256,512]{1,0:T(8,128)(2,1)} %v_ref.3), custom_call_target="tpu_custom_call" | custom-call | tf_op jit(solution)/shard_map/pallas_call | solution.py:336
  1.4 4.5 %collective-permute-start = (bf16[16,1024]{1,0:T(8,128)(2,1)}, bf16[16,1024]{1,0:T(8,128)(2,1)S(1)}, u32[]{:S(2)}, u32[]{:S(2)}) collective-permute-start(bf16[16,1024]{1,0:T(8,128)(2,1)} %shard_map.118), channel_id=1, source_target_pairs={{0,8},{8,16},{16,24},{24,32},{32,40},{40,48},{48,56},{56,64},{64,7... | collective-permute-start | bytes 98312 | tf_op jit(solution)/shard_map/ppermute | solution.py:347
  5.9 1.3 %collective-permute-done.rim_ref = bf16[16,1024]{1,0:T(8,128)(2,1)S(1)} collective-permute-done((bf16[16,1024]{1,0:T(8,128)(2,1)}, bf16[16,1024]{1,0:T(8,128)(2,1)S(1)}, u32[]{:S(2)}, u32[]{:S(2)}) %collective-permute-start) | collective-permute-done | bytes 32800 | tf_op jit(solution)/shard_map/ppermute | solution.py:347
  7.2 0.0 copy-start.2
  7.2 0.9 %copy-done.2 = bf16[256,512]{1,0:T(8,128)(2,1)S(1)} copy-done((bf16[256,512]{1,0:T(8,128)(2,1)S(1)}, bf16[256,512]{1,0:T(8,128)(2,1)}, u32[]{:S(2)}) %copy-start.2) | copy-done | bytes 262168
  8.1 0.0 copy-start.3
  8.1 0.9 copy-done.3
  9.0 0.0 copy-start.6
  9.0 0.7 copy-done.6
  9.7 0.0 copy-start.7
  9.7 0.7 copy-done.7
  10.4 0.0 copy-start.8
  10.4 0.7 copy-done.8
  11.1 0.0 copy-start.9
  11.1 0.7 copy-done.9
  11.8 0.0 copy-start.12
  11.8 0.7 copy-done.12
  12.5 0.0 copy-start.4
  12.5 0.0 copy-start.10
  12.5 0.0 copy-start.11
  12.5 0.0 copy-start.13
  12.5 11.1 %shard_map.119 = (bf16[4,256,256]{2,1,0:T(8,128)(2,1)S(1)}, bf16[2,256,128]{2,1,0:T(8,128)(2,1)S(1)}, bf16[2,128,256]{2,1,0:T(8,128)(2,1)S(1)}, bf16[2,128,256]{2,1,0:T(8,128)(2,1)S(1)}) custom-call(bf16[256,256]{1,0:T(8,128)(2,1)S(1)} %copy-done.3, bf16[256,512]{1,0:T(8,128)(2,1)S(1)} %copy-done.2, bf16[16,1024]{1,0:T(8,128)(2,1)S(1)} %collective-permute-done.rim_ref, ...), custom_call_target="tpu_custom_call" | custom-call | flops 4000000000 | bytes 2000000 | tf_op jit(solution)/shard_map/pallas_call | solution.py:318
  23.6 0.1 collective-permute-start.1
  23.7 1.3 %collective-permute-done.1.got_ref.other_ref = bf16[2,128,256]{2,1,0:T(8,128)(2,1)S(1)} collective-permute-done((bf16[2,128,256]{2,1,0:T(8,128)(2,1)S(1)}, bf16[2,128,256]{2,1,0:T(8,128)(2,1)S(1)}, u32[]{:S(2)}, u32[]{:S(2)}) %collective-permute-start.1) | collective-permute-done | bytes 131104 | tf_op jit(solution)/shard_map/ppermute | solution.py:356
  25.1 0.2 shard_map.121.own_ref
  25.3 3.3 %collective-permute-start.4 = (bf16[2,128,256]{2,1,0:T(8,128)(2,1)S(1)}, bf16[2,128,256]{2,1,0:T(8,128)(2,1)S(1)}, u32[]{:S(2)}, u32[]{:S(2)}) collective-permute-start(bf16[2,128,256]{2,1,0:T(8,128)(2,1)S(1)} %shard_map.121.own_ref), channel_id=1, source_target_pairs={{0,48},{8,56},{16,0},{24,8},{32,16},{40,24},{48,32},{56,40},{64,11... | collective-permute-start | bytes 393224 | tf_op jit(solution)/shard_map/ppermute | solution.py:358
  28.6 0.5 collective-permute-start.3
  29.1 0.6 collective-permute-start.2
  29.7 4.1 %collective-permute-done.4.three_ref = bf16[2,128,256]{2,1,0:T(8,128)(2,1)S(1)} collective-permute-done((bf16[2,128,256]{2,1,0:T(8,128)(2,1)S(1)}, bf16[2,128,256]{2,1,0:T(8,128)(2,1)S(1)}, u32[]{:S(2)}, u32[]{:S(2)}) %collective-permute-start.4) | collective-permute-done | bytes 131104 | tf_op jit(solution)/shard_map/ppermute | solution.py:358
  33.7 0.7 collective-permute-done.3.two_ref
  34.5 3.8 %collective-permute-done.2.one_ref = bf16[2,128,256]{2,1,0:T(8,128)(2,1)S(1)} collective-permute-done((bf16[2,128,256]{2,1,0:T(8,128)(2,1)S(1)}, bf16[2,128,256]{2,1,0:T(8,128)(2,1)S(1)}, u32[]{:S(2)}, u32[]{:S(2)}) %collective-permute-start.2) | collective-permute-done | bytes 131104 | tf_op jit(solution)/shard_map/ppermute | solution.py:358
  38.3 0.7 shard_map.122
  39.0 2.8 %collective-permute-start.7 = (bf16[2,128,256]{2,1,0:T(8,128)(2,1)S(1)}, bf16[2,128,256]{2,1,0:T(8,128)(2,1)S(1)}, u32[]{:S(2)}, u32[]{:S(2)}) collective-permute-start(bf16[2,128,256]{2,1,0:T(8,128)(2,1)S(1)} %get-tuple-element.21.own_ref), channel_id=1, source_target_pairs={{0,192},{8,200},{16,208},{24,216},{32,224},{40,232},{48,240},{56,2... | collective-permute-start | bytes 393224 | tf_op jit(solution)/shard_map/ppermute | solution.py:370
  41.8 0.3 collective-permute-start.6
  42.2 0.7 collective-permute-start.5
  42.8 4.1 %collective-permute-done.7.three_ref = bf16[2,128,256]{2,1,0:T(8,128)(2,1)S(1)} collective-permute-done((bf16[2,128,256]{2,1,0:T(8,128)(2,1)S(1)}, bf16[2,128,256]{2,1,0:T(8,128)(2,1)S(1)}, u32[]{:S(2)}, u32[]{:S(2)}) %collective-permute-start.7) | collective-permute-done | bytes 131104 | tf_op jit(solution)/shard_map/ppermute | solution.py:370
  46.9 0.6 collective-permute-done.6.two_ref
  47.6 4.0 %collective-permute-done.5.one_ref = bf16[2,128,256]{2,1,0:T(8,128)(2,1)S(1)} collective-permute-done((bf16[2,128,256]{2,1,0:T(8,128)(2,1)S(1)}, bf16[2,128,256]{2,1,0:T(8,128)(2,1)S(1)}, u32[]{:S(2)}, u32[]{:S(2)}) %collective-permute-start.5) | collective-permute-done | bytes 131104 | tf_op jit(solution)/shard_map/ppermute | solution.py:370
  51.5 0.9 shard_map.123
  52.4 0.6 collective-permute-start.8
  53.0 0.0 copy-done.4
  53.0 0.0 copy-done.10
  53.0 0.0 copy-done.11
  53.0 0.0 copy-done.13
  53.0 0.0 copy-start
  53.0 0.0 copy-start.1
  53.1 0.0 copy-start.5
  53.1 0.8 shard_map.120
  53.9 0.0 collective-permute-done.8.got_ref
  53.9 0.7 copy-done
  54.6 0.0 copy-done.1
  54.6 0.0 copy-done.5
  54.6 1.3 %shard_map.124 = bf16[256,2048]{1,0:T(8,128)(2,1)S(1)} custom-call(f32[4,256,128]{2,1,0:T(8,128)S(1)} %get-tuple-element.17.local_ref, bf16[4,256,128]{2,1,0:T(8,128)(2,1)S(1)} %get-tuple-element.18.reach_ref, bf16[2,128,128]{2,1,0:T(8,128)(2,1)S(1)} %get-tuple-element.23.mine_ref, bf16[2,128,128]{2,1,0:T(8,128)(2,1)S(1)} %collective-permute-done.8.got_ref, ...), custom_call_target="tpu_custom_call" | custom-call | flops 600000000 | bytes 4000000 | tf_op jit(solution)/shard_map/pallas_call | solution.py:318
  55.9 37.2 %all_to_all.5.in_ref = bf16[8,32,2048]{2,1,0:T(8,128)(2,1)S(1)} all-to-all(bf16[8,32,2048]{2,1,0:T(8,128)(2,1)S(1)} %bitcast.3), channel_id=1, replica_groups=mesh['ctx'=32,'head'=8] {'head'}, dimensions={0} | all-to-all | bytes 2097152 | tf_op jit(solution)/shard_map/all_to_all | solution.py:391
  93.1 0.8 shard_map.125
Async XLA Ops:
  1.4 5.8 %collective-permute-start = (bf16[16,1024]{1,0:T(8,128)(2,1)}, bf16[16,1024]{1,0:T(8,128)(2,1)S(1)}, u32[]{:S(2)}, u32[]{:S(2)}) collective-permute-start(bf16[16,1024]{1,0:T(8,128)(2,1)} %shard_map.118), channel_id=1, source_target_pairs={{0,8},{8,16},{16,24},{24,32},{32,40},{40,48},{48,56},{56,64},{64,7... | collective-permute-start | bytes 98312 | tf_op jit(solution)/shard_map/ppermute | solution.py:347
  7.2 0.9 %copy-start.2 = (bf16[256,512]{1,0:T(8,128)(2,1)S(1)}, bf16[256,512]{1,0:T(8,128)(2,1)}, u32[]{:S(2)}) copy-start(bf16[256,512]{1,0:T(8,128)(2,1)} %v_ref.3) | copy-start | bytes 786436
  8.1 0.9 copy-start.3
  9.0 0.7 copy-start.6
  9.7 0.7 copy-start.7
  10.4 0.7 copy-start.8
  11.1 0.7 copy-start.9
  11.8 0.7 copy-start.12
  12.5 40.5 %copy-start.4 = (bf16[256,256]{1,0:T(8,128)(2,1)S(1)}, bf16[256,256]{1,0:T(8,128)(2,1)}, u32[]{:S(2)}) copy-start(bf16[256,256]{1,0:T(8,128)(2,1)} %q_ref.3) | copy-start | bytes 393220
  12.5 40.5 %copy-start.10 = (f32[4,256]{1,0:T(4,128)S(1)}, f32[4,256]{1,0:T(4,128)}, u32[]{:S(2)}) copy-start(f32[4,256]{1,0:T(4,128)} %decay_ref.3) | copy-start | bytes 12292
  12.5 40.5 %copy-start.11 = (f32[4,256]{1,0:T(4,128)S(1)}, f32[4,256]{1,0:T(4,128)}, u32[]{:S(2)}) copy-start(f32[4,256]{1,0:T(4,128)} %wq_ref.1) | copy-start | bytes 12292
  12.5 40.5 %copy-start.13 = (s32[256]{0:T(256)S(1)}, s32[256]{0:T(256)}, u32[]{:S(2)}) copy-start(s32[256]{0:T(256)} %param.18) | copy-start | bytes 3076
  23.6 1.4 %collective-permute-start.1 = (bf16[2,128,256]{2,1,0:T(8,128)(2,1)S(1)}, bf16[2,128,256]{2,1,0:T(8,128)(2,1)S(1)}, u32[]{:S(2)}, u32[]{:S(2)}) collective-permute-start(bf16[2,128,256]{2,1,0:T(8,128)(2,1)S(1)} %get-tuple-element.20), channel_id=1, source_target_pairs={{0,8},{8,0},{16,24},{24,16},{32,40},{40,32},{48,56},{56,48},{64,72... | collective-permute-start | bytes 393224 | tf_op jit(solution)/shard_map/ppermute | solution.py:356
  25.3 8.5 %collective-permute-start.4 = (bf16[2,128,256]{2,1,0:T(8,128)(2,1)S(1)}, bf16[2,128,256]{2,1,0:T(8,128)(2,1)S(1)}, u32[]{:S(2)}, u32[]{:S(2)}) collective-permute-start(bf16[2,128,256]{2,1,0:T(8,128)(2,1)S(1)} %shard_map.121.own_ref), channel_id=1, source_target_pairs={{0,48},{8,56},{16,0},{24,8},{32,16},{40,24},{48,32},{56,40},{64,11... | collective-permute-start | bytes 393224 | tf_op jit(solution)/shard_map/ppermute | solution.py:358
  28.6 5.9 %collective-permute-start.3 = (bf16[2,128,256]{2,1,0:T(8,128)(2,1)S(1)}, bf16[2,128,256]{2,1,0:T(8,128)(2,1)S(1)}, u32[]{:S(2)}, u32[]{:S(2)}) collective-permute-start(bf16[2,128,256]{2,1,0:T(8,128)(2,1)S(1)} %shard_map.121.own_ref), channel_id=1, source_target_pairs={{0,32},{8,40},{16,48},{24,56},{32,0},{40,8},{48,16},{56,24},{64,96... | collective-permute-start | bytes 393224 | tf_op jit(solution)/shard_map/ppermute | solution.py:358
  29.1 9.2 %collective-permute-start.2 = (bf16[2,128,256]{2,1,0:T(8,128)(2,1)S(1)}, bf16[2,128,256]{2,1,0:T(8,128)(2,1)S(1)}, u32[]{:S(2)}, u32[]{:S(2)}) collective-permute-start(bf16[2,128,256]{2,1,0:T(8,128)(2,1)S(1)} %shard_map.121.own_ref), channel_id=1, source_target_pairs={{0,16},{8,24},{16,32},{24,40},{32,48},{40,56},{48,0},{56,8},{64,80... | collective-permute-start | bytes 393224 | tf_op jit(solution)/shard_map/ppermute | solution.py:358
  39.0 7.9 %collective-permute-start.7 = (bf16[2,128,256]{2,1,0:T(8,128)(2,1)S(1)}, bf16[2,128,256]{2,1,0:T(8,128)(2,1)S(1)}, u32[]{:S(2)}, u32[]{:S(2)}) collective-permute-start(bf16[2,128,256]{2,1,0:T(8,128)(2,1)S(1)} %get-tuple-element.21.own_ref), channel_id=1, source_target_pairs={{0,192},{8,200},{16,208},{24,216},{32,224},{40,232},{48,240},{56,2... | collective-permute-start | bytes 393224 | tf_op jit(solution)/shard_map/ppermute | solution.py:370
  41.8 5.8 %collective-permute-start.6 = (bf16[2,128,256]{2,1,0:T(8,128)(2,1)S(1)}, bf16[2,128,256]{2,1,0:T(8,128)(2,1)S(1)}, u32[]{:S(2)}, u32[]{:S(2)}) collective-permute-start(bf16[2,128,256]{2,1,0:T(8,128)(2,1)S(1)} %get-tuple-element.21.own_ref), channel_id=1, source_target_pairs={{0,128},{8,136},{16,144},{24,152},{32,160},{40,168},{48,176},{56,1... | collective-permute-start | bytes 393224 | tf_op jit(solution)/shard_map/ppermute | solution.py:370
  42.2 9.4 %collective-permute-start.5 = (bf16[2,128,256]{2,1,0:T(8,128)(2,1)S(1)}, bf16[2,128,256]{2,1,0:T(8,128)(2,1)S(1)}, u32[]{:S(2)}, u32[]{:S(2)}) collective-permute-start(bf16[2,128,256]{2,1,0:T(8,128)(2,1)S(1)} %get-tuple-element.21.own_ref), channel_id=1, source_target_pairs={{0,64},{8,72},{16,80},{24,88},{32,96},{40,104},{48,112},{56,120},{... | collective-permute-start | bytes 393224 | tf_op jit(solution)/shard_map/ppermute | solution.py:370
  52.4 1.5 %collective-permute-start.8 = (bf16[2,128,128]{2,1,0:T(8,128)(2,1)S(1)}, bf16[2,128,128]{2,1,0:T(8,128)(2,1)S(1)}, u32[]{:S(2)}, u32[]{:S(2)}) collective-permute-start(bf16[2,128,128]{2,1,0:T(8,128)(2,1)S(1)} %get-tuple-element.24), channel_id=1, source_target_pairs={{0,8},{8,0},{16,24},{24,16},{32,40},{40,32},{48,56},{56,48},{64,72... | collective-permute-start | bytes 196616 | tf_op jit(solution)/shard_map/ppermute | solution.py:376
  53.0 1.6 %copy-start = (bf16[512,2048]{1,0:T(8,128)(2,1)S(1)}, bf16[512,2048]{1,0:T(8,128)(2,1)}, u32[]{:S(2)}) copy-start(bf16[512,2048]{1,0:T(8,128)(2,1)} %weight_ref.1) | copy-start | bytes 6291460
  53.0 1.6 %copy-start.1 = (bf16[256,512]{1,0:T(8,128)(2,1)S(1)}, bf16[256,512]{1,0:T(8,128)(2,1)}, u32[]{:S(2)}) copy-start(bf16[256,512]{1,0:T(8,128)(2,1)} %gate_ref.1) | copy-start | bytes 786436
  53.1 1.6 %copy-start.5 = (f32[128]{0:T(128)S(1)}, f32[128]{0:T(128)}, u32[]{:S(2)}) copy-start(f32[128]{0:T(128)} %param.22) | copy-start | bytes 1540

commit v2 on v1

--- a/solution.py
+++ b/solution.py
@@ -145,31 +145,99 @@
     return guess.astype(F32) + mm(guess, rest.astype(BF16))
 
 
-def pack_kernel(q_ref, k_ref, v_ref, out_ref):
-    out_ref[:, 0:256] = q_ref[...]
-    out_ref[:, 256:512] = k_ref[...]
-    out_ref[:, 512:1024] = v_ref[...]
-
-
-def map_kernel(
-    k_ref, v_ref, rim_ref, decay_ref, beta_ref, doc_ref, wk_ref, wv_ref,
-    wu_ref, kb_ref, own_ref, give_ref, ext_ref,
+def pack_kernel(k_ref, v_ref, q_ref, out_ref, sems):
+    rows = pl.ds(TOK - RIM, RIM)
+    copies = [
+        pltpu.make_async_copy(k_ref.at[rows], out_ref.at[:, 0:256], sems.at[0]),
+        pltpu.make_async_copy(v_ref.at[rows], out_ref.at[:, 256:768], sems.at[1]),
+        pltpu.make_async_copy(q_ref.at[rows], out_ref.at[:, 768:1024], sems.at[2]),
+    ]
+    for copy in copies:
+        copy.start()
+    for copy in copies:
+        copy.wait()
+
+
+def half_kernel(weight_ref, after_ref, out_ref, sem):
+    core = lax.axis_index("ctx") % CORES
+    rows = weight_ref.shape[0] // CORES
+    copy = pltpu.make_async_copy(weight_ref.at[pl.ds(core * rows, rows)], out_ref, sem)
+    copy.start()
+    copy.wait()
+
+
+def early_kernel(
+    k_hbm, v_hbm, decay_hbm, beta_hbm, doc_hbm, wk_hbm, wv_hbm,
+    key_ref, value_ref, factor_ref, carry_ref, last_ref, start_ref, head_ref,
+    k_ref, v_ref, decay_ref, beta_ref, doc_ref, wk_ref, wv_ref, ext_ref, sems,
 ):
+    moves = (
+        (doc_hbm, doc_ref), (decay_hbm, decay_ref), (beta_hbm, beta_ref), (k_hbm, k_ref),
+        (wk_hbm, wk_ref), (v_hbm, v_ref), (wv_hbm, wv_ref),
+    )
+    copies = [pltpu.make_async_copy(a, b, sems.at[i]) for i, (a, b) in enumerate(moves)]
+    for copy in copies:
+        copy.start()
     row, col = rows_and_columns()
     lower = (col <= row).astype(BF16)
     eye = (col == row).astype(BF16)
-    rim = rim_ref[...].astype(F32)[8:16]
+    for copy in copies[:3]:
+        copy.wait()
     start = spread([local_start(doc_ref)], eye, 1)[0]
-    valid = tap_masks(start)
-    key_conv = short_conv(ext_ref, k_ref, rim[:, 256:512], wk_ref, valid)
-    value_conv = short_conv(ext_ref, v_ref, rim[:, 512:1024], wv_ref, valid)
-    keys = [k.astype(BF16) for k in unit_keys(key_conv)]
+    start_ref[...] = start[0:RIM]
     decay = decay_ref[...]
     beta = beta_ref[...]
     cum_row = sum(mm_t(piece, lower) for piece in parts(decay, 3))
     cum_col = spread([decay[h : h + 1] for h in range(HEADS)], lower, 3)
     beta_col = spread([beta[h : h + 1] for h in range(HEADS)], eye, 2)
     keep = linked_mask(start)
+    for h in range(HEADS):
+        fade = fading(cum_col[h], cum_row[h : h + 1], start, keep)
+        beta_wide = jnp.concatenate([beta_col[h], beta_col[h]], axis=1)
+        factor_ref[h] = jnp.where(col < row, beta_wide * fade, 0.0)
+        carry_ref[h] = jnp.where(start < 0.0, jnp.exp(cum_col[h]), 0.0)
+        last_ref[h : h + 1] = fade[TOK - 1 : TOK, :]
+    for copy in copies[3:]:
+        copy.wait()
+    valid = tap_masks(start)
+    key_conv = short_conv(ext_ref, k_ref, jnp.zeros((8, 256), F32), wk_ref, valid)
+    for g, key in enumerate(unit_keys(key_conv)):
+        key_ref[g] = key.astype(BF16)
+    value_conv = short_conv(ext_ref, v_ref, jnp.zeros((8, 512), F32), wv_ref, valid)
+    value_ref[...] = value_conv.astype(BF16)
+    head_ref[:, 0:256] = k_ref[0:RIM, :]
+    head_ref[:, 256:768] = v_ref[0:RIM, :]
+
+
+def first_rows(rim, own, w_ref, start):
+    width = own.shape[1]
+    ext = jnp.concatenate([rim, own], axis=0)
+    token = lax.broadcasted_iota(jnp.int32, (8, 128), 0).astype(F32)
+    total = own * w_ref[0:1, :]
+    for tap in range(1, TAPS):
+        mask = jnp.concatenate([start <= token - tap] * (width // 128), axis=1)
+        total = total + jnp.where(mask, ext[8 - tap : 16 - tap] * w_ref[tap : tap + 1, :], 0.0)
+    return total * jax.nn.sigmoid(total)
+
+
+def map_kernel(
+    rim_ref, head_ref, start_ref, key_ref, value_ref, factor_ref, carry_ref, last_ref, beta_ref,
+    wk_ref, wv_ref, wu_ref, kb_ref, own_ref, give_ref,
+):
+    row, col = rows_and_columns()
+    rim = rim_ref[...].astype(F32)[8:16]
+    head = head_ref[...].astype(F32)[0:8]
+    start = start_ref[0:8]
+    first_keys = unit_keys(first_rows(rim[:, 0:256], head[:, 0:256], wk_ref, start))
+    first_values = first_rows(rim[:, 256:768], head[:, 256:768], wv_ref, start)
+
+    def patched(first, whole):
+        whole = whole.astype(F32)
+        return jnp.concatenate([first, whole[8:]], axis=0)
+
+    keys = [patched(first_keys[g], key_ref[g]).astype(BF16) for g in range(GROUPS)]
+    values = patched(first_values, value_ref[...]).astype(BF16)
+    beta = beta_ref[...]
     gram = [mm_t(k, k) for k in keys]
     flipped = [k.astype(F32).T for k in keys]
     core = lax.axis_index("ctx") % CORES
@@ -178,18 +246,13 @@
     for h in range(HEADS):
         g = h // 2
         key = keys[g].astype(F32)
-        fade = fading(cum_col[h], cum_row[h : h + 1], start, keep)
-        beta_wide = jnp.concatenate([beta_col[h], beta_col[h]], axis=1)
-        a = jnp.where(col < row, beta_wide * fade * gram[g], 0.0)
-        t = unit_lower_inverse(a, row, col) * beta[h : h + 1]
-        carry = jnp.where(start < 0.0, jnp.exp(cum_col[h]), 0.0)
-        right = jnp.concatenate(
-            [(carry * key).astype(BF16), value_conv[:, h * DV : (h + 1) * DV].astype(BF16)], axis=1
-        )
+        t = unit_lower_inverse(factor_ref[h] * gram[g], row, col) * beta[h : h + 1]
+        carry = carry_ref[h]
+        right = jnp.concatenate([(carry * key).astype(BF16), values[:, h * DV : (h + 1) * DV]], axis=1)
         high, low = parts(t, 2)
         solved = (mm(high, right) + mm(low, right)).astype(BF16)
         wu_ref[h] = solved
-        faded = (flipped[g] * fade[TOK - 1 : TOK, :]).astype(BF16)
+        faded = (flipped[g] * last_ref[h : h + 1, :]).astype(BF16)
         both = mm(faded, solved)
         r, c = rows_and_columns((DK, DK))
         diagonal = jnp.where(r == c, jnp.broadcast_to(carry[TOK - 1 : TOK, :], (DK, DK)), 0.0)
@@ -212,7 +275,7 @@
     eye = (col == row).astype(BF16)
     rim = rim_ref[...].astype(F32)[8:16]
     start = spread([local_start(doc_ref)], eye, 1)[0]
-    query_conv = short_conv(ext_ref, q_ref, rim[:, 0:256], wq_ref, tap_masks(start))
+    query_conv = short_conv(ext_ref, q_ref, rim[:, 768:1024], wq_ref, tap_masks(start))
     decay = decay_ref[...]
     cum_row = sum(mm_t(piece, lower) for piece in parts(decay, 3))
     cum_col = spread([decay[h : h + 1] for h in range(HEADS)], lower, 3)
@@ -246,7 +309,7 @@
         out_ref[k] = joined(first, later).astype(BF16)
 
 
-def row_kernel(own_ref, one_ref, two_ref, three_ref, before_ref, total_ref, slots):
+def row_kernel(own_ref, one_ref, two_ref, three_ref, after_ref, before_ref, total_ref, slots):
     x = (lax.axis_index("ctx") // CORES) % CHIPS_X
     for step, ref in enumerate((own_ref, one_ref, two_ref, three_ref)):
         slots[(x + CHIPS_X - step) % CHIPS_X] = ref[...]
@@ -284,24 +347,36 @@
         give_ref[k] = jnp.where(core == 0, after, state).astype(BF16)
 
 
-def project_kernel(
-    local_ref, reach_ref, mine_ref, got_ref, gate_ref, gain_ref, weight_ref, out_ref,
-    weight_buf, normed_buf, sem,
-):
-    load = pltpu.make_async_copy(weight_ref, weight_buf, sem)
-    load.start()
+def norm_kernel(local_ref, reach_ref, mine_ref, got_ref, gate_ref, gain_ref, keep_ref, give_ref):
     core = lax.axis_index("ctx") % CORES
+    side = lax.axis_index("head") % 2
     for h in range(HEADS):
         state = jnp.where(core == h // 2, mine_ref[h % 2], got_ref[h % 2])
         heads = local_ref[h] + mm(reach_ref[h], state)
         inv = lax.rsqrt(jnp.mean(heads * heads, axis=-1, keepdims=True) + EPS)
         gate = gate_ref[:, h * DV : (h + 1) * DV].astype(F32)
         gate = gate * jax.nn.sigmoid(gate)
-        normed_buf[:, h * DV : (h + 1) * DV] = (heads * inv * gain_ref[...] * gate).astype(BF16)
-    load.wait()
-    normed = normed_buf[...]
-    for part in range(0, weight_buf.shape[1], 512):
-        out_ref[:, part : part + 512] = mm(normed, weight_buf[:, part : part + 512]).astype(BF16)
+        normed = (heads * inv * gain_ref[...] * gate).astype(BF16)
+        rows = TOK // 8
+        for block in range(4):
+            even = normed[2 * block * rows : (2 * block + 1) * rows]
+            odd = normed[(2 * block + 1) * rows : (2 * block + 2) * rows]
+            at = (slice(block * rows, (block + 1) * rows), slice(h * DV, (h + 1) * DV))
+            keep_ref[at] = jnp.where(side == 0, even, odd)
+            give_ref[at] = jnp.where(side == 0, odd, even)
+
+
+def project_kernel(keep_ref, got_ref, own_ref, near_ref, far_ref, out_ref):
+    core = lax.axis_index("ctx") % CORES
+    keep = keep_ref[...]
+    got = got_ref[...]
+    half = got.shape[1] // 2
+    first = jnp.where(core == 0, got[:, :half], got[:, half:])
+    second = jnp.where(core == 0, got[:, half:], got[:, :half])
+    for part in range(0, own_ref.shape[1], 512):
+        at = slice(part, part + 512)
+        total = mm(keep, own_ref[:, at]) + mm(first, near_ref[:, at]) + mm(second, far_ref[:, at])
+        out_ref[:, at] = total.astype(BF16)
 
 
 def sum_kernel(in_ref, out_ref):
@@ -312,14 +387,15 @@
 
 
 VMEM = pl.BlockSpec(memory_space=pltpu.VMEM)
-
-
-def call(kernel, outs, inputs, scratch=(), flops=0, moved=0, limit=32, specs=None):
+HBM = pl.BlockSpec(memory_space=pltpu.HBM)
+
+
+def call(kernel, outs, inputs, scratch=(), flops=0, moved=0, limit=32, specs=None, out_specs=None):
     return pl.pallas_call(
         kernel,
         out_shape=[jax.ShapeDtypeStruct(s, t) for s, t in outs],
         in_specs=[VMEM] * len(inputs) if specs is None else specs,
-        out_specs=[VMEM] * len(outs),
+        out_specs=[VMEM] * len(outs) if out_specs is None else out_specs,
         scratch_shapes=list(scratch),
         compiler_params=pltpu.CompilerParams(vmem_limit_bytes=limit * MIB),
         cost_estimate=pl.CostEstimate(flops=flops, bytes_accessed=moved, transcendentals=0),
@@ -332,25 +408,39 @@
 ):
     doc_row = doc_start.reshape(1, TOK)
     gain_row = norm_gain.reshape(1, DV)
-    last = TOK // RIM - 1
-    rim = pl.pallas_call(
-        pack_kernel,
-        grid=(1,),
-        out_shape=jax.ShapeDtypeStruct((RIM, 1024), BF16),
-        in_specs=[
-            pl.BlockSpec((RIM, 256), lambda i: (last, 0)),
-            pl.BlockSpec((RIM, 256), lambda i: (last, 0)),
-            pl.BlockSpec((RIM, 512), lambda i: (last, 0)),
+    width = out_weight.shape[1]
+    (edge,) = call(
+        pack_kernel, [((RIM, 1024), BF16)], [key_in, value_in, query_in],
+        [pltpu.SemaphoreType.DMA((3,))], specs=[HBM] * 3, out_specs=[HBM], limit=60,
+    )
+    rim = lax.ppermute(edge, "ctx", [(i, i + 1) for i in range(CTX - 1)])
+    (half,) = call(
+        half_kernel, [((out_weight.shape[0] // CORES, width), BF16)], [out_weight, edge],
+        [pltpu.SemaphoreType.DMA], specs=[HBM] * 2, out_specs=[HBM], limit=60,
+    )
+    near_weight = lax.ppermute(half, "head", [(i, i ^ 1) for i in range(8)])
+    wide = (2, DK, DK + DV)
+    early = call(
+        early_kernel,
+        [
+            ((GROUPS, TOK, DK), BF16), ((TOK, HEADS * DV), BF16), ((HEADS, TOK, TOK), F32),
+            ((HEADS, TOK, 128), F32), ((HEADS, TOK), F32), ((RIM, 128), F32), ((RIM, 768), BF16),
         ],
-        out_specs=pl.BlockSpec((RIM, 1024), lambda i: (0, 0)),
-    )(query_in, key_in, value_in)
-    rim = lax.ppermute(rim, "ctx", [(i, i + 1) for i in range(CTX - 1)])
-    wide = (2, DK, DK + DV)
+        [key_in, value_in, log_decay, beta_gate, doc_row, conv_key, conv_value],
+        [
+            pltpu.VMEM((TOK, 256), BF16), pltpu.VMEM((TOK, 512), BF16),
+            pltpu.VMEM((HEADS, TOK), F32), pltpu.VMEM((HEADS, TOK), F32),
+            pltpu.VMEM((1, TOK), jnp.int32), pltpu.VMEM((TAPS, 256), F32),
+            pltpu.VMEM((TAPS, 512), F32), pltpu.VMEM((8 + TOK, 512), F32),
+            pltpu.SemaphoreType.DMA((7,)),
+        ],
+        flops=500_000_000, moved=1_500_000, specs=[HBM] * 7, limit=50,
+    )
+    keys, values, factor, carry, last, start, head = early
     solved, keys, own, give = call(
         map_kernel,
         [((HEADS, TOK, DK + DV), BF16), ((GROUPS, TOK, DK), BF16), (wide, BF16), (wide, BF16)],
-        [key_in, value_in, rim, log_decay, beta_gate, doc_row, conv_key, conv_value],
-        [pltpu.VMEM((8 + TOK, 512), F32)],
+        [rim, head, start, keys, values, factor, carry, last, beta_gate, conv_key, conv_value],
         flops=4_000_000_000, moved=2_000_000,
     )
     other = lax.ppermute(give, "ctx", core_swap())
@@ -364,35 +454,37 @@
         flops=2_000_000_000, moved=2_000_000,
     )
     before, total = call(
-        row_kernel, [(wide, BF16), (wide, BF16)], [pair] + near,
+        row_kernel, [(wide, BF16), (wide, BF16)], [pair] + near + [reach],
         [pltpu.VMEM((CHIPS_X,) + wide, BF16)], flops=60_000_000, moved=800_000,
+        specs=[VMEM] * 4 + [HBM],
     )
     far = [lax.ppermute(total, "ctx", along_y(k)) for k in (1, 2, 3)]
+    late_weight, _ = lax.optimization_barrier((near_weight, total))
+    far_weight = lax.ppermute(late_weight, "ctx", core_swap())
     narrow = (2, DK, DV)
     mine, to_other = call(
         state_kernel, [(narrow, BF16), (narrow, BF16)], [total] + far + [before, own, other],
         [pltpu.VMEM((CHIPS_Y,) + wide, BF16)], flops=60_000_000, moved=1_000_000,
     )
     got = lax.ppermute(to_other, "ctx", core_swap())
-    width = out_weight.shape[1]
+    rows = (TOK // 2, HEADS * DV)
+    keep, to_near = call(
+        norm_kernel, [(rows, BF16), (rows, BF16)],
+        [local, reach, mine, got, out_gate, gain_row],
+        flops=100_000_000, moved=1_500_000,
+    )
+    brought = lax.ppermute(to_near, "head", [(i, i ^ 1) for i in range(8)])
     (partial,) = call(
-        project_kernel,
-        [((TOK, width), BF16)],
-        [local, reach, mine, got, out_gate, gain_row, out_weight],
-        [
-            pltpu.VMEM(out_weight.shape, BF16),
-            pltpu.VMEM((TOK, HEADS * DV), BF16),
-            pltpu.SemaphoreType.DMA,
-        ],
+        project_kernel, [((TOK // 2, width), BF16)],
+        [keep, brought, out_weight, near_weight, far_weight],
         flops=600_000_000, moved=4_000_000,
-        specs=[VMEM] * 6 + [pl.BlockSpec(memory_space=pl.ANY)],
-    )
-    groups = lax.axis_size("head")
+    )
     blocks = lax.all_to_all(
-        partial.reshape(groups, TOK // groups, width), "head", 0, 0
+        partial.reshape(4, TOK // 8, width), "head", 0, 0,
+        axis_index_groups=[[0, 2, 4, 6], [1, 3, 5, 7]],
     )
     (mixed,) = call(
-        sum_kernel, [((TOK // groups, width), BF16)], [blocks], flops=1_000_000, moved=1_200_000
+        sum_kernel, [((TOK // 8, width), BF16)], [blocks], flops=1_000_000, moved=1_200_000
     )
     return mixed
 

time: 94.3 us -> 112 us (1.19)
  the two profiles are of different devices: /device:TPU:1 before, /device:TPU:6 now
where the time goes in v2:
time: 112 us
  Pallas kernels  51.7 us (46%)
  blocking collectives  23.5 us (21%)
  waiting for transfers between devices  20.8 us (19%)
  starting transfers between devices  15.4 us (14%)
    pallas_call x11, Pallas kernels, call(): pl.pallas_call(kernel, out_shape=[jax.ShapeDtypeStruct(s, t) for s, t in...  51.7 us
    all_to_all x1, blocking collectives, on_device(): lax.all_to_all(partial.reshape(4, TOK // 8, width), 'head', 0, 0, axis_in...  23.5 us
    ppermute x3, starting transfers between devices, on_device(): far = [lax.ppermute(total, 'ctx', along_y(k)) for k in (1, 2, 3)]  7.67 us
    ppermute x3, waiting for transfers between devices, on_device(): near = [lax.ppermute(pair, 'ctx', along_x(k)) for k in (1, 2, 3)]  6.34 us
    ppermute x1, waiting for transfers between devices, on_device(): brought = lax.ppermute(to_near, 'head', [(i, i ^ 1) for i in range(8)])  5.45 us
    ppermute x3, waiting for transfers between devices, on_device(): far = [lax.ppermute(total, 'ctx', along_y(k)) for k in (1, 2, 3)]  5.27 us
    ppermute x3, starting transfers between devices, on_device(): near = [lax.ppermute(pair, 'ctx', along_x(k)) for k in (1, 2, 3)]  2.98 us
  transfers between devices with their start and end apart: 12, of which 9 were waited for; matrix products, arithmetic and copies ran while one was open for 0% of the time, Pallas kernels for 14%

profile of v2, /device:TPU:6, one launch (start us, length us, event | category | flops | bytes accessed | tf_op | source)
XLA Modules:
  0.0 111.8 jit_solution(15955517127014017272)
XLA Ops:
  0.0 0.0 copy-start.3
  0.0 0.0 copy-start.1
  0.0 0.0 copy-start.9
  0.0 0.0 copy-start.11
  0.0 0.0 copy-start.7
  0.0 0.0 copy-start.8
  0.0 0.0 copy-start.6
  0.0 2.1 %shard_map.118.after_ref = bf16[16,1024]{1,0:T(8,128)(2,1)} custom-call(bf16[256,256]{1,0:T(8,128)(2,1)} %k_hbm.1, bf16[256,512]{1,0:T(8,128)(2,1)} %v_hbm.1, bf16[256,256]{1,0:T(8,128)(2,1)} %q_ref.3), custom_call_target="tpu_custom_call" | custom-call | tf_op jit(solution)/shard_map/pallas_call | solution.py:394
  2.2 0.0 copy-start.12
  2.2 32.9 %shard_map.126 = bf16[256,2048]{1,0:T(8,128)(2,1)} custom-call(bf16[512,2048]{1,0:T(8,128)(2,1)} %own_ref.1, bf16[16,1024]{1,0:T(8,128)(2,1)} %shard_map.118.after_ref), custom_call_target="tpu_custom_call" | custom-call | tf_op jit(solution)/shard_map/pallas_call | solution.py:394
  35.1 2.0 %collective-permute-start.10 = (bf16[256,2048]{1,0:T(8,128)(2,1)}, bf16[256,2048]{1,0:T(8,128)(2,1)S(1)}, u32[]{:S(2)}, u32[]{:S(2)}) collective-permute-start(bf16[256,2048]{1,0:T(8,128)(2,1)} %shard_map.126), channel_id=1, source_target_pairs={{0,1},{1,0},{2,3},{3,2},{4,5},{5,4},{6,7},{7,6},{8,9},{9,8},{10,11... | collective-permute-start | bytes 3145736 | tf_op jit(solution)/shard_map/ppermute | solution.py:421
  37.1 0.0 copy-done.12
  37.1 1.9 %collective-permute-start = (bf16[16,1024]{1,0:T(8,128)(2,1)S(1)}, bf16[16,1024]{1,0:T(8,128)(2,1)S(1)}, u32[]{:S(2)}, u32[]{:S(2)}) collective-permute-start(bf16[16,1024]{1,0:T(8,128)(2,1)S(1)} %copy-done.12), channel_id=1, source_target_pairs={{0,8},{8,16},{16,24},{24,32},{32,40},{40,48},{48,56},{56,64},{64,7... | collective-permute-start | bytes 98312 | tf_op jit(solution)/shard_map/ppermute | solution.py:416
  39.0 0.0 copy-done.3
  39.0 0.0 copy-done.1
  39.1 0.0 copy-done.9
  39.1 0.0 copy-done.11
  39.1 0.0 copy-done.7
  39.1 0.0 copy-done.8
  39.1 0.0 copy-done.6
  39.1 1.8 %shard_map.119 = (bf16[2,256,128]{2,1,0:T(8,128)(2,1)S(1)}, bf16[256,512]{1,0:T(8,128)(2,1)S(1)}, f32[4,256,256]{2,1,0:T(8,128)S(1)}, f32[4,256,128]{2,1,0:T(8,1...) custom-call(bf16[256,256]{1,0:T(8,128)(2,1)S(1)} %copy-done.3, ...), custom_call_target="tpu_custom_call" | custom-call | flops 500000000 | bytes 1500000 | tf_op jit(solution)/shard_map/pallas_call | solution.py:394
  40.9 1.4 %collective-permute-done.rim_ref = bf16[16,1024]{1,0:T(8,128)(2,1)S(1)} collective-permute-done((bf16[16,1024]{1,0:T(8,128)(2,1)S(1)}, bf16[16,1024]{1,0:T(8,128)(2,1)S(1)}, u32[]{:S(2)}, u32[]{:S(2)}) %collective-permute-start) | collective-permute-done | bytes 32800 | tf_op jit(solution)/shard_map/ppermute | solution.py:416
  42.3 0.0 copy-start.4
  42.3 0.0 copy-start.10
  42.3 10.3 %shard_map.120 = (bf16[4,256,256]{2,1,0:T(8,128)(2,1)S(1)}, bf16[2,256,128]{2,1,0:T(8,128)(2,1)S(1)}, bf16[2,128,256]{2,1,0:T(8,128)(2,1)S(1)}, bf16[2,128,256]{2,1,0:T(8,128)(2,1)S(1)}) custom-call(bf16[16,1024]{1,0:T(8,128)(2,1)S(1)} %collective-permute-done.rim_ref, bf16[16,768]{1,0:T(8,128)(2,1)S(1)} %get-tuple-element.25.head_ref, ...), custom_call_target="tpu_custom_call" | custom-call | flops 4000000000 | bytes 2000000 | tf_op jit(solution)/shard_map/pallas_call | solution.py:394
  52.7 0.3 collective-permute-start.1
  53.0 1.1 %collective-permute-done.1.got_ref.other_ref = bf16[2,128,256]{2,1,0:T(8,128)(2,1)S(1)} collective-permute-done((bf16[2,128,256]{2,1,0:T(8,128)(2,1)S(1)}, bf16[2,128,256]{2,1,0:T(8,128)(2,1)S(1)}, u32[]{:S(2)}, u32[]{:S(2)}) %collective-permute-start.1) | collective-permute-done | bytes 131104 | tf_op jit(solution)/shard_map/ppermute | solution.py:446
  54.1 0.2 shard_map.122.own_ref
  54.3 0.4 collective-permute-start.2
  54.8 2.6 %collective-permute-start.3 = (bf16[2,128,256]{2,1,0:T(8,128)(2,1)S(1)}, bf16[2,128,256]{2,1,0:T(8,128)(2,1)S(1)}, u32[]{:S(2)}, u32[]{:S(2)}) collective-permute-start(bf16[2,128,256]{2,1,0:T(8,128)(2,1)S(1)} %shard_map.122.own_ref), channel_id=1, source_target_pairs={{0,32},{8,40},{16,48},{24,56},{32,0},{40,8},{48,16},{56,24},{64,96... | collective-permute-start | bytes 393224 | tf_op jit(solution)/shard_map/ppermute | solution.py:448
  57.3 0.0 collective-permute-start.4
  57.3 0.0 copy-done.4
  57.3 0.0 copy-done.10
  57.3 0.0 copy-start.2
  57.3 0.0 copy-start.5
  57.3 0.8 shard_map.121
  58.2 0.0 copy-start
  58.2 2.5 %collective-permute-done.2.one_ref = bf16[2,128,256]{2,1,0:T(8,128)(2,1)S(1)} collective-permute-done((bf16[2,128,256]{2,1,0:T(8,128)(2,1)S(1)}, bf16[2,128,256]{2,1,0:T(8,128)(2,1)S(1)}, u32[]{:S(2)}, u32[]{:S(2)}) %collective-permute-start.2) | collective-permute-done | bytes 131104 | tf_op jit(solution)/shard_map/ppermute | solution.py:448
  60.7 1.9 %collective-permute-done.3.two_ref = bf16[2,128,256]{2,1,0:T(8,128)(2,1)S(1)} collective-permute-done((bf16[2,128,256]{2,1,0:T(8,128)(2,1)S(1)}, bf16[2,128,256]{2,1,0:T(8,128)(2,1)S(1)}, u32[]{:S(2)}, u32[]{:S(2)}) %collective-permute-start.3) | collective-permute-done | bytes 131104 | tf_op jit(solution)/shard_map/ppermute | solution.py:448
  62.6 1.9 %collective-permute-done.4.three_ref = bf16[2,128,256]{2,1,0:T(8,128)(2,1)S(1)} collective-permute-done((bf16[2,128,256]{2,1,0:T(8,128)(2,1)S(1)}, bf16[2,128,256]{2,1,0:T(8,128)(2,1)S(1)}, u32[]{:S(2)}, u32[]{:S(2)}) %collective-permute-start.4) | collective-permute-done | bytes 131104 | tf_op jit(solution)/shard_map/ppermute | solution.py:448
  64.5 0.7 shard_map.123
  65.2 0.0 collective-permute-done.10.near_ref
  65.3 0.3 collective-permute-start.11
  65.5 3.4 %collective-permute-start.5 = (bf16[2,128,256]{2,1,0:T(8,128)(2,1)S(1)}, bf16[2,128,256]{2,1,0:T(8,128)(2,1)S(1)}, u32[]{:S(2)}, u32[]{:S(2)}) collective-permute-start(bf16[2,128,256]{2,1,0:T(8,128)(2,1)S(1)} %get-tuple-element.38.own_ref), channel_id=1, source_target_pairs={{0,64},{8,72},{16,80},{24,88},{32,96},{40,104},{48,112},{56,120},{... | collective-permute-start | bytes 393224 | tf_op jit(solution)/shard_map/ppermute | solution.py:461
  69.0 2.9 %collective-permute-start.6 = (bf16[2,128,256]{2,1,0:T(8,128)(2,1)S(1)}, bf16[2,128,256]{2,1,0:T(8,128)(2,1)S(1)}, u32[]{:S(2)}, u32[]{:S(2)}) collective-permute-start(bf16[2,128,256]{2,1,0:T(8,128)(2,1)S(1)} %get-tuple-element.38.own_ref), channel_id=1, source_target_pairs={{0,128},{8,136},{16,144},{24,152},{32,160},{40,168},{48,176},{56,1... | collective-permute-start | bytes 393224 | tf_op jit(solution)/shard_map/ppermute | solution.py:461
  71.9 1.3 %collective-permute-start.7 = (bf16[2,128,256]{2,1,0:T(8,128)(2,1)S(1)}, bf16[2,128,256]{2,1,0:T(8,128)(2,1)S(1)}, u32[]{:S(2)}, u32[]{:S(2)}) collective-permute-start(bf16[2,128,256]{2,1,0:T(8,128)(2,1)S(1)} %get-tuple-element.38.own_ref), channel_id=1, source_target_pairs={{0,192},{8,200},{16,208},{24,216},{32,224},{40,232},{48,240},{56,2... | collective-permute-start | bytes 393224 | tf_op jit(solution)/shard_map/ppermute | solution.py:461
  73.2 1.3 %collective-permute-done.5.one_ref = bf16[2,128,256]{2,1,0:T(8,128)(2,1)S(1)} collective-permute-done((bf16[2,128,256]{2,1,0:T(8,128)(2,1)S(1)}, bf16[2,128,256]{2,1,0:T(8,128)(2,1)S(1)}, u32[]{:S(2)}, u32[]{:S(2)}) %collective-permute-start.5) | collective-permute-done | bytes 131104 | tf_op jit(solution)/shard_map/ppermute | solution.py:461
  74.5 4.0 %collective-permute-done.6.two_ref = bf16[2,128,256]{2,1,0:T(8,128)(2,1)S(1)} collective-permute-done((bf16[2,128,256]{2,1,0:T(8,128)(2,1)S(1)}, bf16[2,128,256]{2,1,0:T(8,128)(2,1)S(1)}, u32[]{:S(2)}, u32[]{:S(2)}) %collective-permute-start.6) | collective-permute-done | bytes 131104 | tf_op jit(solution)/shard_map/ppermute | solution.py:461
  78.5 0.0 collective-permute-done.7.three_ref
  78.5 0.9 shard_map.124
  79.4 0.1 collective-permute-start.8
  79.5 1.2 %collective-permute-done.8.got_ref = bf16[2,128,128]{2,1,0:T(8,128)(2,1)S(1)} collective-permute-done((bf16[2,128,128]{2,1,0:T(8,128)(2,1)S(1)}, bf16[2,128,128]{2,1,0:T(8,128)(2,1)S(1)}, u32[]{:S(2)}, u32[]{:S(2)}) %collective-permute-start.8) | collective-permute-done | bytes 65568 | tf_op jit(solution)/shard_map/ppermute | solution.py:469
  80.7 0.0 copy-done.2
  80.7 0.0 copy-done.5
  80.7 0.4 shard_map.125
  81.2 0.2 collective-permute-start.9
  81.4 5.4 %collective-permute-done.9.got_ref = bf16[128,512]{1,0:T(8,128)(2,1)S(1)} collective-permute-done((bf16[128,512]{1,0:T(8,128)(2,1)S(1)}, bf16[128,512]{1,0:T(8,128)(2,1)S(1)}, u32[]{:S(2)}, u32[]{:S(2)}) %collective-permute-start.9) | collective-permute-done | bytes 131104 | tf_op jit(solution)/shard_map/ppermute | solution.py:476
  86.8 0.0 collective-permute-done.11.far_ref
  86.8 0.0 copy-done
  86.8 0.7 shard_map.127
  87.5 23.5 %all_to_all.5.in_ref = bf16[4,32,2048]{2,1,0:T(8,128)(2,1)S(1)} all-to-all(bf16[4,32,2048]{2,1,0:T(8,128)(2,1)S(1)} %bitcast.3), channel_id=1, replica_groups={{0,2,4,6},{1,3,5,7},{8,10,12,14},{9,11,13,15},{16,18,20,22},{17,19,21,2..., dimensions={0} | all-to-all | bytes 1048576 | tf_op jit(solution)/shard_map/all_to_all | solution.py:482
  111.0 0.7 shard_map.128
Async XLA Ops:
  0.0 39.0 %copy-start.3 = (bf16[256,256]{1,0:T(8,128)(2,1)S(1)}, bf16[256,256]{1,0:T(8,128)(2,1)}, u32[]{:S(2)}) copy-start(bf16[256,256]{1,0:T(8,128)(2,1)} %k_hbm.1) | copy-start | bytes 393220
  0.0 39.0 %copy-start.1 = (bf16[256,512]{1,0:T(8,128)(2,1)S(1)}, bf16[256,512]{1,0:T(8,128)(2,1)}, u32[]{:S(2)}) copy-start(bf16[256,512]{1,0:T(8,128)(2,1)} %v_hbm.1) | copy-start | bytes 786436
  0.0 39.1 %copy-start.9 = (f32[4,256]{1,0:T(4,128)S(1)}, f32[4,256]{1,0:T(4,128)}, u32[]{:S(2)}) copy-start(f32[4,256]{1,0:T(4,128)} %decay_ref.1) | copy-start | bytes 12292
  0.0 39.1 %copy-start.11 = (s32[256]{0:T(256)S(1)}, s32[256]{0:T(256)}, u32[]{:S(2)}) copy-start(s32[256]{0:T(256)} %param.18) | copy-start | bytes 3076
  0.0 39.1 %copy-start.7 = (f32[4,256]{1,0:T(4,128)S(1)}, f32[4,256]{1,0:T(4,128)}, u32[]{:S(2)}) copy-start(f32[4,256]{1,0:T(4,128)} %beta_ref.1) | copy-start | bytes 12292
  0.0 39.1 %copy-start.8 = (f32[4,256]{1,0:T(4,128)S(1)}, f32[4,256]{1,0:T(4,128)}, u32[]{:S(2)}) copy-start(f32[4,256]{1,0:T(4,128)} %wk_ref.1) | copy-start | bytes 12292
  0.0 39.1 %copy-start.6 = (f32[4,512]{1,0:T(4,128)S(1)}, f32[4,512]{1,0:T(4,128)}, u32[]{:S(2)}) copy-start(f32[4,512]{1,0:T(4,128)} %wv_ref.1) | copy-start | bytes 24580
  2.2 34.9 %copy-start.12 = (bf16[16,1024]{1,0:T(8,128)(2,1)S(1)}, bf16[16,1024]{1,0:T(8,128)(2,1)}, u32[]{:S(2)}) copy-start(bf16[16,1024]{1,0:T(8,128)(2,1)} %shard_map.118.after_ref) | copy-start | bytes 98308
  35.1 30.1 %collective-permute-start.10 = (bf16[256,2048]{1,0:T(8,128)(2,1)}, bf16[256,2048]{1,0:T(8,128)(2,1)S(1)}, u32[]{:S(2)}, u32[]{:S(2)}) collective-permute-start(bf16[256,2048]{1,0:T(8,128)(2,1)} %shard_map.126), channel_id=1, source_target_pairs={{0,1},{1,0},{2,3},{3,2},{4,5},{5,4},{6,7},{7,6},{8,9},{9,8},{10,11... | collective-permute-start | bytes 3145736 | tf_op jit(solution)/shard_map/ppermute | solution.py:421
  37.1 5.2 %collective-permute-start = (bf16[16,1024]{1,0:T(8,128)(2,1)S(1)}, bf16[16,1024]{1,0:T(8,128)(2,1)S(1)}, u32[]{:S(2)}, u32[]{:S(2)}) collective-permute-start(bf16[16,1024]{1,0:T(8,128)(2,1)S(1)} %copy-done.12), channel_id=1, source_target_pairs={{0,8},{8,16},{16,24},{24,32},{32,40},{40,48},{48,56},{56,64},{64,7... | collective-permute-start | bytes 98312 | tf_op jit(solution)/shard_map/ppermute | solution.py:416
  42.3 15.0 %copy-start.4 = (bf16[256,256]{1,0:T(8,128)(2,1)S(1)}, bf16[256,256]{1,0:T(8,128)(2,1)}, u32[]{:S(2)}) copy-start(bf16[256,256]{1,0:T(8,128)(2,1)} %q_ref.3) | copy-start | bytes 393220
  42.3 15.0 %copy-start.10 = (f32[4,256]{1,0:T(4,128)S(1)}, f32[4,256]{1,0:T(4,128)}, u32[]{:S(2)}) copy-start(f32[4,256]{1,0:T(4,128)} %wq_ref.1) | copy-start | bytes 12292
  52.7 1.4 %collective-permute-start.1 = (bf16[2,128,256]{2,1,0:T(8,128)(2,1)S(1)}, bf16[2,128,256]{2,1,0:T(8,128)(2,1)S(1)}, u32[]{:S(2)}, u32[]{:S(2)}) collective-permute-start(bf16[2,128,256]{2,1,0:T(8,128)(2,1)S(1)} %get-tuple-element.37), channel_id=1, source_target_pairs={{0,8},{8,0},{16,24},{24,16},{32,40},{40,32},{48,56},{56,48},{64,72... | collective-permute-start | bytes 393224 | tf_op jit(solution)/shard_map/ppermute | solution.py:446
  54.3 6.4 %collective-permute-start.2 = (bf16[2,128,256]{2,1,0:T(8,128)(2,1)S(1)}, bf16[2,128,256]{2,1,0:T(8,128)(2,1)S(1)}, u32[]{:S(2)}, u32[]{:S(2)}) collective-permute-start(bf16[2,128,256]{2,1,0:T(8,128)(2,1)S(1)} %shard_map.122.own_ref), channel_id=1, source_target_pairs={{0,16},{8,24},{16,32},{24,40},{32,48},{40,56},{48,0},{56,8},{64,80... | collective-permute-start | bytes 393224 | tf_op jit(solution)/shard_map/ppermute | solution.py:448
  54.8 7.9 %collective-permute-start.3 = (bf16[2,128,256]{2,1,0:T(8,128)(2,1)S(1)}, bf16[2,128,256]{2,1,0:T(8,128)(2,1)S(1)}, u32[]{:S(2)}, u32[]{:S(2)}) collective-permute-start(bf16[2,128,256]{2,1,0:T(8,128)(2,1)S(1)} %shard_map.122.own_ref), channel_id=1, source_target_pairs={{0,32},{8,40},{16,48},{24,56},{32,0},{40,8},{48,16},{56,24},{64,96... | collective-permute-start | bytes 393224 | tf_op jit(solution)/shard_map/ppermute | solution.py:448
  57.3 7.2 %collective-permute-start.4 = (bf16[2,128,256]{2,1,0:T(8,128)(2,1)S(1)}, bf16[2,128,256]{2,1,0:T(8,128)(2,1)S(1)}, u32[]{:S(2)}, u32[]{:S(2)}) collective-permute-start(bf16[2,128,256]{2,1,0:T(8,128)(2,1)S(1)} %shard_map.122.own_ref), channel_id=1, source_target_pairs={{0,48},{8,56},{16,0},{24,8},{32,16},{40,24},{48,32},{56,40},{64,11... | collective-permute-start | bytes 393224 | tf_op jit(solution)/shard_map/ppermute | solution.py:448
  57.3 23.4 %copy-start.2 = (bf16[256,512]{1,0:T(8,128)(2,1)S(1)}, bf16[256,512]{1,0:T(8,128)(2,1)}, u32[]{:S(2)}) copy-start(bf16[256,512]{1,0:T(8,128)(2,1)} %gate_ref.1) | copy-start | bytes 786436
  57.3 23.4 %copy-start.5 = (f32[128]{0:T(128)S(1)}, f32[128]{0:T(128)}, u32[]{:S(2)}) copy-start(f32[128]{0:T(128)} %param.22) | copy-start | bytes 1540
  58.2 28.6 %copy-start = (bf16[512,2048]{1,0:T(8,128)(2,1)S(1)}, bf16[512,2048]{1,0:T(8,128)(2,1)}, u32[]{:S(2)}) copy-start(bf16[512,2048]{1,0:T(8,128)(2,1)} %own_ref.1) | copy-start | bytes 6291460
  65.3 21.6 %collective-permute-start.11 = (bf16[256,2048]{1,0:T(8,128)(2,1)S(1)}, bf16[256,2048]{1,0:T(8,128)(2,1)S(1)}, u32[]{:S(2)}, u32[]{:S(2)}) collective-permute-start(bf16[256,2048]{1,0:T(8,128)(2,1)S(1)} %collective-permute-done.10.near_ref), channel_id=1, source_target_pairs={{0,8},{8,0},{16,24},{24,16},{32,40},{40,32},{48,56},{56,48},{64,72... | collective-permute-start | bytes 3145736 | tf_op jit(solution)/shard_map/ppermute | solution.py:463
  65.5 8.9 %collective-permute-start.5 = (bf16[2,128,256]{2,1,0:T(8,128)(2,1)S(1)}, bf16[2,128,256]{2,1,0:T(8,128)(2,1)S(1)}, u32[]{:S(2)}, u32[]{:S(2)}) collective-permute-start(bf16[2,128,256]{2,1,0:T(8,128)(2,1)S(1)} %get-tuple-element.38.own_ref), channel_id=1, source_target_pairs={{0,64},{8,72},{16,80},{24,88},{32,96},{40,104},{48,112},{56,120},{... | collective-permute-start | bytes 393224 | tf_op jit(solution)/shard_map/ppermute | solution.py:461
  69.0 9.5 %collective-permute-start.6 = (bf16[2,128,256]{2,1,0:T(8,128)(2,1)S(1)}, bf16[2,128,256]{2,1,0:T(8,128)(2,1)S(1)}, u32[]{:S(2)}, u32[]{:S(2)}) collective-permute-start(bf16[2,128,256]{2,1,0:T(8,128)(2,1)S(1)} %get-tuple-element.38.own_ref), channel_id=1, source_target_pairs={{0,128},{8,136},{16,144},{24,152},{32,160},{40,168},{48,176},{56,1... | collective-permute-start | bytes 393224 | tf_op jit(solution)/shard_map/ppermute | solution.py:461
  71.9 6.6 %collective-permute-start.7 = (bf16[2,128,256]{2,1,0:T(8,128)(2,1)S(1)}, bf16[2,128,256]{2,1,0:T(8,128)(2,1)S(1)}, u32[]{:S(2)}, u32[]{:S(2)}) collective-permute-start(bf16[2,128,256]{2,1,0:T(8,128)(2,1)S(1)} %get-tuple-element.38.own_ref), channel_id=1, source_target_pairs={{0,192},{8,200},{16,208},{24,216},{32,224},{40,232},{48,240},{56,2... | collective-permute-start | bytes 393224 | tf_op jit(solution)/shard_map/ppermute | solution.py:461
  79.4 1.3 %collective-permute-start.8 = (bf16[2,128,128]{2,1,0:T(8,128)(2,1)S(1)}, bf16[2,128,128]{2,1,0:T(8,128)(2,1)S(1)}, u32[]{:S(2)}, u32[]{:S(2)}) collective-permute-start(bf16[2,128,128]{2,1,0:T(8,128)(2,1)S(1)} %get-tuple-element.41), channel_id=1, source_target_pairs={{0,8},{8,0},{16,24},{24,16},{32,40},{40,32},{48,56},{56,48},{64,72... | collective-permute-start | bytes 196616 | tf_op jit(solution)/shard_map/ppermute | solution.py:469
  81.2 5.6 %collective-permute-start.9 = (bf16[128,512]{1,0:T(8,128)(2,1)S(1)}, bf16[128,512]{1,0:T(8,128)(2,1)S(1)}, u32[]{:S(2)}, u32[]{:S(2)}) collective-permute-start(bf16[128,512]{1,0:T(8,128)(2,1)S(1)} %get-tuple-element.43), channel_id=1, source_target_pairs={{0,1},{1,0},{2,3},{3,2},{4,5},{5,4},{6,7},{7,6},{8,9},{9,8},{10,11... | collective-permute-start | bytes 393224 | tf_op jit(solution)/shard_map/ppermute | solution.py:476

commit v3 on v2

--- a/solution.py
+++ b/solution.py
@@ -145,17 +145,10 @@
     return guess.astype(F32) + mm(guess, rest.astype(BF16))
 
 
-def pack_kernel(k_ref, v_ref, q_ref, out_ref, sems):
-    rows = pl.ds(TOK - RIM, RIM)
-    copies = [
-        pltpu.make_async_copy(k_ref.at[rows], out_ref.at[:, 0:256], sems.at[0]),
-        pltpu.make_async_copy(v_ref.at[rows], out_ref.at[:, 256:768], sems.at[1]),
-        pltpu.make_async_copy(q_ref.at[rows], out_ref.at[:, 768:1024], sems.at[2]),
-    ]
-    for copy in copies:
-        copy.start()
-    for copy in copies:
-        copy.wait()
+def pack_kernel(k_ref, v_ref, q_ref, out_ref):
+    out_ref[:, 0:256] = k_ref[...]
+    out_ref[:, 256:768] = v_ref[...]
+    out_ref[:, 768:1024] = q_ref[...]
 
 
 def half_kernel(weight_ref, after_ref, out_ref, sem):
@@ -409,16 +402,16 @@
     doc_row = doc_start.reshape(1, TOK)
     gain_row = norm_gain.reshape(1, DV)
     width = out_weight.shape[1]
-    (edge,) = call(
-        pack_kernel, [((RIM, 1024), BF16)], [key_in, value_in, query_in],
-        [pltpu.SemaphoreType.DMA((3,))], specs=[HBM] * 3, out_specs=[HBM], limit=60,
-    )
+    last = TOK // RIM - 1
+    edge = pl.pallas_call(
+        pack_kernel,
+        grid=(1,),
+        out_shape=jax.ShapeDtypeStruct((RIM, 1024), BF16),
+        in_specs=[pl.BlockSpec((RIM, n), lambda i: (last, 0)) for n in (256, 512, 256)],
+        out_specs=pl.BlockSpec((RIM, 1024), lambda i: (0, 0)),
+        compiler_params=pltpu.CompilerParams(vmem_limit_bytes=60 * MIB),
+    )(key_in, value_in, query_in)
     rim = lax.ppermute(edge, "ctx", [(i, i + 1) for i in range(CTX - 1)])
-    (half,) = call(
-        half_kernel, [((out_weight.shape[0] // CORES, width), BF16)], [out_weight, edge],
-        [pltpu.SemaphoreType.DMA], specs=[HBM] * 2, out_specs=[HBM], limit=60,
-    )
-    near_weight = lax.ppermute(half, "head", [(i, i ^ 1) for i in range(8)])
     wide = (2, DK, DK + DV)
     early = call(
         early_kernel,
@@ -436,11 +429,16 @@
         ],
         flops=500_000_000, moved=1_500_000, specs=[HBM] * 7, limit=50,
     )
-    keys, values, factor, carry, last, start, head = early
+    keys, values, factor, carry, final, start, head = early
+    (half,) = call(
+        half_kernel, [((out_weight.shape[0] // CORES, width), BF16)], [out_weight, start],
+        [pltpu.SemaphoreType.DMA], specs=[HBM] * 2, limit=62,
+    )
+    near_weight = lax.ppermute(half, "head", [(i, i ^ 1) for i in range(8)])
     solved, keys, own, give = call(
         map_kernel,
         [((HEADS, TOK, DK + DV), BF16), ((GROUPS, TOK, DK), BF16), (wide, BF16), (wide, BF16)],
-        [rim, head, start, keys, values, factor, carry, last, beta_gate, conv_key, conv_value],
+        [rim, head, start, keys, values, factor, carry, final, beta_gate, conv_key, conv_value],
         flops=4_000_000_000, moved=2_000_000,
     )
     other = lax.ppermute(give, "ctx", core_swap())

time: 112 us -> 90.1 us (0.80); the launches traced: 112 us -> 88.5 us
  Pallas kernels: 51.7 us -> 20.2 us
  local copies, waits for them, and re-layouts: 0.06 us -> 5.93 us
  waiting for transfers between devices: 20.8 us -> 25 us
  starting transfers between devices: 15.4 us -> 13.6 us
    pallas_call x11 -> x10, Pallas kernels: 51.7 us -> 18.9 us  [call(): pl.pallas_call(kernel, out_shape=[jax.ShapeDtypeStruct(s, t) for s, t in...]
    unnamed x26 -> x38, local copies, waits for them, and re-layouts: 0.06 us -> 5.93 us
    ppermute x3, waiting for transfers between devices: 5.27 us -> 8.27 us  [on_device(): far = [lax.ppermute(total, 'ctx', along_y(k)) for k in (1, 2, 3)]]
    ppermute x3, starting transfers between devices: 7.67 us -> 4.94 us  [on_device(): far = [lax.ppermute(total, 'ctx', along_y(k)) for k in (1, 2, 3)]]
    ppermute x1, waiting for transfers between devices: 1.41 us -> 3.52 us  [on_device(): rim = lax.ppermute(edge, 'ctx', [(i, i + 1) for i in range(CTX - 1)])]
    pallas_call x0 -> x1, Pallas kernels: none -> 1.35 us  [on_device(): pl.pallas_call(pack_kernel, grid=(1,), out_shape=jax.ShapeDtypeStruct((RI...]
    ppermute x3, starting transfers between devices: 2.98 us -> 4.12 us  [on_device(): near = [lax.ppermute(pair, 'ctx', along_x(k)) for k in (1, 2, 3)]]
  transfers between devices with their start and end apart: 12 -> 12, of which waited for: 9 -> 9; matrix products, arithmetic and copies ran while one was open for 0% -> 0% of each run, Pallas kernels for 14% -> 17%
where the time goes in v3:
time: 90.1 us; the launch traced here: 88.5 us
  waiting for transfers between devices  25 us (28%)
  blocking collectives  23.5 us (26%)
  Pallas kernels  20.2 us (22%)
  starting transfers between devices  13.6 us (15%)
  local copies, waits for them, and re-layouts  5.93 us (7%)
    all_to_all x1, blocking collectives, on_device(): lax.all_to_all(partial.reshape(4, TOK // 8, width), 'head', 0, 0, axis_in...  23.5 us
    pallas_call x10, Pallas kernels, call(): pl.pallas_call(kernel, out_shape=[jax.ShapeDtypeStruct(s, t) for s, t in...  18.9 us
    ppermute x3, waiting for transfers between devices, on_device(): far = [lax.ppermute(total, 'ctx', along_y(k)) for k in (1, 2, 3)]  8.27 us
    unnamed x38, local copies, waits for them, and re-layouts  5.93 us
    ppermute x1, waiting for transfers between devices, on_device(): brought = lax.ppermute(to_near, 'head', [(i, i ^ 1) for i in range(8)])  5.45 us
    ppermute x3, waiting for transfers between devices, on_device(): near = [lax.ppermute(pair, 'ctx', along_x(k)) for k in (1, 2, 3)]  5.22 us
    ppermute x3, starting transfers between devices, on_device(): far = [lax.ppermute(total, 'ctx', along_y(k)) for k in (1, 2, 3)]  4.94 us
    ppermute x3, starting transfers between devices, on_device(): near = [lax.ppermute(pair, 'ctx', along_x(k)) for k in (1, 2, 3)]  4.12 us
  transfers between devices with their start and end apart: 12, of which 9 were waited for; matrix products, arithmetic and copies ran while one was open for 0% of the time, Pallas kernels for 17%

profile of v3, /device:TPU:6, one launch (start us, length us, event | category | flops | bytes accessed | tf_op | source)
XLA Modules:
  0.0 88.5 jit_solution(9522143718340560302)
XLA Ops:
  0.0 0.0 copy-start.1
  0.0 0.9 %copy-done.1 = bf16[256,512]{1,0:T(8,128)(2,1)S(1)} copy-done((bf16[256,512]{1,0:T(8,128)(2,1)S(1)}, bf16[256,512]{1,0:T(8,128)(2,1)}, u32[]{:S(2)}) %copy-start.1) | copy-done | bytes 262168
  1.0 0.9 %copy-done.3 = bf16[256,256]{1,0:T(8,128)(2,1)S(1)} copy-done((bf16[256,256]{1,0:T(8,128)(2,1)S(1)}, bf16[256,256]{1,0:T(8,128)(2,1)}, u32[]{:S(2)}) %copy-start.3) | copy-done | bytes 131096
  1.9 0.7 copy-done.8
  2.6 0.7 copy-done.10
  3.2 0.7 copy-done.12
  3.9 0.7 copy-done.14
  4.6 0.7 copy-done.17
  5.3 1.8 %shard_map.119 = (bf16[2,256,128]{2,1,0:T(8,128)(2,1)S(1)}, bf16[256,512]{1,0:T(8,128)(2,1)S(1)}, f32[4,256,256]{2,1,0:T(8,128)S(1)}, f32[4,256,128]{2,1,0:T(8,1...) custom-call(bf16[256,256]{1,0:T(8,128)(2,1)S(1)} %copy-done.3, ...), custom_call_target="tpu_custom_call" | custom-call | flops 500000000 | bytes 1500000 | tf_op jit(solution)/shard_map/pallas_call | solution.py:387
  7.1 0.0 copy-start.5
  7.1 0.6 copy-done.5
  7.7 2.3 %shard_map.126 = bf16[256,2048]{1,0:T(8,128)(2,1)} custom-call(bf16[512,2048]{1,0:T(8,128)(2,1)} %own_ref.1, f32[16,128]{1,0:T(8,128)} %copy-done.5), custom_call_target="tpu_custom_call" | custom-call | tf_op jit(solution)/shard_map/pallas_call | solution.py:387
  10.0 2.0 %collective-permute-start.10 = (bf16[256,2048]{1,0:T(8,128)(2,1)}, bf16[256,2048]{1,0:T(8,128)(2,1)S(1)}, u32[]{:S(2)}, u32[]{:S(2)}) collective-permute-start(bf16[256,2048]{1,0:T(8,128)(2,1)} %shard_map.126), channel_id=1, source_target_pairs={{0,1},{1,0},{2,3},{3,2},{4,5},{5,4},{6,7},{7,6},{8,9},{9,8},{10,11... | collective-permute-start | bytes 3145736 | tf_op jit(solution)/shard_map/ppermute | solution.py:437
  12.0 1.3 %shard_map.118 = bf16[16,1024]{1,0:T(8,128)(2,1)} custom-call(bf16[256,256]{1,0:T(8,128)(2,1)} %k_hbm.1, bf16[256,512]{1,0:T(8,128)(2,1)} %v_hbm.1, bf16[256,256]{1,0:T(8,128)(2,1)} %q_ref.3), custom_call_target="tpu_custom_call" | custom-call | tf_op jit(solution)/shard_map/pallas_call | solution.py:406
  13.3 1.9 %collective-permute-start = (bf16[16,1024]{1,0:T(8,128)(2,1)}, bf16[16,1024]{1,0:T(8,128)(2,1)S(1)}, u32[]{:S(2)}, u32[]{:S(2)}) collective-permute-start(bf16[16,1024]{1,0:T(8,128)(2,1)} %shard_map.118), channel_id=1, source_target_pairs={{0,8},{8,16},{16,24},{24,32},{32,40},{40,48},{48,56},{56,64},{64,7... | collective-permute-start | bytes 98312 | tf_op jit(solution)/shard_map/ppermute | solution.py:414
  15.2 3.5 %collective-permute-done.rim_ref = bf16[16,1024]{1,0:T(8,128)(2,1)S(1)} collective-permute-done((bf16[16,1024]{1,0:T(8,128)(2,1)}, bf16[16,1024]{1,0:T(8,128)(2,1)S(1)}, u32[]{:S(2)}, u32[]{:S(2)}) %collective-permute-start) | collective-permute-done | bytes 32800 | tf_op jit(solution)/shard_map/ppermute | solution.py:414
  18.7 0.0 copy-done.9
  18.8 0.0 copy-done.11
  18.8 0.0 copy-done.13
  18.8 0.0 copy-done.6
  18.8 0.0 copy-start.4
  18.8 0.0 copy-start.15
  18.8 0.0 copy-start.16
  18.8 0.0 copy-start.18
  18.8 10.3 %shard_map.120 = (bf16[4,256,256]{2,1,0:T(8,128)(2,1)S(1)}, bf16[2,256,128]{2,1,0:T(8,128)(2,1)S(1)}, bf16[2,128,256]{2,1,0:T(8,128)(2,1)S(1)}, bf16[2,128,256]{2,1,0:T(8,128)(2,1)S(1)}) custom-call(bf16[16,1024]{1,0:T(8,128)(2,1)S(1)} %collective-permute-done.rim_ref, bf16[16,768]{1,0:T(8,128)(2,1)S(1)} %get-tuple-element.25.head_ref, ...), custom_call_target="tpu_custom_call" | custom-call | flops 4000000000 | bytes 2000000 | tf_op jit(solution)/shard_map/pallas_call | solution.py:387
  29.2 0.1 collective-permute-start.1
  29.3 1.3 %collective-permute-done.1.got_ref.other_ref = bf16[2,128,256]{2,1,0:T(8,128)(2,1)S(1)} collective-permute-done((bf16[2,128,256]{2,1,0:T(8,128)(2,1)S(1)}, bf16[2,128,256]{2,1,0:T(8,128)(2,1)S(1)}, u32[]{:S(2)}, u32[]{:S(2)}) %collective-permute-start.1) | collective-permute-done | bytes 131104 | tf_op jit(solution)/shard_map/ppermute | solution.py:444
  30.6 0.2 shard_map.122.own_ref
  30.8 0.9 %collective-permute-start.4 = (bf16[2,128,256]{2,1,0:T(8,128)(2,1)S(1)}, bf16[2,128,256]{2,1,0:T(8,128)(2,1)S(1)}, u32[]{:S(2)}, u32[]{:S(2)}) collective-permute-start(bf16[2,128,256]{2,1,0:T(8,128)(2,1)S(1)} %shard_map.122.own_ref), channel_id=1, source_target_pairs={{0,48},{8,56},{16,0},{24,8},{32,16},{40,24},{48,32},{56,40},{64,11... | collective-permute-start | bytes 393224 | tf_op jit(solution)/shard_map/ppermute | solution.py:446
  31.7 0.7 collective-permute-start.3
  32.4 2.5 %collective-permute-start.2 = (bf16[2,128,256]{2,1,0:T(8,128)(2,1)S(1)}, bf16[2,128,256]{2,1,0:T(8,128)(2,1)S(1)}, u32[]{:S(2)}, u32[]{:S(2)}) collective-permute-start(bf16[2,128,256]{2,1,0:T(8,128)(2,1)S(1)} %shard_map.122.own_ref), channel_id=1, source_target_pairs={{0,16},{8,24},{16,32},{24,40},{32,48},{40,56},{48,0},{56,8},{64,80... | collective-permute-start | bytes 393224 | tf_op jit(solution)/shard_map/ppermute | solution.py:446
  34.9 0.0 copy-done.4
  34.9 0.0 copy-done.15
  34.9 0.0 copy-done.16
  34.9 0.0 copy-done.18
  34.9 0.0 copy-start.2
  34.9 0.0 copy-start.7
  34.9 0.8 shard_map.121
  35.8 0.0 copy-start
  35.8 4.6 %collective-permute-done.4.three_ref = bf16[2,128,256]{2,1,0:T(8,128)(2,1)S(1)} collective-permute-done((bf16[2,128,256]{2,1,0:T(8,128)(2,1)S(1)}, bf16[2,128,256]{2,1,0:T(8,128)(2,1)S(1)}, u32[]{:S(2)}, u32[]{:S(2)}) %collective-permute-start.4) | collective-permute-done | bytes 131104 | tf_op jit(solution)/shard_map/ppermute | solution.py:446
  40.4 0.0 collective-permute-done.3.two_ref
  40.4 0.6 collective-permute-done.2.one_ref
  41.0 0.7 shard_map.123
  41.7 0.0 collective-permute-done.10.near_ref
  41.7 0.3 collective-permute-start.11
  42.0 3.3 %collective-permute-start.7 = (bf16[2,128,256]{2,1,0:T(8,128)(2,1)S(1)}, bf16[2,128,256]{2,1,0:T(8,128)(2,1)S(1)}, u32[]{:S(2)}, u32[]{:S(2)}) collective-permute-start(bf16[2,128,256]{2,1,0:T(8,128)(2,1)S(1)} %get-tuple-element.38.own_ref), channel_id=1, source_target_pairs={{0,192},{8,200},{16,208},{24,216},{32,224},{40,232},{48,240},{56,2... | collective-permute-start | bytes 393224 | tf_op jit(solution)/shard_map/ppermute | solution.py:459
  45.3 0.6 collective-permute-start.6
  46.0 1.0 %collective-permute-start.5 = (bf16[2,128,256]{2,1,0:T(8,128)(2,1)S(1)}, bf16[2,128,256]{2,1,0:T(8,128)(2,1)S(1)}, u32[]{:S(2)}, u32[]{:S(2)}) collective-permute-start(bf16[2,128,256]{2,1,0:T(8,128)(2,1)S(1)} %get-tuple-element.38.own_ref), channel_id=1, source_target_pairs={{0,64},{8,72},{16,80},{24,88},{32,96},{40,104},{48,112},{56,120},{... | collective-permute-start | bytes 393224 | tf_op jit(solution)/shard_map/ppermute | solution.py:459
  46.9 4.6 %collective-permute-done.7.three_ref = bf16[2,128,256]{2,1,0:T(8,128)(2,1)S(1)} collective-permute-done((bf16[2,128,256]{2,1,0:T(8,128)(2,1)S(1)}, bf16[2,128,256]{2,1,0:T(8,128)(2,1)S(1)}, u32[]{:S(2)}, u32[]{:S(2)}) %collective-permute-start.7) | collective-permute-done | bytes 131104 | tf_op jit(solution)/shard_map/ppermute | solution.py:459
  51.5 1.7 %collective-permute-done.6.two_ref = bf16[2,128,256]{2,1,0:T(8,128)(2,1)S(1)} collective-permute-done((bf16[2,128,256]{2,1,0:T(8,128)(2,1)S(1)}, bf16[2,128,256]{2,1,0:T(8,128)(2,1)S(1)}, u32[]{:S(2)}, u32[]{:S(2)}) %collective-permute-start.6) | collective-permute-done | bytes 131104 | tf_op jit(solution)/shard_map/ppermute | solution.py:459
  53.2 2.0 %collective-permute-done.5.one_ref = bf16[2,128,256]{2,1,0:T(8,128)(2,1)S(1)} collective-permute-done((bf16[2,128,256]{2,1,0:T(8,128)(2,1)S(1)}, bf16[2,128,256]{2,1,0:T(8,128)(2,1)S(1)}, u32[]{:S(2)}, u32[]{:S(2)}) %collective-permute-start.5) | collective-permute-done | bytes 131104 | tf_op jit(solution)/shard_map/ppermute | solution.py:459
  55.2 0.9 %shard_map.124 = (bf16[2,128,128]{2,1,0:T(8,128)(2,1)S(1)}, bf16[2,128,128]{2,1,0:T(8,128)(2,1)S(1)}) custom-call(bf16[2,128,256]{2,1,0:T(8,128)(2,1)S(1)} %get-tuple-element.38.own_ref, bf16[2,128,256]{2,1,0:T(8,128)(2,1)S(1)} %collective-permute-done.5.one_ref, bf16[2,128,256]{2,1,0:T(8,128)(2,1)S(1)} %collective-permute-done.6.two_ref, ...), custom_call_target="tpu_custom_call" | custom-call | flops 60000000 | bytes 1000000 | tf_op jit(solution)/shard_map/pallas_call | solution.py:387
  56.1 0.1 collective-permute-start.8
  56.2 1.2 %collective-permute-done.8.got_ref = bf16[2,128,128]{2,1,0:T(8,128)(2,1)S(1)} collective-permute-done((bf16[2,128,128]{2,1,0:T(8,128)(2,1)S(1)}, bf16[2,128,128]{2,1,0:T(8,128)(2,1)S(1)}, u32[]{:S(2)}, u32[]{:S(2)}) %collective-permute-start.8) | collective-permute-done | bytes 65568 | tf_op jit(solution)/shard_map/ppermute | solution.py:467
  57.5 0.0 copy-done.2
  57.5 0.0 copy-done.7
  57.5 0.4 shard_map.125
  57.9 0.2 collective-permute-start.9
  58.1 5.4 %collective-permute-done.9.got_ref = bf16[128,512]{1,0:T(8,128)(2,1)S(1)} collective-permute-done((bf16[128,512]{1,0:T(8,128)(2,1)S(1)}, bf16[128,512]{1,0:T(8,128)(2,1)S(1)}, u32[]{:S(2)}, u32[]{:S(2)}) %collective-permute-start.9) | collective-permute-done | bytes 131104 | tf_op jit(solution)/shard_map/ppermute | solution.py:474
  63.5 0.0 collective-permute-done.11.far_ref
  63.5 0.0 copy-done
  63.5 0.7 shard_map.127
  64.3 23.5 %all_to_all.5.in_ref = bf16[4,32,2048]{2,1,0:T(8,128)(2,1)S(1)} all-to-all(bf16[4,32,2048]{2,1,0:T(8,128)(2,1)S(1)} %bitcast.3), channel_id=1, replica_groups={{0,2,4,6},{1,3,5,7},{8,10,12,14},{9,11,13,15},{16,18,20,22},{17,19,21,2..., dimensions={0} | all-to-all | bytes 1048576 | tf_op jit(solution)/shard_map/all_to_all | solution.py:480
  87.8 0.7 shard_map.128
  (10 shorter events, 0.0 us)
Async XLA Ops:
  0.0 0.9 %copy-start.1 = (bf16[256,512]{1,0:T(8,128)(2,1)S(1)}, bf16[256,512]{1,0:T(8,128)(2,1)}, u32[]{:S(2)}) copy-start(bf16[256,512]{1,0:T(8,128)(2,1)} %v_hbm.1) | copy-start | bytes 786436
  1.0 0.9 %copy-start.3 = (bf16[256,256]{1,0:T(8,128)(2,1)S(1)}, bf16[256,256]{1,0:T(8,128)(2,1)}, u32[]{:S(2)}) copy-start(bf16[256,256]{1,0:T(8,128)(2,1)} %k_hbm.1) | copy-start | bytes 393220
  1.9 0.7 copy-start.8
  2.6 0.7 copy-start.10
  3.2 0.7 copy-start.12
  3.9 0.7 copy-start.14
  4.6 0.7 copy-start.17
  7.1 0.6 copy-start.5
  7.7 11.1 %copy-start.9 = (f32[4,512]{1,0:T(4,128)S(1)}, f32[4,512]{1,0:T(4,128)}, u32[]{:S(2)}) copy-start(f32[4,512]{1,0:T(4,128)} %wv_ref.1) | copy-start | bytes 24580
  7.7 11.1 %copy-start.11 = (f32[4,256]{1,0:T(4,128)S(1)}, f32[4,256]{1,0:T(4,128)}, u32[]{:S(2)}) copy-start(f32[4,256]{1,0:T(4,128)} %beta_ref.1) | copy-start | bytes 12292
  7.7 11.1 %copy-start.13 = (f32[4,256]{1,0:T(4,128)S(1)}, f32[4,256]{1,0:T(4,128)}, u32[]{:S(2)}) copy-start(f32[4,256]{1,0:T(4,128)} %wk_ref.1) | copy-start | bytes 12292
  7.7 11.1 %copy-start.6 = (f32[16,128]{1,0:T(8,128)S(1)}, f32[16,128]{1,0:T(8,128)}, u32[]{:S(2)}) copy-start(f32[16,128]{1,0:T(8,128)} %copy-done.5) | copy-start | bytes 24580
  10.0 31.8 %collective-permute-start.10 = (bf16[256,2048]{1,0:T(8,128)(2,1)}, bf16[256,2048]{1,0:T(8,128)(2,1)S(1)}, u32[]{:S(2)}, u32[]{:S(2)}) collective-permute-start(bf16[256,2048]{1,0:T(8,128)(2,1)} %shard_map.126), channel_id=1, source_target_pairs={{0,1},{1,0},{2,3},{3,2},{4,5},{5,4},{6,7},{7,6},{8,9},{9,8},{10,11... | collective-permute-start | bytes 3145736 | tf_op jit(solution)/shard_map/ppermute | solution.py:437
  13.3 5.4 %collective-permute-start = (bf16[16,1024]{1,0:T(8,128)(2,1)}, bf16[16,1024]{1,0:T(8,128)(2,1)S(1)}, u32[]{:S(2)}, u32[]{:S(2)}) collective-permute-start(bf16[16,1024]{1,0:T(8,128)(2,1)} %shard_map.118), channel_id=1, source_target_pairs={{0,8},{8,16},{16,24},{24,32},{32,40},{40,48},{48,56},{56,64},{64,7... | collective-permute-start | bytes 98312 | tf_op jit(solution)/shard_map/ppermute | solution.py:414
  18.8 16.1 %copy-start.4 = (bf16[256,256]{1,0:T(8,128)(2,1)S(1)}, bf16[256,256]{1,0:T(8,128)(2,1)}, u32[]{:S(2)}) copy-start(bf16[256,256]{1,0:T(8,128)(2,1)} %q_ref.3) | copy-start | bytes 393220
  18.8 16.1 %copy-start.15 = (f32[4,256]{1,0:T(4,128)S(1)}, f32[4,256]{1,0:T(4,128)}, u32[]{:S(2)}) copy-start(f32[4,256]{1,0:T(4,128)} %decay_ref.1) | copy-start | bytes 12292
  18.8 16.1 %copy-start.16 = (f32[4,256]{1,0:T(4,128)S(1)}, f32[4,256]{1,0:T(4,128)}, u32[]{:S(2)}) copy-start(f32[4,256]{1,0:T(4,128)} %wq_ref.1) | copy-start | bytes 12292
  18.8 16.1 %copy-start.18 = (s32[256]{0:T(256)S(1)}, s32[256]{0:T(256)}, u32[]{:S(2)}) copy-start(s32[256]{0:T(256)} %param.18) | copy-start | bytes 3076
  29.2 1.4 %collective-permute-start.1 = (bf16[2,128,256]{2,1,0:T(8,128)(2,1)S(1)}, bf16[2,128,256]{2,1,0:T(8,128)(2,1)S(1)}, u32[]{:S(2)}, u32[]{:S(2)}) collective-permute-start(bf16[2,128,256]{2,1,0:T(8,128)(2,1)S(1)} %get-tuple-element.37), channel_id=1, source_target_pairs={{0,8},{8,0},{16,24},{24,16},{32,40},{40,32},{48,56},{56,48},{64,72... | collective-permute-start | bytes 393224 | tf_op jit(solution)/shard_map/ppermute | solution.py:444
  30.8 9.6 %collective-permute-start.4 = (bf16[2,128,256]{2,1,0:T(8,128)(2,1)S(1)}, bf16[2,128,256]{2,1,0:T(8,128)(2,1)S(1)}, u32[]{:S(2)}, u32[]{:S(2)}) collective-permute-start(bf16[2,128,256]{2,1,0:T(8,128)(2,1)S(1)} %shard_map.122.own_ref), channel_id=1, source_target_pairs={{0,48},{8,56},{16,0},{24,8},{32,16},{40,24},{48,32},{56,40},{64,11... | collective-permute-start | bytes 393224 | tf_op jit(solution)/shard_map/ppermute | solution.py:446
  31.7 8.7 %collective-permute-start.3 = (bf16[2,128,256]{2,1,0:T(8,128)(2,1)S(1)}, bf16[2,128,256]{2,1,0:T(8,128)(2,1)S(1)}, u32[]{:S(2)}, u32[]{:S(2)}) collective-permute-start(bf16[2,128,256]{2,1,0:T(8,128)(2,1)S(1)} %shard_map.122.own_ref), channel_id=1, source_target_pairs={{0,32},{8,40},{16,48},{24,56},{32,0},{40,8},{48,16},{56,24},{64,96... | collective-permute-start | bytes 393224 | tf_op jit(solution)/shard_map/ppermute | solution.py:446
  32.4 8.6 %collective-permute-start.2 = (bf16[2,128,256]{2,1,0:T(8,128)(2,1)S(1)}, bf16[2,128,256]{2,1,0:T(8,128)(2,1)S(1)}, u32[]{:S(2)}, u32[]{:S(2)}) collective-permute-start(bf16[2,128,256]{2,1,0:T(8,128)(2,1)S(1)} %shard_map.122.own_ref), channel_id=1, source_target_pairs={{0,16},{8,24},{16,32},{24,40},{32,48},{40,56},{48,0},{56,8},{64,80... | collective-permute-start | bytes 393224 | tf_op jit(solution)/shard_map/ppermute | solution.py:446
  34.9 22.5 %copy-start.2 = (bf16[256,512]{1,0:T(8,128)(2,1)S(1)}, bf16[256,512]{1,0:T(8,128)(2,1)}, u32[]{:S(2)}) copy-start(bf16[256,512]{1,0:T(8,128)(2,1)} %gate_ref.1) | copy-start | bytes 786436
  34.9 22.5 %copy-start.7 = (f32[128]{0:T(128)S(1)}, f32[128]{0:T(128)}, u32[]{:S(2)}) copy-start(f32[128]{0:T(128)} %param.22) | copy-start | bytes 1540
  35.8 27.8 %copy-start = (bf16[512,2048]{1,0:T(8,128)(2,1)S(1)}, bf16[512,2048]{1,0:T(8,128)(2,1)}, u32[]{:S(2)}) copy-start(bf16[512,2048]{1,0:T(8,128)(2,1)} %own_ref.1) | copy-start | bytes 6291460
  41.7 21.8 %collective-permute-start.11 = (bf16[256,2048]{1,0:T(8,128)(2,1)S(1)}, bf16[256,2048]{1,0:T(8,128)(2,1)S(1)}, u32[]{:S(2)}, u32[]{:S(2)}) collective-permute-start(bf16[256,2048]{1,0:T(8,128)(2,1)S(1)} %collective-permute-done.10.near_ref), channel_id=1, source_target_pairs={{0,8},{8,0},{16,24},{24,16},{32,40},{40,32},{48,56},{56,48},{64,72... | collective-permute-start | bytes 3145736 | tf_op jit(solution)/shard_map/ppermute | solution.py:461
  42.0 9.5 %collective-permute-start.7 = (bf16[2,128,256]{2,1,0:T(8,128)(2,1)S(1)}, bf16[2,128,256]{2,1,0:T(8,128)(2,1)S(1)}, u32[]{:S(2)}, u32[]{:S(2)}) collective-permute-start(bf16[2,128,256]{2,1,0:T(8,128)(2,1)S(1)} %get-tuple-element.38.own_ref), channel_id=1, source_target_pairs={{0,192},{8,200},{16,208},{24,216},{32,224},{40,232},{48,240},{56,2... | collective-permute-start | bytes 393224 | tf_op jit(solution)/shard_map/ppermute | solution.py:459
  45.3 7.9 %collective-permute-start.6 = (bf16[2,128,256]{2,1,0:T(8,128)(2,1)S(1)}, bf16[2,128,256]{2,1,0:T(8,128)(2,1)S(1)}, u32[]{:S(2)}, u32[]{:S(2)}) collective-permute-start(bf16[2,128,256]{2,1,0:T(8,128)(2,1)S(1)} %get-tuple-element.38.own_ref), channel_id=1, source_target_pairs={{0,128},{8,136},{16,144},{24,152},{32,160},{40,168},{48,176},{56,1... | collective-permute-start | bytes 393224 | tf_op jit(solution)/shard_map/ppermute | solution.py:459
  46.0 9.2 %collective-permute-start.5 = (bf16[2,128,256]{2,1,0:T(8,128)(2,1)S(1)}, bf16[2,128,256]{2,1,0:T(8,128)(2,1)S(1)}, u32[]{:S(2)}, u32[]{:S(2)}) collective-permute-start(bf16[2,128,256]{2,1,0:T(8,128)(2,1)S(1)} %get-tuple-element.38.own_ref), channel_id=1, source_target_pairs={{0,64},{8,72},{16,80},{24,88},{32,96},{40,104},{48,112},{56,120},{... | collective-permute-start | bytes 393224 | tf_op jit(solution)/shard_map/ppermute | solution.py:459
  56.1 1.3 %collective-permute-start.8 = (bf16[2,128,128]{2,1,0:T(8,128)(2,1)S(1)}, bf16[2,128,128]{2,1,0:T(8,128)(2,1)S(1)}, u32[]{:S(2)}, u32[]{:S(2)}) collective-permute-start(bf16[2,128,128]{2,1,0:T(8,128)(2,1)S(1)} %get-tuple-element.41), channel_id=1, source_target_pairs={{0,8},{8,0},{16,24},{24,16},{32,40},{40,32},{48,56},{56,48},{64,72... | collective-permute-start | bytes 196616 | tf_op jit(solution)/shard_map/ppermute | solution.py:467
  57.9 5.6 %collective-permute-start.9 = (bf16[128,512]{1,0:T(8,128)(2,1)S(1)}, bf16[128,512]{1,0:T(8,128)(2,1)S(1)}, u32[]{:S(2)}, u32[]{:S(2)}) collective-permute-start(bf16[128,512]{1,0:T(8,128)(2,1)S(1)} %get-tuple-element.43), channel_id=1, source_target_pairs={{0,1},{1,0},{2,3},{3,2},{4,5},{5,4},{6,7},{7,6},{8,9},{9,8},{10,11... | collective-permute-start | bytes 393224 | tf_op jit(solution)/shard_map/ppermute | solution.py:474

commit v4 on v3

--- a/solution.py
+++ b/solution.py
@@ -151,31 +151,13 @@
     out_ref[:, 768:1024] = q_ref[...]
 
 
-def half_kernel(weight_ref, after_ref, out_ref, sem):
-    core = lax.axis_index("ctx") % CORES
-    rows = weight_ref.shape[0] // CORES
-    copy = pltpu.make_async_copy(weight_ref.at[pl.ds(core * rows, rows)], out_ref, sem)
-    copy.start()
-    copy.wait()
-
-
 def early_kernel(
-    k_hbm, v_hbm, decay_hbm, beta_hbm, doc_hbm, wk_hbm, wv_hbm,
-    key_ref, value_ref, factor_ref, carry_ref, last_ref, start_ref, head_ref,
-    k_ref, v_ref, decay_ref, beta_ref, doc_ref, wk_ref, wv_ref, ext_ref, sems,
-):
-    moves = (
-        (doc_hbm, doc_ref), (decay_hbm, decay_ref), (beta_hbm, beta_ref), (k_hbm, k_ref),
-        (wk_hbm, wk_ref), (v_hbm, v_ref), (wv_hbm, wv_ref),
-    )
-    copies = [pltpu.make_async_copy(a, b, sems.at[i]) for i, (a, b) in enumerate(moves)]
-    for copy in copies:
-        copy.start()
+    k_ref, v_ref, decay_ref, beta_ref, doc_ref, wk_ref, wv_ref, edge_ref,
+    key_ref, value_ref, factor_ref, carry_ref, last_ref, start_ref, head_ref, ext_ref,
+):
     row, col = rows_and_columns()
     lower = (col <= row).astype(BF16)
     eye = (col == row).astype(BF16)
-    for copy in copies[:3]:
-        copy.wait()
     start = spread([local_start(doc_ref)], eye, 1)[0]
     start_ref[...] = start[0:RIM]
     decay = decay_ref[...]
@@ -190,8 +172,6 @@
         factor_ref[h] = jnp.where(col < row, beta_wide * fade, 0.0)
         carry_ref[h] = jnp.where(start < 0.0, jnp.exp(cum_col[h]), 0.0)
         last_ref[h : h + 1] = fade[TOK - 1 : TOK, :]
-    for copy in copies[3:]:
-        copy.wait()
     valid = tap_masks(start)
     key_conv = short_conv(ext_ref, k_ref, jnp.zeros((8, 256), F32), wk_ref, valid)
     for g, key in enumerate(unit_keys(key_conv)):
@@ -359,17 +339,12 @@
             give_ref[at] = jnp.where(side == 0, odd, even)
 
 
-def project_kernel(keep_ref, got_ref, own_ref, near_ref, far_ref, out_ref):
-    core = lax.axis_index("ctx") % CORES
+def project_kernel(keep_ref, got_ref, own_ref, near_ref, out_ref):
     keep = keep_ref[...]
     got = got_ref[...]
-    half = got.shape[1] // 2
-    first = jnp.where(core == 0, got[:, :half], got[:, half:])
-    second = jnp.where(core == 0, got[:, half:], got[:, :half])
     for part in range(0, own_ref.shape[1], 512):
         at = slice(part, part + 512)
-        total = mm(keep, own_ref[:, at]) + mm(first, near_ref[:, at]) + mm(second, far_ref[:, at])
-        out_ref[:, at] = total.astype(BF16)
+        out_ref[:, at] = (mm(keep, own_ref[:, at]) + mm(got, near_ref[:, at])).astype(BF16)
 
 
 def sum_kernel(in_ref, out_ref):
@@ -383,9 +358,20 @@
 HBM = pl.BlockSpec(memory_space=pltpu.HBM)
 
 
-def call(kernel, outs, inputs, scratch=(), flops=0, moved=0, limit=32, specs=None, out_specs=None):
+def whole(shape):
+    return pl.BlockSpec(shape, lambda i: (0,) * len(shape))
+
+
+def call(
+    kernel, outs, inputs, scratch=(), flops=0, moved=0, limit=32, specs=None, out_specs=None,
+    blocked=False,
+):
+    if blocked:
+        specs = [whole(a.shape) for a in inputs]
+        out_specs = [whole(s) for s, _ in outs]
     return pl.pallas_call(
         kernel,
+        grid=(1,) if blocked else (),
         out_shape=[jax.ShapeDtypeStruct(s, t) for s, t in outs],
         in_specs=[VMEM] * len(inputs) if specs is None else specs,
         out_specs=[VMEM] * len(outs) if out_specs is None else out_specs,
@@ -409,8 +395,11 @@
         out_shape=jax.ShapeDtypeStruct((RIM, 1024), BF16),
         in_specs=[pl.BlockSpec((RIM, n), lambda i: (last, 0)) for n in (256, 512, 256)],
         out_specs=pl.BlockSpec((RIM, 1024), lambda i: (0, 0)),
-        compiler_params=pltpu.CompilerParams(vmem_limit_bytes=60 * MIB),
+        cost_estimate=pl.CostEstimate(flops=5_000_000_000, bytes_accessed=0, transcendentals=0),
     )(key_in, value_in, query_in)
+    near_weight = lax.ppermute(
+        lax.optimization_barrier((out_weight, edge))[0], "head", [(i, i ^ 1) for i in range(8)]
+    )
     rim = lax.ppermute(edge, "ctx", [(i, i + 1) for i in range(CTX - 1)])
     wide = (2, DK, DK + DV)
     early = call(
@@ -419,22 +408,13 @@
             ((GROUPS, TOK, DK), BF16), ((TOK, HEADS * DV), BF16), ((HEADS, TOK, TOK), F32),
             ((HEADS, TOK, 128), F32), ((HEADS, TOK), F32), ((RIM, 128), F32), ((RIM, 768), BF16),
         ],
-        [key_in, value_in, log_decay, beta_gate, doc_row, conv_key, conv_value],
+        [key_in, value_in, log_decay, beta_gate, doc_row, conv_key, conv_value, edge],
         [
-            pltpu.VMEM((TOK, 256), BF16), pltpu.VMEM((TOK, 512), BF16),
-            pltpu.VMEM((HEADS, TOK), F32), pltpu.VMEM((HEADS, TOK), F32),
-            pltpu.VMEM((1, TOK), jnp.int32), pltpu.VMEM((TAPS, 256), F32),
-            pltpu.VMEM((TAPS, 512), F32), pltpu.VMEM((8 + TOK, 512), F32),
-            pltpu.SemaphoreType.DMA((7,)),
+            pltpu.VMEM((8 + TOK, 512), F32),
         ],
-        flops=500_000_000, moved=1_500_000, specs=[HBM] * 7, limit=50,
+        flops=500_000_000, moved=0, limit=48, blocked=True,
     )
     keys, values, factor, carry, final, start, head = early
-    (half,) = call(
-        half_kernel, [((out_weight.shape[0] // CORES, width), BF16)], [out_weight, start],
-        [pltpu.SemaphoreType.DMA], specs=[HBM] * 2, limit=62,
-    )
-    near_weight = lax.ppermute(half, "head", [(i, i ^ 1) for i in range(8)])
     solved, keys, own, give = call(
         map_kernel,
         [((HEADS, TOK, DK + DV), BF16), ((GROUPS, TOK, DK), BF16), (wide, BF16), (wide, BF16)],
@@ -457,8 +437,6 @@
         specs=[VMEM] * 4 + [HBM],
     )
     far = [lax.ppermute(total, "ctx", along_y(k)) for k in (1, 2, 3)]
-    late_weight, _ = lax.optimization_barrier((near_weight, total))
-    far_weight = lax.ppermute(late_weight, "ctx", core_swap())
     narrow = (2, DK, DV)
     mine, to_other = call(
         state_kernel, [(narrow, BF16), (narrow, BF16)], [total] + far + [before, own, other],
@@ -474,7 +452,7 @@
     brought = lax.ppermute(to_near, "head", [(i, i ^ 1) for i in range(8)])
     (partial,) = call(
         project_kernel, [((TOK // 2, width), BF16)],
-        [keep, brought, out_weight, near_weight, far_weight],
+        [keep, brought, out_weight, near_weight],
         flops=600_000_000, moved=4_000_000,
     )
     blocks = lax.all_to_all(

time: 90.1 us -> 79.6 us (0.88)
  the two profiles are of different devices: /device:TPU:6 before, /device:TPU:32 now
where the time goes in v4:
time: 79.6 us; the launch traced here: 79.3 us
  blocking collectives  24.3 us (31%)
  waiting for transfers between devices  21 us (26%)
  Pallas kernels  17.6 us (22%)
  starting transfers between devices  15.3 us (19%)
  local copies, waits for them, and re-layouts  0.91 us (1%)
    all_to_all x1, blocking collectives, on_device(): lax.all_to_all(partial.reshape(4, TOK // 8, width), 'head', 0, 0, axis_in...  24.3 us
    pallas_call x9, Pallas kernels, call(): pl.pallas_call(kernel, grid=(1,) if blocked else (), out_shape=[jax.Shape...  16.1 us
    ppermute x3, waiting for transfers between devices, on_device(): far = [lax.ppermute(total, 'ctx', along_y(k)) for k in (1, 2, 3)]  7.85 us
    ppermute x3, waiting for transfers between devices, on_device(): near = [lax.ppermute(pair, 'ctx', along_x(k)) for k in (1, 2, 3)]  7.08 us
    ppermute x3, starting transfers between devices, on_device(): far = [lax.ppermute(total, 'ctx', along_y(k)) for k in (1, 2, 3)]  4.83 us
    ppermute x3, starting transfers between devices, on_device(): near = [lax.ppermute(pair, 'ctx', along_x(k)) for k in (1, 2, 3)]  4.7 us
    ppermute x1, waiting for transfers between devices, on_device(): brought = lax.ppermute(to_near, 'head', [(i, i ^ 1) for i in range(8)])  3.82 us
    ppermute x1, starting transfers between devices, on_device(): brought = lax.ppermute(to_near, 'head', [(i, i ^ 1) for i in range(8)])  2.01 us
  transfers between devices with their start and end apart: 11, of which 9 were waited for; matrix products, arithmetic and copies ran while one was open for 0% of the time, Pallas kernels for 18%

profile of v4, /device:TPU:32, one launch (start us, length us, event | category | flops | bytes accessed | tf_op | source)
XLA Modules:
  0.0 79.3 jit_solution(16852317007551542328)
XLA Ops:
  0.0 0.0 copy-start.3
  0.0 0.0 copy-start.4
  0.0 0.0 copy-start
  0.0 0.0 copy-start.7
  0.0 0.0 copy-start.9
  0.0 0.0 copy-start.8
  0.0 0.0 copy-start.10
  0.0 0.0 copy-start.12
  0.1 1.5 %shard_map.118.edge_ref = bf16[16,1024]{1,0:T(8,128)(2,1)} custom-call(bf16[256,256]{1,0:T(8,128)(2,1)} %k_ref.3, bf16[256,512]{1,0:T(8,128)(2,1)} %v_ref.3, bf16[256,256]{1,0:T(8,128)(2,1)} %q_ref.3), custom_call_target="tpu_custom_call" | custom-call | flops 5000000000 | tf_op jit(solution)/shard_map/pallas_call | solution.py:392
  1.5 0.1 copy-done
  1.7 1.8 %collective-permute-start.10 = (bf16[512,2048]{1,0:T(8,128)(2,1)S(1)}, bf16[512,2048]{1,0:T(8,128)(2,1)S(1)}, u32[]{:S(2)}, u32[]{:S(2)}) collective-permute-start(bf16[512,2048]{1,0:T(8,128)(2,1)S(1)} %copy-done), channel_id=1, source_target_pairs={{0,1},{1,0},{2,3},{3,2},{4,5},{5,4},{6,7},{7,6},{8,9},{9,8},{10,11... | collective-permute-start | bytes 6291464 | tf_op jit(solution)/shard_map/ppermute | solution.py:400
  3.5 1.3 %collective-permute-start = (bf16[16,1024]{1,0:T(8,128)(2,1)}, bf16[16,1024]{1,0:T(8,128)(2,1)S(1)}, u32[]{:S(2)}, u32[]{:S(2)}) collective-permute-start(bf16[16,1024]{1,0:T(8,128)(2,1)} %shard_map.118.edge_ref), channel_id=1, source_target_pairs={{0,8},{8,16},{16,24},{24,32},{32,40},{40,48},{48,56},{56,64},{64,7... | collective-permute-start | bytes 98312 | tf_op jit(solution)/shard_map/ppermute | solution.py:403
  4.8 0.0 copy-done.3
  4.8 0.0 copy-done.4
  4.8 0.0 copy-done.7
  4.8 0.0 copy-done.9
  4.8 0.0 copy-done.8
  4.8 0.0 copy-done.10
  4.8 0.0 copy-done.12
  4.9 0.0 copy-start.6
  4.9 0.7 copy-done.6
  5.6 1.2 %shard_map.119 = (bf16[2,256,128]{2,1,0:T(8,128)(2,1)S(1)}, bf16[256,512]{1,0:T(8,128)(2,1)S(1)}, f32[4,256,256]{2,1,0:T(8,128)S(1)}, f32[4,256,128]{2,1,0:T(8,1...) custom-call(bf16[256,256]{1,0:T(8,128)(2,1)S(1)} %copy-done.4, ...), custom_call_target="tpu_custom_call" | custom-call | flops 500000000 | tf_op jit(solution)/shard_map/pallas_call | solution.py:372
  6.9 0.0 collective-permute-done.rim_ref
  6.9 0.0 copy-start.5
  6.9 0.0 copy-start.11
  6.9 10.4 %shard_map.120 = (bf16[4,256,256]{2,1,0:T(8,128)(2,1)S(1)}, bf16[2,256,128]{2,1,0:T(8,128)(2,1)S(1)}, bf16[2,128,256]{2,1,0:T(8,128)(2,1)S(1)}, bf16[2,128,256]{2,1,0:T(8,128)(2,1)S(1)}) custom-call(bf16[16,1024]{1,0:T(8,128)(2,1)S(1)} %collective-permute-done.rim_ref, bf16[16,768]{1,0:T(8,128)(2,1)S(1)} %get-tuple-element.25.head_ref, ...), custom_call_target="tpu_custom_call" | custom-call | flops 4000000000 | bytes 2000000 | tf_op jit(solution)/shard_map/pallas_call | solution.py:372
  17.3 0.6 collective-permute-start.1
  17.9 1.0 %collective-permute-done.1.got_ref.other_ref = bf16[2,128,256]{2,1,0:T(8,128)(2,1)S(1)} collective-permute-done((bf16[2,128,256]{2,1,0:T(8,128)(2,1)S(1)}, bf16[2,128,256]{2,1,0:T(8,128)(2,1)S(1)}, u32[]{:S(2)}, u32[]{:S(2)}) %collective-permute-start.1) | collective-permute-done | bytes 131104 | tf_op jit(solution)/shard_map/ppermute | solution.py:424
  18.8 0.2 shard_map.122.own_ref
  19.0 3.0 %collective-permute-start.4 = (bf16[2,128,256]{2,1,0:T(8,128)(2,1)S(1)}, bf16[2,128,256]{2,1,0:T(8,128)(2,1)S(1)}, u32[]{:S(2)}, u32[]{:S(2)}) collective-permute-start(bf16[2,128,256]{2,1,0:T(8,128)(2,1)S(1)} %shard_map.122.own_ref), channel_id=1, source_target_pairs={{0,48},{8,56},{16,0},{24,8},{32,16},{40,24},{48,32},{56,40},{64,11... | collective-permute-start | bytes 393224 | tf_op jit(solution)/shard_map/ppermute | solution.py:426
  22.0 0.8 %collective-permute-start.3 = (bf16[2,128,256]{2,1,0:T(8,128)(2,1)S(1)}, bf16[2,128,256]{2,1,0:T(8,128)(2,1)S(1)}, u32[]{:S(2)}, u32[]{:S(2)}) collective-permute-start(bf16[2,128,256]{2,1,0:T(8,128)(2,1)S(1)} %shard_map.122.own_ref), channel_id=1, source_target_pairs={{0,32},{8,40},{16,48},{24,56},{32,0},{40,8},{48,16},{56,24},{64,96... | collective-permute-start | bytes 393224 | tf_op jit(solution)/shard_map/ppermute | solution.py:426
  22.8 0.9 %collective-permute-start.2 = (bf16[2,128,256]{2,1,0:T(8,128)(2,1)S(1)}, bf16[2,128,256]{2,1,0:T(8,128)(2,1)S(1)}, u32[]{:S(2)}, u32[]{:S(2)}) collective-permute-start(bf16[2,128,256]{2,1,0:T(8,128)(2,1)S(1)} %shard_map.122.own_ref), channel_id=1, source_target_pairs={{0,16},{8,24},{16,32},{24,40},{32,48},{40,56},{48,0},{56,8},{64,80... | collective-permute-start | bytes 393224 | tf_op jit(solution)/shard_map/ppermute | solution.py:426
  23.7 0.0 copy-done.5
  23.7 0.0 copy-done.11
  23.7 0.0 copy-start.1
  23.7 0.0 copy-start.2
  23.7 0.8 %shard_map.121 = (f32[4,256,128]{2,1,0:T(8,128)S(1)}, bf16[4,256,128]{2,1,0:T(8,128)(2,1)S(1)}) custom-call(bf16[256,256]{1,0:T(8,128)(2,1)S(1)} %copy-done.5, bf16[16,1024]{1,0:T(8,128)(2,1)S(1)} %collective-permute-done.rim_ref, f32[4,256]{1,0:T(4,128)S(1)} %copy-done.10, s32[1,256]{1,0:T(1,128)S(1)} %bitcast.6, f32[4,256]{1,0:T(4,128)S(1)} %copy-done.11, ...), custom_call_target="tpu_custom_call" | custom-call | flops 2000000000 | bytes 2000000 | tf_op jit(solution)/shard_map/pallas_call | solution.py:372
  24.6 3.4 %collective-permute-done.4.three_ref = bf16[2,128,256]{2,1,0:T(8,128)(2,1)S(1)} collective-permute-done((bf16[2,128,256]{2,1,0:T(8,128)(2,1)S(1)}, bf16[2,128,256]{2,1,0:T(8,128)(2,1)S(1)}, u32[]{:S(2)}, u32[]{:S(2)}) %collective-permute-start.4) | collective-permute-done | bytes 131104 | tf_op jit(solution)/shard_map/ppermute | solution.py:426
  28.0 1.9 %collective-permute-done.3.two_ref = bf16[2,128,256]{2,1,0:T(8,128)(2,1)S(1)} collective-permute-done((bf16[2,128,256]{2,1,0:T(8,128)(2,1)S(1)}, bf16[2,128,256]{2,1,0:T(8,128)(2,1)S(1)}, u32[]{:S(2)}, u32[]{:S(2)}) %collective-permute-start.3) | collective-permute-done | bytes 131104 | tf_op jit(solution)/shard_map/ppermute | solution.py:426
  29.9 1.7 %collective-permute-done.2.one_ref = bf16[2,128,256]{2,1,0:T(8,128)(2,1)S(1)} collective-permute-done((bf16[2,128,256]{2,1,0:T(8,128)(2,1)S(1)}, bf16[2,128,256]{2,1,0:T(8,128)(2,1)S(1)}, u32[]{:S(2)}, u32[]{:S(2)}) %collective-permute-start.2) | collective-permute-done | bytes 131104 | tf_op jit(solution)/shard_map/ppermute | solution.py:426
  31.7 0.7 shard_map.123
  32.4 3.2 %collective-permute-start.7 = (bf16[2,128,256]{2,1,0:T(8,128)(2,1)S(1)}, bf16[2,128,256]{2,1,0:T(8,128)(2,1)S(1)}, u32[]{:S(2)}, u32[]{:S(2)}) collective-permute-start(bf16[2,128,256]{2,1,0:T(8,128)(2,1)S(1)} %get-tuple-element.38.own_ref), channel_id=1, source_target_pairs={{0,192},{8,200},{16,208},{24,216},{32,224},{40,232},{48,240},{56,2... | collective-permute-start | bytes 393224 | tf_op jit(solution)/shard_map/ppermute | solution.py:439
  35.6 0.7 collective-permute-start.6
  36.3 0.9 %collective-permute-start.5 = (bf16[2,128,256]{2,1,0:T(8,128)(2,1)S(1)}, bf16[2,128,256]{2,1,0:T(8,128)(2,1)S(1)}, u32[]{:S(2)}, u32[]{:S(2)}) collective-permute-start(bf16[2,128,256]{2,1,0:T(8,128)(2,1)S(1)} %get-tuple-element.38.own_ref), channel_id=1, source_target_pairs={{0,64},{8,72},{16,80},{24,88},{32,96},{40,104},{48,112},{56,120},{... | collective-permute-start | bytes 393224 | tf_op jit(solution)/shard_map/ppermute | solution.py:439
  37.2 4.1 %collective-permute-done.7.three_ref = bf16[2,128,256]{2,1,0:T(8,128)(2,1)S(1)} collective-permute-done((bf16[2,128,256]{2,1,0:T(8,128)(2,1)S(1)}, bf16[2,128,256]{2,1,0:T(8,128)(2,1)S(1)}, u32[]{:S(2)}, u32[]{:S(2)}) %collective-permute-start.7) | collective-permute-done | bytes 131104 | tf_op jit(solution)/shard_map/ppermute | solution.py:439
  41.4 2.2 %collective-permute-done.6.two_ref = bf16[2,128,256]{2,1,0:T(8,128)(2,1)S(1)} collective-permute-done((bf16[2,128,256]{2,1,0:T(8,128)(2,1)S(1)}, bf16[2,128,256]{2,1,0:T(8,128)(2,1)S(1)}, u32[]{:S(2)}, u32[]{:S(2)}) %collective-permute-start.6) | collective-permute-done | bytes 131104 | tf_op jit(solution)/shard_map/ppermute | solution.py:439
  43.5 1.5 %collective-permute-done.5.one_ref = bf16[2,128,256]{2,1,0:T(8,128)(2,1)S(1)} collective-permute-done((bf16[2,128,256]{2,1,0:T(8,128)(2,1)S(1)}, bf16[2,128,256]{2,1,0:T(8,128)(2,1)S(1)}, u32[]{:S(2)}, u32[]{:S(2)}) %collective-permute-start.5) | collective-permute-done | bytes 131104 | tf_op jit(solution)/shard_map/ppermute | solution.py:439
  45.1 0.9 %shard_map.124 = (bf16[2,128,128]{2,1,0:T(8,128)(2,1)S(1)}, bf16[2,128,128]{2,1,0:T(8,128)(2,1)S(1)}) custom-call(bf16[2,128,256]{2,1,0:T(8,128)(2,1)S(1)} %get-tuple-element.38.own_ref, bf16[2,128,256]{2,1,0:T(8,128)(2,1)S(1)} %collective-permute-done.5.one_ref, bf16[2,128,256]{2,1,0:T(8,128)(2,1)S(1)} %collective-permute-done.6.two_ref, ...), custom_call_target="tpu_custom_call" | custom-call | flops 60000000 | bytes 1000000 | tf_op jit(solution)/shard_map/pallas_call | solution.py:372
  46.0 0.1 collective-permute-start.8
  46.1 1.2 %collective-permute-done.8.got_ref = bf16[2,128,128]{2,1,0:T(8,128)(2,1)S(1)} collective-permute-done((bf16[2,128,128]{2,1,0:T(8,128)(2,1)S(1)}, bf16[2,128,128]{2,1,0:T(8,128)(2,1)S(1)}, u32[]{:S(2)}, u32[]{:S(2)}) %collective-permute-start.8) | collective-permute-done | bytes 65568 | tf_op jit(solution)/shard_map/ppermute | solution.py:445
  47.3 0.0 copy-done.1
  47.3 0.0 copy-done.2
  47.3 0.4 shard_map.125
  47.7 2.0 %collective-permute-start.9 = (bf16[128,512]{1,0:T(8,128)(2,1)S(1)}, bf16[128,512]{1,0:T(8,128)(2,1)S(1)}, u32[]{:S(2)}, u32[]{:S(2)}) collective-permute-start(bf16[128,512]{1,0:T(8,128)(2,1)S(1)} %get-tuple-element.43), channel_id=1, source_target_pairs={{0,1},{1,0},{2,3},{3,2},{4,5},{5,4},{6,7},{7,6},{8,9},{9,8},{10,11... | collective-permute-start | bytes 393224 | tf_op jit(solution)/shard_map/ppermute | solution.py:452
  49.8 3.8 %collective-permute-done.9.got_ref = bf16[128,512]{1,0:T(8,128)(2,1)S(1)} collective-permute-done((bf16[128,512]{1,0:T(8,128)(2,1)S(1)}, bf16[128,512]{1,0:T(8,128)(2,1)S(1)}, u32[]{:S(2)}, u32[]{:S(2)}) %collective-permute-start.9) | collective-permute-done | bytes 131104 | tf_op jit(solution)/shard_map/ppermute | solution.py:452
  53.6 0.0 collective-permute-done.10.near_ref
  53.6 0.8 shard_map.126
  54.3 24.3 %all_to_all.5.in_ref = bf16[4,32,2048]{2,1,0:T(8,128)(2,1)S(1)} all-to-all(bf16[4,32,2048]{2,1,0:T(8,128)(2,1)S(1)} %bitcast.3), channel_id=1, replica_groups={{0,2,4,6},{1,3,5,7},{8,10,12,14},{9,11,13,15},{16,18,20,22},{17,19,21,2..., dimensions={0} | all-to-all | bytes 1048576 | tf_op jit(solution)/shard_map/all_to_all | solution.py:458
  78.6 0.7 shard_map.127
Async XLA Ops:
  0.0 4.8 %copy-start.3 = (bf16[256,512]{1,0:T(8,128)(2,1)S(1)}, bf16[256,512]{1,0:T(8,128)(2,1)}, u32[]{:S(2)}) copy-start(bf16[256,512]{1,0:T(8,128)(2,1)} %v_ref.3) | copy-start | bytes 786436
  0.0 4.8 %copy-start.4 = (bf16[256,256]{1,0:T(8,128)(2,1)S(1)}, bf16[256,256]{1,0:T(8,128)(2,1)}, u32[]{:S(2)}) copy-start(bf16[256,256]{1,0:T(8,128)(2,1)} %k_ref.3) | copy-start | bytes 393220
  0.0 1.7 %copy-start = (bf16[512,2048]{1,0:T(8,128)(2,1)S(1)}, bf16[512,2048]{1,0:T(8,128)(2,1)}, u32[]{:S(2)}) copy-start(bf16[512,2048]{1,0:T(8,128)(2,1)} %own_ref.1) | copy-start | bytes 6291460
  0.0 4.8 %copy-start.7 = (f32[4,512]{1,0:T(4,128)S(1)}, f32[4,512]{1,0:T(4,128)}, u32[]{:S(2)}) copy-start(f32[4,512]{1,0:T(4,128)} %wv_ref.3) | copy-start | bytes 24580
  0.0 4.8 %copy-start.9 = (f32[4,256]{1,0:T(4,128)S(1)}, f32[4,256]{1,0:T(4,128)}, u32[]{:S(2)}) copy-start(f32[4,256]{1,0:T(4,128)} %wk_ref.3) | copy-start | bytes 12292
  0.0 4.8 %copy-start.8 = (f32[4,256]{1,0:T(4,128)S(1)}, f32[4,256]{1,0:T(4,128)}, u32[]{:S(2)}) copy-start(f32[4,256]{1,0:T(4,128)} %beta_ref.3) | copy-start | bytes 12292
  0.0 4.8 %copy-start.10 = (f32[4,256]{1,0:T(4,128)S(1)}, f32[4,256]{1,0:T(4,128)}, u32[]{:S(2)}) copy-start(f32[4,256]{1,0:T(4,128)} %decay_ref.3) | copy-start | bytes 12292
  0.0 4.8 %copy-start.12 = (s32[256]{0:T(256)S(1)}, s32[256]{0:T(256)}, u32[]{:S(2)}) copy-start(s32[256]{0:T(256)} %param.18) | copy-start | bytes 3076
  1.7 51.9 %collective-permute-start.10 = (bf16[512,2048]{1,0:T(8,128)(2,1)S(1)}, bf16[512,2048]{1,0:T(8,128)(2,1)S(1)}, u32[]{:S(2)}, u32[]{:S(2)}) collective-permute-start(bf16[512,2048]{1,0:T(8,128)(2,1)S(1)} %copy-done), channel_id=1, source_target_pairs={{0,1},{1,0},{2,3},{3,2},{4,5},{5,4},{6,7},{7,6},{8,9},{9,8},{10,11... | collective-permute-start | bytes 6291464 | tf_op jit(solution)/shard_map/ppermute | solution.py:400
  3.5 3.4 %collective-permute-start = (bf16[16,1024]{1,0:T(8,128)(2,1)}, bf16[16,1024]{1,0:T(8,128)(2,1)S(1)}, u32[]{:S(2)}, u32[]{:S(2)}) collective-permute-start(bf16[16,1024]{1,0:T(8,128)(2,1)} %shard_map.118.edge_ref), channel_id=1, source_target_pairs={{0,8},{8,16},{16,24},{24,32},{32,40},{40,48},{48,56},{56,64},{64,7... | collective-permute-start | bytes 98312 | tf_op jit(solution)/shard_map/ppermute | solution.py:403
  4.9 0.8 copy-start.6
  6.9 16.9 %copy-start.5 = (bf16[256,256]{1,0:T(8,128)(2,1)S(1)}, bf16[256,256]{1,0:T(8,128)(2,1)}, u32[]{:S(2)}) copy-start(bf16[256,256]{1,0:T(8,128)(2,1)} %q_ref.3) | copy-start | bytes 393220
  6.9 16.8 %copy-start.11 = (f32[4,256]{1,0:T(4,128)S(1)}, f32[4,256]{1,0:T(4,128)}, u32[]{:S(2)}) copy-start(f32[4,256]{1,0:T(4,128)} %wq_ref.1) | copy-start | bytes 12292
  17.3 1.6 %collective-permute-start.1 = (bf16[2,128,256]{2,1,0:T(8,128)(2,1)S(1)}, bf16[2,128,256]{2,1,0:T(8,128)(2,1)S(1)}, u32[]{:S(2)}, u32[]{:S(2)}) collective-permute-start(bf16[2,128,256]{2,1,0:T(8,128)(2,1)S(1)} %get-tuple-element.37), channel_id=1, source_target_pairs={{0,8},{8,0},{16,24},{24,16},{32,40},{40,32},{48,56},{56,48},{64,72... | collective-permute-start | bytes 393224 | tf_op jit(solution)/shard_map/ppermute | solution.py:424
  19.0 9.0 %collective-permute-start.4 = (bf16[2,128,256]{2,1,0:T(8,128)(2,1)S(1)}, bf16[2,128,256]{2,1,0:T(8,128)(2,1)S(1)}, u32[]{:S(2)}, u32[]{:S(2)}) collective-permute-start(bf16[2,128,256]{2,1,0:T(8,128)(2,1)S(1)} %shard_map.122.own_ref), channel_id=1, source_target_pairs={{0,48},{8,56},{16,0},{24,8},{32,16},{40,24},{48,32},{56,40},{64,11... | collective-permute-start | bytes 393224 | tf_op jit(solution)/shard_map/ppermute | solution.py:426
  22.0 7.9 %collective-permute-start.3 = (bf16[2,128,256]{2,1,0:T(8,128)(2,1)S(1)}, bf16[2,128,256]{2,1,0:T(8,128)(2,1)S(1)}, u32[]{:S(2)}, u32[]{:S(2)}) collective-permute-start(bf16[2,128,256]{2,1,0:T(8,128)(2,1)S(1)} %shard_map.122.own_ref), channel_id=1, source_target_pairs={{0,32},{8,40},{16,48},{24,56},{32,0},{40,8},{48,16},{56,24},{64,96... | collective-permute-start | bytes 393224 | tf_op jit(solution)/shard_map/ppermute | solution.py:426
  22.8 8.8 %collective-permute-start.2 = (bf16[2,128,256]{2,1,0:T(8,128)(2,1)S(1)}, bf16[2,128,256]{2,1,0:T(8,128)(2,1)S(1)}, u32[]{:S(2)}, u32[]{:S(2)}) collective-permute-start(bf16[2,128,256]{2,1,0:T(8,128)(2,1)S(1)} %shard_map.122.own_ref), channel_id=1, source_target_pairs={{0,16},{8,24},{16,32},{24,40},{32,48},{40,56},{48,0},{56,8},{64,80... | collective-permute-start | bytes 393224 | tf_op jit(solution)/shard_map/ppermute | solution.py:426
  23.7 23.6 %copy-start.1 = (bf16[256,512]{1,0:T(8,128)(2,1)S(1)}, bf16[256,512]{1,0:T(8,128)(2,1)}, u32[]{:S(2)}) copy-start(bf16[256,512]{1,0:T(8,128)(2,1)} %gate_ref.1) | copy-start | bytes 786436
  23.7 23.6 %copy-start.2 = (f32[128]{0:T(128)S(1)}, f32[128]{0:T(128)}, u32[]{:S(2)}) copy-start(f32[128]{0:T(128)} %param.22) | copy-start | bytes 1540
  32.4 9.0 %collective-permute-start.7 = (bf16[2,128,256]{2,1,0:T(8,128)(2,1)S(1)}, bf16[2,128,256]{2,1,0:T(8,128)(2,1)S(1)}, u32[]{:S(2)}, u32[]{:S(2)}) collective-permute-start(bf16[2,128,256]{2,1,0:T(8,128)(2,1)S(1)} %get-tuple-element.38.own_ref), channel_id=1, source_target_pairs={{0,192},{8,200},{16,208},{24,216},{32,224},{40,232},{48,240},{56,2... | collective-permute-start | bytes 393224 | tf_op jit(solution)/shard_map/ppermute | solution.py:439
  35.6 7.9 %collective-permute-start.6 = (bf16[2,128,256]{2,1,0:T(8,128)(2,1)S(1)}, bf16[2,128,256]{2,1,0:T(8,128)(2,1)S(1)}, u32[]{:S(2)}, u32[]{:S(2)}) collective-permute-start(bf16[2,128,256]{2,1,0:T(8,128)(2,1)S(1)} %get-tuple-element.38.own_ref), channel_id=1, source_target_pairs={{0,128},{8,136},{16,144},{24,152},{32,160},{40,168},{48,176},{56,1... | collective-permute-start | bytes 393224 | tf_op jit(solution)/shard_map/ppermute | solution.py:439
  36.3 8.8 %collective-permute-start.5 = (bf16[2,128,256]{2,1,0:T(8,128)(2,1)S(1)}, bf16[2,128,256]{2,1,0:T(8,128)(2,1)S(1)}, u32[]{:S(2)}, u32[]{:S(2)}) collective-permute-start(bf16[2,128,256]{2,1,0:T(8,128)(2,1)S(1)} %get-tuple-element.38.own_ref), channel_id=1, source_target_pairs={{0,64},{8,72},{16,80},{24,88},{32,96},{40,104},{48,112},{56,120},{... | collective-permute-start | bytes 393224 | tf_op jit(solution)/shard_map/ppermute | solution.py:439
  46.0 1.3 %collective-permute-start.8 = (bf16[2,128,128]{2,1,0:T(8,128)(2,1)S(1)}, bf16[2,128,128]{2,1,0:T(8,128)(2,1)S(1)}, u32[]{:S(2)}, u32[]{:S(2)}) collective-permute-start(bf16[2,128,128]{2,1,0:T(8,128)(2,1)S(1)} %get-tuple-element.41), channel_id=1, source_target_pairs={{0,8},{8,0},{16,24},{24,16},{32,40},{40,32},{48,56},{56,48},{64,72... | collective-permute-start | bytes 196616 | tf_op jit(solution)/shard_map/ppermute | solution.py:445
  47.7 5.8 %collective-permute-start.9 = (bf16[128,512]{1,0:T(8,128)(2,1)S(1)}, bf16[128,512]{1,0:T(8,128)(2,1)S(1)}, u32[]{:S(2)}, u32[]{:S(2)}) collective-permute-start(bf16[128,512]{1,0:T(8,128)(2,1)S(1)} %get-tuple-element.43), channel_id=1, source_target_pairs={{0,1},{1,0},{2,3},{3,2},{4,5},{5,4},{6,7},{7,6},{8,9},{9,8},{10,11... | collective-permute-start | bytes 393224 | tf_op jit(solution)/shard_map/ppermute | solution.py:452

commit v5 on v4

--- a/solution.py
+++ b/solution.py
@@ -123,26 +123,99 @@
     return (col <= row) & (begin <= col.astype(F32))
 
 
-def unit_lower_inverse(a, row, col):
-    apart = row ^ col
-    eye = (row == col).astype(F32)
-    d = jnp.where(apart < 8, a, 0.0)
-    db = d.astype(BF16)
-    square = mm(db, db).astype(BF16)
-    t = eye - d
-    t = t + mm(t.astype(BF16), square)
-    fourth = mm(square, square).astype(BF16)
-    t = t + mm(t.astype(BF16), fourth)
-    size = 8
-    while size < TOK:
-        e = jnp.where((apart >= size) & (apart < 2 * size), a, 0.0).astype(BF16)
-        tb = t.astype(BF16)
-        t = t - mm(mm(tb, e).astype(BF16), tb)
-        size *= 2
-    guess = t.astype(BF16)
-    high, low = parts(a, 2)
-    rest = eye - guess.astype(F32) - mm(high, guess) - mm(low, guess)
-    return guess.astype(F32) + mm(guess, rest.astype(BF16))
+LEVELS = (8, 16, 32, 64)
+
+
+def block_masks():
+    row, col = rows_and_columns()
+    out = []
+    for size in LEVELS:
+        shift = size.bit_length() - 1
+        r, c = row >> shift, col >> shift
+        out.append((r == c).astype(F32).astype(BF16))
+        out.append(((r == c + 1) & ((c & 1) == 0)).astype(F32).astype(BF16))
+    return out
+
+
+def grow(compact, mask):
+    if compact.shape[0] < 16:
+        compact = jnp.concatenate([compact] * (16 // compact.shape[0]), axis=0)
+    compact = compact.astype(BF16)
+    return jnp.concatenate([compact] * (TOK // compact.shape[0]), axis=0) * mask
+
+
+def high_low(value):
+    high = value.astype(BF16).astype(F32)
+    return high, value - high
+
+
+def times(left, right, mask):
+    size = left.shape[0]
+    left_high, left_low = high_low(left)
+    right_high, right_low = high_low(right)
+    stacked = jnp.concatenate([left_high, left_low], axis=0).astype(BF16)
+    total = mm(stacked, grow(right_high, mask))
+    return total[:size] + total[size:] + mm(left_high.astype(BF16), grow(right_low, mask))
+
+
+def gather_blocks(a, size, below):
+    lane = lax.broadcasted_iota(jnp.int32, (size, 128), 1) >> (size.bit_length() - 1)
+    out = []
+    for half in range(2):
+        total = None
+        for k in range(128 // size):
+            block = half * (128 // size) + k
+            if below and block % 2:
+                continue
+            top = (block + (1 if below else 0)) * size
+            piece = jnp.where(lane == k, a[top : top + size, half * 128 : half * 128 + 128], 0.0)
+            total = piece if total is None else total + piece
+        out.append(total)
+    return jnp.concatenate(out, axis=1)
+
+
+def each(fn, *lists):
+    return [fn(*items) for items in zip(*lists)]
+
+
+def half_inverses(many, masks):
+    row, col = rows_and_columns((8, TOK))
+    eye = ((col & 7) == row).astype(F32)
+    d = each(lambda a: gather_blocks(a, 8, False), many)
+    t = each(lambda d: eye - d, d)
+    square = each(lambda d: times(d, d, masks[0]), d)
+    both = each(lambda t, s: times(jnp.concatenate([t, s], axis=0), s, masks[0]), t, square)
+    t = each(lambda t, b: t + b[:8], t, both)
+    t = each(lambda t, b: t + times(t, b[8:], masks[0]), t, both)
+    for i, size in enumerate(LEVELS):
+        e = each(lambda a: gather_blocks(a, size, True), many)
+        y = each(lambda e, t: times(e, t, masks[2 * i]), e, t)
+        z = each(lambda t, y: times(t, y, masks[2 * i + 1]), t, y)
+        lane = lax.broadcasted_iota(jnp.int32, (size, TOK), 1)
+        left = ((lane >> (size.bit_length() - 1)) & 1) == 0
+        t = each(
+            lambda t, z: jnp.concatenate([jnp.where(left, t, 0.0), jnp.where(left, -z, t)], axis=0),
+            t, z,
+        )
+    return t
+
+
+def solve_halves(a, t, beta, right):
+    scaled = each(lambda t, b: parts(t * b, 2), t, beta)
+    plain = each(lambda t: parts(t[:, 128:], 2), t)
+    cross = each(lambda a: parts(a[128:, :128], 2), a)
+    first = each(
+        lambda s, r: (mm(s[0][:, :128], r[:128]) + mm(s[1][:, :128], r[:128])).astype(BF16),
+        scaled, right,
+    )
+    moved = each(lambda c, x: (mm(c[0], x) + mm(c[1], x)).astype(BF16), cross, first)
+    second = each(
+        lambda s, r, p, y: (
+            mm(s[0][:, 128:], r[128:]) + mm(s[1][:, 128:], r[128:]) - mm(p[0], y) - mm(p[1], y)
+        ).astype(BF16),
+        scaled, right, plain, moved,
+    )
+    return each(lambda x, y: jnp.concatenate([x, y], axis=0), first, second)
 
 
 def pack_kernel(k_ref, v_ref, q_ref, out_ref):
@@ -153,7 +226,7 @@
 
 def early_kernel(
     k_ref, v_ref, decay_ref, beta_ref, doc_ref, wk_ref, wv_ref, edge_ref,
-    key_ref, value_ref, factor_ref, carry_ref, last_ref, start_ref, head_ref, ext_ref,
+    key_ref, value_ref, factor_ref, carry_ref, last_ref, start_ref, head_ref, mask_ref, ext_ref,
 ):
     row, col = rows_and_columns()
     lower = (col <= row).astype(BF16)
@@ -180,6 +253,8 @@
     value_ref[...] = value_conv.astype(BF16)
     head_ref[:, 0:256] = k_ref[0:RIM, :]
     head_ref[:, 256:768] = v_ref[0:RIM, :]
+    for i, mask in enumerate(block_masks()):
+        mask_ref[i] = mask
 
 
 def first_rows(rim, own, w_ref, start):
@@ -195,9 +270,8 @@
 
 def map_kernel(
     rim_ref, head_ref, start_ref, key_ref, value_ref, factor_ref, carry_ref, last_ref, beta_ref,
-    wk_ref, wv_ref, wu_ref, kb_ref, own_ref, give_ref,
+    wk_ref, wv_ref, mask_ref, wu_ref, kb_ref, own_ref, give_ref,
 ):
-    row, col = rows_and_columns()
     rim = rim_ref[...].astype(F32)[8:16]
     head = head_ref[...].astype(F32)[0:8]
     start = start_ref[0:8]
@@ -216,20 +290,29 @@
     core = lax.axis_index("ctx") % CORES
     for g in range(GROUPS):
         kb_ref[g] = keys[g]
-    for h in range(HEADS):
-        g = h // 2
-        key = keys[g].astype(F32)
-        t = unit_lower_inverse(factor_ref[h] * gram[g], row, col) * beta[h : h + 1]
-        carry = carry_ref[h]
-        right = jnp.concatenate([(carry * key).astype(BF16), values[:, h * DV : (h + 1) * DV]], axis=1)
-        high, low = parts(t, 2)
-        solved = (mm(high, right) + mm(low, right)).astype(BF16)
-        wu_ref[h] = solved
-        faded = (flipped[g] * last_ref[h : h + 1, :]).astype(BF16)
-        both = mm(faded, solved)
-        r, c = rows_and_columns((DK, DK))
-        diagonal = jnp.where(r == c, jnp.broadcast_to(carry[TOK - 1 : TOK, :], (DK, DK)), 0.0)
-        step = jnp.concatenate([diagonal - both[:, :DK], both[:, DK:]], axis=1).astype(BF16)
+    heads = range(HEADS)
+    masks = [mask_ref[i] for i in range(2 * len(LEVELS))]
+    a = [factor_ref[h] * gram[h // 2] for h in heads]
+    inverses = half_inverses(a, masks)
+    right = [
+        jnp.concatenate(
+            [
+                (carry_ref[h] * keys[h // 2].astype(F32)).astype(BF16),
+                values[:, h * DV : (h + 1) * DV],
+            ],
+            axis=1,
+        )
+        for h in heads
+    ]
+    solved = solve_halves(a, inverses, [beta[h : h + 1] for h in heads], right)
+    faded = [(flipped[h // 2] * last_ref[h : h + 1, :]).astype(BF16) for h in heads]
+    both = each(mm, faded, solved)
+    r, c = rows_and_columns((DK, DK))
+    for h in heads:
+        wu_ref[h] = solved[h]
+        decay = jnp.broadcast_to(carry_ref[h, TOK - 1 : TOK, :], (DK, DK))
+        diagonal = jnp.where(r == c, decay, 0.0)
+        step = jnp.concatenate([diagonal - both[h][:, :DK], both[h][:, DK:]], axis=1).astype(BF16)
 
         @pl.when(core == h // 2)
         def _():
@@ -322,6 +405,7 @@
 
 def norm_kernel(local_ref, reach_ref, mine_ref, got_ref, gate_ref, gain_ref, keep_ref, give_ref):
     core = lax.axis_index("ctx") % CORES
+    place = lax.axis_index("head") // 2
     side = lax.axis_index("head") % 2
     for h in range(HEADS):
         state = jnp.where(core == h // 2, mine_ref[h % 2], got_ref[h % 2])
@@ -334,23 +418,27 @@
         for block in range(4):
             even = normed[2 * block * rows : (2 * block + 1) * rows]
             odd = normed[(2 * block + 1) * rows : (2 * block + 2) * rows]
-            at = (slice(block * rows, (block + 1) * rows), slice(h * DV, (h + 1) * DV))
+            top = pl.multiple_of(((block + 4 - place) % 4) * rows, rows)
+            at = (pl.ds(top, rows), slice(h * DV, (h + 1) * DV))
             keep_ref[at] = jnp.where(side == 0, even, odd)
             give_ref[at] = jnp.where(side == 0, odd, even)
 
 
-def project_kernel(keep_ref, got_ref, own_ref, near_ref, out_ref):
+def project_kernel(keep_ref, got_ref, own_ref, near_ref, *out_refs):
     keep = keep_ref[...]
     got = got_ref[...]
     for part in range(0, own_ref.shape[1], 512):
         at = slice(part, part + 512)
-        out_ref[:, at] = (mm(keep, own_ref[:, at]) + mm(got, near_ref[:, at])).astype(BF16)
-
-
-def sum_kernel(in_ref, out_ref):
-    total = in_ref[0].astype(F32)
-    for k in range(1, in_ref.shape[0]):
-        total = total + in_ref[k].astype(F32)
+        total = mm(keep, own_ref[:, at]) + mm(got, near_ref[:, at])
+        rows = total.shape[0] // len(out_refs)
+        for k, out_ref in enumerate(out_refs):
+            out_ref[:, at] = total[k * rows : (k + 1) * rows].astype(out_ref.dtype)
+
+
+def sum_kernel(own_ref, one_ref, two_ref, three_ref, out_ref):
+    total = own_ref[...]
+    for ref in (one_ref, two_ref, three_ref):
+        total = total + ref[...].astype(F32)
     out_ref[...] = total.astype(BF16)
 
 
@@ -407,6 +495,7 @@
         [
             ((GROUPS, TOK, DK), BF16), ((TOK, HEADS * DV), BF16), ((HEADS, TOK, TOK), F32),
             ((HEADS, TOK, 128), F32), ((HEADS, TOK), F32), ((RIM, 128), F32), ((RIM, 768), BF16),
+            ((2 * len(LEVELS), TOK, TOK), BF16),
         ],
         [key_in, value_in, log_decay, beta_gate, doc_row, conv_key, conv_value, edge],
         [
@@ -414,11 +503,11 @@
         ],
         flops=500_000_000, moved=0, limit=48, blocked=True,
     )
-    keys, values, factor, carry, final, start, head = early
+    keys, values, factor, carry, final, start, head, masks = early
     solved, keys, own, give = call(
         map_kernel,
         [((HEADS, TOK, DK + DV), BF16), ((GROUPS, TOK, DK), BF16), (wide, BF16), (wide, BF16)],
-        [rim, head, start, keys, values, factor, carry, final, beta_gate, conv_key, conv_value],
+        [rim, head, start, keys, values, factor, carry, final, beta_gate, conv_key, conv_value, masks],
         flops=4_000_000_000, moved=2_000_000,
     )
     other = lax.ppermute(give, "ctx", core_swap())
@@ -450,18 +539,16 @@
         flops=100_000_000, moved=1_500_000,
     )
     brought = lax.ppermute(to_near, "head", [(i, i ^ 1) for i in range(8)])
-    (partial,) = call(
-        project_kernel, [((TOK // 2, width), BF16)],
+    block = (TOK // 8, width)
+    partials = call(
+        project_kernel, [(block, F32)] + [(block, BF16)] * 3,
         [keep, brought, out_weight, near_weight],
         flops=600_000_000, moved=4_000_000,
     )
-    blocks = lax.all_to_all(
-        partial.reshape(4, TOK // 8, width), "head", 0, 0,
-        axis_index_groups=[[0, 2, 4, 6], [1, 3, 5, 7]],
-    )
-    (mixed,) = call(
-        sum_kernel, [((TOK // 8, width), BF16)], [blocks], flops=1_000_000, moved=1_200_000
-    )
+    terms = [partials[0]] + [
+        lax.ppermute(partials[k], "head", [(i, (i + 2 * k) % 8) for i in range(8)]) for k in (2, 1, 3)
+    ]
+    (mixed,) = call(sum_kernel, [(block, BF16)], terms, flops=1_000_000, moved=800_000)
     return mixed
 
 

time: 79.6 us -> 73.4 us (0.922)
  the two profiles are of different devices: /device:TPU:32 before, /device:TPU:6 now
where the time goes in v5:
time: 73.4 us; the launch traced here: 72.2 us
  waiting for transfers between devices  33.8 us (46%)
  starting transfers between devices  26.5 us (36%)
  Pallas kernels  10.8 us (15%)
  local copies, waits for them, and re-layouts  0.91 us (1%)
    ppermute x1, waiting for transfers between devices, on_device(): brought = lax.ppermute(to_near, 'head', [(i, i ^ 1) for i in range(8)])  11.8 us
    ppermute x3, starting transfers between devices, on_device(): lax.ppermute(partials[k], 'head', [(i, (i + 2 * k) % 8) for i in range(8)])  11.2 us
    pallas_call x9, Pallas kernels, call(): pl.pallas_call(kernel, grid=(1,) if blocked else (), out_shape=[jax.Shape...  9.31 us
    ppermute x3, starting transfers between devices, on_device(): far = [lax.ppermute(total, 'ctx', along_y(k)) for k in (1, 2, 3)]  7.49 us
    ppermute x3, waiting for transfers between devices, on_device(): lax.ppermute(partials[k], 'head', [(i, (i + 2 * k) % 8) for i in range(8)])  7.46 us
    ppermute x3, waiting for transfers between devices, on_device(): near = [lax.ppermute(pair, 'ctx', along_x(k)) for k in (1, 2, 3)]  6.55 us
    ppermute x3, waiting for transfers between devices, on_device(): far = [lax.ppermute(total, 'ctx', along_y(k)) for k in (1, 2, 3)]  4.54 us
    ppermute x3, starting transfers between devices, on_device(): near = [lax.ppermute(pair, 'ctx', along_x(k)) for k in (1, 2, 3)]  2.94 us
  transfers between devices with their start and end apart: 14, of which 12 were waited for; matrix products, arithmetic and copies ran while one was open for 0% of the time, Pallas kernels for 11%

profile of v5, /device:TPU:6, one launch (start us, length us, event | category | flops | bytes accessed | tf_op | source)
XLA Modules:
  0.0 72.2 jit_solution(15409641411122768218)
XLA Ops:
  0.0 0.0 copy-start.4
  0.0 0.0 copy-start.3
  0.0 0.0 copy-start
  0.0 0.0 copy-start.12
  0.0 0.0 copy-start.10
  0.0 0.0 copy-start.8
  0.0 0.0 copy-start.9
  0.0 0.0 copy-start.7
  0.1 1.5 %shard_map.118.edge_ref = bf16[16,1024]{1,0:T(8,128)(2,1)} custom-call(bf16[256,256]{1,0:T(8,128)(2,1)} %k_ref.3, bf16[256,512]{1,0:T(8,128)(2,1)} %v_ref.3, bf16[256,256]{1,0:T(8,128)(2,1)} %q_ref.3), custom_call_target="tpu_custom_call" | custom-call | flops 5000000000 | tf_op jit(solution)/shard_map/pallas_call | solution.py:480
  1.5 0.1 copy-done
  1.7 1.9 %collective-permute-start.10 = (bf16[512,2048]{1,0:T(8,128)(2,1)S(1)}, bf16[512,2048]{1,0:T(8,128)(2,1)S(1)}, u32[]{:S(2)}, u32[]{:S(2)}) collective-permute-start(bf16[512,2048]{1,0:T(8,128)(2,1)S(1)} %copy-done), channel_id=1, source_target_pairs={{0,1},{1,0},{2,3},{3,2},{4,5},{5,4},{6,7},{7,6},{8,9},{9,8},{10,11... | collective-permute-start | bytes 6291464 | tf_op jit(solution)/shard_map/ppermute | solution.py:488
  3.6 1.9 %collective-permute-start = (bf16[16,1024]{1,0:T(8,128)(2,1)}, bf16[16,1024]{1,0:T(8,128)(2,1)S(1)}, u32[]{:S(2)}, u32[]{:S(2)}) collective-permute-start(bf16[16,1024]{1,0:T(8,128)(2,1)} %shard_map.118.edge_ref), channel_id=1, source_target_pairs={{0,8},{8,16},{16,24},{24,32},{32,40},{40,48},{48,56},{56,64},{64,7... | collective-permute-start | bytes 98312 | tf_op jit(solution)/shard_map/ppermute | solution.py:491
  5.5 0.0 copy-done.4
  5.5 0.0 copy-done.3
  5.5 0.0 copy-done.12
  5.5 0.0 copy-done.10
  5.5 0.0 copy-done.8
  5.5 0.0 copy-done.9
  5.6 0.0 copy-done.7
  5.6 0.0 copy-start.6
  5.6 0.7 %copy-done.6 = bf16[16,1024]{1,0:T(8,128)(2,1)S(1)} copy-done((bf16[16,1024]{1,0:T(8,128)(2,1)S(1)}, bf16[16,1024]{1,0:T(8,128)(2,1)}, u32[]{:S(2)}) %copy-start.6) | copy-done | bytes 32792
  6.3 1.4 %shard_map.119 = (bf16[2,256,128]{2,1,0:T(8,128)(2,1)S(1)}, bf16[256,512]{1,0:T(8,128)(2,1)S(1)}, f32[4,256,256]{2,1,0:T(8,128)S(1)}, f32[4,256,128]{2,1,0:T(8,1...) custom-call(bf16[256,256]{1,0:T(8,128)(2,1)S(1)} %copy-done.4, ...), custom_call_target="tpu_custom_call" | custom-call | flops 500000000 | tf_op jit(solution)/shard_map/pallas_call | solution.py:460
  7.8 1.2 %collective-permute-done.rim_ref = bf16[16,1024]{1,0:T(8,128)(2,1)S(1)} collective-permute-done((bf16[16,1024]{1,0:T(8,128)(2,1)}, bf16[16,1024]{1,0:T(8,128)(2,1)S(1)}, u32[]{:S(2)}, u32[]{:S(2)}) %collective-permute-start) | collective-permute-done | bytes 32800 | tf_op jit(solution)/shard_map/ppermute | solution.py:491
  9.0 0.0 copy-start.5
  9.0 0.0 copy-start.11
  9.0 3.4 %shard_map.120 = (bf16[4,256,256]{2,1,0:T(8,128)(2,1)S(1)}, bf16[2,256,128]{2,1,0:T(8,128)(2,1)S(1)}, bf16[2,128,256]{2,1,0:T(8,128)(2,1)S(1)}, bf16[2,128,256]{2,1,0:T(8,128)(2,1)S(1)}) custom-call(bf16[16,1024]{1,0:T(8,128)(2,1)S(1)} %collective-permute-done.rim_ref, bf16[16,768]{1,0:T(8,128)(2,1)S(1)} %get-tuple-element.30.head_ref, ...), custom_call_target="tpu_custom_call" | custom-call | flops 4000000000 | bytes 2000000 | tf_op jit(solution)/shard_map/pallas_call | solution.py:460
  12.4 0.5 collective-permute-start.1
  12.9 1.0 %collective-permute-done.1.got_ref.other_ref = bf16[2,128,256]{2,1,0:T(8,128)(2,1)S(1)} collective-permute-done((bf16[2,128,256]{2,1,0:T(8,128)(2,1)S(1)}, bf16[2,128,256]{2,1,0:T(8,128)(2,1)S(1)}, u32[]{:S(2)}, u32[]{:S(2)}) %collective-permute-start.1) | collective-permute-done | bytes 131104 | tf_op jit(solution)/shard_map/ppermute | solution.py:513
  13.9 0.2 shard_map.122.own_ref
  14.0 0.6 collective-permute-start.2
  14.6 2.4 %collective-permute-start.3 = (bf16[2,128,256]{2,1,0:T(8,128)(2,1)S(1)}, bf16[2,128,256]{2,1,0:T(8,128)(2,1)S(1)}, u32[]{:S(2)}, u32[]{:S(2)}) collective-permute-start(bf16[2,128,256]{2,1,0:T(8,128)(2,1)S(1)} %shard_map.122.own_ref), channel_id=1, source_target_pairs={{0,32},{8,40},{16,48},{24,56},{32,0},{40,8},{48,16},{56,24},{64,96... | collective-permute-start | bytes 393224 | tf_op jit(solution)/shard_map/ppermute | solution.py:515
  17.0 0.0 collective-permute-start.4
  17.0 0.0 copy-done.5
  17.0 0.0 copy-done.11
  17.0 0.0 copy-start.1
  17.0 0.0 copy-start.2
  17.0 0.8 %shard_map.121 = (f32[4,256,128]{2,1,0:T(8,128)S(1)}, bf16[4,256,128]{2,1,0:T(8,128)(2,1)S(1)}) custom-call(bf16[256,256]{1,0:T(8,128)(2,1)S(1)} %copy-done.5, bf16[16,1024]{1,0:T(8,128)(2,1)S(1)} %collective-permute-done.rim_ref, f32[4,256]{1,0:T(4,128)S(1)} %copy-done.10, s32[1,256]{1,0:T(1,128)S(1)} %bitcast.4, f32[4,256]{1,0:T(4,128)S(1)} %copy-done.11, ...), custom_call_target="tpu_custom_call" | custom-call | flops 2000000000 | bytes 2000000 | tf_op jit(solution)/shard_map/pallas_call | solution.py:460
  17.8 2.6 %collective-permute-done.2.one_ref = bf16[2,128,256]{2,1,0:T(8,128)(2,1)S(1)} collective-permute-done((bf16[2,128,256]{2,1,0:T(8,128)(2,1)S(1)}, bf16[2,128,256]{2,1,0:T(8,128)(2,1)S(1)}, u32[]{:S(2)}, u32[]{:S(2)}) %collective-permute-start.2) | collective-permute-done | bytes 131104 | tf_op jit(solution)/shard_map/ppermute | solution.py:515
  20.4 2.0 %collective-permute-done.3.two_ref = bf16[2,128,256]{2,1,0:T(8,128)(2,1)S(1)} collective-permute-done((bf16[2,128,256]{2,1,0:T(8,128)(2,1)S(1)}, bf16[2,128,256]{2,1,0:T(8,128)(2,1)S(1)}, u32[]{:S(2)}, u32[]{:S(2)}) %collective-permute-start.3) | collective-permute-done | bytes 131104 | tf_op jit(solution)/shard_map/ppermute | solution.py:515
  22.5 1.9 %collective-permute-done.4.three_ref = bf16[2,128,256]{2,1,0:T(8,128)(2,1)S(1)} collective-permute-done((bf16[2,128,256]{2,1,0:T(8,128)(2,1)S(1)}, bf16[2,128,256]{2,1,0:T(8,128)(2,1)S(1)}, u32[]{:S(2)}, u32[]{:S(2)}) %collective-permute-start.4) | collective-permute-done | bytes 131104 | tf_op jit(solution)/shard_map/ppermute | solution.py:515
  24.4 0.7 shard_map.123
  25.1 3.2 %collective-permute-start.5 = (bf16[2,128,256]{2,1,0:T(8,128)(2,1)S(1)}, bf16[2,128,256]{2,1,0:T(8,128)(2,1)S(1)}, u32[]{:S(2)}, u32[]{:S(2)}) collective-permute-start(bf16[2,128,256]{2,1,0:T(8,128)(2,1)S(1)} %get-tuple-element.44.own_ref), channel_id=1, source_target_pairs={{0,64},{8,72},{16,80},{24,88},{32,96},{40,104},{48,112},{56,120},{... | collective-permute-start | bytes 393224 | tf_op jit(solution)/shard_map/ppermute | solution.py:528
  28.3 2.9 %collective-permute-start.6 = (bf16[2,128,256]{2,1,0:T(8,128)(2,1)S(1)}, bf16[2,128,256]{2,1,0:T(8,128)(2,1)S(1)}, u32[]{:S(2)}, u32[]{:S(2)}) collective-permute-start(bf16[2,128,256]{2,1,0:T(8,128)(2,1)S(1)} %get-tuple-element.44.own_ref), channel_id=1, source_target_pairs={{0,128},{8,136},{16,144},{24,152},{32,160},{40,168},{48,176},{56,1... | collective-permute-start | bytes 393224 | tf_op jit(solution)/shard_map/ppermute | solution.py:528
  31.3 1.3 %collective-permute-start.7 = (bf16[2,128,256]{2,1,0:T(8,128)(2,1)S(1)}, bf16[2,128,256]{2,1,0:T(8,128)(2,1)S(1)}, u32[]{:S(2)}, u32[]{:S(2)}) collective-permute-start(bf16[2,128,256]{2,1,0:T(8,128)(2,1)S(1)} %get-tuple-element.44.own_ref), channel_id=1, source_target_pairs={{0,192},{8,200},{16,208},{24,216},{32,224},{40,232},{48,240},{56,2... | collective-permute-start | bytes 393224 | tf_op jit(solution)/shard_map/ppermute | solution.py:528
  32.6 0.7 collective-permute-done.5.one_ref
  33.3 3.9 %collective-permute-done.6.two_ref = bf16[2,128,256]{2,1,0:T(8,128)(2,1)S(1)} collective-permute-done((bf16[2,128,256]{2,1,0:T(8,128)(2,1)S(1)}, bf16[2,128,256]{2,1,0:T(8,128)(2,1)S(1)}, u32[]{:S(2)}, u32[]{:S(2)}) %collective-permute-start.6) | collective-permute-done | bytes 131104 | tf_op jit(solution)/shard_map/ppermute | solution.py:528
  37.1 0.0 collective-permute-done.7.three_ref
  37.1 0.9 %shard_map.124 = (bf16[2,128,128]{2,1,0:T(8,128)(2,1)S(1)}, bf16[2,128,128]{2,1,0:T(8,128)(2,1)S(1)}) custom-call(bf16[2,128,256]{2,1,0:T(8,128)(2,1)S(1)} %get-tuple-element.44.own_ref, bf16[2,128,256]{2,1,0:T(8,128)(2,1)S(1)} %collective-permute-done.5.one_ref, bf16[2,128,256]{2,1,0:T(8,128)(2,1)S(1)} %collective-permute-done.6.two_ref, ...), custom_call_target="tpu_custom_call" | custom-call | flops 60000000 | bytes 1000000 | tf_op jit(solution)/shard_map/pallas_call | solution.py:460
  38.0 0.3 collective-permute-start.8
  38.3 1.2 %collective-permute-done.8.got_ref = bf16[2,128,128]{2,1,0:T(8,128)(2,1)S(1)} collective-permute-done((bf16[2,128,128]{2,1,0:T(8,128)(2,1)S(1)}, bf16[2,128,128]{2,1,0:T(8,128)(2,1)S(1)}, u32[]{:S(2)}, u32[]{:S(2)}) %collective-permute-start.8) | collective-permute-done | bytes 65568 | tf_op jit(solution)/shard_map/ppermute | solution.py:534
  39.6 0.0 copy-done.1
  39.6 0.0 copy-done.2
  39.6 0.4 shard_map.125
  40.0 0.2 collective-permute-start.9
  40.2 11.8 %collective-permute-done.9.got_ref = bf16[128,512]{1,0:T(8,128)(2,1)S(1)} collective-permute-done((bf16[128,512]{1,0:T(8,128)(2,1)S(1)}, bf16[128,512]{1,0:T(8,128)(2,1)S(1)}, u32[]{:S(2)}, u32[]{:S(2)}) %collective-permute-start.9) | collective-permute-done | bytes 131104 | tf_op jit(solution)/shard_map/ppermute | solution.py:541
  52.0 0.0 collective-permute-done.10.near_ref
  52.0 0.8 %shard_map.126 = (f32[32,2048]{1,0:T(8,128)S(1)}, bf16[32,2048]{1,0:T(8,128)(2,1)S(1)}, bf16[32,2048]{1,0:T(8,128)(2,1)S(1)}, bf16[32,2048]{1,0:T(8,128)(2,1)S(1)}) custom-call(bf16[128,512]{1,0:T(8,128)(2,1)S(1)} %get-tuple-element.48.keep_ref, bf16[128,512]{1,0:T(8,128)(2,1)S(1)} %collective-permute-done.9.got_ref, bf16[512,2048]{1,0:T(8,128)(2,1)S(1)} %copy-done, ...), custom_call_target="tpu_custom_call" | custom-call | flops 600000000 | bytes 4000000 | tf_op jit(solution)/shard_map/pallas_call | solution.py:460
  52.8 7.1 %collective-permute-start.11 = (bf16[32,2048]{1,0:T(8,128)(2,1)S(1)}, bf16[32,2048]{1,0:T(8,128)(2,1)S(1)}, u32[]{:S(2)}, u32[]{:S(2)}) collective-permute-start(bf16[32,2048]{1,0:T(8,128)(2,1)S(1)} %get-tuple-element.52), channel_id=1, source_target_pairs={{0,4},{1,5},{2,6},{3,7},{4,0},{5,1},{6,2},{7,3},{8,12},{9,13},{10,... | collective-permute-start | bytes 393224 | tf_op jit(solution)/shard_map/ppermute | solution.py:549
  59.9 1.5 %collective-permute-start.12 = (bf16[32,2048]{1,0:T(8,128)(2,1)S(1)}, bf16[32,2048]{1,0:T(8,128)(2,1)S(1)}, u32[]{:S(2)}, u32[]{:S(2)}) collective-permute-start(bf16[32,2048]{1,0:T(8,128)(2,1)S(1)} %get-tuple-element.53), channel_id=1, source_target_pairs={{0,2},{1,3},{2,4},{3,5},{4,6},{5,7},{6,0},{7,1},{8,10},{9,11},{10,... | collective-permute-start | bytes 393224 | tf_op jit(solution)/shard_map/ppermute | solution.py:549
  61.4 2.7 %collective-permute-start.13 = (bf16[32,2048]{1,0:T(8,128)(2,1)S(1)}, bf16[32,2048]{1,0:T(8,128)(2,1)S(1)}, u32[]{:S(2)}, u32[]{:S(2)}) collective-permute-start(bf16[32,2048]{1,0:T(8,128)(2,1)S(1)} %get-tuple-element.54), channel_id=1, source_target_pairs={{0,6},{1,7},{2,0},{3,1},{4,2},{5,3},{6,4},{7,5},{8,14},{9,15},{10,... | collective-permute-start | bytes 393224 | tf_op jit(solution)/shard_map/ppermute | solution.py:549
  64.0 2.3 %collective-permute-done.11.one_ref = bf16[32,2048]{1,0:T(8,128)(2,1)S(1)} collective-permute-done((bf16[32,2048]{1,0:T(8,128)(2,1)S(1)}, bf16[32,2048]{1,0:T(8,128)(2,1)S(1)}, u32[]{:S(2)}, u32[]{:S(2)}) %collective-permute-start.11) | collective-permute-done | bytes 131104 | tf_op jit(solution)/shard_map/ppermute | solution.py:549
  66.3 2.2 %collective-permute-done.12.two_ref = bf16[32,2048]{1,0:T(8,128)(2,1)S(1)} collective-permute-done((bf16[32,2048]{1,0:T(8,128)(2,1)S(1)}, bf16[32,2048]{1,0:T(8,128)(2,1)S(1)}, u32[]{:S(2)}, u32[]{:S(2)}) %collective-permute-start.12) | collective-permute-done | bytes 131104 | tf_op jit(solution)/shard_map/ppermute | solution.py:549
  68.5 3.0 %collective-permute-done.13.three_ref = bf16[32,2048]{1,0:T(8,128)(2,1)S(1)} collective-permute-done((bf16[32,2048]{1,0:T(8,128)(2,1)S(1)}, bf16[32,2048]{1,0:T(8,128)(2,1)S(1)}, u32[]{:S(2)}, u32[]{:S(2)}) %collective-permute-start.13) | collective-permute-done | bytes 131104 | tf_op jit(solution)/shard_map/ppermute | solution.py:549
  71.5 0.7 shard_map.127
Async XLA Ops:
  0.0 5.5 %copy-start.4 = (bf16[256,256]{1,0:T(8,128)(2,1)S(1)}, bf16[256,256]{1,0:T(8,128)(2,1)}, u32[]{:S(2)}) copy-start(bf16[256,256]{1,0:T(8,128)(2,1)} %k_ref.3) | copy-start | bytes 393220
  0.0 5.5 %copy-start.3 = (bf16[256,512]{1,0:T(8,128)(2,1)S(1)}, bf16[256,512]{1,0:T(8,128)(2,1)}, u32[]{:S(2)}) copy-start(bf16[256,512]{1,0:T(8,128)(2,1)} %v_ref.3) | copy-start | bytes 786436
  0.0 1.7 %copy-start = (bf16[512,2048]{1,0:T(8,128)(2,1)S(1)}, bf16[512,2048]{1,0:T(8,128)(2,1)}, u32[]{:S(2)}) copy-start(bf16[512,2048]{1,0:T(8,128)(2,1)} %own_ref.1) | copy-start | bytes 6291460
  0.0 5.5 %copy-start.12 = (s32[256]{0:T(256)S(1)}, s32[256]{0:T(256)}, u32[]{:S(2)}) copy-start(s32[256]{0:T(256)} %param.18) | copy-start | bytes 3076
  0.0 5.5 %copy-start.10 = (f32[4,256]{1,0:T(4,128)S(1)}, f32[4,256]{1,0:T(4,128)}, u32[]{:S(2)}) copy-start(f32[4,256]{1,0:T(4,128)} %decay_ref.3) | copy-start | bytes 12292
  0.0 5.5 %copy-start.8 = (f32[4,256]{1,0:T(4,128)S(1)}, f32[4,256]{1,0:T(4,128)}, u32[]{:S(2)}) copy-start(f32[4,256]{1,0:T(4,128)} %beta_ref.3) | copy-start | bytes 12292
  0.0 5.5 %copy-start.9 = (f32[4,256]{1,0:T(4,128)S(1)}, f32[4,256]{1,0:T(4,128)}, u32[]{:S(2)}) copy-start(f32[4,256]{1,0:T(4,128)} %wk_ref.3) | copy-start | bytes 12292
  0.0 5.5 %copy-start.7 = (f32[4,512]{1,0:T(4,128)S(1)}, f32[4,512]{1,0:T(4,128)}, u32[]{:S(2)}) copy-start(f32[4,512]{1,0:T(4,128)} %wv_ref.3) | copy-start | bytes 24580
  1.7 50.4 %collective-permute-start.10 = (bf16[512,2048]{1,0:T(8,128)(2,1)S(1)}, bf16[512,2048]{1,0:T(8,128)(2,1)S(1)}, u32[]{:S(2)}, u32[]{:S(2)}) collective-permute-start(bf16[512,2048]{1,0:T(8,128)(2,1)S(1)} %copy-done), channel_id=1, source_target_pairs={{0,1},{1,0},{2,3},{3,2},{4,5},{5,4},{6,7},{7,6},{8,9},{9,8},{10,11... | collective-permute-start | bytes 6291464 | tf_op jit(solution)/shard_map/ppermute | solution.py:488
  3.6 5.4 %collective-permute-start = (bf16[16,1024]{1,0:T(8,128)(2,1)}, bf16[16,1024]{1,0:T(8,128)(2,1)S(1)}, u32[]{:S(2)}, u32[]{:S(2)}) collective-permute-start(bf16[16,1024]{1,0:T(8,128)(2,1)} %shard_map.118.edge_ref), channel_id=1, source_target_pairs={{0,8},{8,16},{16,24},{24,32},{32,40},{40,48},{48,56},{56,64},{64,7... | collective-permute-start | bytes 98312 | tf_op jit(solution)/shard_map/ppermute | solution.py:491
  5.6 0.8 %copy-start.6 = (bf16[16,1024]{1,0:T(8,128)(2,1)S(1)}, bf16[16,1024]{1,0:T(8,128)(2,1)}, u32[]{:S(2)}) copy-start(bf16[16,1024]{1,0:T(8,128)(2,1)} %shard_map.118.edge_ref) | copy-start | bytes 98308
  9.0 8.0 %copy-start.5 = (bf16[256,256]{1,0:T(8,128)(2,1)S(1)}, bf16[256,256]{1,0:T(8,128)(2,1)}, u32[]{:S(2)}) copy-start(bf16[256,256]{1,0:T(8,128)(2,1)} %q_ref.3) | copy-start | bytes 393220
  9.0 8.0 %copy-start.11 = (f32[4,256]{1,0:T(4,128)S(1)}, f32[4,256]{1,0:T(4,128)}, u32[]{:S(2)}) copy-start(f32[4,256]{1,0:T(4,128)} %wq_ref.1) | copy-start | bytes 12292
  12.4 1.5 %collective-permute-start.1 = (bf16[2,128,256]{2,1,0:T(8,128)(2,1)S(1)}, bf16[2,128,256]{2,1,0:T(8,128)(2,1)S(1)}, u32[]{:S(2)}, u32[]{:S(2)}) collective-permute-start(bf16[2,128,256]{2,1,0:T(8,128)(2,1)S(1)} %get-tuple-element.43), channel_id=1, source_target_pairs={{0,8},{8,0},{16,24},{24,16},{32,40},{40,32},{48,56},{56,48},{64,72... | collective-permute-start | bytes 393224 | tf_op jit(solution)/shard_map/ppermute | solution.py:513
  14.0 6.4 %collective-permute-start.2 = (bf16[2,128,256]{2,1,0:T(8,128)(2,1)S(1)}, bf16[2,128,256]{2,1,0:T(8,128)(2,1)S(1)}, u32[]{:S(2)}, u32[]{:S(2)}) collective-permute-start(bf16[2,128,256]{2,1,0:T(8,128)(2,1)S(1)} %shard_map.122.own_ref), channel_id=1, source_target_pairs={{0,16},{8,24},{16,32},{24,40},{32,48},{40,56},{48,0},{56,8},{64,80... | collective-permute-start | bytes 393224 | tf_op jit(solution)/shard_map/ppermute | solution.py:515
  14.6 7.9 %collective-permute-start.3 = (bf16[2,128,256]{2,1,0:T(8,128)(2,1)S(1)}, bf16[2,128,256]{2,1,0:T(8,128)(2,1)S(1)}, u32[]{:S(2)}, u32[]{:S(2)}) collective-permute-start(bf16[2,128,256]{2,1,0:T(8,128)(2,1)S(1)} %shard_map.122.own_ref), channel_id=1, source_target_pairs={{0,32},{8,40},{16,48},{24,56},{32,0},{40,8},{48,16},{56,24},{64,96... | collective-permute-start | bytes 393224 | tf_op jit(solution)/shard_map/ppermute | solution.py:515
  17.0 7.4 %collective-permute-start.4 = (bf16[2,128,256]{2,1,0:T(8,128)(2,1)S(1)}, bf16[2,128,256]{2,1,0:T(8,128)(2,1)S(1)}, u32[]{:S(2)}, u32[]{:S(2)}) collective-permute-start(bf16[2,128,256]{2,1,0:T(8,128)(2,1)S(1)} %shard_map.122.own_ref), channel_id=1, source_target_pairs={{0,48},{8,56},{16,0},{24,8},{32,16},{40,24},{48,32},{56,40},{64,11... | collective-permute-start | bytes 393224 | tf_op jit(solution)/shard_map/ppermute | solution.py:515
  17.0 22.6 %copy-start.1 = (bf16[256,512]{1,0:T(8,128)(2,1)S(1)}, bf16[256,512]{1,0:T(8,128)(2,1)}, u32[]{:S(2)}) copy-start(bf16[256,512]{1,0:T(8,128)(2,1)} %gate_ref.1) | copy-start | bytes 786436
  17.0 22.6 %copy-start.2 = (f32[128]{0:T(128)S(1)}, f32[128]{0:T(128)}, u32[]{:S(2)}) copy-start(f32[128]{0:T(128)} %param.22) | copy-start | bytes 1540
  25.1 8.2 %collective-permute-start.5 = (bf16[2,128,256]{2,1,0:T(8,128)(2,1)S(1)}, bf16[2,128,256]{2,1,0:T(8,128)(2,1)S(1)}, u32[]{:S(2)}, u32[]{:S(2)}) collective-permute-start(bf16[2,128,256]{2,1,0:T(8,128)(2,1)S(1)} %get-tuple-element.44.own_ref), channel_id=1, source_target_pairs={{0,64},{8,72},{16,80},{24,88},{32,96},{40,104},{48,112},{56,120},{... | collective-permute-start | bytes 393224 | tf_op jit(solution)/shard_map/ppermute | solution.py:528
  28.3 8.8 %collective-permute-start.6 = (bf16[2,128,256]{2,1,0:T(8,128)(2,1)S(1)}, bf16[2,128,256]{2,1,0:T(8,128)(2,1)S(1)}, u32[]{:S(2)}, u32[]{:S(2)}) collective-permute-start(bf16[2,128,256]{2,1,0:T(8,128)(2,1)S(1)} %get-tuple-element.44.own_ref), channel_id=1, source_target_pairs={{0,128},{8,136},{16,144},{24,152},{32,160},{40,168},{48,176},{56,1... | collective-permute-start | bytes 393224 | tf_op jit(solution)/shard_map/ppermute | solution.py:528
  31.3 5.9 %collective-permute-start.7 = (bf16[2,128,256]{2,1,0:T(8,128)(2,1)S(1)}, bf16[2,128,256]{2,1,0:T(8,128)(2,1)S(1)}, u32[]{:S(2)}, u32[]{:S(2)}) collective-permute-start(bf16[2,128,256]{2,1,0:T(8,128)(2,1)S(1)} %get-tuple-element.44.own_ref), channel_id=1, source_target_pairs={{0,192},{8,200},{16,208},{24,216},{32,224},{40,232},{48,240},{56,2... | collective-permute-start | bytes 393224 | tf_op jit(solution)/shard_map/ppermute | solution.py:528
  38.0 1.5 %collective-permute-start.8 = (bf16[2,128,128]{2,1,0:T(8,128)(2,1)S(1)}, bf16[2,128,128]{2,1,0:T(8,128)(2,1)S(1)}, u32[]{:S(2)}, u32[]{:S(2)}) collective-permute-start(bf16[2,128,128]{2,1,0:T(8,128)(2,1)S(1)} %get-tuple-element.47), channel_id=1, source_target_pairs={{0,8},{8,0},{16,24},{24,16},{32,40},{40,32},{48,56},{56,48},{64,72... | collective-permute-start | bytes 196616 | tf_op jit(solution)/shard_map/ppermute | solution.py:534
  40.0 12.0 %collective-permute-start.9 = (bf16[128,512]{1,0:T(8,128)(2,1)S(1)}, bf16[128,512]{1,0:T(8,128)(2,1)S(1)}, u32[]{:S(2)}, u32[]{:S(2)}) collective-permute-start(bf16[128,512]{1,0:T(8,128)(2,1)S(1)} %get-tuple-element.49), channel_id=1, source_target_pairs={{0,1},{1,0},{2,3},{3,2},{4,5},{5,4},{6,7},{7,6},{8,9},{9,8},{10,11... | collective-permute-start | bytes 393224 | tf_op jit(solution)/shard_map/ppermute | solution.py:541
  52.8 13.5 %collective-permute-start.11 = (bf16[32,2048]{1,0:T(8,128)(2,1)S(1)}, bf16[32,2048]{1,0:T(8,128)(2,1)S(1)}, u32[]{:S(2)}, u32[]{:S(2)}) collective-permute-start(bf16[32,2048]{1,0:T(8,128)(2,1)S(1)} %get-tuple-element.52), channel_id=1, source_target_pairs={{0,4},{1,5},{2,6},{3,7},{4,0},{5,1},{6,2},{7,3},{8,12},{9,13},{10,... | collective-permute-start | bytes 393224 | tf_op jit(solution)/shard_map/ppermute | solution.py:549
  59.9 8.6 %collective-permute-start.12 = (bf16[32,2048]{1,0:T(8,128)(2,1)S(1)}, bf16[32,2048]{1,0:T(8,128)(2,1)S(1)}, u32[]{:S(2)}, u32[]{:S(2)}) collective-permute-start(bf16[32,2048]{1,0:T(8,128)(2,1)S(1)} %get-tuple-element.53), channel_id=1, source_target_pairs={{0,2},{1,3},{2,4},{3,5},{4,6},{5,7},{6,0},{7,1},{8,10},{9,11},{10,... | collective-permute-start | bytes 393224 | tf_op jit(solution)/shard_map/ppermute | solution.py:549
  61.4 10.1 %collective-permute-start.13 = (bf16[32,2048]{1,0:T(8,128)(2,1)S(1)}, bf16[32,2048]{1,0:T(8,128)(2,1)S(1)}, u32[]{:S(2)}, u32[]{:S(2)}) collective-permute-start(bf16[32,2048]{1,0:T(8,128)(2,1)S(1)} %get-tuple-element.54), channel_id=1, source_target_pairs={{0,6},{1,7},{2,0},{3,1},{4,2},{5,3},{6,4},{7,5},{8,14},{9,15},{10,... | collective-permute-start | bytes 393224 | tf_op jit(solution)/shard_map/ppermute | solution.py:549

commit v6 on v5

--- a/solution.py
+++ b/solution.py
@@ -44,6 +44,10 @@
         for x in range(4)
         for c in range(2)
     ]
+
+
+def around_z(step):
+    return [(i, (i + step) % 8) for i in range(8)]
 
 
 def mm(left, right):
@@ -218,10 +222,15 @@
     return each(lambda x, y: jnp.concatenate([x, y], axis=0), first, second)
 
 
-def pack_kernel(k_ref, v_ref, q_ref, out_ref):
+def pack_kernel(k_ref, v_ref, q_ref, weight_ref, out_ref, half_ref, sem):
+    core = lax.axis_index("ctx") % CORES
+    rows = weight_ref.shape[0] // CORES
+    copy = pltpu.make_async_copy(weight_ref.at[pl.ds(core * rows, rows)], half_ref, sem)
+    copy.start()
     out_ref[:, 0:256] = k_ref[...]
     out_ref[:, 256:768] = v_ref[...]
     out_ref[:, 768:1024] = q_ref[...]
+    copy.wait()
 
 
 def early_kernel(
@@ -403,41 +412,59 @@
         give_ref[k] = jnp.where(core == 0, after, state).astype(BF16)
 
 
-def norm_kernel(local_ref, reach_ref, mine_ref, got_ref, gate_ref, gain_ref, keep_ref, give_ref):
+KEPT = (0, -3, 2)
+TO_RIGHT = (1, -2, 3)
+TO_LEFT = (-1, -4)
+
+
+def norm_kernel(
+    local_ref, reach_ref, mine_ref, got_ref, gate_ref, gain_ref, keep_ref, right_ref, left_ref, normed_ref
+):
     core = lax.axis_index("ctx") % CORES
-    place = lax.axis_index("head") // 2
-    side = lax.axis_index("head") % 2
+    place = lax.axis_index("head")
     for h in range(HEADS):
         state = jnp.where(core == h // 2, mine_ref[h % 2], got_ref[h % 2])
         heads = local_ref[h] + mm(reach_ref[h], state)
         inv = lax.rsqrt(jnp.mean(heads * heads, axis=-1, keepdims=True) + EPS)
         gate = gate_ref[:, h * DV : (h + 1) * DV].astype(F32)
         gate = gate * jax.nn.sigmoid(gate)
-        normed = (heads * inv * gain_ref[...] * gate).astype(BF16)
-        rows = TOK // 8
-        for block in range(4):
-            even = normed[2 * block * rows : (2 * block + 1) * rows]
-            odd = normed[(2 * block + 1) * rows : (2 * block + 2) * rows]
-            top = pl.multiple_of(((block + 4 - place) % 4) * rows, rows)
-            at = (pl.ds(top, rows), slice(h * DV, (h + 1) * DV))
-            keep_ref[at] = jnp.where(side == 0, even, odd)
-            give_ref[at] = jnp.where(side == 0, odd, even)
-
-
-def project_kernel(keep_ref, got_ref, own_ref, near_ref, *out_refs):
+        normed_ref[:, h * DV : (h + 1) * DV] = (heads * inv * gain_ref[...] * gate).astype(BF16)
+    rows = TOK // 8
+    for steps, ref in ((KEPT, keep_ref), (TO_RIGHT, right_ref), (TO_LEFT, left_ref)):
+        for k, step in enumerate(steps):
+            top = pl.multiple_of(((place + step + 8) % 8) * rows, rows)
+            ref[k * rows : (k + 1) * rows, :] = normed_ref[pl.ds(top, rows), :]
+
+
+def project_kernel(
+    keep_ref, left_ref, right_ref, own_ref, left_w_ref, left_w2_ref, right_w_ref, right_w2_ref,
+    *out_refs,
+):
+    core = lax.axis_index("ctx") % CORES
     keep = keep_ref[...]
-    got = got_ref[...]
+
+    def halves(rows):
+        half = rows.shape[1] // 2
+        first, second = rows[:, :half], rows[:, half:]
+        return jnp.where(core == 0, first, second), jnp.where(core == 0, second, first)
+
+    left, left2 = halves(left_ref[...])
+    right, right2 = halves(right_ref[...])
+    rows = TOK // 8
     for part in range(0, own_ref.shape[1], 512):
         at = slice(part, part + 512)
-        total = mm(keep, own_ref[:, at]) + mm(got, near_ref[:, at])
-        rows = total.shape[0] // len(out_refs)
+        total = mm(keep, own_ref[:, at]) + mm(left, left_w_ref[:, at]) + mm(left2, left_w2_ref[:, at])
+        more = mm(right, right_w_ref[:, at]) + mm(right2, right_w2_ref[:, at])
         for k, out_ref in enumerate(out_refs):
-            out_ref[:, at] = total[k * rows : (k + 1) * rows].astype(out_ref.dtype)
-
-
-def sum_kernel(own_ref, one_ref, two_ref, three_ref, out_ref):
+            term = total[k * rows : (k + 1) * rows]
+            if k < len(TO_LEFT):
+                term = term + more[k * rows : (k + 1) * rows]
+            out_ref[:, at] = term.astype(out_ref.dtype)
+
+
+def sum_kernel(own_ref, one_ref, two_ref, out_ref):
     total = own_ref[...]
-    for ref in (one_ref, two_ref, three_ref):
+    for ref in (one_ref, two_ref):
         total = total + ref[...].astype(F32)
     out_ref[...] = total.astype(BF16)
 
@@ -477,17 +504,21 @@
     gain_row = norm_gain.reshape(1, DV)
     width = out_weight.shape[1]
     last = TOK // RIM - 1
-    edge = pl.pallas_call(
+    edge, half = pl.pallas_call(
         pack_kernel,
         grid=(1,),
-        out_shape=jax.ShapeDtypeStruct((RIM, 1024), BF16),
-        in_specs=[pl.BlockSpec((RIM, n), lambda i: (last, 0)) for n in (256, 512, 256)],
-        out_specs=pl.BlockSpec((RIM, 1024), lambda i: (0, 0)),
+        out_shape=[
+            jax.ShapeDtypeStruct((RIM, 1024), BF16),
+            jax.ShapeDtypeStruct((out_weight.shape[0] // CORES, width), BF16),
+        ],
+        in_specs=[pl.BlockSpec((RIM, n), lambda i: (last, 0)) for n in (256, 512, 256)] + [HBM],
+        out_specs=[pl.BlockSpec((RIM, 1024), lambda i: (0, 0)), VMEM],
+        scratch_shapes=[pltpu.SemaphoreType.DMA],
+        compiler_params=pltpu.CompilerParams(vmem_limit_bytes=54 * MIB),
         cost_estimate=pl.CostEstimate(flops=5_000_000_000, bytes_accessed=0, transcendentals=0),
-    )(key_in, value_in, query_in)
-    near_weight = lax.ppermute(
-        lax.optimization_barrier((out_weight, edge))[0], "head", [(i, i ^ 1) for i in range(8)]
-    )
+    )(key_in, value_in, query_in, out_weight)
+    left_half = lax.ppermute(half, "head", around_z(1))
+    right_half = lax.ppermute(half, "head", around_z(-1))
     rim = lax.ppermute(edge, "ctx", [(i, i + 1) for i in range(CTX - 1)])
     wide = (2, DK, DK + DV)
     early = call(
@@ -532,23 +563,38 @@
         [pltpu.VMEM((CHIPS_Y,) + wide, BF16)], flops=60_000_000, moved=1_000_000,
     )
     got = lax.ppermute(to_other, "ctx", core_swap())
-    rows = (TOK // 2, HEADS * DV)
-    keep, to_near = call(
-        norm_kernel, [(rows, BF16), (rows, BF16)],
+    left_late, right_late, _ = lax.optimization_barrier((left_half, right_half, got))
+    left_half2 = lax.ppermute(left_late, "ctx", core_swap())
+    right_half2 = lax.ppermute(right_late, "ctx", core_swap())
+    block = TOK // 8
+
+    def normed_rows(steps):
+        return ((len(steps) * block, HEADS * DV), BF16)
+
+    keep, to_right, to_left = call(
+        norm_kernel, [normed_rows(KEPT), normed_rows(TO_RIGHT), normed_rows(TO_LEFT)],
         [local, reach, mine, got, out_gate, gain_row],
+        [pltpu.VMEM((TOK, HEADS * DV), BF16)],
         flops=100_000_000, moved=1_500_000,
     )
-    brought = lax.ppermute(to_near, "head", [(i, i ^ 1) for i in range(8)])
-    block = (TOK // 8, width)
-    partials = call(
-        project_kernel, [(block, F32)] + [(block, BF16)] * 3,
-        [keep, brought, out_weight, near_weight],
-        flops=600_000_000, moved=4_000_000,
-    )
-    terms = [partials[0]] + [
-        lax.ppermute(partials[k], "head", [(i, (i + 2 * k) % 8) for i in range(8)]) for k in (2, 1, 3)
-    ]
-    (mixed,) = call(sum_kernel, [(block, BF16)], terms, flops=1_000_000, moved=800_000)
+    from_left = lax.ppermute(to_right, "head", around_z(1))
+    from_right = lax.ppermute(to_left, "head", around_z(-1))
+    own_part, back_part, ahead_part = call(
+        project_kernel, [((block, width), F32)] + [((block, width), BF16)] * 2,
+        [
+            keep, from_left, from_right, out_weight, left_half, left_half2, right_half, right_half2
+        ],
+        flops=600_000_000, moved=6_000_000,
+    )
+    (mixed,) = call(
+        sum_kernel, [((block, width), BF16)],
+        [
+            own_part,
+            lax.ppermute(back_part, "head", around_z(-3)),
+            lax.ppermute(ahead_part, "head", around_z(2)),
+        ],
+        flops=1_000_000, moved=800_000,
+    )
     return mixed
 
 

time: 73.4 us -> 66.7 us (0.909)
  waiting for transfers between devices: 33.8 us -> 24.6 us
  Pallas kernels: 10.8 us -> 12.7 us
  starting transfers between devices: 26.5 us -> 27.9 us
    ppermute x5 -> x8, waiting for transfers between devices: 19.3 us -> 10.1 us  [the longest x1 7.21 us: on_device(): lax.ppermute(back_part, 'head', around_z(-3))]
    ppermute x5 -> x8, starting transfers between devices: 13.4 us -> 14.9 us  [the longest x1 4.03 us: on_device(): right_half = lax.ppermute(half, 'head', around_z(-1))]
    pallas_call x1, Pallas kernels: 1.49 us -> 2.99 us  [on_device(): pl.pallas_call(pack_kernel, grid=(1,), out_shape=[jax.ShapeDtypeStruct((R...]
  transfers between devices with their start and end apart: 14 -> 17, of which waited for: 12 -> 11; matrix products, arithmetic and copies ran while one was open for 0% -> 0% of each run, Pallas kernels for 11% -> 12%
where the time goes in v6:
time: 66.7 us; the launch traced here: 66.2 us
  starting transfers between devices  27.9 us (42%)
  waiting for transfers between devices  24.6 us (37%)
  Pallas kernels  12.7 us (19%)
  local copies, waits for them, and re-layouts  0.81 us (1%)
    pallas_call x9, Pallas kernels, call(): pl.pallas_call(kernel, grid=(1,) if blocked else (), out_shape=[jax.Shape...  9.71 us
    ppermute x3, starting transfers between devices, on_device(): far = [lax.ppermute(total, 'ctx', along_y(k)) for k in (1, 2, 3)]  7.49 us
    ppermute x1, waiting for transfers between devices, on_device(): lax.ppermute(back_part, 'head', around_z(-3))  7.21 us
    ppermute x3, waiting for transfers between devices, on_device(): near = [lax.ppermute(pair, 'ctx', along_x(k)) for k in (1, 2, 3)]  6.53 us
    ppermute x3, waiting for transfers between devices, on_device(): far = [lax.ppermute(total, 'ctx', along_y(k)) for k in (1, 2, 3)]  4.53 us
    ppermute x1, starting transfers between devices, on_device(): right_half = lax.ppermute(half, 'head', around_z(-1))  4.03 us
    ppermute x1, starting transfers between devices, on_device(): from_right = lax.ppermute(to_left, 'head', around_z(-1))  3.22 us
    pallas_call x1, Pallas kernels, on_device(): pl.pallas_call(pack_kernel, grid=(1,), out_shape=[jax.ShapeDtypeStruct((R...  2.99 us
  transfers between devices with their start and end apart: 17, of which 11 were waited for; matrix products, arithmetic and copies ran while one was open for 0% of the time, Pallas kernels for 12%

profile of v6, /device:TPU:6, one launch (start us, length us, event | category | flops | bytes accessed | tf_op | source)
XLA Modules:
  0.0 66.2 jit_solution(6360033936569545211)
XLA Ops:
  0.0 0.0 copy-start.12
  0.0 0.0 copy-start.8
  0.0 0.0 copy-start.9
  0.0 0.0 copy-start.7
  0.0 3.0 %shard_map.118 = (bf16[16,1024]{1,0:T(8,128)(2,1)}, bf16[256,2048]{1,0:T(8,128)(2,1)}) custom-call(bf16[256,256]{1,0:T(8,128)(2,1)} %k_ref.3, bf16[256,512]{1,0:T(8,128)(2,1)} %v_ref.3, bf16[256,256]{1,0:T(8,128)(2,1)} %q_ref.3, bf16[512,2048]{1,0:T(8,128)(2,1)} %own_ref.1), custom_call_target="tpu_custom_call" | custom-call | flops 5000000000 | tf_op jit(solution)/shard_map/pallas_call | solution.py:507
  3.0 2.0 %collective-permute-start.11 = (bf16[256,2048]{1,0:T(8,128)(2,1)}, bf16[256,2048]{1,0:T(8,128)(2,1)S(1)}, u32[]{:S(2)}, u32[]{:S(2)}) collective-permute-start(bf16[256,2048]{1,0:T(8,128)(2,1)} %get-tuple-element.55), channel_id=1, source_target_pairs={{0,1},{1,2},{2,3},{3,4},{4,5},{5,6},{6,7},{7,0},{8,9},{9,10},{10,1... | collective-permute-start | bytes 3145736 | tf_op jit(solution)/shard_map/ppermute | solution.py:520
  5.0 4.0 %collective-permute-start.12 = (bf16[256,2048]{1,0:T(8,128)(2,1)}, bf16[256,2048]{1,0:T(8,128)(2,1)S(1)}, u32[]{:S(2)}, u32[]{:S(2)}) collective-permute-start(bf16[256,2048]{1,0:T(8,128)(2,1)} %get-tuple-element.55), channel_id=1, source_target_pairs={{0,7},{1,0},{2,1},{3,2},{4,3},{5,4},{6,5},{7,6},{8,15},{9,8},{10,9... | collective-permute-start | bytes 3145736 | tf_op jit(solution)/shard_map/ppermute | solution.py:521
  9.1 1.9 %collective-permute-start = (bf16[16,1024]{1,0:T(8,128)(2,1)}, bf16[16,1024]{1,0:T(8,128)(2,1)S(1)}, u32[]{:S(2)}, u32[]{:S(2)}) collective-permute-start(bf16[16,1024]{1,0:T(8,128)(2,1)} %get-tuple-element.33.edge_ref), channel_id=1, source_target_pairs={{0,8},{8,16},{16,24},{24,32},{32,40},{40,48},{48,56},{56,64},{64,7... | collective-permute-start | bytes 98312 | tf_op jit(solution)/shard_map/ppermute | solution.py:522
  11.0 0.0 copy-done.4
  11.0 0.0 copy-done.3
  11.0 0.0 copy-done.10
  11.0 0.0 copy-done.12
  11.0 0.0 copy-done.8
  11.0 0.0 copy-done.9
  11.0 0.0 copy-done.7
  11.1 0.0 copy-start.6
  11.1 0.7 %copy-done.6 = bf16[16,1024]{1,0:T(8,128)(2,1)S(1)} copy-done((bf16[16,1024]{1,0:T(8,128)(2,1)S(1)}, bf16[16,1024]{1,0:T(8,128)(2,1)}, u32[]{:S(2)}) %copy-start.6) | copy-done | bytes 32792
  11.8 1.4 %shard_map.119 = (bf16[2,256,128]{2,1,0:T(8,128)(2,1)S(1)}, bf16[256,512]{1,0:T(8,128)(2,1)S(1)}, f32[4,256,256]{2,1,0:T(8,128)S(1)}, f32[4,256,128]{2,1,0:T(8,1...) custom-call(bf16[256,256]{1,0:T(8,128)(2,1)S(1)} %copy-done.4, ...), custom_call_target="tpu_custom_call" | custom-call | flops 500000000 | tf_op jit(solution)/shard_map/pallas_call | solution.py:487
  13.3 1.2 %collective-permute-done.rim_ref = bf16[16,1024]{1,0:T(8,128)(2,1)S(1)} collective-permute-done((bf16[16,1024]{1,0:T(8,128)(2,1)}, bf16[16,1024]{1,0:T(8,128)(2,1)S(1)}, u32[]{:S(2)}, u32[]{:S(2)}) %collective-permute-start) | collective-permute-done | bytes 32800 | tf_op jit(solution)/shard_map/ppermute | solution.py:522
  14.5 3.4 %shard_map.120 = (bf16[4,256,256]{2,1,0:T(8,128)(2,1)S(1)}, bf16[2,256,128]{2,1,0:T(8,128)(2,1)S(1)}, bf16[2,128,256]{2,1,0:T(8,128)(2,1)S(1)}, bf16[2,128,256]{2,1,0:T(8,128)(2,1)S(1)}) custom-call(bf16[16,1024]{1,0:T(8,128)(2,1)S(1)} %collective-permute-done.rim_ref, bf16[16,768]{1,0:T(8,128)(2,1)S(1)} %get-tuple-element.34.head_ref, ...), custom_call_target="tpu_custom_call" | custom-call | flops 4000000000 | bytes 2000000 | tf_op jit(solution)/shard_map/pallas_call | solution.py:487
  17.9 0.5 collective-permute-start.1
  18.4 1.0 %collective-permute-done.1.got_ref.other_ref = bf16[2,128,256]{2,1,0:T(8,128)(2,1)S(1)} collective-permute-done((bf16[2,128,256]{2,1,0:T(8,128)(2,1)S(1)}, bf16[2,128,256]{2,1,0:T(8,128)(2,1)S(1)}, u32[]{:S(2)}, u32[]{:S(2)}) %collective-permute-start.1) | collective-permute-done | bytes 131104 | tf_op jit(solution)/shard_map/ppermute | solution.py:544
  19.3 0.2 shard_map.122.own_ref
  19.5 0.6 collective-permute-start.2
  20.1 2.4 %collective-permute-start.3 = (bf16[2,128,256]{2,1,0:T(8,128)(2,1)S(1)}, bf16[2,128,256]{2,1,0:T(8,128)(2,1)S(1)}, u32[]{:S(2)}, u32[]{:S(2)}) collective-permute-start(bf16[2,128,256]{2,1,0:T(8,128)(2,1)S(1)} %shard_map.122.own_ref), channel_id=1, source_target_pairs={{0,32},{8,40},{16,48},{24,56},{32,0},{40,8},{48,16},{56,24},{64,96... | collective-permute-start | bytes 393224 | tf_op jit(solution)/shard_map/ppermute | solution.py:546
  22.5 0.0 collective-permute-start.4
  22.5 0.0 copy-done.5
  22.5 0.0 copy-done.11
  22.5 0.0 copy-start.1
  22.5 0.0 copy-start.2
  22.5 0.8 %shard_map.121 = (f32[4,256,128]{2,1,0:T(8,128)S(1)}, bf16[4,256,128]{2,1,0:T(8,128)(2,1)S(1)}) custom-call(bf16[256,256]{1,0:T(8,128)(2,1)S(1)} %copy-done.5, bf16[16,1024]{1,0:T(8,128)(2,1)S(1)} %collective-permute-done.rim_ref, f32[4,256]{1,0:T(4,128)S(1)} %copy-done.10, s32[1,256]{1,0:T(1,128)S(1)} %bitcast.4, f32[4,256]{1,0:T(4,128)S(1)} %copy-done.11, ...), custom_call_target="tpu_custom_call" | custom-call | flops 2000000000 | bytes 2000000 | tf_op jit(solution)/shard_map/pallas_call | solution.py:487
  23.3 0.0 copy-start
  23.4 2.6 %collective-permute-done.2.one_ref = bf16[2,128,256]{2,1,0:T(8,128)(2,1)S(1)} collective-permute-done((bf16[2,128,256]{2,1,0:T(8,128)(2,1)S(1)}, bf16[2,128,256]{2,1,0:T(8,128)(2,1)S(1)}, u32[]{:S(2)}, u32[]{:S(2)}) %collective-permute-start.2) | collective-permute-done | bytes 131104 | tf_op jit(solution)/shard_map/ppermute | solution.py:546
  25.9 2.0 %collective-permute-done.3.two_ref = bf16[2,128,256]{2,1,0:T(8,128)(2,1)S(1)} collective-permute-done((bf16[2,128,256]{2,1,0:T(8,128)(2,1)S(1)}, bf16[2,128,256]{2,1,0:T(8,128)(2,1)S(1)}, u32[]{:S(2)}, u32[]{:S(2)}) %collective-permute-start.3) | collective-permute-done | bytes 131104 | tf_op jit(solution)/shard_map/ppermute | solution.py:546
  28.0 1.9 %collective-permute-done.4.three_ref = bf16[2,128,256]{2,1,0:T(8,128)(2,1)S(1)} collective-permute-done((bf16[2,128,256]{2,1,0:T(8,128)(2,1)S(1)}, bf16[2,128,256]{2,1,0:T(8,128)(2,1)S(1)}, u32[]{:S(2)}, u32[]{:S(2)}) %collective-permute-start.4) | collective-permute-done | bytes 131104 | tf_op jit(solution)/shard_map/ppermute | solution.py:546
  29.9 0.7 %shard_map.123 = (bf16[2,128,256]{2,1,0:T(8,128)(2,1)S(1)}, bf16[2,128,256]{2,1,0:T(8,128)(2,1)S(1)}) custom-call(bf16[2,128,256]{2,1,0:T(8,128)(2,1)S(1)} %shard_map.122.own_ref, bf16[2,128,256]{2,1,0:T(8,128)(2,1)S(1)} %collective-permute-done.2.one_ref, bf16[2,128,256]{2,1,0:T(8,128)(2,1)S(1)} %collective-permute-done.3.two_ref, ...), custom_call_target="tpu_custom_call" | custom-call | flops 60000000 | bytes 800000 | tf_op jit(solution)/shard_map/pallas_call | solution.py:487
  30.6 3.2 %collective-permute-start.5 = (bf16[2,128,256]{2,1,0:T(8,128)(2,1)S(1)}, bf16[2,128,256]{2,1,0:T(8,128)(2,1)S(1)}, u32[]{:S(2)}, u32[]{:S(2)}) collective-permute-start(bf16[2,128,256]{2,1,0:T(8,128)(2,1)S(1)} %get-tuple-element.48.own_ref), channel_id=1, source_target_pairs={{0,64},{8,72},{16,80},{24,88},{32,96},{40,104},{48,112},{56,120},{... | collective-permute-start | bytes 393224 | tf_op jit(solution)/shard_map/ppermute | solution.py:559
  33.8 2.9 %collective-permute-start.6 = (bf16[2,128,256]{2,1,0:T(8,128)(2,1)S(1)}, bf16[2,128,256]{2,1,0:T(8,128)(2,1)S(1)}, u32[]{:S(2)}, u32[]{:S(2)}) collective-permute-start(bf16[2,128,256]{2,1,0:T(8,128)(2,1)S(1)} %get-tuple-element.48.own_ref), channel_id=1, source_target_pairs={{0,128},{8,136},{16,144},{24,152},{32,160},{40,168},{48,176},{56,1... | collective-permute-start | bytes 393224 | tf_op jit(solution)/shard_map/ppermute | solution.py:559
  36.7 1.3 %collective-permute-start.7 = (bf16[2,128,256]{2,1,0:T(8,128)(2,1)S(1)}, bf16[2,128,256]{2,1,0:T(8,128)(2,1)S(1)}, u32[]{:S(2)}, u32[]{:S(2)}) collective-permute-start(bf16[2,128,256]{2,1,0:T(8,128)(2,1)S(1)} %get-tuple-element.48.own_ref), channel_id=1, source_target_pairs={{0,192},{8,200},{16,208},{24,216},{32,224},{40,232},{48,240},{56,2... | collective-permute-start | bytes 393224 | tf_op jit(solution)/shard_map/ppermute | solution.py:559
  38.1 0.7 %collective-permute-done.5.one_ref = bf16[2,128,256]{2,1,0:T(8,128)(2,1)S(1)} collective-permute-done((bf16[2,128,256]{2,1,0:T(8,128)(2,1)S(1)}, bf16[2,128,256]{2,1,0:T(8,128)(2,1)S(1)}, u32[]{:S(2)}, u32[]{:S(2)}) %collective-permute-start.5) | collective-permute-done | bytes 131104 | tf_op jit(solution)/shard_map/ppermute | solution.py:559
  38.8 3.9 %collective-permute-done.6.two_ref = bf16[2,128,256]{2,1,0:T(8,128)(2,1)S(1)} collective-permute-done((bf16[2,128,256]{2,1,0:T(8,128)(2,1)S(1)}, bf16[2,128,256]{2,1,0:T(8,128)(2,1)S(1)}, u32[]{:S(2)}, u32[]{:S(2)}) %collective-permute-start.6) | collective-permute-done | bytes 131104 | tf_op jit(solution)/shard_map/ppermute | solution.py:559
  42.6 0.0 collective-permute-done.7.three_ref
  42.6 0.9 %shard_map.124 = (bf16[2,128,128]{2,1,0:T(8,128)(2,1)S(1)}, bf16[2,128,128]{2,1,0:T(8,128)(2,1)S(1)}) custom-call(bf16[2,128,256]{2,1,0:T(8,128)(2,1)S(1)} %get-tuple-element.48.own_ref, bf16[2,128,256]{2,1,0:T(8,128)(2,1)S(1)} %collective-permute-done.5.one_ref, bf16[2,128,256]{2,1,0:T(8,128)(2,1)S(1)} %collective-permute-done.6.two_ref, ...), custom_call_target="tpu_custom_call" | custom-call | flops 60000000 | bytes 1000000 | tf_op jit(solution)/shard_map/pallas_call | solution.py:487
  43.5 0.1 collective-permute-start.8
  43.6 1.2 %collective-permute-done.8.got_ref = bf16[2,128,128]{2,1,0:T(8,128)(2,1)S(1)} collective-permute-done((bf16[2,128,128]{2,1,0:T(8,128)(2,1)S(1)}, bf16[2,128,128]{2,1,0:T(8,128)(2,1)S(1)}, u32[]{:S(2)}, u32[]{:S(2)}) %collective-permute-start.8) | collective-permute-done | bytes 65568 | tf_op jit(solution)/shard_map/ppermute | solution.py:565
  44.9 0.0 collective-permute-done.11.left_w_ref
  44.9 0.0 collective-permute-done.12.right_w_ref
  44.9 0.2 collective-permute-start.13
  45.0 0.4 collective-permute-start.14
  45.4 0.0 copy-done.1
  45.4 0.0 copy-done.2
  45.4 0.4 shard_map.125
  45.8 0.1 collective-permute-start.9
  45.9 3.2 %collective-permute-start.10 = (bf16[64,512]{1,0:T(8,128)(2,1)S(1)}, bf16[64,512]{1,0:T(8,128)(2,1)S(1)}, u32[]{:S(2)}, u32[]{:S(2)}) collective-permute-start(bf16[64,512]{1,0:T(8,128)(2,1)S(1)} %get-tuple-element.54), channel_id=1, source_target_pairs={{0,7},{1,0},{2,1},{3,2},{4,3},{5,4},{6,5},{7,6},{8,15},{9,8},{10,9... | collective-permute-start | bytes 196616 | tf_op jit(solution)/shard_map/ppermute | solution.py:581
  49.1 1.9 %collective-permute-done.10.right_ref = bf16[64,512]{1,0:T(8,128)(2,1)S(1)} collective-permute-done((bf16[64,512]{1,0:T(8,128)(2,1)S(1)}, bf16[64,512]{1,0:T(8,128)(2,1)S(1)}, u32[]{:S(2)}, u32[]{:S(2)}) %collective-permute-start.10) | collective-permute-done | bytes 65568 | tf_op jit(solution)/shard_map/ppermute | solution.py:581
  51.0 0.9 %collective-permute-done.9.left_ref = bf16[96,512]{1,0:T(8,128)(2,1)S(1)} collective-permute-done((bf16[96,512]{1,0:T(8,128)(2,1)S(1)}, bf16[96,512]{1,0:T(8,128)(2,1)S(1)}, u32[]{:S(2)}, u32[]{:S(2)}) %collective-permute-start.9) | collective-permute-done | bytes 98336 | tf_op jit(solution)/shard_map/ppermute | solution.py:580
  52.0 0.0 collective-permute-done.13.left_w2_ref
  52.0 0.0 collective-permute-done.14.right_w2_ref
  52.0 1.2 %shard_map.126 = (f32[32,2048]{1,0:T(8,128)S(1)}, bf16[32,2048]{1,0:T(8,128)(2,1)S(1)}, bf16[32,2048]{1,0:T(8,128)(2,1)S(1)}) custom-call(bf16[96,512]{1,0:T(8,128)(2,1)S(1)} %get-tuple-element.52.keep_ref, bf16[96,512]{1,0:T(8,128)(2,1)S(1)} %collective-permute-done.9.left_ref, bf16[64,512]{1,0:T(8,128)(2,1)S(1)} %collective-permute-done.10.right_ref, ...), custom_call_target="tpu_custom_call" | custom-call | flops 600000000 | bytes 6000000 | tf_op jit(solution)/shard_map/pallas_call | solution.py:487
  53.2 2.2 %collective-permute-start.15 = (bf16[32,2048]{1,0:T(8,128)(2,1)S(1)}, bf16[32,2048]{1,0:T(8,128)(2,1)S(1)}, u32[]{:S(2)}, u32[]{:S(2)}) collective-permute-start(bf16[32,2048]{1,0:T(8,128)(2,1)S(1)} %get-tuple-element.59), channel_id=1, source_target_pairs={{0,5},{1,6},{2,7},{3,0},{4,1},{5,2},{6,3},{7,4},{8,13},{9,14},{10,... | collective-permute-start | bytes 393224 | tf_op jit(solution)/shard_map/ppermute | solution.py:593
  55.3 2.9 %collective-permute-start.16 = (bf16[32,2048]{1,0:T(8,128)(2,1)S(1)}, bf16[32,2048]{1,0:T(8,128)(2,1)S(1)}, u32[]{:S(2)}, u32[]{:S(2)}) collective-permute-start(bf16[32,2048]{1,0:T(8,128)(2,1)S(1)} %get-tuple-element.60), channel_id=1, source_target_pairs={{0,2},{1,3},{2,4},{3,5},{4,6},{5,7},{6,0},{7,1},{8,10},{9,11},{10,... | collective-permute-start | bytes 393224 | tf_op jit(solution)/shard_map/ppermute | solution.py:594
  58.3 7.2 %collective-permute-done.15.one_ref = bf16[32,2048]{1,0:T(8,128)(2,1)S(1)} collective-permute-done((bf16[32,2048]{1,0:T(8,128)(2,1)S(1)}, bf16[32,2048]{1,0:T(8,128)(2,1)S(1)}, u32[]{:S(2)}, u32[]{:S(2)}) %collective-permute-start.15) | collective-permute-done | bytes 131104 | tf_op jit(solution)/shard_map/ppermute | solution.py:593
  65.5 0.0 collective-permute-done.16.two_ref
  65.5 0.7 %shard_map.127 = bf16[32,2048]{1,0:T(8,128)(2,1)} custom-call(f32[32,2048]{1,0:T(8,128)S(1)} %get-tuple-element.58.own_ref, bf16[32,2048]{1,0:T(8,128)(2,1)S(1)} %collective-permute-done.15.one_ref, bf16[32,2048]{1,0:T(8,128)(2,1)S(1)} %collective-permute-done.16.two_ref), custom_call_target="tpu_custom_call" | custom-call | flops 1000000 | bytes 800000 | tf_op jit(solution)/shard_map/pallas_call | solution.py:487
  (6 shorter events, 0.0 us)
Async XLA Ops:
  0.0 11.0 %copy-start.4 = (bf16[256,256]{1,0:T(8,128)(2,1)S(1)}, bf16[256,256]{1,0:T(8,128)(2,1)}, u32[]{:S(2)}) copy-start(bf16[256,256]{1,0:T(8,128)(2,1)} %k_ref.3) | copy-start | bytes 393220
  0.0 11.0 %copy-start.3 = (bf16[256,512]{1,0:T(8,128)(2,1)S(1)}, bf16[256,512]{1,0:T(8,128)(2,1)}, u32[]{:S(2)}) copy-start(bf16[256,512]{1,0:T(8,128)(2,1)} %v_ref.3) | copy-start | bytes 786436
  0.0 11.0 %copy-start.10 = (f32[4,256]{1,0:T(4,128)S(1)}, f32[4,256]{1,0:T(4,128)}, u32[]{:S(2)}) copy-start(f32[4,256]{1,0:T(4,128)} %decay_ref.3) | copy-start | bytes 12292
  0.0 11.0 %copy-start.12 = (s32[256]{0:T(256)S(1)}, s32[256]{0:T(256)}, u32[]{:S(2)}) copy-start(s32[256]{0:T(256)} %param.18) | copy-start | bytes 3076
  0.0 11.0 %copy-start.8 = (f32[4,256]{1,0:T(4,128)S(1)}, f32[4,256]{1,0:T(4,128)}, u32[]{:S(2)}) copy-start(f32[4,256]{1,0:T(4,128)} %beta_ref.3) | copy-start | bytes 12292
  0.0 11.0 %copy-start.9 = (f32[4,256]{1,0:T(4,128)S(1)}, f32[4,256]{1,0:T(4,128)}, u32[]{:S(2)}) copy-start(f32[4,256]{1,0:T(4,128)} %wk_ref.3) | copy-start | bytes 12292
  0.0 11.0 %copy-start.7 = (f32[4,512]{1,0:T(4,128)S(1)}, f32[4,512]{1,0:T(4,128)}, u32[]{:S(2)}) copy-start(f32[4,512]{1,0:T(4,128)} %wv_ref.3) | copy-start | bytes 24580
  3.0 41.8 %collective-permute-start.11 = (bf16[256,2048]{1,0:T(8,128)(2,1)}, bf16[256,2048]{1,0:T(8,128)(2,1)S(1)}, u32[]{:S(2)}, u32[]{:S(2)}) collective-permute-start(bf16[256,2048]{1,0:T(8,128)(2,1)} %get-tuple-element.55), channel_id=1, source_target_pairs={{0,1},{1,2},{2,3},{3,4},{4,5},{5,6},{6,7},{7,0},{8,9},{9,10},{10,1... | collective-permute-start | bytes 3145736 | tf_op jit(solution)/shard_map/ppermute | solution.py:520
  5.0 39.8 %collective-permute-start.12 = (bf16[256,2048]{1,0:T(8,128)(2,1)}, bf16[256,2048]{1,0:T(8,128)(2,1)S(1)}, u32[]{:S(2)}, u32[]{:S(2)}) collective-permute-start(bf16[256,2048]{1,0:T(8,128)(2,1)} %get-tuple-element.55), channel_id=1, source_target_pairs={{0,7},{1,0},{2,1},{3,2},{4,3},{5,4},{6,5},{7,6},{8,15},{9,8},{10,9... | collective-permute-start | bytes 3145736 | tf_op jit(solution)/shard_map/ppermute | solution.py:521
  9.1 5.4 %collective-permute-start = (bf16[16,1024]{1,0:T(8,128)(2,1)}, bf16[16,1024]{1,0:T(8,128)(2,1)S(1)}, u32[]{:S(2)}, u32[]{:S(2)}) collective-permute-start(bf16[16,1024]{1,0:T(8,128)(2,1)} %get-tuple-element.33.edge_ref), channel_id=1, source_target_pairs={{0,8},{8,16},{16,24},{24,32},{32,40},{40,48},{48,56},{56,64},{64,7... | collective-permute-start | bytes 98312 | tf_op jit(solution)/shard_map/ppermute | solution.py:522
  11.1 0.8 %copy-start.6 = (bf16[16,1024]{1,0:T(8,128)(2,1)S(1)}, bf16[16,1024]{1,0:T(8,128)(2,1)}, u32[]{:S(2)}) copy-start(bf16[16,1024]{1,0:T(8,128)(2,1)} %get-tuple-element.33.edge_ref) | copy-start | bytes 98308
  14.5 8.0 %copy-start.5 = (bf16[256,256]{1,0:T(8,128)(2,1)S(1)}, bf16[256,256]{1,0:T(8,128)(2,1)}, u32[]{:S(2)}) copy-start(bf16[256,256]{1,0:T(8,128)(2,1)} %q_ref.3) | copy-start | bytes 393220
  14.5 8.0 %copy-start.11 = (f32[4,256]{1,0:T(4,128)S(1)}, f32[4,256]{1,0:T(4,128)}, u32[]{:S(2)}) copy-start(f32[4,256]{1,0:T(4,128)} %wq_ref.1) | copy-start | bytes 12292
  17.9 1.5 %collective-permute-start.1 = (bf16[2,128,256]{2,1,0:T(8,128)(2,1)S(1)}, bf16[2,128,256]{2,1,0:T(8,128)(2,1)S(1)}, u32[]{:S(2)}, u32[]{:S(2)}) collective-permute-start(bf16[2,128,256]{2,1,0:T(8,128)(2,1)S(1)} %get-tuple-element.47), channel_id=1, source_target_pairs={{0,8},{8,0},{16,24},{24,16},{32,40},{40,32},{48,56},{56,48},{64,72... | collective-permute-start | bytes 393224 | tf_op jit(solution)/shard_map/ppermute | solution.py:544
  19.5 6.4 %collective-permute-start.2 = (bf16[2,128,256]{2,1,0:T(8,128)(2,1)S(1)}, bf16[2,128,256]{2,1,0:T(8,128)(2,1)S(1)}, u32[]{:S(2)}, u32[]{:S(2)}) collective-permute-start(bf16[2,128,256]{2,1,0:T(8,128)(2,1)S(1)} %shard_map.122.own_ref), channel_id=1, source_target_pairs={{0,16},{8,24},{16,32},{24,40},{32,48},{40,56},{48,0},{56,8},{64,80... | collective-permute-start | bytes 393224 | tf_op jit(solution)/shard_map/ppermute | solution.py:546
  20.1 7.9 %collective-permute-start.3 = (bf16[2,128,256]{2,1,0:T(8,128)(2,1)S(1)}, bf16[2,128,256]{2,1,0:T(8,128)(2,1)S(1)}, u32[]{:S(2)}, u32[]{:S(2)}) collective-permute-start(bf16[2,128,256]{2,1,0:T(8,128)(2,1)S(1)} %shard_map.122.own_ref), channel_id=1, source_target_pairs={{0,32},{8,40},{16,48},{24,56},{32,0},{40,8},{48,16},{56,24},{64,96... | collective-permute-start | bytes 393224 | tf_op jit(solution)/shard_map/ppermute | solution.py:546
  22.5 7.4 %collective-permute-start.4 = (bf16[2,128,256]{2,1,0:T(8,128)(2,1)S(1)}, bf16[2,128,256]{2,1,0:T(8,128)(2,1)S(1)}, u32[]{:S(2)}, u32[]{:S(2)}) collective-permute-start(bf16[2,128,256]{2,1,0:T(8,128)(2,1)S(1)} %shard_map.122.own_ref), channel_id=1, source_target_pairs={{0,48},{8,56},{16,0},{24,8},{32,16},{40,24},{48,32},{56,40},{64,11... | collective-permute-start | bytes 393224 | tf_op jit(solution)/shard_map/ppermute | solution.py:546
  22.5 22.9 %copy-start.1 = (bf16[256,512]{1,0:T(8,128)(2,1)S(1)}, bf16[256,512]{1,0:T(8,128)(2,1)}, u32[]{:S(2)}) copy-start(bf16[256,512]{1,0:T(8,128)(2,1)} %gate_ref.1) | copy-start | bytes 786436
  22.5 22.9 %copy-start.2 = (f32[128]{0:T(128)S(1)}, f32[128]{0:T(128)}, u32[]{:S(2)}) copy-start(f32[128]{0:T(128)} %param.22) | copy-start | bytes 1540
  23.3 28.6 %copy-start = (bf16[512,2048]{1,0:T(8,128)(2,1)S(1)}, bf16[512,2048]{1,0:T(8,128)(2,1)}, u32[]{:S(2)}) copy-start(bf16[512,2048]{1,0:T(8,128)(2,1)} %own_ref.1) | copy-start | bytes 6291460
  30.6 8.2 %collective-permute-start.5 = (bf16[2,128,256]{2,1,0:T(8,128)(2,1)S(1)}, bf16[2,128,256]{2,1,0:T(8,128)(2,1)S(1)}, u32[]{:S(2)}, u32[]{:S(2)}) collective-permute-start(bf16[2,128,256]{2,1,0:T(8,128)(2,1)S(1)} %get-tuple-element.48.own_ref), channel_id=1, source_target_pairs={{0,64},{8,72},{16,80},{24,88},{32,96},{40,104},{48,112},{56,120},{... | collective-permute-start | bytes 393224 | tf_op jit(solution)/shard_map/ppermute | solution.py:559
  33.8 8.8 %collective-permute-start.6 = (bf16[2,128,256]{2,1,0:T(8,128)(2,1)S(1)}, bf16[2,128,256]{2,1,0:T(8,128)(2,1)S(1)}, u32[]{:S(2)}, u32[]{:S(2)}) collective-permute-start(bf16[2,128,256]{2,1,0:T(8,128)(2,1)S(1)} %get-tuple-element.48.own_ref), channel_id=1, source_target_pairs={{0,128},{8,136},{16,144},{24,152},{32,160},{40,168},{48,176},{56,1... | collective-permute-start | bytes 393224 | tf_op jit(solution)/shard_map/ppermute | solution.py:559
  36.7 5.9 %collective-permute-start.7 = (bf16[2,128,256]{2,1,0:T(8,128)(2,1)S(1)}, bf16[2,128,256]{2,1,0:T(8,128)(2,1)S(1)}, u32[]{:S(2)}, u32[]{:S(2)}) collective-permute-start(bf16[2,128,256]{2,1,0:T(8,128)(2,1)S(1)} %get-tuple-element.48.own_ref), channel_id=1, source_target_pairs={{0,192},{8,200},{16,208},{24,216},{32,224},{40,232},{48,240},{56,2... | collective-permute-start | bytes 393224 | tf_op jit(solution)/shard_map/ppermute | solution.py:559
  43.5 1.3 %collective-permute-start.8 = (bf16[2,128,128]{2,1,0:T(8,128)(2,1)S(1)}, bf16[2,128,128]{2,1,0:T(8,128)(2,1)S(1)}, u32[]{:S(2)}, u32[]{:S(2)}) collective-permute-start(bf16[2,128,128]{2,1,0:T(8,128)(2,1)S(1)} %get-tuple-element.51), channel_id=1, source_target_pairs={{0,8},{8,0},{16,24},{24,16},{32,40},{40,32},{48,56},{56,48},{64,72... | collective-permute-start | bytes 196616 | tf_op jit(solution)/shard_map/ppermute | solution.py:565
  44.9 7.1 %collective-permute-start.13 = (bf16[256,2048]{1,0:T(8,128)(2,1)S(1)}, bf16[256,2048]{1,0:T(8,128)(2,1)S(1)}, u32[]{:S(2)}, u32[]{:S(2)}) collective-permute-start(bf16[256,2048]{1,0:T(8,128)(2,1)S(1)} %collective-permute-done.11.left_w_ref), channel_id=1, source_target_pairs={{0,8},{8,0},{16,24},{24,16},{32,40},{40,32},{48,56},{56,48},{64,72... | collective-permute-start | bytes 3145736 | tf_op jit(solution)/shard_map/ppermute | solution.py:567
  45.0 6.9 %collective-permute-start.14 = (bf16[256,2048]{1,0:T(8,128)(2,1)S(1)}, bf16[256,2048]{1,0:T(8,128)(2,1)S(1)}, u32[]{:S(2)}, u32[]{:S(2)}) collective-permute-start(bf16[256,2048]{1,0:T(8,128)(2,1)S(1)} %collective-permute-done.12.right_w_ref), channel_id=1, source_target_pairs={{0,8},{8,0},{16,24},{24,16},{32,40},{40,32},{48,56},{56,48},{64,72... | collective-permute-start | bytes 3145736 | tf_op jit(solution)/shard_map/ppermute | solution.py:568
  45.8 6.1 %collective-permute-start.9 = (bf16[96,512]{1,0:T(8,128)(2,1)S(1)}, bf16[96,512]{1,0:T(8,128)(2,1)S(1)}, u32[]{:S(2)}, u32[]{:S(2)}) collective-permute-start(bf16[96,512]{1,0:T(8,128)(2,1)S(1)} %get-tuple-element.53), channel_id=1, source_target_pairs={{0,1},{1,2},{2,3},{3,4},{4,5},{5,6},{6,7},{7,0},{8,9},{9,10},{10,1... | collective-permute-start | bytes 294920 | tf_op jit(solution)/shard_map/ppermute | solution.py:580
  45.9 5.1 %collective-permute-start.10 = (bf16[64,512]{1,0:T(8,128)(2,1)S(1)}, bf16[64,512]{1,0:T(8,128)(2,1)S(1)}, u32[]{:S(2)}, u32[]{:S(2)}) collective-permute-start(bf16[64,512]{1,0:T(8,128)(2,1)S(1)} %get-tuple-element.54), channel_id=1, source_target_pairs={{0,7},{1,0},{2,1},{3,2},{4,3},{5,4},{6,5},{7,6},{8,15},{9,8},{10,9... | collective-permute-start | bytes 196616 | tf_op jit(solution)/shard_map/ppermute | solution.py:581
  53.2 12.3 %collective-permute-start.15 = (bf16[32,2048]{1,0:T(8,128)(2,1)S(1)}, bf16[32,2048]{1,0:T(8,128)(2,1)S(1)}, u32[]{:S(2)}, u32[]{:S(2)}) collective-permute-start(bf16[32,2048]{1,0:T(8,128)(2,1)S(1)} %get-tuple-element.59), channel_id=1, source_target_pairs={{0,5},{1,6},{2,7},{3,0},{4,1},{5,2},{6,3},{7,4},{8,13},{9,14},{10,... | collective-permute-start | bytes 393224 | tf_op jit(solution)/shard_map/ppermute | solution.py:593
  55.3 10.2 %collective-permute-start.16 = (bf16[32,2048]{1,0:T(8,128)(2,1)S(1)}, bf16[32,2048]{1,0:T(8,128)(2,1)S(1)}, u32[]{:S(2)}, u32[]{:S(2)}) collective-permute-start(bf16[32,2048]{1,0:T(8,128)(2,1)S(1)} %get-tuple-element.60), channel_id=1, source_target_pairs={{0,2},{1,3},{2,4},{3,5},{4,6},{5,7},{6,0},{7,1},{8,10},{9,11},{10,... | collective-permute-start | bytes 393224 | tf_op jit(solution)/shard_map/ppermute | solution.py:594

commit v7 on v6

--- a/solution.py
+++ b/solution.py
@@ -48,6 +48,14 @@
 
 def around_z(step):
     return [(i, (i + step) % 8) for i in range(8)]
+
+
+def neighbours_by_core():
+    return [
+        (ctx * 8 + (z + (1 if ctx % CORES else -1)) % 8, ctx * 8 + z)
+        for ctx in range(CTX)
+        for z in range(8)
+    ]
 
 
 def mm(left, right):
@@ -222,19 +230,14 @@
     return each(lambda x, y: jnp.concatenate([x, y], axis=0), first, second)
 
 
-def pack_kernel(k_ref, v_ref, q_ref, weight_ref, out_ref, half_ref, sem):
-    core = lax.axis_index("ctx") % CORES
-    rows = weight_ref.shape[0] // CORES
-    copy = pltpu.make_async_copy(weight_ref.at[pl.ds(core * rows, rows)], half_ref, sem)
-    copy.start()
+def pack_kernel(k_ref, v_ref, q_ref, out_ref):
     out_ref[:, 0:256] = k_ref[...]
     out_ref[:, 256:768] = v_ref[...]
     out_ref[:, 768:1024] = q_ref[...]
-    copy.wait()
 
 
 def early_kernel(
-    k_ref, v_ref, decay_ref, beta_ref, doc_ref, wk_ref, wv_ref, edge_ref,
+    k_ref, v_ref, decay_ref, beta_ref, doc_ref, wk_ref, wv_ref,
     key_ref, value_ref, factor_ref, carry_ref, last_ref, start_ref, head_ref, mask_ref, ext_ref,
 ):
     row, col = rows_and_columns()
@@ -436,30 +439,21 @@
             ref[k * rows : (k + 1) * rows, :] = normed_ref[pl.ds(top, rows), :]
 
 
-def project_kernel(
-    keep_ref, left_ref, right_ref, own_ref, left_w_ref, left_w2_ref, right_w_ref, right_w2_ref,
-    *out_refs,
-):
+def project_kernel(keep_ref, left_ref, right_ref, own_ref, near_ref, far_ref, *out_refs):
     core = lax.axis_index("ctx") % CORES
     keep = keep_ref[...]
-
-    def halves(rows):
-        half = rows.shape[1] // 2
-        first, second = rows[:, :half], rows[:, half:]
-        return jnp.where(core == 0, first, second), jnp.where(core == 0, second, first)
-
-    left, left2 = halves(left_ref[...])
-    right, right2 = halves(right_ref[...])
+    left = left_ref[...]
+    right = right_ref[...]
+    none = jnp.zeros((left.shape[0] - right.shape[0], right.shape[1]), BF16)
+    right = jnp.concatenate([right, none], axis=0)
+    near = jnp.where(core == 0, left, right)
+    far = jnp.where(core == 0, right, left)
     rows = TOK // 8
     for part in range(0, own_ref.shape[1], 512):
         at = slice(part, part + 512)
-        total = mm(keep, own_ref[:, at]) + mm(left, left_w_ref[:, at]) + mm(left2, left_w2_ref[:, at])
-        more = mm(right, right_w_ref[:, at]) + mm(right2, right_w2_ref[:, at])
+        total = mm(keep, own_ref[:, at]) + mm(near, near_ref[:, at]) + mm(far, far_ref[:, at])
         for k, out_ref in enumerate(out_refs):
-            term = total[k * rows : (k + 1) * rows]
-            if k < len(TO_LEFT):
-                term = term + more[k * rows : (k + 1) * rows]
-            out_ref[:, at] = term.astype(out_ref.dtype)
+            out_ref[:, at] = total[k * rows : (k + 1) * rows].astype(out_ref.dtype)
 
 
 def sum_kernel(own_ref, one_ref, two_ref, out_ref):
@@ -504,22 +498,18 @@
     gain_row = norm_gain.reshape(1, DV)
     width = out_weight.shape[1]
     last = TOK // RIM - 1
-    edge, half = pl.pallas_call(
+    edge = pl.pallas_call(
         pack_kernel,
         grid=(1,),
-        out_shape=[
-            jax.ShapeDtypeStruct((RIM, 1024), BF16),
-            jax.ShapeDtypeStruct((out_weight.shape[0] // CORES, width), BF16),
-        ],
-        in_specs=[pl.BlockSpec((RIM, n), lambda i: (last, 0)) for n in (256, 512, 256)] + [HBM],
-        out_specs=[pl.BlockSpec((RIM, 1024), lambda i: (0, 0)), VMEM],
-        scratch_shapes=[pltpu.SemaphoreType.DMA],
-        compiler_params=pltpu.CompilerParams(vmem_limit_bytes=54 * MIB),
+        out_shape=jax.ShapeDtypeStruct((RIM, 1024), BF16),
+        in_specs=[pl.BlockSpec((RIM, n), lambda i: (last, 0)) for n in (256, 512, 256)],
+        out_specs=pl.BlockSpec((RIM, 1024), lambda i: (0, 0)),
         cost_estimate=pl.CostEstimate(flops=5_000_000_000, bytes_accessed=0, transcendentals=0),
-    )(key_in, value_in, query_in, out_weight)
-    left_half = lax.ppermute(half, "head", around_z(1))
-    right_half = lax.ppermute(half, "head", around_z(-1))
-    rim = lax.ppermute(edge, "ctx", [(i, i + 1) for i in range(CTX - 1)])
+    )(key_in, value_in, query_in)
+    near_weight = lax.ppermute(
+        lax.optimization_barrier((out_weight, edge))[0], ("ctx", "head"), neighbours_by_core()
+    )
+    rim = lax.ppermute(edge, "ctx", [(i, (i + 1) % CTX) for i in range(CTX)])
     wide = (2, DK, DK + DV)
     early = call(
         early_kernel,
@@ -528,7 +518,7 @@
             ((HEADS, TOK, 128), F32), ((HEADS, TOK), F32), ((RIM, 128), F32), ((RIM, 768), BF16),
             ((2 * len(LEVELS), TOK, TOK), BF16),
         ],
-        [key_in, value_in, log_decay, beta_gate, doc_row, conv_key, conv_value, edge],
+        [key_in, value_in, log_decay, beta_gate, doc_row, conv_key, conv_value],
         [
             pltpu.VMEM((8 + TOK, 512), F32),
         ],
@@ -563,9 +553,8 @@
         [pltpu.VMEM((CHIPS_Y,) + wide, BF16)], flops=60_000_000, moved=1_000_000,
     )
     got = lax.ppermute(to_other, "ctx", core_swap())
-    left_late, right_late, _ = lax.optimization_barrier((left_half, right_half, got))
-    left_half2 = lax.ppermute(left_late, "ctx", core_swap())
-    right_half2 = lax.ppermute(right_late, "ctx", core_swap())
+    late_weight, _ = lax.optimization_barrier((near_weight, got))
+    far_weight = lax.ppermute(late_weight, "ctx", core_swap())
     block = TOK // 8
 
     def normed_rows(steps):
@@ -582,7 +571,7 @@
     own_part, back_part, ahead_part = call(
         project_kernel, [((block, width), F32)] + [((block, width), BF16)] * 2,
         [
-            keep, from_left, from_right, out_weight, left_half, left_half2, right_half, right_half2
+            keep, from_left, from_right, out_weight, near_weight, far_weight
         ],
         flops=600_000_000, moved=6_000_000,
     )

time: 66.7 us -> 62 us (0.930)
  starting transfers between devices: 27.9 us -> 23.2 us
  waiting for transfers between devices: 24.6 us -> 27.2 us
  Pallas kernels: 12.7 us -> 11.2 us
    ppermute x3, starting transfers between devices: 7.49 us -> 3.35 us  [on_device(): far = [lax.ppermute(total, 'ctx', along_y(k)) for k in (1, 2, 3)]]
    ppermute x3, starting transfers between devices: 2.94 us -> 5.89 us  [on_device(): near = [lax.ppermute(pair, 'ctx', along_x(k)) for k in (1, 2, 3)]]
    ppermute x5 -> x3, starting transfers between devices: 8.44 us -> 5.57 us  [the longest x1 3.49 us: on_device(): rim = lax.ppermute(edge, 'ctx', [(i, (i + 1) % CTX) for i in range(CTX)])]
    ppermute x3, waiting for transfers between devices: 4.53 us -> 6.47 us  [on_device(): far = [lax.ppermute(total, 'ctx', along_y(k)) for k in (1, 2, 3)]]
    pallas_call x1, Pallas kernels: 2.99 us -> 1.49 us  [on_device(): pl.pallas_call(pack_kernel, grid=(1,), out_shape=jax.ShapeDtypeStruct((RI...]
    ppermute x3, waiting for transfers between devices: 6.53 us -> 7.48 us  [on_device(): near = [lax.ppermute(pair, 'ctx', along_x(k)) for k in (1, 2, 3)]]
  transfers between devices with their start and end apart: 17 -> 15, of which waited for: 11 -> 11; matrix products, arithmetic and copies ran while one was open for 0% -> 0% of each run, Pallas kernels for 12% -> 13%
where the time goes in v7:
time: 62 us; the launch traced here: 61.9 us
  waiting for transfers between devices  27.2 us (44%)
  starting transfers between devices  23.2 us (37%)
  Pallas kernels  11.2 us (18%)
    pallas_call x9, Pallas kernels, call(): pl.pallas_call(kernel, grid=(1,) if blocked else (), out_shape=[jax.Shape...  9.69 us
    ppermute x3, waiting for transfers between devices, on_device(): near = [lax.ppermute(pair, 'ctx', along_x(k)) for k in (1, 2, 3)]  7.48 us
    ppermute x1, waiting for transfers between devices, on_device(): lax.ppermute(back_part, 'head', around_z(-3))  6.89 us
    ppermute x3, waiting for transfers between devices, on_device(): far = [lax.ppermute(total, 'ctx', along_y(k)) for k in (1, 2, 3)]  6.47 us
    ppermute x3, starting transfers between devices, on_device(): near = [lax.ppermute(pair, 'ctx', along_x(k)) for k in (1, 2, 3)]  5.89 us
    ppermute x1, starting transfers between devices, on_device(): rim = lax.ppermute(edge, 'ctx', [(i, (i + 1) % CTX) for i in range(CTX)])  3.49 us
    ppermute x3, starting transfers between devices, on_device(): far = [lax.ppermute(total, 'ctx', along_y(k)) for k in (1, 2, 3)]  3.35 us
    ppermute x1, starting transfers between devices, on_device(): lax.ppermute(ahead_part, 'head', around_z(2))  3.23 us
  transfers between devices with their start and end apart: 15, of which 11 were waited for; matrix products, arithmetic and copies ran while one was open for 0% of the time, Pallas kernels for 13%

profile of v7, /device:TPU:6, one launch (start us, length us, event | category | flops | bytes accessed | tf_op | source)
XLA Modules:
  0.0 61.9 jit_solution(2159349507537186892)
XLA Ops:
  0.0 0.0 copy-start.4
  0.0 0.0 copy-start.3
  0.0 0.0 copy-start
  0.0 0.0 copy-start.9
  0.0 0.0 copy-start.11
  0.0 0.0 copy-start.7
  0.0 0.0 copy-start.8
  0.0 0.0 copy-start.6
  0.1 1.5 %shard_map.118 = bf16[16,1024]{1,0:T(8,128)(2,1)} custom-call(bf16[256,256]{1,0:T(8,128)(2,1)} %k_ref.3, bf16[256,512]{1,0:T(8,128)(2,1)} %v_ref.3, bf16[256,256]{1,0:T(8,128)(2,1)} %q_ref.3), custom_call_target="tpu_custom_call" | custom-call | flops 5000000000 | tf_op jit(solution)/shard_map/pallas_call | solution.py:501
  1.5 0.1 copy-done
  1.7 1.9 %collective-permute-start.11 = (bf16[512,2048]{1,0:T(8,128)(2,1)S(1)}, bf16[512,2048]{1,0:T(8,128)(2,1)S(1)}, u32[]{:S(2)}, u32[]{:S(2)}) collective-permute-start(bf16[512,2048]{1,0:T(8,128)(2,1)S(1)} %copy-done), channel_id=1, source_target_pairs={{7,0},{0,1},{1,2},{2,3},{3,4},{4,5},{5,6},{6,7},{9,8},{10,9},{11,1... | collective-permute-start | bytes 6291464 | tf_op jit(solution)/shard_map/ppermute | solution.py:509
  3.6 3.5 %collective-permute-start = (bf16[16,1024]{1,0:T(8,128)(2,1)}, bf16[16,1024]{1,0:T(8,128)(2,1)S(1)}, u32[]{:S(2)}, u32[]{:S(2)}) collective-permute-start(bf16[16,1024]{1,0:T(8,128)(2,1)} %shard_map.118), channel_id=1, source_target_pairs={{0,8},{8,16},{16,24},{24,32},{32,40},{40,48},{48,56},{56,64},{64,7... | collective-permute-start | bytes 98312 | tf_op jit(solution)/shard_map/ppermute | solution.py:512
  7.1 0.0 copy-done.4
  7.1 0.0 copy-done.3
  7.1 0.0 copy-done.9
  7.1 0.0 copy-done.11
  7.1 0.0 copy-done.7
  7.1 0.0 copy-done.8
  7.1 0.0 copy-done.6
  7.1 1.5 %shard_map.119 = (bf16[2,256,128]{2,1,0:T(8,128)(2,1)S(1)}, bf16[256,512]{1,0:T(8,128)(2,1)S(1)}, f32[4,256,256]{2,1,0:T(8,128)S(1)}, f32[4,256,128]{2,1,0:T(8,1...) custom-call(bf16[256,256]{1,0:T(8,128)(2,1)S(1)} %copy-done.4, ...), custom_call_target="tpu_custom_call" | custom-call | flops 500000000 | tf_op jit(solution)/shard_map/pallas_call | solution.py:481
  8.6 0.7 %collective-permute-done.rim_ref = bf16[16,1024]{1,0:T(8,128)(2,1)S(1)} collective-permute-done((bf16[16,1024]{1,0:T(8,128)(2,1)}, bf16[16,1024]{1,0:T(8,128)(2,1)S(1)}, u32[]{:S(2)}, u32[]{:S(2)}) %collective-permute-start) | collective-permute-done | bytes 32800 | tf_op jit(solution)/shard_map/ppermute | solution.py:512
  9.3 0.0 copy-start.5
  9.3 0.0 copy-start.10
  9.3 3.4 %shard_map.120 = (bf16[4,256,256]{2,1,0:T(8,128)(2,1)S(1)}, bf16[2,256,128]{2,1,0:T(8,128)(2,1)S(1)}, bf16[2,128,256]{2,1,0:T(8,128)(2,1)S(1)}, bf16[2,128,256]{2,1,0:T(8,128)(2,1)S(1)}) custom-call(bf16[16,1024]{1,0:T(8,128)(2,1)S(1)} %collective-permute-done.rim_ref, bf16[16,768]{1,0:T(8,128)(2,1)S(1)} %get-tuple-element.31.head_ref, ...), custom_call_target="tpu_custom_call" | custom-call | flops 4000000000 | bytes 2000000 | tf_op jit(solution)/shard_map/pallas_call | solution.py:481
  12.7 0.1 collective-permute-start.1
  12.8 1.3 %collective-permute-done.1.got_ref.other_ref = bf16[2,128,256]{2,1,0:T(8,128)(2,1)S(1)} collective-permute-done((bf16[2,128,256]{2,1,0:T(8,128)(2,1)S(1)}, bf16[2,128,256]{2,1,0:T(8,128)(2,1)S(1)}, u32[]{:S(2)}, u32[]{:S(2)}) %collective-permute-start.1) | collective-permute-done | bytes 131104 | tf_op jit(solution)/shard_map/ppermute | solution.py:534
  14.1 0.2 shard_map.122.own_ref
  14.3 4.9 %collective-permute-start.2 = (bf16[2,128,256]{2,1,0:T(8,128)(2,1)S(1)}, bf16[2,128,256]{2,1,0:T(8,128)(2,1)S(1)}, u32[]{:S(2)}, u32[]{:S(2)}) collective-permute-start(bf16[2,128,256]{2,1,0:T(8,128)(2,1)S(1)} %shard_map.122.own_ref), channel_id=1, source_target_pairs={{0,16},{8,24},{16,32},{24,40},{32,48},{40,56},{48,0},{56,8},{64,80... | collective-permute-start | bytes 393224 | tf_op jit(solution)/shard_map/ppermute | solution.py:536
  19.2 0.0 collective-permute-start.3
  19.2 1.0 %collective-permute-start.4 = (bf16[2,128,256]{2,1,0:T(8,128)(2,1)S(1)}, bf16[2,128,256]{2,1,0:T(8,128)(2,1)S(1)}, u32[]{:S(2)}, u32[]{:S(2)}) collective-permute-start(bf16[2,128,256]{2,1,0:T(8,128)(2,1)S(1)} %shard_map.122.own_ref), channel_id=1, source_target_pairs={{0,48},{8,56},{16,0},{24,8},{32,16},{40,24},{48,32},{56,40},{64,11... | collective-permute-start | bytes 393224 | tf_op jit(solution)/shard_map/ppermute | solution.py:536
  20.2 0.0 copy-done.5
  20.2 0.0 copy-done.10
  20.2 0.0 copy-start.1
  20.2 0.0 copy-start.2
  20.2 0.8 %shard_map.121 = (f32[4,256,128]{2,1,0:T(8,128)S(1)}, bf16[4,256,128]{2,1,0:T(8,128)(2,1)S(1)}) custom-call(bf16[256,256]{1,0:T(8,128)(2,1)S(1)} %copy-done.5, bf16[16,1024]{1,0:T(8,128)(2,1)S(1)} %collective-permute-done.rim_ref, f32[4,256]{1,0:T(4,128)S(1)} %copy-done.9, s32[1,256]{1,0:T(1,128)S(1)} %bitcast.4, f32[4,256]{1,0:T(4,128)S(1)} %copy-done.10, ...), custom_call_target="tpu_custom_call" | custom-call | flops 2000000000 | bytes 2000000 | tf_op jit(solution)/shard_map/pallas_call | solution.py:481
  21.1 4.1 %collective-permute-done.2.one_ref = bf16[2,128,256]{2,1,0:T(8,128)(2,1)S(1)} collective-permute-done((bf16[2,128,256]{2,1,0:T(8,128)(2,1)S(1)}, bf16[2,128,256]{2,1,0:T(8,128)(2,1)S(1)}, u32[]{:S(2)}, u32[]{:S(2)}) %collective-permute-start.2) | collective-permute-done | bytes 131104 | tf_op jit(solution)/shard_map/ppermute | solution.py:536
  25.1 2.0 %collective-permute-done.3.two_ref = bf16[2,128,256]{2,1,0:T(8,128)(2,1)S(1)} collective-permute-done((bf16[2,128,256]{2,1,0:T(8,128)(2,1)S(1)}, bf16[2,128,256]{2,1,0:T(8,128)(2,1)S(1)}, u32[]{:S(2)}, u32[]{:S(2)}) %collective-permute-start.3) | collective-permute-done | bytes 131104 | tf_op jit(solution)/shard_map/ppermute | solution.py:536
  27.1 1.4 %collective-permute-done.4.three_ref = bf16[2,128,256]{2,1,0:T(8,128)(2,1)S(1)} collective-permute-done((bf16[2,128,256]{2,1,0:T(8,128)(2,1)S(1)}, bf16[2,128,256]{2,1,0:T(8,128)(2,1)S(1)}, u32[]{:S(2)}, u32[]{:S(2)}) %collective-permute-start.4) | collective-permute-done | bytes 131104 | tf_op jit(solution)/shard_map/ppermute | solution.py:536
  28.5 0.7 %shard_map.123 = (bf16[2,128,256]{2,1,0:T(8,128)(2,1)S(1)}, bf16[2,128,256]{2,1,0:T(8,128)(2,1)S(1)}) custom-call(bf16[2,128,256]{2,1,0:T(8,128)(2,1)S(1)} %shard_map.122.own_ref, bf16[2,128,256]{2,1,0:T(8,128)(2,1)S(1)} %collective-permute-done.2.one_ref, bf16[2,128,256]{2,1,0:T(8,128)(2,1)S(1)} %collective-permute-done.3.two_ref, ...), custom_call_target="tpu_custom_call" | custom-call | flops 60000000 | bytes 800000 | tf_op jit(solution)/shard_map/pallas_call | solution.py:481
  29.2 0.1 collective-permute-start.5
  29.3 2.2 %collective-permute-start.6 = (bf16[2,128,256]{2,1,0:T(8,128)(2,1)S(1)}, bf16[2,128,256]{2,1,0:T(8,128)(2,1)S(1)}, u32[]{:S(2)}, u32[]{:S(2)}) collective-permute-start(bf16[2,128,256]{2,1,0:T(8,128)(2,1)S(1)} %get-tuple-element.45.own_ref), channel_id=1, source_target_pairs={{0,128},{8,136},{16,144},{24,152},{32,160},{40,168},{48,176},{56,1... | collective-permute-start | bytes 393224 | tf_op jit(solution)/shard_map/ppermute | solution.py:549
  31.5 1.1 %collective-permute-start.7 = (bf16[2,128,256]{2,1,0:T(8,128)(2,1)S(1)}, bf16[2,128,256]{2,1,0:T(8,128)(2,1)S(1)}, u32[]{:S(2)}, u32[]{:S(2)}) collective-permute-start(bf16[2,128,256]{2,1,0:T(8,128)(2,1)S(1)} %get-tuple-element.45.own_ref), channel_id=1, source_target_pairs={{0,192},{8,200},{16,208},{24,216},{32,224},{40,232},{48,240},{56,2... | collective-permute-start | bytes 393224 | tf_op jit(solution)/shard_map/ppermute | solution.py:549
  32.6 5.9 %collective-permute-done.5.one_ref = bf16[2,128,256]{2,1,0:T(8,128)(2,1)S(1)} collective-permute-done((bf16[2,128,256]{2,1,0:T(8,128)(2,1)S(1)}, bf16[2,128,256]{2,1,0:T(8,128)(2,1)S(1)}, u32[]{:S(2)}, u32[]{:S(2)}) %collective-permute-start.5) | collective-permute-done | bytes 131104 | tf_op jit(solution)/shard_map/ppermute | solution.py:549
  38.5 0.0 collective-permute-done.6.two_ref
  38.5 0.6 collective-permute-done.7.three_ref
  39.1 0.9 %shard_map.124 = (bf16[2,128,128]{2,1,0:T(8,128)(2,1)S(1)}, bf16[2,128,128]{2,1,0:T(8,128)(2,1)S(1)}) custom-call(bf16[2,128,256]{2,1,0:T(8,128)(2,1)S(1)} %get-tuple-element.45.own_ref, bf16[2,128,256]{2,1,0:T(8,128)(2,1)S(1)} %collective-permute-done.5.one_ref, bf16[2,128,256]{2,1,0:T(8,128)(2,1)S(1)} %collective-permute-done.6.two_ref, ...), custom_call_target="tpu_custom_call" | custom-call | flops 60000000 | bytes 1000000 | tf_op jit(solution)/shard_map/pallas_call | solution.py:481
  40.0 0.1 collective-permute-start.8
  40.1 1.2 %collective-permute-done.8.got_ref = bf16[2,128,128]{2,1,0:T(8,128)(2,1)S(1)} collective-permute-done((bf16[2,128,128]{2,1,0:T(8,128)(2,1)S(1)}, bf16[2,128,128]{2,1,0:T(8,128)(2,1)S(1)}, u32[]{:S(2)}, u32[]{:S(2)}) %collective-permute-start.8) | collective-permute-done | bytes 65568 | tf_op jit(solution)/shard_map/ppermute | solution.py:555
  41.3 0.0 collective-permute-done.11.near_ref
  41.3 0.2 collective-permute-start.12
  41.5 0.0 copy-done.1
  41.5 0.0 copy-done.2
  41.5 0.4 shard_map.125
  41.9 0.1 collective-permute-start.9
  42.0 3.2 %collective-permute-start.10 = (bf16[64,512]{1,0:T(8,128)(2,1)S(1)}, bf16[64,512]{1,0:T(8,128)(2,1)S(1)}, u32[]{:S(2)}, u32[]{:S(2)}) collective-permute-start(bf16[64,512]{1,0:T(8,128)(2,1)S(1)} %get-tuple-element.51), channel_id=1, source_target_pairs={{0,7},{1,0},{2,1},{3,2},{4,3},{5,4},{6,5},{7,6},{8,15},{9,8},{10,9... | collective-permute-start | bytes 196616 | tf_op jit(solution)/shard_map/ppermute | solution.py:570
  45.2 1.9 %collective-permute-done.10.right_ref = bf16[64,512]{1,0:T(8,128)(2,1)S(1)} collective-permute-done((bf16[64,512]{1,0:T(8,128)(2,1)S(1)}, bf16[64,512]{1,0:T(8,128)(2,1)S(1)}, u32[]{:S(2)}, u32[]{:S(2)}) %collective-permute-start.10) | collective-permute-done | bytes 65568 | tf_op jit(solution)/shard_map/ppermute | solution.py:570
  47.1 1.1 %collective-permute-done.9.left_ref = bf16[96,512]{1,0:T(8,128)(2,1)S(1)} collective-permute-done((bf16[96,512]{1,0:T(8,128)(2,1)S(1)}, bf16[96,512]{1,0:T(8,128)(2,1)S(1)}, u32[]{:S(2)}, u32[]{:S(2)}) %collective-permute-start.9) | collective-permute-done | bytes 98336 | tf_op jit(solution)/shard_map/ppermute | solution.py:569
  48.3 0.0 collective-permute-done.12.far_ref
  48.3 1.1 %shard_map.126 = (f32[32,2048]{1,0:T(8,128)S(1)}, bf16[32,2048]{1,0:T(8,128)(2,1)S(1)}, bf16[32,2048]{1,0:T(8,128)(2,1)S(1)}) custom-call(bf16[96,512]{1,0:T(8,128)(2,1)S(1)} %get-tuple-element.49.keep_ref, bf16[96,512]{1,0:T(8,128)(2,1)S(1)} %collective-permute-done.9.left_ref, bf16[64,512]{1,0:T(8,128)(2,1)S(1)} %collective-permute-done.10.right_ref, ...), custom_call_target="tpu_custom_call" | custom-call | flops 600000000 | bytes 6000000 | tf_op jit(solution)/shard_map/pallas_call | solution.py:481
  49.4 1.7 %collective-permute-start.13 = (bf16[32,2048]{1,0:T(8,128)(2,1)S(1)}, bf16[32,2048]{1,0:T(8,128)(2,1)S(1)}, u32[]{:S(2)}, u32[]{:S(2)}) collective-permute-start(bf16[32,2048]{1,0:T(8,128)(2,1)S(1)} %get-tuple-element.55), channel_id=1, source_target_pairs={{0,5},{1,6},{2,7},{3,0},{4,1},{5,2},{6,3},{7,4},{8,13},{9,14},{10,... | collective-permute-start | bytes 393224 | tf_op jit(solution)/shard_map/ppermute | solution.py:582
  51.1 3.2 %collective-permute-start.14 = (bf16[32,2048]{1,0:T(8,128)(2,1)S(1)}, bf16[32,2048]{1,0:T(8,128)(2,1)S(1)}, u32[]{:S(2)}, u32[]{:S(2)}) collective-permute-start(bf16[32,2048]{1,0:T(8,128)(2,1)S(1)} %get-tuple-element.56), channel_id=1, source_target_pairs={{0,2},{1,3},{2,4},{3,5},{4,6},{5,7},{6,0},{7,1},{8,10},{9,11},{10,... | collective-permute-start | bytes 393224 | tf_op jit(solution)/shard_map/ppermute | solution.py:583
  54.3 6.9 %collective-permute-done.13.one_ref = bf16[32,2048]{1,0:T(8,128)(2,1)S(1)} collective-permute-done((bf16[32,2048]{1,0:T(8,128)(2,1)S(1)}, bf16[32,2048]{1,0:T(8,128)(2,1)S(1)}, u32[]{:S(2)}, u32[]{:S(2)}) %collective-permute-start.13) | collective-permute-done | bytes 131104 | tf_op jit(solution)/shard_map/ppermute | solution.py:582
  61.2 0.0 collective-permute-done.14.two_ref
  61.2 0.7 %shard_map.127 = bf16[32,2048]{1,0:T(8,128)(2,1)} custom-call(f32[32,2048]{1,0:T(8,128)S(1)} %get-tuple-element.54.own_ref, bf16[32,2048]{1,0:T(8,128)(2,1)S(1)} %collective-permute-done.13.one_ref, bf16[32,2048]{1,0:T(8,128)(2,1)S(1)} %collective-permute-done.14.two_ref), custom_call_target="tpu_custom_call" | custom-call | flops 1000000 | bytes 800000 | tf_op jit(solution)/shard_map/pallas_call | solution.py:481
Async XLA Ops:
  0.0 7.1 %copy-start.4 = (bf16[256,256]{1,0:T(8,128)(2,1)S(1)}, bf16[256,256]{1,0:T(8,128)(2,1)}, u32[]{:S(2)}) copy-start(bf16[256,256]{1,0:T(8,128)(2,1)} %k_ref.3) | copy-start | bytes 393220
  0.0 7.1 %copy-start.3 = (bf16[256,512]{1,0:T(8,128)(2,1)S(1)}, bf16[256,512]{1,0:T(8,128)(2,1)}, u32[]{:S(2)}) copy-start(bf16[256,512]{1,0:T(8,128)(2,1)} %v_ref.3) | copy-start | bytes 786436
  0.0 1.7 %copy-start = (bf16[512,2048]{1,0:T(8,128)(2,1)S(1)}, bf16[512,2048]{1,0:T(8,128)(2,1)}, u32[]{:S(2)}) copy-start(bf16[512,2048]{1,0:T(8,128)(2,1)} %own_ref.1) | copy-start | bytes 6291460
  0.0 7.1 %copy-start.9 = (f32[4,256]{1,0:T(4,128)S(1)}, f32[4,256]{1,0:T(4,128)}, u32[]{:S(2)}) copy-start(f32[4,256]{1,0:T(4,128)} %decay_ref.3) | copy-start | bytes 12292
  0.0 7.1 %copy-start.11 = (s32[256]{0:T(256)S(1)}, s32[256]{0:T(256)}, u32[]{:S(2)}) copy-start(s32[256]{0:T(256)} %param.18) | copy-start | bytes 3076
  0.0 7.1 %copy-start.7 = (f32[4,256]{1,0:T(4,128)S(1)}, f32[4,256]{1,0:T(4,128)}, u32[]{:S(2)}) copy-start(f32[4,256]{1,0:T(4,128)} %beta_ref.3) | copy-start | bytes 12292
  0.0 7.1 %copy-start.8 = (f32[4,256]{1,0:T(4,128)S(1)}, f32[4,256]{1,0:T(4,128)}, u32[]{:S(2)}) copy-start(f32[4,256]{1,0:T(4,128)} %wk_ref.3) | copy-start | bytes 12292
  0.0 7.1 %copy-start.6 = (f32[4,512]{1,0:T(4,128)S(1)}, f32[4,512]{1,0:T(4,128)}, u32[]{:S(2)}) copy-start(f32[4,512]{1,0:T(4,128)} %wv_ref.3) | copy-start | bytes 24580
  1.7 39.7 %collective-permute-start.11 = (bf16[512,2048]{1,0:T(8,128)(2,1)S(1)}, bf16[512,2048]{1,0:T(8,128)(2,1)S(1)}, u32[]{:S(2)}, u32[]{:S(2)}) collective-permute-start(bf16[512,2048]{1,0:T(8,128)(2,1)S(1)} %copy-done), channel_id=1, source_target_pairs={{7,0},{0,1},{1,2},{2,3},{3,4},{4,5},{5,6},{6,7},{9,8},{10,9},{11,1... | collective-permute-start | bytes 6291464 | tf_op jit(solution)/shard_map/ppermute | solution.py:509
  3.6 5.7 %collective-permute-start = (bf16[16,1024]{1,0:T(8,128)(2,1)}, bf16[16,1024]{1,0:T(8,128)(2,1)S(1)}, u32[]{:S(2)}, u32[]{:S(2)}) collective-permute-start(bf16[16,1024]{1,0:T(8,128)(2,1)} %shard_map.118), channel_id=1, source_target_pairs={{0,8},{8,16},{16,24},{24,32},{32,40},{40,48},{48,56},{56,64},{64,7... | collective-permute-start | bytes 98312 | tf_op jit(solution)/shard_map/ppermute | solution.py:512
  9.3 10.9 %copy-start.5 = (bf16[256,256]{1,0:T(8,128)(2,1)S(1)}, bf16[256,256]{1,0:T(8,128)(2,1)}, u32[]{:S(2)}) copy-start(bf16[256,256]{1,0:T(8,128)(2,1)} %q_ref.3) | copy-start | bytes 393220
  9.3 10.9 %copy-start.10 = (f32[4,256]{1,0:T(4,128)S(1)}, f32[4,256]{1,0:T(4,128)}, u32[]{:S(2)}) copy-start(f32[4,256]{1,0:T(4,128)} %wq_ref.1) | copy-start | bytes 12292
  12.7 1.4 %collective-permute-start.1 = (bf16[2,128,256]{2,1,0:T(8,128)(2,1)S(1)}, bf16[2,128,256]{2,1,0:T(8,128)(2,1)S(1)}, u32[]{:S(2)}, u32[]{:S(2)}) collective-permute-start(bf16[2,128,256]{2,1,0:T(8,128)(2,1)S(1)} %get-tuple-element.44), channel_id=1, source_target_pairs={{0,8},{8,0},{16,24},{24,16},{32,40},{40,32},{48,56},{56,48},{64,72... | collective-permute-start | bytes 393224 | tf_op jit(solution)/shard_map/ppermute | solution.py:534
  14.3 10.8 %collective-permute-start.2 = (bf16[2,128,256]{2,1,0:T(8,128)(2,1)S(1)}, bf16[2,128,256]{2,1,0:T(8,128)(2,1)S(1)}, u32[]{:S(2)}, u32[]{:S(2)}) collective-permute-start(bf16[2,128,256]{2,1,0:T(8,128)(2,1)S(1)} %shard_map.122.own_ref), channel_id=1, source_target_pairs={{0,16},{8,24},{16,32},{24,40},{32,48},{40,56},{48,0},{56,8},{64,80... | collective-permute-start | bytes 393224 | tf_op jit(solution)/shard_map/ppermute | solution.py:536
  19.2 7.9 %collective-permute-start.3 = (bf16[2,128,256]{2,1,0:T(8,128)(2,1)S(1)}, bf16[2,128,256]{2,1,0:T(8,128)(2,1)S(1)}, u32[]{:S(2)}, u32[]{:S(2)}) collective-permute-start(bf16[2,128,256]{2,1,0:T(8,128)(2,1)S(1)} %shard_map.122.own_ref), channel_id=1, source_target_pairs={{0,32},{8,40},{16,48},{24,56},{32,0},{40,8},{48,16},{56,24},{64,96... | collective-permute-start | bytes 393224 | tf_op jit(solution)/shard_map/ppermute | solution.py:536
  19.2 9.3 %collective-permute-start.4 = (bf16[2,128,256]{2,1,0:T(8,128)(2,1)S(1)}, bf16[2,128,256]{2,1,0:T(8,128)(2,1)S(1)}, u32[]{:S(2)}, u32[]{:S(2)}) collective-permute-start(bf16[2,128,256]{2,1,0:T(8,128)(2,1)S(1)} %shard_map.122.own_ref), channel_id=1, source_target_pairs={{0,48},{8,56},{16,0},{24,8},{32,16},{40,24},{48,32},{56,40},{64,11... | collective-permute-start | bytes 393224 | tf_op jit(solution)/shard_map/ppermute | solution.py:536
  20.2 21.3 %copy-start.1 = (bf16[256,512]{1,0:T(8,128)(2,1)S(1)}, bf16[256,512]{1,0:T(8,128)(2,1)}, u32[]{:S(2)}) copy-start(bf16[256,512]{1,0:T(8,128)(2,1)} %gate_ref.1) | copy-start | bytes 786436
  20.2 21.3 %copy-start.2 = (f32[128]{0:T(128)S(1)}, f32[128]{0:T(128)}, u32[]{:S(2)}) copy-start(f32[128]{0:T(128)} %param.22) | copy-start | bytes 1540
  29.2 9.2 %collective-permute-start.5 = (bf16[2,128,256]{2,1,0:T(8,128)(2,1)S(1)}, bf16[2,128,256]{2,1,0:T(8,128)(2,1)S(1)}, u32[]{:S(2)}, u32[]{:S(2)}) collective-permute-start(bf16[2,128,256]{2,1,0:T(8,128)(2,1)S(1)} %get-tuple-element.45.own_ref), channel_id=1, source_target_pairs={{0,64},{8,72},{16,80},{24,88},{32,96},{40,104},{48,112},{56,120},{... | collective-permute-start | bytes 393224 | tf_op jit(solution)/shard_map/ppermute | solution.py:549
  29.3 9.1 %collective-permute-start.6 = (bf16[2,128,256]{2,1,0:T(8,128)(2,1)S(1)}, bf16[2,128,256]{2,1,0:T(8,128)(2,1)S(1)}, u32[]{:S(2)}, u32[]{:S(2)}) collective-permute-start(bf16[2,128,256]{2,1,0:T(8,128)(2,1)S(1)} %get-tuple-element.45.own_ref), channel_id=1, source_target_pairs={{0,128},{8,136},{16,144},{24,152},{32,160},{40,168},{48,176},{56,1... | collective-permute-start | bytes 393224 | tf_op jit(solution)/shard_map/ppermute | solution.py:549
  31.5 7.6 %collective-permute-start.7 = (bf16[2,128,256]{2,1,0:T(8,128)(2,1)S(1)}, bf16[2,128,256]{2,1,0:T(8,128)(2,1)S(1)}, u32[]{:S(2)}, u32[]{:S(2)}) collective-permute-start(bf16[2,128,256]{2,1,0:T(8,128)(2,1)S(1)} %get-tuple-element.45.own_ref), channel_id=1, source_target_pairs={{0,192},{8,200},{16,208},{24,216},{32,224},{40,232},{48,240},{56,2... | collective-permute-start | bytes 393224 | tf_op jit(solution)/shard_map/ppermute | solution.py:549
  40.0 1.3 %collective-permute-start.8 = (bf16[2,128,128]{2,1,0:T(8,128)(2,1)S(1)}, bf16[2,128,128]{2,1,0:T(8,128)(2,1)S(1)}, u32[]{:S(2)}, u32[]{:S(2)}) collective-permute-start(bf16[2,128,128]{2,1,0:T(8,128)(2,1)S(1)} %get-tuple-element.48), channel_id=1, source_target_pairs={{0,8},{8,0},{16,24},{24,16},{32,40},{40,32},{48,56},{56,48},{64,72... | collective-permute-start | bytes 196616 | tf_op jit(solution)/shard_map/ppermute | solution.py:555
  41.3 6.9 %collective-permute-start.12 = (bf16[512,2048]{1,0:T(8,128)(2,1)S(1)}, bf16[512,2048]{1,0:T(8,128)(2,1)S(1)}, u32[]{:S(2)}, u32[]{:S(2)}) collective-permute-start(bf16[512,2048]{1,0:T(8,128)(2,1)S(1)} %collective-permute-done.11.near_ref), channel_id=1, source_target_pairs={{0,8},{8,0},{16,24},{24,16},{32,40},{40,32},{48,56},{56,48},{64,72... | collective-permute-start | bytes 6291464 | tf_op jit(solution)/shard_map/ppermute | solution.py:557
  41.9 6.3 %collective-permute-start.9 = (bf16[96,512]{1,0:T(8,128)(2,1)S(1)}, bf16[96,512]{1,0:T(8,128)(2,1)S(1)}, u32[]{:S(2)}, u32[]{:S(2)}) collective-permute-start(bf16[96,512]{1,0:T(8,128)(2,1)S(1)} %get-tuple-element.50), channel_id=1, source_target_pairs={{0,1},{1,2},{2,3},{3,4},{4,5},{5,6},{6,7},{7,0},{8,9},{9,10},{10,1... | collective-permute-start | bytes 294920 | tf_op jit(solution)/shard_map/ppermute | solution.py:569
  42.0 5.1 %collective-permute-start.10 = (bf16[64,512]{1,0:T(8,128)(2,1)S(1)}, bf16[64,512]{1,0:T(8,128)(2,1)S(1)}, u32[]{:S(2)}, u32[]{:S(2)}) collective-permute-start(bf16[64,512]{1,0:T(8,128)(2,1)S(1)} %get-tuple-element.51), channel_id=1, source_target_pairs={{0,7},{1,0},{2,1},{3,2},{4,3},{5,4},{6,5},{7,6},{8,15},{9,8},{10,9... | collective-permute-start | bytes 196616 | tf_op jit(solution)/shard_map/ppermute | solution.py:570
  49.4 11.8 %collective-permute-start.13 = (bf16[32,2048]{1,0:T(8,128)(2,1)S(1)}, bf16[32,2048]{1,0:T(8,128)(2,1)S(1)}, u32[]{:S(2)}, u32[]{:S(2)}) collective-permute-start(bf16[32,2048]{1,0:T(8,128)(2,1)S(1)} %get-tuple-element.55), channel_id=1, source_target_pairs={{0,5},{1,6},{2,7},{3,0},{4,1},{5,2},{6,3},{7,4},{8,13},{9,14},{10,... | collective-permute-start | bytes 393224 | tf_op jit(solution)/shard_map/ppermute | solution.py:582
  51.1 10.1 %collective-permute-start.14 = (bf16[32,2048]{1,0:T(8,128)(2,1)S(1)}, bf16[32,2048]{1,0:T(8,128)(2,1)S(1)}, u32[]{:S(2)}, u32[]{:S(2)}) collective-permute-start(bf16[32,2048]{1,0:T(8,128)(2,1)S(1)} %get-tuple-element.56), channel_id=1, source_target_pairs={{0,2},{1,3},{2,4},{3,5},{4,6},{5,7},{6,0},{7,1},{8,10},{9,11},{10,... | collective-permute-start | bytes 393224 | tf_op jit(solution)/shard_map/ppermute | solution.py:583

commit v8 on v7

--- a/solution.py
+++ b/solution.py
@@ -43,18 +43,6 @@
         for y in range(4)
         for x in range(4)
         for c in range(2)
-    ]
-
-
-def around_z(step):
-    return [(i, (i + step) % 8) for i in range(8)]
-
-
-def neighbours_by_core():
-    return [
-        (ctx * 8 + (z + (1 if ctx % CORES else -1)) % 8, ctx * 8 + z)
-        for ctx in range(CTX)
-        for z in range(8)
     ]
 
 
@@ -383,14 +371,15 @@
         slots[(x + CHIPS_X - step) % CHIPS_X] = ref[...]
     r, c = rows_and_columns((DK, DK + DV))
     start = (r == c).astype(BF16)
+    run = [slots[0, k] for k in range(2)]
+    before = [jnp.where(x == 0, start, first) for first in run]
+    for place in range(1, CHIPS_X):
+        run = [joined(run[k], slots[place, k]).astype(BF16) for k in range(2)]
+        if place < CHIPS_X - 1:
+            before = [jnp.where(x == place + 1, run[k], before[k]) for k in range(2)]
     for k in range(2):
-        run = slots[0, k]
-        before_ref[k] = jnp.where(x == 0, start, run)
-        for place in range(1, CHIPS_X):
-            run = joined(run, slots[place, k]).astype(BF16)
-            if place < CHIPS_X - 1:
-                before_ref[k] = jnp.where(x == place + 1, run, before_ref[k])
-        total_ref[k] = run
+        total_ref[k] = run[k]
+        before_ref[k] = before[k]
 
 
 def state_kernel(
@@ -401,27 +390,37 @@
     y = index // (CORES * CHIPS_X)
     for step, ref in enumerate((own_ref, one_ref, two_ref, three_ref)):
         slots[(y + CHIPS_Y - step) % CHIPS_Y] = ref[...]
+
+    def passed(block, state):
+        return mm(block[:, :DK], state.astype(BF16)) + block[:, DK:].astype(F32)
+
+    states = [jnp.where(y > 0, slots[0, k][:, DK:].astype(F32), 0.0) for k in range(2)]
+    for place in range(1, CHIPS_Y - 1):
+        moved = [passed(slots[place, k], states[k]) for k in range(2)]
+        states = [jnp.where(place < y, moved[k], states[k]) for k in range(2)]
+    states = [passed(before_ref[k], states[k]) for k in range(2)]
+    blocks = [jnp.where(core == 0, mine_ref[k], other_ref[k]) for k in range(2)]
+    after = [passed(blocks[k], states[k]) for k in range(2)]
     for k in range(2):
-        state = jnp.where(y > 0, slots[0, k][:, DK:].astype(F32), 0.0)
-        for place in range(1, CHIPS_Y - 1):
-            block = slots[place, k]
-            moved = mm(block[:, :DK], state.astype(BF16)) + block[:, DK:].astype(F32)
-            state = jnp.where(place < y, moved, state)
-        block = before_ref[k]
-        state = mm(block[:, :DK], state.astype(BF16)) + block[:, DK:].astype(F32)
-        block = jnp.where(core == 0, mine_ref[k], other_ref[k])
-        after = mm(block[:, :DK], state.astype(BF16)) + block[:, DK:].astype(F32)
-        keep_ref[k] = jnp.where(core == 0, state, after).astype(BF16)
-        give_ref[k] = jnp.where(core == 0, after, state).astype(BF16)
+        keep_ref[k] = jnp.where(core == 0, states[k], after[k]).astype(BF16)
+        give_ref[k] = jnp.where(core == 0, after[k], states[k]).astype(BF16)
 
 
 KEPT = (0, -3, 2)
-TO_RIGHT = (1, -2, 3)
-TO_LEFT = (-1, -4)
+TO_AHEAD = (1, -2, 3)
+TO_BEHIND = (-1, -4)
+
+
+def mirrored(step):
+    return [
+        (ctx * 8 + z, ctx * 8 + (z + (-step if ctx % CORES else step)) % 8)
+        for ctx in range(CTX)
+        for z in range(8)
+    ]
 
 
 def norm_kernel(
-    local_ref, reach_ref, mine_ref, got_ref, gate_ref, gain_ref, keep_ref, right_ref, left_ref, normed_ref
+    local_ref, reach_ref, mine_ref, got_ref, gate_ref, gain_ref, keep_ref, ahead_ref, behind_ref, normed_ref
 ):
     core = lax.axis_index("ctx") % CORES
     place = lax.axis_index("head")
@@ -433,25 +432,25 @@
         gate = gate * jax.nn.sigmoid(gate)
         normed_ref[:, h * DV : (h + 1) * DV] = (heads * inv * gain_ref[...] * gate).astype(BF16)
     rows = TOK // 8
-    for steps, ref in ((KEPT, keep_ref), (TO_RIGHT, right_ref), (TO_LEFT, left_ref)):
+    sign = 1 - 2 * core
+    for steps, ref in ((KEPT, keep_ref), (TO_AHEAD, ahead_ref), (TO_BEHIND, behind_ref)):
         for k, step in enumerate(steps):
-            top = pl.multiple_of(((place + step + 8) % 8) * rows, rows)
+            top = pl.multiple_of(((place + sign * step + 8) % 8) * rows, rows)
             ref[k * rows : (k + 1) * rows, :] = normed_ref[pl.ds(top, rows), :]
 
 
-def project_kernel(keep_ref, left_ref, right_ref, own_ref, near_ref, far_ref, *out_refs):
-    core = lax.axis_index("ctx") % CORES
+def project_kernel(keep_ref, behind_ref, ahead_ref, own_ref, behind_w_ref, ahead_w_ref, *out_refs):
     keep = keep_ref[...]
-    left = left_ref[...]
-    right = right_ref[...]
-    none = jnp.zeros((left.shape[0] - right.shape[0], right.shape[1]), BF16)
-    right = jnp.concatenate([right, none], axis=0)
-    near = jnp.where(core == 0, left, right)
-    far = jnp.where(core == 0, right, left)
+    behind = behind_ref[...]
+    ahead = ahead_ref[...]
+    none = jnp.zeros((behind.shape[0] - ahead.shape[0], ahead.shape[1]), BF16)
+    ahead = jnp.concatenate([ahead, none], axis=0)
     rows = TOK // 8
     for part in range(0, own_ref.shape[1], 512):
         at = slice(part, part + 512)
-        total = mm(keep, own_ref[:, at]) + mm(near, near_ref[:, at]) + mm(far, far_ref[:, at])
+        total = (
+            mm(keep, own_ref[:, at]) + mm(behind, behind_w_ref[:, at]) + mm(ahead, ahead_w_ref[:, at])
+        )
         for k, out_ref in enumerate(out_refs):
             out_ref[:, at] = total[k * rows : (k + 1) * rows].astype(out_ref.dtype)
 
@@ -507,7 +506,7 @@
         cost_estimate=pl.CostEstimate(flops=5_000_000_000, bytes_accessed=0, transcendentals=0),
     )(key_in, value_in, query_in)
     near_weight = lax.ppermute(
-        lax.optimization_barrier((out_weight, edge))[0], ("ctx", "head"), neighbours_by_core()
+        lax.optimization_barrier((out_weight, edge))[0], ("ctx", "head"), mirrored(1)
     )
     rim = lax.ppermute(edge, "ctx", [(i, (i + 1) % CTX) for i in range(CTX)])
     wide = (2, DK, DK + DV)
@@ -560,28 +559,23 @@
     def normed_rows(steps):
         return ((len(steps) * block, HEADS * DV), BF16)
 
-    keep, to_right, to_left = call(
-        norm_kernel, [normed_rows(KEPT), normed_rows(TO_RIGHT), normed_rows(TO_LEFT)],
+    keep, to_ahead, to_behind = call(
+        norm_kernel, [normed_rows(KEPT), normed_rows(TO_AHEAD), normed_rows(TO_BEHIND)],
         [local, reach, mine, got, out_gate, gain_row],
         [pltpu.VMEM((TOK, HEADS * DV), BF16)],
         flops=100_000_000, moved=1_500_000,
     )
-    from_left = lax.ppermute(to_right, "head", around_z(1))
-    from_right = lax.ppermute(to_left, "head", around_z(-1))
-    own_part, back_part, ahead_part = call(
+    from_behind = lax.ppermute(to_ahead, ("ctx", "head"), mirrored(1))
+    from_ahead = lax.ppermute(to_behind, ("ctx", "head"), mirrored(-1))
+    own_part, far_part, near_part = call(
         project_kernel, [((block, width), F32)] + [((block, width), BF16)] * 2,
-        [
-            keep, from_left, from_right, out_weight, near_weight, far_weight
-        ],
+        [keep, from_behind, from_ahead, out_weight, near_weight, far_weight],
         flops=600_000_000, moved=6_000_000,
     )
+    far_part = lax.ppermute(far_part, ("ctx", "head"), mirrored(-3))
+    near_part = lax.ppermute(near_part, ("ctx", "head"), mirrored(2))
     (mixed,) = call(
-        sum_kernel, [((block, width), BF16)],
-        [
-            own_part,
-            lax.ppermute(back_part, "head", around_z(-3)),
-            lax.ppermute(ahead_part, "head", around_z(2)),
-        ],
+        sum_kernel, [((block, width), BF16)], [own_part, far_part, near_part],
         flops=1_000_000, moved=800_000,
     )
     return mixed

time: 62 us -> 61.9 us (level)
  transfers between devices with their start and end apart: 15 -> 15, of which waited for: 11 -> 11; matrix products, arithmetic and copies ran while one was open for 0% -> 0% of each run, Pallas kernels for 13% -> 12%
where the time goes in v8:
time: 61.9 us; the launch traced here: 61.7 us
  waiting for transfers between devices  27.5 us (44%)
  starting transfers between devices  23.1 us (37%)
  Pallas kernels  10.8 us (17%)
    pallas_call x9, Pallas kernels, call(): pl.pallas_call(kernel, grid=(1,) if blocked else (), out_shape=[jax.Shape...  9.3 us
    ppermute x3, waiting for transfers between devices, on_device(): near = [lax.ppermute(pair, 'ctx', along_x(k)) for k in (1, 2, 3)]  7.48 us
    ppermute x1, waiting for transfers between devices, on_device(): far_part = lax.ppermute(far_part, ('ctx', 'head'), mirrored(-3))  6.93 us
    ppermute x3, waiting for transfers between devices, on_device(): far = [lax.ppermute(total, 'ctx', along_y(k)) for k in (1, 2, 3)]  6.47 us
    ppermute x3, starting transfers between devices, on_device(): near = [lax.ppermute(pair, 'ctx', along_x(k)) for k in (1, 2, 3)]  5.89 us
    ppermute x1, starting transfers between devices, on_device(): rim = lax.ppermute(edge, 'ctx', [(i, (i + 1) % CTX) for i in range(CTX)])  3.49 us
    ppermute x3, starting transfers between devices, on_device(): far = [lax.ppermute(total, 'ctx', along_y(k)) for k in (1, 2, 3)]  3.35 us
    ppermute x1, starting transfers between devices, on_device(): near_part = lax.ppermute(near_part, ('ctx', 'head'), mirrored(2))  3.24 us
  transfers between devices with their start and end apart: 15, of which 11 were waited for; matrix products, arithmetic and copies ran while one was open for 0% of the time, Pallas kernels for 12%

profile of v8, /device:TPU:6, one launch (start us, length us, event | category | flops | bytes accessed | tf_op | source)
XLA Modules:
  0.0 61.7 jit_solution(10646137140142866164)
XLA Ops:
  0.0 0.0 copy-start.4
  0.0 0.0 copy-start.3
  0.0 0.0 copy-start
  0.0 0.0 copy-start.9
  0.0 0.0 copy-start.11
  0.0 0.0 copy-start.7
  0.0 0.0 copy-start.8
  0.0 0.0 copy-start.6
  0.1 1.5 %shard_map.118 = bf16[16,1024]{1,0:T(8,128)(2,1)} custom-call(bf16[256,256]{1,0:T(8,128)(2,1)} %k_ref.3, bf16[256,512]{1,0:T(8,128)(2,1)} %v_ref.3, bf16[256,256]{1,0:T(8,128)(2,1)} %q_ref.3), custom_call_target="tpu_custom_call" | custom-call | flops 5000000000 | tf_op jit(solution)/shard_map/pallas_call | solution.py:500
  1.5 0.1 copy-done
  1.7 1.9 %collective-permute-start.11 = (bf16[512,2048]{1,0:T(8,128)(2,1)S(1)}, bf16[512,2048]{1,0:T(8,128)(2,1)S(1)}, u32[]{:S(2)}, u32[]{:S(2)}) collective-permute-start(bf16[512,2048]{1,0:T(8,128)(2,1)S(1)} %copy-done), channel_id=1, source_target_pairs={{0,1},{1,2},{2,3},{3,4},{4,5},{5,6},{6,7},{7,0},{8,15},{9,8},{10,9... | collective-permute-start | bytes 6291464 | tf_op jit(solution)/shard_map/ppermute | solution.py:508
  3.6 3.5 %collective-permute-start = (bf16[16,1024]{1,0:T(8,128)(2,1)}, bf16[16,1024]{1,0:T(8,128)(2,1)S(1)}, u32[]{:S(2)}, u32[]{:S(2)}) collective-permute-start(bf16[16,1024]{1,0:T(8,128)(2,1)} %shard_map.118), channel_id=1, source_target_pairs={{0,8},{8,16},{16,24},{24,32},{32,40},{40,48},{48,56},{56,64},{64,7... | collective-permute-start | bytes 98312 | tf_op jit(solution)/shard_map/ppermute | solution.py:511
  7.1 0.0 copy-done.4
  7.1 0.0 copy-done.3
  7.1 0.0 copy-done.9
  7.1 0.0 copy-done.11
  7.1 0.0 copy-done.7
  7.1 0.0 copy-done.8
  7.1 0.0 copy-done.6
  7.1 1.5 %shard_map.119 = (bf16[2,256,128]{2,1,0:T(8,128)(2,1)S(1)}, bf16[256,512]{1,0:T(8,128)(2,1)S(1)}, f32[4,256,256]{2,1,0:T(8,128)S(1)}, f32[4,256,128]{2,1,0:T(8,1...) custom-call(bf16[256,256]{1,0:T(8,128)(2,1)S(1)} %copy-done.4, ...), custom_call_target="tpu_custom_call" | custom-call | flops 500000000 | tf_op jit(solution)/shard_map/pallas_call | solution.py:480
  8.6 0.7 %collective-permute-done.rim_ref = bf16[16,1024]{1,0:T(8,128)(2,1)S(1)} collective-permute-done((bf16[16,1024]{1,0:T(8,128)(2,1)}, bf16[16,1024]{1,0:T(8,128)(2,1)S(1)}, u32[]{:S(2)}, u32[]{:S(2)}) %collective-permute-start) | collective-permute-done | bytes 32800 | tf_op jit(solution)/shard_map/ppermute | solution.py:511
  9.3 0.0 copy-start.5
  9.3 0.0 copy-start.10
  9.3 3.4 %shard_map.120 = (bf16[4,256,256]{2,1,0:T(8,128)(2,1)S(1)}, bf16[2,256,128]{2,1,0:T(8,128)(2,1)S(1)}, bf16[2,128,256]{2,1,0:T(8,128)(2,1)S(1)}, bf16[2,128,256]{2,1,0:T(8,128)(2,1)S(1)}) custom-call(bf16[16,1024]{1,0:T(8,128)(2,1)S(1)} %collective-permute-done.rim_ref, bf16[16,768]{1,0:T(8,128)(2,1)S(1)} %get-tuple-element.31.head_ref, ...), custom_call_target="tpu_custom_call" | custom-call | flops 4000000000 | bytes 2000000 | tf_op jit(solution)/shard_map/pallas_call | solution.py:480
  12.7 0.1 collective-permute-start.1
  12.8 1.3 %collective-permute-done.1.got_ref.other_ref = bf16[2,128,256]{2,1,0:T(8,128)(2,1)S(1)} collective-permute-done((bf16[2,128,256]{2,1,0:T(8,128)(2,1)S(1)}, bf16[2,128,256]{2,1,0:T(8,128)(2,1)S(1)}, u32[]{:S(2)}, u32[]{:S(2)}) %collective-permute-start.1) | collective-permute-done | bytes 131104 | tf_op jit(solution)/shard_map/ppermute | solution.py:533
  14.1 0.2 shard_map.122.own_ref
  14.3 4.9 %collective-permute-start.2 = (bf16[2,128,256]{2,1,0:T(8,128)(2,1)S(1)}, bf16[2,128,256]{2,1,0:T(8,128)(2,1)S(1)}, u32[]{:S(2)}, u32[]{:S(2)}) collective-permute-start(bf16[2,128,256]{2,1,0:T(8,128)(2,1)S(1)} %shard_map.122.own_ref), channel_id=1, source_target_pairs={{0,16},{8,24},{16,32},{24,40},{32,48},{40,56},{48,0},{56,8},{64,80... | collective-permute-start | bytes 393224 | tf_op jit(solution)/shard_map/ppermute | solution.py:535
  19.2 0.0 collective-permute-start.3
  19.2 1.0 %collective-permute-start.4 = (bf16[2,128,256]{2,1,0:T(8,128)(2,1)S(1)}, bf16[2,128,256]{2,1,0:T(8,128)(2,1)S(1)}, u32[]{:S(2)}, u32[]{:S(2)}) collective-permute-start(bf16[2,128,256]{2,1,0:T(8,128)(2,1)S(1)} %shard_map.122.own_ref), channel_id=1, source_target_pairs={{0,48},{8,56},{16,0},{24,8},{32,16},{40,24},{48,32},{56,40},{64,11... | collective-permute-start | bytes 393224 | tf_op jit(solution)/shard_map/ppermute | solution.py:535
  20.2 0.0 copy-done.5
  20.2 0.0 copy-done.10
  20.2 0.0 copy-start.1
  20.2 0.0 copy-start.2
  20.2 0.8 %shard_map.121 = (f32[4,256,128]{2,1,0:T(8,128)S(1)}, bf16[4,256,128]{2,1,0:T(8,128)(2,1)S(1)}) custom-call(bf16[256,256]{1,0:T(8,128)(2,1)S(1)} %copy-done.5, bf16[16,1024]{1,0:T(8,128)(2,1)S(1)} %collective-permute-done.rim_ref, f32[4,256]{1,0:T(4,128)S(1)} %copy-done.9, s32[1,256]{1,0:T(1,128)S(1)} %bitcast.4, f32[4,256]{1,0:T(4,128)S(1)} %copy-done.10, ...), custom_call_target="tpu_custom_call" | custom-call | flops 2000000000 | bytes 2000000 | tf_op jit(solution)/shard_map/pallas_call | solution.py:480
  21.1 4.1 %collective-permute-done.2.one_ref = bf16[2,128,256]{2,1,0:T(8,128)(2,1)S(1)} collective-permute-done((bf16[2,128,256]{2,1,0:T(8,128)(2,1)S(1)}, bf16[2,128,256]{2,1,0:T(8,128)(2,1)S(1)}, u32[]{:S(2)}, u32[]{:S(2)}) %collective-permute-start.2) | collective-permute-done | bytes 131104 | tf_op jit(solution)/shard_map/ppermute | solution.py:535
  25.1 2.0 %collective-permute-done.3.two_ref = bf16[2,128,256]{2,1,0:T(8,128)(2,1)S(1)} collective-permute-done((bf16[2,128,256]{2,1,0:T(8,128)(2,1)S(1)}, bf16[2,128,256]{2,1,0:T(8,128)(2,1)S(1)}, u32[]{:S(2)}, u32[]{:S(2)}) %collective-permute-start.3) | collective-permute-done | bytes 131104 | tf_op jit(solution)/shard_map/ppermute | solution.py:535
  27.1 1.4 %collective-permute-done.4.three_ref = bf16[2,128,256]{2,1,0:T(8,128)(2,1)S(1)} collective-permute-done((bf16[2,128,256]{2,1,0:T(8,128)(2,1)S(1)}, bf16[2,128,256]{2,1,0:T(8,128)(2,1)S(1)}, u32[]{:S(2)}, u32[]{:S(2)}) %collective-permute-start.4) | collective-permute-done | bytes 131104 | tf_op jit(solution)/shard_map/ppermute | solution.py:535
  28.5 0.5 shard_map.123
  29.1 0.1 collective-permute-start.5
  29.2 2.2 %collective-permute-start.6 = (bf16[2,128,256]{2,1,0:T(8,128)(2,1)S(1)}, bf16[2,128,256]{2,1,0:T(8,128)(2,1)S(1)}, u32[]{:S(2)}, u32[]{:S(2)}) collective-permute-start(bf16[2,128,256]{2,1,0:T(8,128)(2,1)S(1)} %get-tuple-element.45.own_ref), channel_id=1, source_target_pairs={{0,128},{8,136},{16,144},{24,152},{32,160},{40,168},{48,176},{56,1... | collective-permute-start | bytes 393224 | tf_op jit(solution)/shard_map/ppermute | solution.py:548
  31.4 1.1 %collective-permute-start.7 = (bf16[2,128,256]{2,1,0:T(8,128)(2,1)S(1)}, bf16[2,128,256]{2,1,0:T(8,128)(2,1)S(1)}, u32[]{:S(2)}, u32[]{:S(2)}) collective-permute-start(bf16[2,128,256]{2,1,0:T(8,128)(2,1)S(1)} %get-tuple-element.45.own_ref), channel_id=1, source_target_pairs={{0,192},{8,200},{16,208},{24,216},{32,224},{40,232},{48,240},{56,2... | collective-permute-start | bytes 393224 | tf_op jit(solution)/shard_map/ppermute | solution.py:548
  32.5 5.9 %collective-permute-done.5.one_ref = bf16[2,128,256]{2,1,0:T(8,128)(2,1)S(1)} collective-permute-done((bf16[2,128,256]{2,1,0:T(8,128)(2,1)S(1)}, bf16[2,128,256]{2,1,0:T(8,128)(2,1)S(1)}, u32[]{:S(2)}, u32[]{:S(2)}) %collective-permute-start.5) | collective-permute-done | bytes 131104 | tf_op jit(solution)/shard_map/ppermute | solution.py:548
  38.3 0.0 collective-permute-done.6.two_ref
  38.3 0.6 %collective-permute-done.7.three_ref = bf16[2,128,256]{2,1,0:T(8,128)(2,1)S(1)} collective-permute-done((bf16[2,128,256]{2,1,0:T(8,128)(2,1)S(1)}, bf16[2,128,256]{2,1,0:T(8,128)(2,1)S(1)}, u32[]{:S(2)}, u32[]{:S(2)}) %collective-permute-start.7) | collective-permute-done | bytes 131104 | tf_op jit(solution)/shard_map/ppermute | solution.py:548
  38.9 0.6 %shard_map.124 = (bf16[2,128,128]{2,1,0:T(8,128)(2,1)S(1)}, bf16[2,128,128]{2,1,0:T(8,128)(2,1)S(1)}) custom-call(bf16[2,128,256]{2,1,0:T(8,128)(2,1)S(1)} %get-tuple-element.45.own_ref, bf16[2,128,256]{2,1,0:T(8,128)(2,1)S(1)} %collective-permute-done.5.one_ref, bf16[2,128,256]{2,1,0:T(8,128)(2,1)S(1)} %collective-permute-done.6.two_ref, ...), custom_call_target="tpu_custom_call" | custom-call | flops 60000000 | bytes 1000000 | tf_op jit(solution)/shard_map/pallas_call | solution.py:480
  39.6 0.3 collective-permute-start.8
  39.8 1.2 %collective-permute-done.8.got_ref = bf16[2,128,128]{2,1,0:T(8,128)(2,1)S(1)} collective-permute-done((bf16[2,128,128]{2,1,0:T(8,128)(2,1)S(1)}, bf16[2,128,128]{2,1,0:T(8,128)(2,1)S(1)}, u32[]{:S(2)}, u32[]{:S(2)}) %collective-permute-start.8) | collective-permute-done | bytes 65568 | tf_op jit(solution)/shard_map/ppermute | solution.py:554
  41.1 0.0 collective-permute-done.11.behind_w_ref
  41.1 0.2 collective-permute-start.12
  41.2 0.0 copy-done.1
  41.2 0.0 copy-done.2
  41.3 0.4 shard_map.125
  41.7 0.1 collective-permute-start.9
  41.8 3.2 %collective-permute-start.10 = (bf16[64,512]{1,0:T(8,128)(2,1)S(1)}, bf16[64,512]{1,0:T(8,128)(2,1)S(1)}, u32[]{:S(2)}, u32[]{:S(2)}) collective-permute-start(bf16[64,512]{1,0:T(8,128)(2,1)S(1)} %get-tuple-element.51), channel_id=1, source_target_pairs={{0,7},{1,0},{2,1},{3,2},{4,3},{5,4},{6,5},{7,6},{8,9},{9,10},{10,1... | collective-permute-start | bytes 196616 | tf_op jit(solution)/shard_map/ppermute | solution.py:569
  45.0 1.9 %collective-permute-done.10.ahead_ref = bf16[64,512]{1,0:T(8,128)(2,1)S(1)} collective-permute-done((bf16[64,512]{1,0:T(8,128)(2,1)S(1)}, bf16[64,512]{1,0:T(8,128)(2,1)S(1)}, u32[]{:S(2)}, u32[]{:S(2)}) %collective-permute-start.10) | collective-permute-done | bytes 65568 | tf_op jit(solution)/shard_map/ppermute | solution.py:569
  46.9 1.4 %collective-permute-done.9.behind_ref = bf16[96,512]{1,0:T(8,128)(2,1)S(1)} collective-permute-done((bf16[96,512]{1,0:T(8,128)(2,1)S(1)}, bf16[96,512]{1,0:T(8,128)(2,1)S(1)}, u32[]{:S(2)}, u32[]{:S(2)}) %collective-permute-start.9) | collective-permute-done | bytes 98336 | tf_op jit(solution)/shard_map/ppermute | solution.py:568
  48.3 0.0 collective-permute-done.12.ahead_w_ref
  48.3 1.2 %shard_map.126 = (f32[32,2048]{1,0:T(8,128)S(1)}, bf16[32,2048]{1,0:T(8,128)(2,1)S(1)}, bf16[32,2048]{1,0:T(8,128)(2,1)S(1)}) custom-call(bf16[96,512]{1,0:T(8,128)(2,1)S(1)} %get-tuple-element.49.keep_ref, bf16[96,512]{1,0:T(8,128)(2,1)S(1)} %collective-permute-done.9.behind_ref, bf16[64,512]{1,0:T(8,128)(2,1)S(1)} %collective-permute-done.10.ahead_ref, ...), custom_call_target="tpu_custom_call" | custom-call | flops 600000000 | bytes 6000000 | tf_op jit(solution)/shard_map/pallas_call | solution.py:480
  49.5 1.4 %collective-permute-start.13 = (bf16[32,2048]{1,0:T(8,128)(2,1)S(1)}, bf16[32,2048]{1,0:T(8,128)(2,1)S(1)}, u32[]{:S(2)}, u32[]{:S(2)}) collective-permute-start(bf16[32,2048]{1,0:T(8,128)(2,1)S(1)} %get-tuple-element.55), channel_id=1, source_target_pairs={{0,5},{1,6},{2,7},{3,0},{4,1},{5,2},{6,3},{7,4},{8,11},{9,12},{10,... | collective-permute-start | bytes 393224 | tf_op jit(solution)/shard_map/ppermute | solution.py:575
  50.9 3.2 %collective-permute-start.14 = (bf16[32,2048]{1,0:T(8,128)(2,1)S(1)}, bf16[32,2048]{1,0:T(8,128)(2,1)S(1)}, u32[]{:S(2)}, u32[]{:S(2)}) collective-permute-start(bf16[32,2048]{1,0:T(8,128)(2,1)S(1)} %get-tuple-element.56), channel_id=1, source_target_pairs={{0,2},{1,3},{2,4},{3,5},{4,6},{5,7},{6,0},{7,1},{8,14},{9,15},{10,... | collective-permute-start | bytes 393224 | tf_op jit(solution)/shard_map/ppermute | solution.py:576
  54.1 6.9 %collective-permute-done.13.one_ref = bf16[32,2048]{1,0:T(8,128)(2,1)S(1)} collective-permute-done((bf16[32,2048]{1,0:T(8,128)(2,1)S(1)}, bf16[32,2048]{1,0:T(8,128)(2,1)S(1)}, u32[]{:S(2)}, u32[]{:S(2)}) %collective-permute-start.13) | collective-permute-done | bytes 131104 | tf_op jit(solution)/shard_map/ppermute | solution.py:575
  61.0 0.0 collective-permute-done.14.two_ref
  61.0 0.7 %shard_map.127 = bf16[32,2048]{1,0:T(8,128)(2,1)} custom-call(f32[32,2048]{1,0:T(8,128)S(1)} %get-tuple-element.54.own_ref, bf16[32,2048]{1,0:T(8,128)(2,1)S(1)} %collective-permute-done.13.one_ref, bf16[32,2048]{1,0:T(8,128)(2,1)S(1)} %collective-permute-done.14.two_ref), custom_call_target="tpu_custom_call" | custom-call | flops 1000000 | bytes 800000 | tf_op jit(solution)/shard_map/pallas_call | solution.py:480
Async XLA Ops:
  0.0 7.1 %copy-start.4 = (bf16[256,256]{1,0:T(8,128)(2,1)S(1)}, bf16[256,256]{1,0:T(8,128)(2,1)}, u32[]{:S(2)}) copy-start(bf16[256,256]{1,0:T(8,128)(2,1)} %k_ref.3) | copy-start | bytes 393220
  0.0 7.1 %copy-start.3 = (bf16[256,512]{1,0:T(8,128)(2,1)S(1)}, bf16[256,512]{1,0:T(8,128)(2,1)}, u32[]{:S(2)}) copy-start(bf16[256,512]{1,0:T(8,128)(2,1)} %v_ref.3) | copy-start | bytes 786436
  0.0 1.7 %copy-start = (bf16[512,2048]{1,0:T(8,128)(2,1)S(1)}, bf16[512,2048]{1,0:T(8,128)(2,1)}, u32[]{:S(2)}) copy-start(bf16[512,2048]{1,0:T(8,128)(2,1)} %own_ref.1) | copy-start | bytes 6291460
  0.0 7.1 %copy-start.9 = (f32[4,256]{1,0:T(4,128)S(1)}, f32[4,256]{1,0:T(4,128)}, u32[]{:S(2)}) copy-start(f32[4,256]{1,0:T(4,128)} %decay_ref.3) | copy-start | bytes 12292
  0.0 7.1 %copy-start.11 = (s32[256]{0:T(256)S(1)}, s32[256]{0:T(256)}, u32[]{:S(2)}) copy-start(s32[256]{0:T(256)} %param.18) | copy-start | bytes 3076
  0.0 7.1 %copy-start.7 = (f32[4,256]{1,0:T(4,128)S(1)}, f32[4,256]{1,0:T(4,128)}, u32[]{:S(2)}) copy-start(f32[4,256]{1,0:T(4,128)} %beta_ref.3) | copy-start | bytes 12292
  0.0 7.1 %copy-start.8 = (f32[4,256]{1,0:T(4,128)S(1)}, f32[4,256]{1,0:T(4,128)}, u32[]{:S(2)}) copy-start(f32[4,256]{1,0:T(4,128)} %wk_ref.3) | copy-start | bytes 12292
  0.0 7.1 %copy-start.6 = (f32[4,512]{1,0:T(4,128)S(1)}, f32[4,512]{1,0:T(4,128)}, u32[]{:S(2)}) copy-start(f32[4,512]{1,0:T(4,128)} %wv_ref.3) | copy-start | bytes 24580
  1.7 39.4 %collective-permute-start.11 = (bf16[512,2048]{1,0:T(8,128)(2,1)S(1)}, bf16[512,2048]{1,0:T(8,128)(2,1)S(1)}, u32[]{:S(2)}, u32[]{:S(2)}) collective-permute-start(bf16[512,2048]{1,0:T(8,128)(2,1)S(1)} %copy-done), channel_id=1, source_target_pairs={{0,1},{1,2},{2,3},{3,4},{4,5},{5,6},{6,7},{7,0},{8,15},{9,8},{10,9... | collective-permute-start | bytes 6291464 | tf_op jit(solution)/shard_map/ppermute | solution.py:508
  3.6 5.7 %collective-permute-start = (bf16[16,1024]{1,0:T(8,128)(2,1)}, bf16[16,1024]{1,0:T(8,128)(2,1)S(1)}, u32[]{:S(2)}, u32[]{:S(2)}) collective-permute-start(bf16[16,1024]{1,0:T(8,128)(2,1)} %shard_map.118), channel_id=1, source_target_pairs={{0,8},{8,16},{16,24},{24,32},{32,40},{40,48},{48,56},{56,64},{64,7... | collective-permute-start | bytes 98312 | tf_op jit(solution)/shard_map/ppermute | solution.py:511
  9.3 10.9 %copy-start.5 = (bf16[256,256]{1,0:T(8,128)(2,1)S(1)}, bf16[256,256]{1,0:T(8,128)(2,1)}, u32[]{:S(2)}) copy-start(bf16[256,256]{1,0:T(8,128)(2,1)} %q_ref.3) | copy-start | bytes 393220
  9.3 10.9 %copy-start.10 = (f32[4,256]{1,0:T(4,128)S(1)}, f32[4,256]{1,0:T(4,128)}, u32[]{:S(2)}) copy-start(f32[4,256]{1,0:T(4,128)} %wq_ref.1) | copy-start | bytes 12292
  12.7 1.4 %collective-permute-start.1 = (bf16[2,128,256]{2,1,0:T(8,128)(2,1)S(1)}, bf16[2,128,256]{2,1,0:T(8,128)(2,1)S(1)}, u32[]{:S(2)}, u32[]{:S(2)}) collective-permute-start(bf16[2,128,256]{2,1,0:T(8,128)(2,1)S(1)} %get-tuple-element.44), channel_id=1, source_target_pairs={{0,8},{8,0},{16,24},{24,16},{32,40},{40,32},{48,56},{56,48},{64,72... | collective-permute-start | bytes 393224 | tf_op jit(solution)/shard_map/ppermute | solution.py:533
  14.3 10.8 %collective-permute-start.2 = (bf16[2,128,256]{2,1,0:T(8,128)(2,1)S(1)}, bf16[2,128,256]{2,1,0:T(8,128)(2,1)S(1)}, u32[]{:S(2)}, u32[]{:S(2)}) collective-permute-start(bf16[2,128,256]{2,1,0:T(8,128)(2,1)S(1)} %shard_map.122.own_ref), channel_id=1, source_target_pairs={{0,16},{8,24},{16,32},{24,40},{32,48},{40,56},{48,0},{56,8},{64,80... | collective-permute-start | bytes 393224 | tf_op jit(solution)/shard_map/ppermute | solution.py:535
  19.2 7.9 %collective-permute-start.3 = (bf16[2,128,256]{2,1,0:T(8,128)(2,1)S(1)}, bf16[2,128,256]{2,1,0:T(8,128)(2,1)S(1)}, u32[]{:S(2)}, u32[]{:S(2)}) collective-permute-start(bf16[2,128,256]{2,1,0:T(8,128)(2,1)S(1)} %shard_map.122.own_ref), channel_id=1, source_target_pairs={{0,32},{8,40},{16,48},{24,56},{32,0},{40,8},{48,16},{56,24},{64,96... | collective-permute-start | bytes 393224 | tf_op jit(solution)/shard_map/ppermute | solution.py:535
  19.2 9.3 %collective-permute-start.4 = (bf16[2,128,256]{2,1,0:T(8,128)(2,1)S(1)}, bf16[2,128,256]{2,1,0:T(8,128)(2,1)S(1)}, u32[]{:S(2)}, u32[]{:S(2)}) collective-permute-start(bf16[2,128,256]{2,1,0:T(8,128)(2,1)S(1)} %shard_map.122.own_ref), channel_id=1, source_target_pairs={{0,48},{8,56},{16,0},{24,8},{32,16},{40,24},{48,32},{56,40},{64,11... | collective-permute-start | bytes 393224 | tf_op jit(solution)/shard_map/ppermute | solution.py:535
  20.2 21.0 %copy-start.1 = (bf16[256,512]{1,0:T(8,128)(2,1)S(1)}, bf16[256,512]{1,0:T(8,128)(2,1)}, u32[]{:S(2)}) copy-start(bf16[256,512]{1,0:T(8,128)(2,1)} %gate_ref.1) | copy-start | bytes 786436
  20.2 21.0 %copy-start.2 = (f32[128]{0:T(128)S(1)}, f32[128]{0:T(128)}, u32[]{:S(2)}) copy-start(f32[128]{0:T(128)} %param.22) | copy-start | bytes 1540
  29.1 9.2 %collective-permute-start.5 = (bf16[2,128,256]{2,1,0:T(8,128)(2,1)S(1)}, bf16[2,128,256]{2,1,0:T(8,128)(2,1)S(1)}, u32[]{:S(2)}, u32[]{:S(2)}) collective-permute-start(bf16[2,128,256]{2,1,0:T(8,128)(2,1)S(1)} %get-tuple-element.45.own_ref), channel_id=1, source_target_pairs={{0,64},{8,72},{16,80},{24,88},{32,96},{40,104},{48,112},{56,120},{... | collective-permute-start | bytes 393224 | tf_op jit(solution)/shard_map/ppermute | solution.py:548
  29.2 9.1 %collective-permute-start.6 = (bf16[2,128,256]{2,1,0:T(8,128)(2,1)S(1)}, bf16[2,128,256]{2,1,0:T(8,128)(2,1)S(1)}, u32[]{:S(2)}, u32[]{:S(2)}) collective-permute-start(bf16[2,128,256]{2,1,0:T(8,128)(2,1)S(1)} %get-tuple-element.45.own_ref), channel_id=1, source_target_pairs={{0,128},{8,136},{16,144},{24,152},{32,160},{40,168},{48,176},{56,1... | collective-permute-start | bytes 393224 | tf_op jit(solution)/shard_map/ppermute | solution.py:548
  31.4 7.6 %collective-permute-start.7 = (bf16[2,128,256]{2,1,0:T(8,128)(2,1)S(1)}, bf16[2,128,256]{2,1,0:T(8,128)(2,1)S(1)}, u32[]{:S(2)}, u32[]{:S(2)}) collective-permute-start(bf16[2,128,256]{2,1,0:T(8,128)(2,1)S(1)} %get-tuple-element.45.own_ref), channel_id=1, source_target_pairs={{0,192},{8,200},{16,208},{24,216},{32,224},{40,232},{48,240},{56,2... | collective-permute-start | bytes 393224 | tf_op jit(solution)/shard_map/ppermute | solution.py:548
  39.6 1.5 %collective-permute-start.8 = (bf16[2,128,128]{2,1,0:T(8,128)(2,1)S(1)}, bf16[2,128,128]{2,1,0:T(8,128)(2,1)S(1)}, u32[]{:S(2)}, u32[]{:S(2)}) collective-permute-start(bf16[2,128,128]{2,1,0:T(8,128)(2,1)S(1)} %get-tuple-element.48), channel_id=1, source_target_pairs={{0,8},{8,0},{16,24},{24,16},{32,40},{40,32},{48,56},{56,48},{64,72... | collective-permute-start | bytes 196616 | tf_op jit(solution)/shard_map/ppermute | solution.py:554
  41.1 7.2 %collective-permute-start.12 = (bf16[512,2048]{1,0:T(8,128)(2,1)S(1)}, bf16[512,2048]{1,0:T(8,128)(2,1)S(1)}, u32[]{:S(2)}, u32[]{:S(2)}) collective-permute-start(bf16[512,2048]{1,0:T(8,128)(2,1)S(1)} %collective-permute-done.11.behind_w_ref), channel_id=1, source_target_pairs={{0,8},{8,0},{16,24},{24,16},{32,40},{40,32},{48,56},{56,48},{64,72... | collective-permute-start | bytes 6291464 | tf_op jit(solution)/shard_map/ppermute | solution.py:556
  41.7 6.6 %collective-permute-start.9 = (bf16[96,512]{1,0:T(8,128)(2,1)S(1)}, bf16[96,512]{1,0:T(8,128)(2,1)S(1)}, u32[]{:S(2)}, u32[]{:S(2)}) collective-permute-start(bf16[96,512]{1,0:T(8,128)(2,1)S(1)} %get-tuple-element.50), channel_id=1, source_target_pairs={{0,1},{1,2},{2,3},{3,4},{4,5},{5,6},{6,7},{7,0},{8,15},{9,8},{10,9... | collective-permute-start | bytes 294920 | tf_op jit(solution)/shard_map/ppermute | solution.py:568
  41.8 5.1 %collective-permute-start.10 = (bf16[64,512]{1,0:T(8,128)(2,1)S(1)}, bf16[64,512]{1,0:T(8,128)(2,1)S(1)}, u32[]{:S(2)}, u32[]{:S(2)}) collective-permute-start(bf16[64,512]{1,0:T(8,128)(2,1)S(1)} %get-tuple-element.51), channel_id=1, source_target_pairs={{0,7},{1,0},{2,1},{3,2},{4,3},{5,4},{6,5},{7,6},{8,9},{9,10},{10,1... | collective-permute-start | bytes 196616 | tf_op jit(solution)/shard_map/ppermute | solution.py:569
  49.5 11.6 %collective-permute-start.13 = (bf16[32,2048]{1,0:T(8,128)(2,1)S(1)}, bf16[32,2048]{1,0:T(8,128)(2,1)S(1)}, u32[]{:S(2)}, u32[]{:S(2)}) collective-permute-start(bf16[32,2048]{1,0:T(8,128)(2,1)S(1)} %get-tuple-element.55), channel_id=1, source_target_pairs={{0,5},{1,6},{2,7},{3,0},{4,1},{5,2},{6,3},{7,4},{8,11},{9,12},{10,... | collective-permute-start | bytes 393224 | tf_op jit(solution)/shard_map/ppermute | solution.py:575
  50.9 10.2 %collective-permute-start.14 = (bf16[32,2048]{1,0:T(8,128)(2,1)S(1)}, bf16[32,2048]{1,0:T(8,128)(2,1)S(1)}, u32[]{:S(2)}, u32[]{:S(2)}) collective-permute-start(bf16[32,2048]{1,0:T(8,128)(2,1)S(1)} %get-tuple-element.56), channel_id=1, source_target_pairs={{0,2},{1,3},{2,4},{3,5},{4,6},{5,7},{6,0},{7,1},{8,14},{9,15},{10,... | collective-permute-start | bytes 393224 | tf_op jit(solution)/shard_map/ppermute | solution.py:576

commit v9 on v8

--- a/solution.py
+++ b/solution.py
@@ -365,7 +365,7 @@
         out_ref[k] = joined(first, later).astype(BF16)
 
 
-def row_kernel(own_ref, one_ref, two_ref, three_ref, after_ref, before_ref, total_ref, slots):
+def row_kernel(own_ref, one_ref, two_ref, three_ref, after_ref, before_ref, total_ref, alone_ref, slots):
     x = (lax.axis_index("ctx") // CORES) % CHIPS_X
     for step, ref in enumerate((own_ref, one_ref, two_ref, three_ref)):
         slots[(x + CHIPS_X - step) % CHIPS_X] = ref[...]
@@ -379,6 +379,7 @@
             before = [jnp.where(x == place + 1, run[k], before[k]) for k in range(2)]
     for k in range(2):
         total_ref[k] = run[k]
+        alone_ref[k] = run[k][:, DK:]
         before_ref[k] = before[k]
 
 
@@ -388,8 +389,9 @@
     index = lax.axis_index("ctx")
     core = index % CORES
     y = index // (CORES * CHIPS_X)
-    for step, ref in enumerate((own_ref, one_ref, two_ref, three_ref)):
+    for step, ref in enumerate((own_ref, one_ref, two_ref)):
         slots[(y + CHIPS_Y - step) % CHIPS_Y] = ref[...]
+    slots[(y + 1) % CHIPS_Y, :, :, DK:] = three_ref[...]
 
     def passed(block, state):
         return mm(block[:, :DK], state.astype(BF16)) + block[:, DK:].astype(F32)
@@ -439,20 +441,31 @@
             ref[k * rows : (k + 1) * rows, :] = normed_ref[pl.ds(top, rows), :]
 
 
-def project_kernel(keep_ref, behind_ref, ahead_ref, own_ref, behind_w_ref, ahead_w_ref, *out_refs):
+def keep_kernel(keep_ref, weight_ref, out_ref):
     keep = keep_ref[...]
-    behind = behind_ref[...]
-    ahead = ahead_ref[...]
-    none = jnp.zeros((behind.shape[0] - ahead.shape[0], ahead.shape[1]), BF16)
-    ahead = jnp.concatenate([ahead, none], axis=0)
+    for part in range(0, weight_ref.shape[1], 512):
+        out_ref[:, part : part + 512] = mm(keep, weight_ref[:, part : part + 512])
+
+
+def remote_kernel(kept_ref, behind_ref, ahead_ref, behind_w_ref, ahead_w_ref, far_ref, near_ref):
     rows = TOK // 8
-    for part in range(0, own_ref.shape[1], 512):
+    behind = behind_ref[rows:, :]
+    ahead = ahead_ref[rows:, :]
+    for part in range(0, kept_ref.shape[1], 512):
         at = slice(part, part + 512)
-        total = (
-            mm(keep, own_ref[:, at]) + mm(behind, behind_w_ref[:, at]) + mm(ahead, ahead_w_ref[:, at])
-        )
-        for k, out_ref in enumerate(out_refs):
-            out_ref[:, at] = total[k * rows : (k + 1) * rows].astype(out_ref.dtype)
+        total = kept_ref[rows:, at] + mm(behind, behind_w_ref[:, at])
+        far_ref[:, at] = (total[:rows] + mm(ahead, ahead_w_ref[:, at])).astype(BF16)
+        near_ref[:, at] = total[rows:].astype(BF16)
+
+
+def own_kernel(kept_ref, behind_ref, ahead_ref, behind_w_ref, ahead_w_ref, out_ref):
+    rows = TOK // 8
+    behind = behind_ref[:rows, :]
+    ahead = ahead_ref[:rows, :]
+    for part in range(0, kept_ref.shape[1], 512):
+        at = slice(part, part + 512)
+        total = kept_ref[:rows, at] + mm(behind, behind_w_ref[:, at])
+        out_ref[:, at] = total + mm(ahead, ahead_w_ref[:, at])
 
 
 def sum_kernel(own_ref, one_ref, two_ref, out_ref):
@@ -540,13 +553,17 @@
         [pltpu.VMEM((8 + TOK, 256), F32)],
         flops=2_000_000_000, moved=2_000_000,
     )
-    before, total = call(
-        row_kernel, [(wide, BF16), (wide, BF16)], [pair] + near + [reach],
+    narrow = (2, DK, DV)
+    before, total, alone = call(
+        row_kernel, [(wide, BF16), (wide, BF16), (narrow, BF16)], [pair] + near + [reach],
         [pltpu.VMEM((CHIPS_X,) + wide, BF16)], flops=60_000_000, moved=800_000,
         specs=[VMEM] * 4 + [HBM],
     )
-    far = [lax.ppermute(total, "ctx", along_y(k)) for k in (1, 2, 3)]
-    narrow = (2, DK, DV)
+    far = [
+        lax.ppermute(total, "ctx", along_y(1)),
+        lax.ppermute(total, "ctx", along_y(2)),
+        lax.ppermute(alone, "ctx", along_y(3)),
+    ]
     mine, to_other = call(
         state_kernel, [(narrow, BF16), (narrow, BF16)], [total] + far + [before, own, other],
         [pltpu.VMEM((CHIPS_Y,) + wide, BF16)], flops=60_000_000, moved=1_000_000,
@@ -567,10 +584,16 @@
     )
     from_behind = lax.ppermute(to_ahead, ("ctx", "head"), mirrored(1))
     from_ahead = lax.ppermute(to_behind, ("ctx", "head"), mirrored(-1))
-    own_part, far_part, near_part = call(
-        project_kernel, [((block, width), F32)] + [((block, width), BF16)] * 2,
-        [keep, from_behind, from_ahead, out_weight, near_weight, far_weight],
-        flops=600_000_000, moved=6_000_000,
+    (kept,) = call(
+        keep_kernel, [((len(KEPT) * block, width), F32)], [keep, out_weight],
+        flops=200_000_000, moved=3_000_000,
+    )
+    gathered = [kept, from_behind, from_ahead, near_weight, far_weight]
+    far_part, near_part = call(
+        remote_kernel, [((block, width), BF16)] * 2, gathered, flops=200_000_000, moved=4_000_000,
+    )
+    (own_part,) = call(
+        own_kernel, [((block, width), F32)], gathered, flops=200_000_000, moved=4_000_000,
     )
     far_part = lax.ppermute(far_part, ("ctx", "head"), mirrored(-3))
     near_part = lax.ppermute(near_part, ("ctx", "head"), mirrored(2))

time: 61.9 us -> 60.7 us (0.981)
  waiting for transfers between devices: 27.5 us -> 25.4 us
  Pallas kernels: 10.8 us -> 11.7 us
    pallas_call x9 -> x11, Pallas kernels: 9.3 us -> 10.3 us  [call(): pl.pallas_call(kernel, grid=(1,) if blocked else (), out_shape=[jax.Shape...]
    ppermute x1, waiting for transfers between devices: 6.93 us -> 6 us  [on_device(): far_part = lax.ppermute(far_part, ('ctx', 'head'), mirrored(-3))]
  transfers between devices with their start and end apart: 15 -> 15, of which waited for: 11 -> 11; matrix products, arithmetic and copies ran while one was open for 0% -> 0% of each run, Pallas kernels for 12% -> 14%
where the time goes in v9:
time: 60.7 us; the launch traced here: 60.6 us
  waiting for transfers between devices  25.4 us (42%)
  starting transfers between devices  23.1 us (38%)
  Pallas kernels  11.7 us (19%)
    pallas_call x11, Pallas kernels, call(): pl.pallas_call(kernel, grid=(1,) if blocked else (), out_shape=[jax.Shape...  10.3 us
    ppermute x3, waiting for transfers between devices, on_device(): near = [lax.ppermute(pair, 'ctx', along_x(k)) for k in (1, 2, 3)]  7.47 us
    ppermute x1, waiting for transfers between devices, on_device(): far_part = lax.ppermute(far_part, ('ctx', 'head'), mirrored(-3))  6 us
    ppermute x3, starting transfers between devices, on_device(): near = [lax.ppermute(pair, 'ctx', along_x(k)) for k in (1, 2, 3)]  5.9 us
    ppermute x1, waiting for transfers between devices, on_device(): lax.ppermute(alone, 'ctx', along_y(3))  5.07 us
    ppermute x1, starting transfers between devices, on_device(): rim = lax.ppermute(edge, 'ctx', [(i, (i + 1) % CTX) for i in range(CTX)])  3.49 us
    ppermute x1, starting transfers between devices, on_device(): from_ahead = lax.ppermute(to_behind, ('ctx', 'head'), mirrored(-1))  3.22 us
    ppermute x1, starting transfers between devices, on_device(): near_part = lax.ppermute(near_part, ('ctx', 'head'), mirrored(2))  3.15 us
  transfers between devices with their start and end apart: 15, of which 11 were waited for; matrix products, arithmetic and copies ran while one was open for 0% of the time, Pallas kernels for 14%

profile of v9, /device:TPU:6, one launch (start us, length us, event | category | flops | bytes accessed | tf_op | source)
XLA Modules:
  0.0 60.6 jit_solution(3316868473114893427)
XLA Ops:
  0.0 0.0 copy-start.4
  0.0 0.0 copy-start.3
  0.0 0.0 copy-start
  0.0 0.0 copy-start.11
  0.0 0.0 copy-start.9
  0.0 0.0 copy-start.7
  0.0 0.0 copy-start.8
  0.0 0.0 copy-start.6
  0.1 1.5 %shard_map.118 = bf16[16,1024]{1,0:T(8,128)(2,1)} custom-call(bf16[256,256]{1,0:T(8,128)(2,1)} %k_ref.3, bf16[256,512]{1,0:T(8,128)(2,1)} %v_ref.3, bf16[256,256]{1,0:T(8,128)(2,1)} %q_ref.3), custom_call_target="tpu_custom_call" | custom-call | flops 5000000000 | tf_op jit(solution)/shard_map/pallas_call | solution.py:513
  1.5 0.1 copy-done
  1.7 1.9 %collective-permute-start.11 = (bf16[512,2048]{1,0:T(8,128)(2,1)S(1)}, bf16[512,2048]{1,0:T(8,128)(2,1)S(1)}, u32[]{:S(2)}, u32[]{:S(2)}) collective-permute-start(bf16[512,2048]{1,0:T(8,128)(2,1)S(1)} %copy-done), channel_id=1, source_target_pairs={{0,1},{1,2},{2,3},{3,4},{4,5},{5,6},{6,7},{7,0},{8,15},{9,8},{10,9... | collective-permute-start | bytes 6291464 | tf_op jit(solution)/shard_map/ppermute | solution.py:521
  3.6 3.5 %collective-permute-start = (bf16[16,1024]{1,0:T(8,128)(2,1)}, bf16[16,1024]{1,0:T(8,128)(2,1)S(1)}, u32[]{:S(2)}, u32[]{:S(2)}) collective-permute-start(bf16[16,1024]{1,0:T(8,128)(2,1)} %shard_map.118), channel_id=1, source_target_pairs={{0,8},{8,16},{16,24},{24,32},{32,40},{40,48},{48,56},{56,64},{64,7... | collective-permute-start | bytes 98312 | tf_op jit(solution)/shard_map/ppermute | solution.py:524
  7.1 0.0 copy-done.4
  7.1 0.0 copy-done.3
  7.1 0.0 copy-done.11
  7.1 0.0 copy-done.9
  7.1 0.0 copy-done.7
  7.1 0.0 copy-done.8
  7.1 0.0 copy-done.6
  7.1 1.5 %shard_map.119 = (bf16[2,256,128]{2,1,0:T(8,128)(2,1)S(1)}, bf16[256,512]{1,0:T(8,128)(2,1)S(1)}, f32[4,256,256]{2,1,0:T(8,128)S(1)}, f32[4,256,128]{2,1,0:T(8,1...) custom-call(bf16[256,256]{1,0:T(8,128)(2,1)S(1)} %copy-done.4, ...), custom_call_target="tpu_custom_call" | custom-call | flops 500000000 | tf_op jit(solution)/shard_map/pallas_call | solution.py:493
  8.6 0.7 %collective-permute-done.rim_ref = bf16[16,1024]{1,0:T(8,128)(2,1)S(1)} collective-permute-done((bf16[16,1024]{1,0:T(8,128)(2,1)}, bf16[16,1024]{1,0:T(8,128)(2,1)S(1)}, u32[]{:S(2)}, u32[]{:S(2)}) %collective-permute-start) | collective-permute-done | bytes 32800 | tf_op jit(solution)/shard_map/ppermute | solution.py:524
  9.3 0.0 copy-start.5
  9.3 0.0 copy-start.10
  9.3 3.4 %shard_map.120 = (bf16[4,256,256]{2,1,0:T(8,128)(2,1)S(1)}, bf16[2,256,128]{2,1,0:T(8,128)(2,1)S(1)}, bf16[2,128,256]{2,1,0:T(8,128)(2,1)S(1)}, bf16[2,128,256]{2,1,0:T(8,128)(2,1)S(1)}) custom-call(bf16[16,1024]{1,0:T(8,128)(2,1)S(1)} %collective-permute-done.rim_ref, bf16[16,768]{1,0:T(8,128)(2,1)S(1)} %get-tuple-element.31.head_ref, ...), custom_call_target="tpu_custom_call" | custom-call | flops 4000000000 | bytes 2000000 | tf_op jit(solution)/shard_map/pallas_call | solution.py:493
  12.7 0.1 collective-permute-start.1
  12.8 1.3 %collective-permute-done.1.got_ref.other_ref = bf16[2,128,256]{2,1,0:T(8,128)(2,1)S(1)} collective-permute-done((bf16[2,128,256]{2,1,0:T(8,128)(2,1)S(1)}, bf16[2,128,256]{2,1,0:T(8,128)(2,1)S(1)}, u32[]{:S(2)}, u32[]{:S(2)}) %collective-permute-start.1) | collective-permute-done | bytes 131104 | tf_op jit(solution)/shard_map/ppermute | solution.py:546
  14.1 0.2 shard_map.122.own_ref
  14.3 4.9 %collective-permute-start.2 = (bf16[2,128,256]{2,1,0:T(8,128)(2,1)S(1)}, bf16[2,128,256]{2,1,0:T(8,128)(2,1)S(1)}, u32[]{:S(2)}, u32[]{:S(2)}) collective-permute-start(bf16[2,128,256]{2,1,0:T(8,128)(2,1)S(1)} %shard_map.122.own_ref), channel_id=1, source_target_pairs={{0,16},{8,24},{16,32},{24,40},{32,48},{40,56},{48,0},{56,8},{64,80... | collective-permute-start | bytes 393224 | tf_op jit(solution)/shard_map/ppermute | solution.py:548
  19.2 0.0 collective-permute-start.3
  19.2 1.0 %collective-permute-start.4 = (bf16[2,128,256]{2,1,0:T(8,128)(2,1)S(1)}, bf16[2,128,256]{2,1,0:T(8,128)(2,1)S(1)}, u32[]{:S(2)}, u32[]{:S(2)}) collective-permute-start(bf16[2,128,256]{2,1,0:T(8,128)(2,1)S(1)} %shard_map.122.own_ref), channel_id=1, source_target_pairs={{0,48},{8,56},{16,0},{24,8},{32,16},{40,24},{48,32},{56,40},{64,11... | collective-permute-start | bytes 393224 | tf_op jit(solution)/shard_map/ppermute | solution.py:548
  20.2 0.0 copy-done.5
  20.2 0.0 copy-done.10
  20.2 0.8 %shard_map.121 = (f32[4,256,128]{2,1,0:T(8,128)S(1)}, bf16[4,256,128]{2,1,0:T(8,128)(2,1)S(1)}) custom-call(bf16[256,256]{1,0:T(8,128)(2,1)S(1)} %copy-done.5, bf16[16,1024]{1,0:T(8,128)(2,1)S(1)} %collective-permute-done.rim_ref, f32[4,256]{1,0:T(4,128)S(1)} %copy-done.9, s32[1,256]{1,0:T(1,128)S(1)} %bitcast.4, f32[4,256]{1,0:T(4,128)S(1)} %copy-done.10, ...), custom_call_target="tpu_custom_call" | custom-call | flops 2000000000 | bytes 2000000 | tf_op jit(solution)/shard_map/pallas_call | solution.py:493
  21.1 4.1 %collective-permute-done.2.one_ref = bf16[2,128,256]{2,1,0:T(8,128)(2,1)S(1)} collective-permute-done((bf16[2,128,256]{2,1,0:T(8,128)(2,1)S(1)}, bf16[2,128,256]{2,1,0:T(8,128)(2,1)S(1)}, u32[]{:S(2)}, u32[]{:S(2)}) %collective-permute-start.2) | collective-permute-done | bytes 131104 | tf_op jit(solution)/shard_map/ppermute | solution.py:548
  25.1 2.0 %collective-permute-done.3.two_ref = bf16[2,128,256]{2,1,0:T(8,128)(2,1)S(1)} collective-permute-done((bf16[2,128,256]{2,1,0:T(8,128)(2,1)S(1)}, bf16[2,128,256]{2,1,0:T(8,128)(2,1)S(1)}, u32[]{:S(2)}, u32[]{:S(2)}) %collective-permute-start.3) | collective-permute-done | bytes 131104 | tf_op jit(solution)/shard_map/ppermute | solution.py:548
  27.1 1.4 %collective-permute-done.4.three_ref = bf16[2,128,256]{2,1,0:T(8,128)(2,1)S(1)} collective-permute-done((bf16[2,128,256]{2,1,0:T(8,128)(2,1)S(1)}, bf16[2,128,256]{2,1,0:T(8,128)(2,1)S(1)}, u32[]{:S(2)}, u32[]{:S(2)}) %collective-permute-start.4) | collective-permute-done | bytes 131104 | tf_op jit(solution)/shard_map/ppermute | solution.py:548
  28.5 0.5 shard_map.123
  29.1 0.1 collective-permute-start.5
  29.2 2.2 %collective-permute-start.6 = (bf16[2,128,256]{2,1,0:T(8,128)(2,1)S(1)}, bf16[2,128,256]{2,1,0:T(8,128)(2,1)S(1)}, u32[]{:S(2)}, u32[]{:S(2)}) collective-permute-start(bf16[2,128,256]{2,1,0:T(8,128)(2,1)S(1)} %get-tuple-element.45.own_ref), channel_id=1, source_target_pairs={{0,128},{8,136},{16,144},{24,152},{32,160},{40,168},{48,176},{56,1... | collective-permute-start | bytes 393224 | tf_op jit(solution)/shard_map/ppermute | solution.py:564
  31.4 1.1 %collective-permute-start.7 = (bf16[2,128,128]{2,1,0:T(8,128)(2,1)S(1)}, bf16[2,128,128]{2,1,0:T(8,128)(2,1)S(1)}, u32[]{:S(2)}, u32[]{:S(2)}) collective-permute-start(bf16[2,128,128]{2,1,0:T(8,128)(2,1)S(1)} %get-tuple-element.46), channel_id=1, source_target_pairs={{0,192},{8,200},{16,208},{24,216},{32,224},{40,232},{48,240},{56,2... | collective-permute-start | bytes 196616 | tf_op jit(solution)/shard_map/ppermute | solution.py:565
  32.5 5.1 %collective-permute-done.7.three_ref = bf16[2,128,128]{2,1,0:T(8,128)(2,1)S(1)} collective-permute-done((bf16[2,128,128]{2,1,0:T(8,128)(2,1)S(1)}, bf16[2,128,128]{2,1,0:T(8,128)(2,1)S(1)}, u32[]{:S(2)}, u32[]{:S(2)}) %collective-permute-start.7) | collective-permute-done | bytes 65568 | tf_op jit(solution)/shard_map/ppermute | solution.py:565
  37.5 0.8 %collective-permute-done.5.one_ref = bf16[2,128,256]{2,1,0:T(8,128)(2,1)S(1)} collective-permute-done((bf16[2,128,256]{2,1,0:T(8,128)(2,1)S(1)}, bf16[2,128,256]{2,1,0:T(8,128)(2,1)S(1)}, u32[]{:S(2)}, u32[]{:S(2)}) %collective-permute-start.5) | collective-permute-done | bytes 131104 | tf_op jit(solution)/shard_map/ppermute | solution.py:563
  38.3 0.0 collective-permute-done.6.two_ref
  38.3 0.6 %shard_map.124 = (bf16[2,128,128]{2,1,0:T(8,128)(2,1)S(1)}, bf16[2,128,128]{2,1,0:T(8,128)(2,1)S(1)}) custom-call(bf16[2,128,256]{2,1,0:T(8,128)(2,1)S(1)} %get-tuple-element.45.own_ref, bf16[2,128,256]{2,1,0:T(8,128)(2,1)S(1)} %collective-permute-done.5.one_ref, bf16[2,128,256]{2,1,0:T(8,128)(2,1)S(1)} %collective-permute-done.6.two_ref, ...), custom_call_target="tpu_custom_call" | custom-call | flops 60000000 | bytes 1000000 | tf_op jit(solution)/shard_map/pallas_call | solution.py:493
  38.9 0.3 collective-permute-start.8
  39.2 1.2 %collective-permute-done.8.got_ref = bf16[2,128,128]{2,1,0:T(8,128)(2,1)S(1)} collective-permute-done((bf16[2,128,128]{2,1,0:T(8,128)(2,1)S(1)}, bf16[2,128,128]{2,1,0:T(8,128)(2,1)S(1)}, u32[]{:S(2)}, u32[]{:S(2)}) %collective-permute-start.8) | collective-permute-done | bytes 65568 | tf_op jit(solution)/shard_map/ppermute | solution.py:571
  40.5 0.0 collective-permute-done.11.behind_w_ref
  40.5 0.2 collective-permute-start.12
  40.6 0.0 copy-done.1
  40.6 0.0 copy-done.2
  40.6 0.4 shard_map.125
  41.1 0.1 collective-permute-start.9
  41.2 3.2 %collective-permute-start.10 = (bf16[64,512]{1,0:T(8,128)(2,1)S(1)}, bf16[64,512]{1,0:T(8,128)(2,1)S(1)}, u32[]{:S(2)}, u32[]{:S(2)}) collective-permute-start(bf16[64,512]{1,0:T(8,128)(2,1)S(1)} %get-tuple-element.52), channel_id=1, source_target_pairs={{0,7},{1,0},{2,1},{3,2},{4,3},{5,4},{6,5},{7,6},{8,9},{9,10},{10,1... | collective-permute-start | bytes 196616 | tf_op jit(solution)/shard_map/ppermute | solution.py:586
  44.4 0.5 shard_map.126.kept_ref
  44.9 1.4 %collective-permute-done.10.ahead_ref = bf16[64,512]{1,0:T(8,128)(2,1)S(1)} collective-permute-done((bf16[64,512]{1,0:T(8,128)(2,1)S(1)}, bf16[64,512]{1,0:T(8,128)(2,1)S(1)}, u32[]{:S(2)}, u32[]{:S(2)}) %collective-permute-start.10) | collective-permute-done | bytes 65568 | tf_op jit(solution)/shard_map/ppermute | solution.py:586
  46.3 1.4 %collective-permute-done.9.behind_ref = bf16[96,512]{1,0:T(8,128)(2,1)S(1)} collective-permute-done((bf16[96,512]{1,0:T(8,128)(2,1)S(1)}, bf16[96,512]{1,0:T(8,128)(2,1)S(1)}, u32[]{:S(2)}, u32[]{:S(2)}) %collective-permute-start.9) | collective-permute-done | bytes 98336 | tf_op jit(solution)/shard_map/ppermute | solution.py:585
  47.7 0.0 collective-permute-done.12.ahead_w_ref
  47.7 0.8 %shard_map.128 = (bf16[32,2048]{1,0:T(8,128)(2,1)S(1)}, bf16[32,2048]{1,0:T(8,128)(2,1)S(1)}) custom-call(f32[96,2048]{1,0:T(8,128)S(1)} %shard_map.126.kept_ref, bf16[96,512]{1,0:T(8,128)(2,1)S(1)} %collective-permute-done.9.behind_ref, bf16[64,512]{1,0:T(8,128)(2,1)S(1)} %collective-permute-done.10.ahead_ref, ...), custom_call_target="tpu_custom_call" | custom-call | flops 200000000 | bytes 4000000 | tf_op jit(solution)/shard_map/pallas_call | solution.py:493
  48.5 1.4 %collective-permute-start.13 = (bf16[32,2048]{1,0:T(8,128)(2,1)S(1)}, bf16[32,2048]{1,0:T(8,128)(2,1)S(1)}, u32[]{:S(2)}, u32[]{:S(2)}) collective-permute-start(bf16[32,2048]{1,0:T(8,128)(2,1)S(1)} %get-tuple-element.55), channel_id=1, source_target_pairs={{0,5},{1,6},{2,7},{3,0},{4,1},{5,2},{6,3},{7,4},{8,11},{9,12},{10,... | collective-permute-start | bytes 393224 | tf_op jit(solution)/shard_map/ppermute | solution.py:598
  49.9 3.2 %collective-permute-start.14 = (bf16[32,2048]{1,0:T(8,128)(2,1)S(1)}, bf16[32,2048]{1,0:T(8,128)(2,1)S(1)}, u32[]{:S(2)}, u32[]{:S(2)}) collective-permute-start(bf16[32,2048]{1,0:T(8,128)(2,1)S(1)} %get-tuple-element.56), channel_id=1, source_target_pairs={{0,2},{1,3},{2,4},{3,5},{4,6},{5,7},{6,0},{7,1},{8,14},{9,15},{10,... | collective-permute-start | bytes 393224 | tf_op jit(solution)/shard_map/ppermute | solution.py:599
  53.1 0.8 %shard_map.127.own_ref = f32[32,2048]{1,0:T(8,128)S(1)} custom-call(f32[96,2048]{1,0:T(8,128)S(1)} %shard_map.126.kept_ref, bf16[96,512]{1,0:T(8,128)(2,1)S(1)} %collective-permute-done.9.behind_ref, bf16[64,512]{1,0:T(8,128)(2,1)S(1)} %collective-permute-done.10.ahead_ref, bf16[512,2048]{1,0:T(8,128)(2,1)S(1)} %collective-permute-done.11.behind_w_ref, ...), custom_call_target="tpu_custom_call" | custom-call | flops 200000000 | bytes 4000000 | tf_op jit(solution)/shard_map/pallas_call | solution.py:493
  53.9 6.0 %collective-permute-done.13.one_ref = bf16[32,2048]{1,0:T(8,128)(2,1)S(1)} collective-permute-done((bf16[32,2048]{1,0:T(8,128)(2,1)S(1)}, bf16[32,2048]{1,0:T(8,128)(2,1)S(1)}, u32[]{:S(2)}, u32[]{:S(2)}) %collective-permute-start.13) | collective-permute-done | bytes 131104 | tf_op jit(solution)/shard_map/ppermute | solution.py:598
  59.9 0.0 collective-permute-done.14.two_ref
  59.9 0.7 %shard_map.129 = bf16[32,2048]{1,0:T(8,128)(2,1)} custom-call(f32[32,2048]{1,0:T(8,128)S(1)} %shard_map.127.own_ref, bf16[32,2048]{1,0:T(8,128)(2,1)S(1)} %collective-permute-done.13.one_ref, bf16[32,2048]{1,0:T(8,128)(2,1)S(1)} %collective-permute-done.14.two_ref), custom_call_target="tpu_custom_call" | custom-call | flops 1000000 | bytes 800000 | tf_op jit(solution)/shard_map/pallas_call | solution.py:493
  (2 shorter events, 0.0 us)
Async XLA Ops:
  0.0 7.1 %copy-start.4 = (bf16[256,256]{1,0:T(8,128)(2,1)S(1)}, bf16[256,256]{1,0:T(8,128)(2,1)}, u32[]{:S(2)}) copy-start(bf16[256,256]{1,0:T(8,128)(2,1)} %k_ref.3) | copy-start | bytes 393220
  0.0 7.1 %copy-start.3 = (bf16[256,512]{1,0:T(8,128)(2,1)S(1)}, bf16[256,512]{1,0:T(8,128)(2,1)}, u32[]{:S(2)}) copy-start(bf16[256,512]{1,0:T(8,128)(2,1)} %v_ref.3) | copy-start | bytes 786436
  0.0 1.7 %copy-start = (bf16[512,2048]{1,0:T(8,128)(2,1)S(1)}, bf16[512,2048]{1,0:T(8,128)(2,1)}, u32[]{:S(2)}) copy-start(bf16[512,2048]{1,0:T(8,128)(2,1)} %weight_ref.1) | copy-start | bytes 6291460
  0.0 7.1 %copy-start.11 = (s32[256]{0:T(256)S(1)}, s32[256]{0:T(256)}, u32[]{:S(2)}) copy-start(s32[256]{0:T(256)} %param.18) | copy-start | bytes 3076
  0.0 7.1 %copy-start.9 = (f32[4,256]{1,0:T(4,128)S(1)}, f32[4,256]{1,0:T(4,128)}, u32[]{:S(2)}) copy-start(f32[4,256]{1,0:T(4,128)} %decay_ref.3) | copy-start | bytes 12292
  0.0 7.1 %copy-start.7 = (f32[4,256]{1,0:T(4,128)S(1)}, f32[4,256]{1,0:T(4,128)}, u32[]{:S(2)}) copy-start(f32[4,256]{1,0:T(4,128)} %beta_ref.3) | copy-start | bytes 12292
  0.0 7.1 %copy-start.8 = (f32[4,256]{1,0:T(4,128)S(1)}, f32[4,256]{1,0:T(4,128)}, u32[]{:S(2)}) copy-start(f32[4,256]{1,0:T(4,128)} %wk_ref.3) | copy-start | bytes 12292
  0.0 7.1 %copy-start.6 = (f32[4,512]{1,0:T(4,128)S(1)}, f32[4,512]{1,0:T(4,128)}, u32[]{:S(2)}) copy-start(f32[4,512]{1,0:T(4,128)} %wv_ref.3) | copy-start | bytes 24580
  1.7 38.8 %collective-permute-start.11 = (bf16[512,2048]{1,0:T(8,128)(2,1)S(1)}, bf16[512,2048]{1,0:T(8,128)(2,1)S(1)}, u32[]{:S(2)}, u32[]{:S(2)}) collective-permute-start(bf16[512,2048]{1,0:T(8,128)(2,1)S(1)} %copy-done), channel_id=1, source_target_pairs={{0,1},{1,2},{2,3},{3,4},{4,5},{5,6},{6,7},{7,0},{8,15},{9,8},{10,9... | collective-permute-start | bytes 6291464 | tf_op jit(solution)/shard_map/ppermute | solution.py:521
  3.6 5.7 %collective-permute-start = (bf16[16,1024]{1,0:T(8,128)(2,1)}, bf16[16,1024]{1,0:T(8,128)(2,1)S(1)}, u32[]{:S(2)}, u32[]{:S(2)}) collective-permute-start(bf16[16,1024]{1,0:T(8,128)(2,1)} %shard_map.118), channel_id=1, source_target_pairs={{0,8},{8,16},{16,24},{24,32},{32,40},{40,48},{48,56},{56,64},{64,7... | collective-permute-start | bytes 98312 | tf_op jit(solution)/shard_map/ppermute | solution.py:524
  9.3 10.9 %copy-start.5 = (bf16[256,256]{1,0:T(8,128)(2,1)S(1)}, bf16[256,256]{1,0:T(8,128)(2,1)}, u32[]{:S(2)}) copy-start(bf16[256,256]{1,0:T(8,128)(2,1)} %q_ref.3) | copy-start | bytes 393220
  9.3 10.9 %copy-start.10 = (f32[4,256]{1,0:T(4,128)S(1)}, f32[4,256]{1,0:T(4,128)}, u32[]{:S(2)}) copy-start(f32[4,256]{1,0:T(4,128)} %wq_ref.1) | copy-start | bytes 12292
  12.7 1.4 %collective-permute-start.1 = (bf16[2,128,256]{2,1,0:T(8,128)(2,1)S(1)}, bf16[2,128,256]{2,1,0:T(8,128)(2,1)S(1)}, u32[]{:S(2)}, u32[]{:S(2)}) collective-permute-start(bf16[2,128,256]{2,1,0:T(8,128)(2,1)S(1)} %get-tuple-element.44), channel_id=1, source_target_pairs={{0,8},{8,0},{16,24},{24,16},{32,40},{40,32},{48,56},{56,48},{64,72... | collective-permute-start | bytes 393224 | tf_op jit(solution)/shard_map/ppermute | solution.py:546
  14.3 10.8 %collective-permute-start.2 = (bf16[2,128,256]{2,1,0:T(8,128)(2,1)S(1)}, bf16[2,128,256]{2,1,0:T(8,128)(2,1)S(1)}, u32[]{:S(2)}, u32[]{:S(2)}) collective-permute-start(bf16[2,128,256]{2,1,0:T(8,128)(2,1)S(1)} %shard_map.122.own_ref), channel_id=1, source_target_pairs={{0,16},{8,24},{16,32},{24,40},{32,48},{40,56},{48,0},{56,8},{64,80... | collective-permute-start | bytes 393224 | tf_op jit(solution)/shard_map/ppermute | solution.py:548
  19.2 7.9 %collective-permute-start.3 = (bf16[2,128,256]{2,1,0:T(8,128)(2,1)S(1)}, bf16[2,128,256]{2,1,0:T(8,128)(2,1)S(1)}, u32[]{:S(2)}, u32[]{:S(2)}) collective-permute-start(bf16[2,128,256]{2,1,0:T(8,128)(2,1)S(1)} %shard_map.122.own_ref), channel_id=1, source_target_pairs={{0,32},{8,40},{16,48},{24,56},{32,0},{40,8},{48,16},{56,24},{64,96... | collective-permute-start | bytes 393224 | tf_op jit(solution)/shard_map/ppermute | solution.py:548
  19.2 9.3 %collective-permute-start.4 = (bf16[2,128,256]{2,1,0:T(8,128)(2,1)S(1)}, bf16[2,128,256]{2,1,0:T(8,128)(2,1)S(1)}, u32[]{:S(2)}, u32[]{:S(2)}) collective-permute-start(bf16[2,128,256]{2,1,0:T(8,128)(2,1)S(1)} %shard_map.122.own_ref), channel_id=1, source_target_pairs={{0,48},{8,56},{16,0},{24,8},{32,16},{40,24},{48,32},{56,40},{64,11... | collective-permute-start | bytes 393224 | tf_op jit(solution)/shard_map/ppermute | solution.py:548
  20.2 20.4 %copy-start.1 = (bf16[256,512]{1,0:T(8,128)(2,1)S(1)}, bf16[256,512]{1,0:T(8,128)(2,1)}, u32[]{:S(2)}) copy-start(bf16[256,512]{1,0:T(8,128)(2,1)} %gate_ref.1) | copy-start | bytes 786436
  20.2 20.4 %copy-start.2 = (f32[128]{0:T(128)S(1)}, f32[128]{0:T(128)}, u32[]{:S(2)}) copy-start(f32[128]{0:T(128)} %param.22) | copy-start | bytes 1540
  29.1 9.2 %collective-permute-start.5 = (bf16[2,128,256]{2,1,0:T(8,128)(2,1)S(1)}, bf16[2,128,256]{2,1,0:T(8,128)(2,1)S(1)}, u32[]{:S(2)}, u32[]{:S(2)}) collective-permute-start(bf16[2,128,256]{2,1,0:T(8,128)(2,1)S(1)} %get-tuple-element.45.own_ref), channel_id=1, source_target_pairs={{0,64},{8,72},{16,80},{24,88},{32,96},{40,104},{48,112},{56,120},{... | collective-permute-start | bytes 393224 | tf_op jit(solution)/shard_map/ppermute | solution.py:563
  29.2 9.1 %collective-permute-start.6 = (bf16[2,128,256]{2,1,0:T(8,128)(2,1)S(1)}, bf16[2,128,256]{2,1,0:T(8,128)(2,1)S(1)}, u32[]{:S(2)}, u32[]{:S(2)}) collective-permute-start(bf16[2,128,256]{2,1,0:T(8,128)(2,1)S(1)} %get-tuple-element.45.own_ref), channel_id=1, source_target_pairs={{0,128},{8,136},{16,144},{24,152},{32,160},{40,168},{48,176},{56,1... | collective-permute-start | bytes 393224 | tf_op jit(solution)/shard_map/ppermute | solution.py:564
  31.4 6.1 %collective-permute-start.7 = (bf16[2,128,128]{2,1,0:T(8,128)(2,1)S(1)}, bf16[2,128,128]{2,1,0:T(8,128)(2,1)S(1)}, u32[]{:S(2)}, u32[]{:S(2)}) collective-permute-start(bf16[2,128,128]{2,1,0:T(8,128)(2,1)S(1)} %get-tuple-element.46), channel_id=1, source_target_pairs={{0,192},{8,200},{16,208},{24,216},{32,224},{40,232},{48,240},{56,2... | collective-permute-start | bytes 196616 | tf_op jit(solution)/shard_map/ppermute | solution.py:565
  38.9 1.5 %collective-permute-start.8 = (bf16[2,128,128]{2,1,0:T(8,128)(2,1)S(1)}, bf16[2,128,128]{2,1,0:T(8,128)(2,1)S(1)}, u32[]{:S(2)}, u32[]{:S(2)}) collective-permute-start(bf16[2,128,128]{2,1,0:T(8,128)(2,1)S(1)} %get-tuple-element.49), channel_id=1, source_target_pairs={{0,8},{8,0},{16,24},{24,16},{32,40},{40,32},{48,56},{56,48},{64,72... | collective-permute-start | bytes 196616 | tf_op jit(solution)/shard_map/ppermute | solution.py:571
  40.5 7.2 %collective-permute-start.12 = (bf16[512,2048]{1,0:T(8,128)(2,1)S(1)}, bf16[512,2048]{1,0:T(8,128)(2,1)S(1)}, u32[]{:S(2)}, u32[]{:S(2)}) collective-permute-start(bf16[512,2048]{1,0:T(8,128)(2,1)S(1)} %collective-permute-done.11.behind_w_ref), channel_id=1, source_target_pairs={{0,8},{8,0},{16,24},{24,16},{32,40},{40,32},{48,56},{56,48},{64,72... | collective-permute-start | bytes 6291464 | tf_op jit(solution)/shard_map/ppermute | solution.py:573
  41.1 6.6 %collective-permute-start.9 = (bf16[96,512]{1,0:T(8,128)(2,1)S(1)}, bf16[96,512]{1,0:T(8,128)(2,1)S(1)}, u32[]{:S(2)}, u32[]{:S(2)}) collective-permute-start(bf16[96,512]{1,0:T(8,128)(2,1)S(1)} %get-tuple-element.51), channel_id=1, source_target_pairs={{0,1},{1,2},{2,3},{3,4},{4,5},{5,6},{6,7},{7,0},{8,15},{9,8},{10,9... | collective-permute-start | bytes 294920 | tf_op jit(solution)/shard_map/ppermute | solution.py:585
  41.2 5.1 %collective-permute-start.10 = (bf16[64,512]{1,0:T(8,128)(2,1)S(1)}, bf16[64,512]{1,0:T(8,128)(2,1)S(1)}, u32[]{:S(2)}, u32[]{:S(2)}) collective-permute-start(bf16[64,512]{1,0:T(8,128)(2,1)S(1)} %get-tuple-element.52), channel_id=1, source_target_pairs={{0,7},{1,0},{2,1},{3,2},{4,3},{5,4},{6,5},{7,6},{8,9},{9,10},{10,1... | collective-permute-start | bytes 196616 | tf_op jit(solution)/shard_map/ppermute | solution.py:586
  48.5 11.4 %collective-permute-start.13 = (bf16[32,2048]{1,0:T(8,128)(2,1)S(1)}, bf16[32,2048]{1,0:T(8,128)(2,1)S(1)}, u32[]{:S(2)}, u32[]{:S(2)}) collective-permute-start(bf16[32,2048]{1,0:T(8,128)(2,1)S(1)} %get-tuple-element.55), channel_id=1, source_target_pairs={{0,5},{1,6},{2,7},{3,0},{4,1},{5,2},{6,3},{7,4},{8,11},{9,12},{10,... | collective-permute-start | bytes 393224 | tf_op jit(solution)/shard_map/ppermute | solution.py:598
  49.9 10.0 %collective-permute-start.14 = (bf16[32,2048]{1,0:T(8,128)(2,1)S(1)}, bf16[32,2048]{1,0:T(8,128)(2,1)S(1)}, u32[]{:S(2)}, u32[]{:S(2)}) collective-permute-start(bf16[32,2048]{1,0:T(8,128)(2,1)S(1)} %get-tuple-element.56), channel_id=1, source_target_pairs={{0,2},{1,3},{2,4},{3,5},{4,6},{5,7},{6,0},{7,1},{8,14},{9,15},{10,... | collective-permute-start | bytes 393224 | tf_op jit(solution)/shard_map/ppermute | solution.py:599

commit v10 on v9

--- a/solution.py
+++ b/solution.py
@@ -28,13 +28,8 @@
     return [(i, i ^ 1) for i in range(CTX)]
 
 
-def along_x(step):
-    return [
-        ((y * 4 + x) * 2 + c, (y * 4 + (x + step) % 4) * 2 + c)
-        for y in range(4)
-        for x in range(4)
-        for c in range(2)
-    ]
+def pairs_x(step):
+    return [(i, i ^ (step * CORES)) for i in range(CTX)]
 
 
 def along_y(step):
@@ -124,10 +119,11 @@
 
 
 LEVELS = (8, 16, 32, 64)
+HALF = TOK // 2
 
 
 def block_masks():
-    row, col = rows_and_columns()
+    row, col = rows_and_columns((HALF, HALF))
     out = []
     for size in LEVELS:
         shift = size.bit_length() - 1
@@ -141,7 +137,7 @@
     if compact.shape[0] < 16:
         compact = jnp.concatenate([compact] * (16 // compact.shape[0]), axis=0)
     compact = compact.astype(BF16)
-    return jnp.concatenate([compact] * (TOK // compact.shape[0]), axis=0) * mask
+    return jnp.concatenate([compact] * (HALF // compact.shape[0]), axis=0) * mask
 
 
 def high_low(value):
@@ -159,27 +155,21 @@
 
 
 def gather_blocks(a, size, below):
-    lane = lax.broadcasted_iota(jnp.int32, (size, 128), 1) >> (size.bit_length() - 1)
-    out = []
-    for half in range(2):
-        total = None
-        for k in range(128 // size):
-            block = half * (128 // size) + k
-            if below and block % 2:
-                continue
-            top = (block + (1 if below else 0)) * size
-            piece = jnp.where(lane == k, a[top : top + size, half * 128 : half * 128 + 128], 0.0)
-            total = piece if total is None else total + piece
-        out.append(total)
-    return jnp.concatenate(out, axis=1)
+    lane = lax.broadcasted_iota(jnp.int32, (size, HALF), 1) >> (size.bit_length() - 1)
+    total = None
+    for k in range(0, HALF // size, 2 if below else 1):
+        top = (k + (1 if below else 0)) * size
+        piece = jnp.where(lane == k, a[top : top + size, :], 0.0)
+        total = piece if total is None else total + piece
+    return total
 
 
 def each(fn, *lists):
     return [fn(*items) for items in zip(*lists)]
 
 
-def half_inverses(many, masks):
-    row, col = rows_and_columns((8, TOK))
+def unit_inverses(many, masks):
+    row, col = rows_and_columns((8, HALF))
     eye = ((col & 7) == row).astype(F32)
     d = each(lambda a: gather_blocks(a, 8, False), many)
     t = each(lambda d: eye - d, d)
@@ -191,7 +181,7 @@
         e = each(lambda a: gather_blocks(a, size, True), many)
         y = each(lambda e, t: times(e, t, masks[2 * i]), e, t)
         z = each(lambda t, y: times(t, y, masks[2 * i + 1]), t, y)
-        lane = lax.broadcasted_iota(jnp.int32, (size, TOK), 1)
+        lane = lax.broadcasted_iota(jnp.int32, (size, HALF), 1)
         left = ((lane >> (size.bit_length() - 1)) & 1) == 0
         t = each(
             lambda t, z: jnp.concatenate([jnp.where(left, t, 0.0), jnp.where(left, -z, t)], axis=0),
@@ -200,20 +190,20 @@
     return t
 
 
-def solve_halves(a, t, beta, right):
-    scaled = each(lambda t, b: parts(t * b, 2), t, beta)
-    plain = each(lambda t: parts(t[:, 128:], 2), t)
-    cross = each(lambda a: parts(a[128:, :128], 2), a)
+def solve_halves(a, upper, lower, beta, right):
+    upper_beta = each(lambda t, b: parts(t * b[:, :HALF], 2), upper, beta)
+    lower_beta = each(lambda t, b: parts(t * b[:, HALF:], 2), lower, beta)
+    plain = each(lambda t: parts(t, 2), lower)
+    cross = each(lambda a: parts(a[HALF:, :HALF], 2), a)
     first = each(
-        lambda s, r: (mm(s[0][:, :128], r[:128]) + mm(s[1][:, :128], r[:128])).astype(BF16),
-        scaled, right,
+        lambda s, r: (mm(s[0], r[:HALF]) + mm(s[1], r[:HALF])).astype(BF16), upper_beta, right
     )
     moved = each(lambda c, x: (mm(c[0], x) + mm(c[1], x)).astype(BF16), cross, first)
     second = each(
         lambda s, r, p, y: (
-            mm(s[0][:, 128:], r[128:]) + mm(s[1][:, 128:], r[128:]) - mm(p[0], y) - mm(p[1], y)
+            mm(s[0], r[HALF:]) + mm(s[1], r[HALF:]) - mm(p[0], y) - mm(p[1], y)
         ).astype(BF16),
-        scaled, right, plain, moved,
+        lower_beta, right, plain, moved,
     )
     return each(lambda x, y: jnp.concatenate([x, y], axis=0), first, second)
 
@@ -293,7 +283,7 @@
     heads = range(HEADS)
     masks = [mask_ref[i] for i in range(2 * len(LEVELS))]
     a = [factor_ref[h] * gram[h // 2] for h in heads]
-    inverses = half_inverses(a, masks)
+    inverses = unit_inverses([m[:HALF, :HALF] for m in a] + [m[HALF:, HALF:] for m in a], masks)
     right = [
         jnp.concatenate(
             [
@@ -304,7 +294,7 @@
         )
         for h in heads
     ]
-    solved = solve_halves(a, inverses, [beta[h : h + 1] for h in heads], right)
+    solved = solve_halves(a, inverses[:HEADS], inverses[HEADS:], [beta[h : h + 1] for h in heads], right)
     faded = [(flipped[h // 2] * last_ref[h : h + 1, :]).astype(BF16) for h in heads]
     both = each(mm, faded, solved)
     r, c = rows_and_columns((DK, DK))
@@ -368,7 +358,7 @@
 def row_kernel(own_ref, one_ref, two_ref, three_ref, after_ref, before_ref, total_ref, alone_ref, slots):
     x = (lax.axis_index("ctx") // CORES) % CHIPS_X
     for step, ref in enumerate((own_ref, one_ref, two_ref, three_ref)):
-        slots[(x + CHIPS_X - step) % CHIPS_X] = ref[...]
+        slots[x ^ step] = ref[...]
     r, c = rows_and_columns((DK, DK + DV))
     start = (r == c).astype(BF16)
     run = [slots[0, k] for k in range(2)]
@@ -528,7 +518,7 @@
         [
             ((GROUPS, TOK, DK), BF16), ((TOK, HEADS * DV), BF16), ((HEADS, TOK, TOK), F32),
             ((HEADS, TOK, 128), F32), ((HEADS, TOK), F32), ((RIM, 128), F32), ((RIM, 768), BF16),
-            ((2 * len(LEVELS), TOK, TOK), BF16),
+            ((2 * len(LEVELS), HALF, HALF), BF16),
         ],
         [key_in, value_in, log_decay, beta_gate, doc_row, conv_key, conv_value],
         [
@@ -545,7 +535,7 @@
     )
     other = lax.ppermute(give, "ctx", core_swap())
     (pair,) = call(pair_kernel, [(wide, BF16)], [own, other], flops=20_000_000, moved=400_000)
-    near = [lax.ppermute(pair, "ctx", along_x(k)) for k in (1, 2, 3)]
+    near = [lax.ppermute(pair, "ctx", pairs_x(k)) for k in (1, 2, 3)]
     local, reach = call(
         output_kernel,
         [((HEADS, TOK, DV), F32), ((HEADS, TOK, DK), BF16)],

time: 60.7 us -> 60.7 us (level)
    pallas_call x11, Pallas kernels: 10.3 us -> 9.62 us  [call(): pl.pallas_call(kernel, grid=(1,) if blocked else (), out_shape=[jax.Shape...]
  transfers between devices with their start and end apart: 15 -> 15, of which waited for: 11 -> 10; matrix products, arithmetic and copies ran while one was open for 0% -> 0% of each run, Pallas kernels for 14% -> 13%
where the time goes in v10:
time: 60.7 us; the launch traced here: 60.6 us
  waiting for transfers between devices  25.8 us (43%)
  starting transfers between devices  23.4 us (39%)
  Pallas kernels  11.1 us (18%)
    pallas_call x11, Pallas kernels, call(): pl.pallas_call(kernel, grid=(1,) if blocked else (), out_shape=[jax.Shape...  9.62 us
    ppermute x3, waiting for transfers between devices, on_device(): near = [lax.ppermute(pair, 'ctx', pairs_x(k)) for k in (1, 2, 3)]  7.79 us
    ppermute x3, starting transfers between devices, on_device(): near = [lax.ppermute(pair, 'ctx', pairs_x(k)) for k in (1, 2, 3)]  6.41 us
    ppermute x1, waiting for transfers between devices, on_device(): far_part = lax.ppermute(far_part, ('ctx', 'head'), mirrored(-3))  6.01 us
    ppermute x1, waiting for transfers between devices, on_device(): lax.ppermute(alone, 'ctx', along_y(3))  4.88 us
    ppermute x1, starting transfers between devices, on_device(): rim = lax.ppermute(edge, 'ctx', [(i, (i + 1) % CTX) for i in range(CTX)])  3.49 us
    ppermute x1, starting transfers between devices, on_device(): from_ahead = lax.ppermute(to_behind, ('ctx', 'head'), mirrored(-1))  3.22 us
    ppermute x1, starting transfers between devices, on_device(): near_part = lax.ppermute(near_part, ('ctx', 'head'), mirrored(2))  3.17 us
  transfers between devices with their start and end apart: 15, of which 10 were waited for; matrix products, arithmetic and copies ran while one was open for 0% of the time, Pallas kernels for 13%

profile of v10, /device:TPU:6, one launch (start us, length us, event | category | flops | bytes accessed | tf_op | source)
XLA Modules:
  0.0 60.6 jit_solution(18297146744674328282)
XLA Ops:
  0.0 0.0 copy-start.3
  0.0 0.0 copy-start
  0.0 0.0 copy-start.11
  0.0 0.0 copy-start.9
  0.0 0.0 copy-start.7
  0.0 0.0 copy-start.8
  0.0 0.0 copy-start.6
  0.1 1.5 %shard_map.118 = bf16[16,1024]{1,0:T(8,128)(2,1)} custom-call(bf16[256,256]{1,0:T(8,128)(2,1)} %k_ref.3, bf16[256,512]{1,0:T(8,128)(2,1)} %v_ref.3, bf16[256,256]{1,0:T(8,128)(2,1)} %q_ref.3), custom_call_target="tpu_custom_call" | custom-call | flops 5000000000 | tf_op jit(solution)/shard_map/pallas_call | solution.py:503
  1.5 0.1 copy-done
  1.7 1.9 %collective-permute-start.11 = (bf16[512,2048]{1,0:T(8,128)(2,1)S(1)}, bf16[512,2048]{1,0:T(8,128)(2,1)S(1)}, u32[]{:S(2)}, u32[]{:S(2)}) collective-permute-start(bf16[512,2048]{1,0:T(8,128)(2,1)S(1)} %copy-done), channel_id=1, source_target_pairs={{0,1},{1,2},{2,3},{3,4},{4,5},{5,6},{6,7},{7,0},{8,15},{9,8},{10,9... | collective-permute-start | bytes 6291464 | tf_op jit(solution)/shard_map/ppermute | solution.py:511
  3.6 3.5 %collective-permute-start = (bf16[16,1024]{1,0:T(8,128)(2,1)}, bf16[16,1024]{1,0:T(8,128)(2,1)S(1)}, u32[]{:S(2)}, u32[]{:S(2)}) collective-permute-start(bf16[16,1024]{1,0:T(8,128)(2,1)} %shard_map.118), channel_id=1, source_target_pairs={{0,8},{8,16},{16,24},{24,32},{32,40},{40,48},{48,56},{56,64},{64,7... | collective-permute-start | bytes 98312 | tf_op jit(solution)/shard_map/ppermute | solution.py:514
  7.1 0.0 copy-done.4
  7.1 0.0 copy-done.3
  7.1 0.0 copy-done.11
  7.1 0.0 copy-done.9
  7.1 0.0 copy-done.7
  7.1 0.0 copy-done.8
  7.1 0.0 copy-done.6
  7.1 1.3 %shard_map.119 = (bf16[2,256,128]{2,1,0:T(8,128)(2,1)S(1)}, bf16[256,512]{1,0:T(8,128)(2,1)S(1)}, f32[4,256,256]{2,1,0:T(8,128)S(1)}, f32[4,256,128]{2,1,0:T(8,1...) custom-call(bf16[256,256]{1,0:T(8,128)(2,1)S(1)} %copy-done.4, ...), custom_call_target="tpu_custom_call" | custom-call | flops 500000000 | tf_op jit(solution)/shard_map/pallas_call | solution.py:483
  8.4 0.9 %collective-permute-done.rim_ref = bf16[16,1024]{1,0:T(8,128)(2,1)S(1)} collective-permute-done((bf16[16,1024]{1,0:T(8,128)(2,1)}, bf16[16,1024]{1,0:T(8,128)(2,1)S(1)}, u32[]{:S(2)}, u32[]{:S(2)}) %collective-permute-start) | collective-permute-done | bytes 32800 | tf_op jit(solution)/shard_map/ppermute | solution.py:514
  9.3 0.0 copy-start.5
  9.3 2.9 %shard_map.120 = (bf16[4,256,256]{2,1,0:T(8,128)(2,1)S(1)}, bf16[2,256,128]{2,1,0:T(8,128)(2,1)S(1)}, bf16[2,128,256]{2,1,0:T(8,128)(2,1)S(1)}, bf16[2,128,256]{2,1,0:T(8,128)(2,1)S(1)}) custom-call(bf16[16,1024]{1,0:T(8,128)(2,1)S(1)} %collective-permute-done.rim_ref, bf16[16,768]{1,0:T(8,128)(2,1)S(1)} %get-tuple-element.31.head_ref, ...), custom_call_target="tpu_custom_call" | custom-call | flops 4000000000 | bytes 2000000 | tf_op jit(solution)/shard_map/pallas_call | solution.py:483
  12.2 0.1 collective-permute-start.1
  12.3 1.3 %collective-permute-done.1.got_ref.other_ref = bf16[2,128,256]{2,1,0:T(8,128)(2,1)S(1)} collective-permute-done((bf16[2,128,256]{2,1,0:T(8,128)(2,1)S(1)}, bf16[2,128,256]{2,1,0:T(8,128)(2,1)S(1)}, u32[]{:S(2)}, u32[]{:S(2)}) %collective-permute-start.1) | collective-permute-done | bytes 131104 | tf_op jit(solution)/shard_map/ppermute | solution.py:536
  13.6 0.2 shard_map.122.own_ref
  13.8 0.6 %collective-permute-start.2 = (bf16[2,128,256]{2,1,0:T(8,128)(2,1)S(1)}, bf16[2,128,256]{2,1,0:T(8,128)(2,1)S(1)}, u32[]{:S(2)}, u32[]{:S(2)}) collective-permute-start(bf16[2,128,256]{2,1,0:T(8,128)(2,1)S(1)} %shard_map.122.own_ref), channel_id=1, source_target_pairs={{0,16},{8,24},{16,0},{24,8},{32,48},{40,56},{48,32},{56,40},{64,80... | collective-permute-start | bytes 393224 | tf_op jit(solution)/shard_map/ppermute | solution.py:538
  14.5 5.8 %collective-permute-start.3 = (bf16[2,128,256]{2,1,0:T(8,128)(2,1)S(1)}, bf16[2,128,256]{2,1,0:T(8,128)(2,1)S(1)}, u32[]{:S(2)}, u32[]{:S(2)}) collective-permute-start(bf16[2,128,256]{2,1,0:T(8,128)(2,1)S(1)} %shard_map.122.own_ref), channel_id=1, source_target_pairs={{0,32},{8,40},{16,48},{24,56},{32,0},{40,8},{48,16},{56,24},{64,96... | collective-permute-start | bytes 393224 | tf_op jit(solution)/shard_map/ppermute | solution.py:538
  20.2 0.0 collective-permute-start.4
  20.2 0.0 copy-done.5
  20.2 0.0 copy-done.10
  20.3 0.0 copy-start.1
  20.3 0.0 copy-start.2
  20.3 0.8 %shard_map.121 = (f32[4,256,128]{2,1,0:T(8,128)S(1)}, bf16[4,256,128]{2,1,0:T(8,128)(2,1)S(1)}) custom-call(bf16[256,256]{1,0:T(8,128)(2,1)S(1)} %copy-done.5, bf16[16,1024]{1,0:T(8,128)(2,1)S(1)} %collective-permute-done.rim_ref, f32[4,256]{1,0:T(4,128)S(1)} %copy-done.9, s32[1,256]{1,0:T(1,128)S(1)} %bitcast.4, f32[4,256]{1,0:T(4,128)S(1)} %copy-done.10, ...), custom_call_target="tpu_custom_call" | custom-call | flops 2000000000 | bytes 2000000 | tf_op jit(solution)/shard_map/pallas_call | solution.py:483
  21.1 0.0 collective-permute-done.2.one_ref
  21.1 5.5 %collective-permute-done.3.two_ref = bf16[2,128,256]{2,1,0:T(8,128)(2,1)S(1)} collective-permute-done((bf16[2,128,256]{2,1,0:T(8,128)(2,1)S(1)}, bf16[2,128,256]{2,1,0:T(8,128)(2,1)S(1)}, u32[]{:S(2)}, u32[]{:S(2)}) %collective-permute-start.3) | collective-permute-done | bytes 131104 | tf_op jit(solution)/shard_map/ppermute | solution.py:538
  26.7 2.2 %collective-permute-done.4.three_ref = bf16[2,128,256]{2,1,0:T(8,128)(2,1)S(1)} collective-permute-done((bf16[2,128,256]{2,1,0:T(8,128)(2,1)S(1)}, bf16[2,128,256]{2,1,0:T(8,128)(2,1)S(1)}, u32[]{:S(2)}, u32[]{:S(2)}) %collective-permute-start.4) | collective-permute-done | bytes 131104 | tf_op jit(solution)/shard_map/ppermute | solution.py:538
  28.9 0.6 shard_map.123
  29.5 0.1 collective-permute-start.5
  29.6 2.2 %collective-permute-start.6 = (bf16[2,128,256]{2,1,0:T(8,128)(2,1)S(1)}, bf16[2,128,256]{2,1,0:T(8,128)(2,1)S(1)}, u32[]{:S(2)}, u32[]{:S(2)}) collective-permute-start(bf16[2,128,256]{2,1,0:T(8,128)(2,1)S(1)} %get-tuple-element.45.own_ref), channel_id=1, source_target_pairs={{0,128},{8,136},{16,144},{24,152},{32,160},{40,168},{48,176},{56,1... | collective-permute-start | bytes 393224 | tf_op jit(solution)/shard_map/ppermute | solution.py:554
  31.8 1.1 %collective-permute-start.7 = (bf16[2,128,128]{2,1,0:T(8,128)(2,1)S(1)}, bf16[2,128,128]{2,1,0:T(8,128)(2,1)S(1)}, u32[]{:S(2)}, u32[]{:S(2)}) collective-permute-start(bf16[2,128,128]{2,1,0:T(8,128)(2,1)S(1)} %get-tuple-element.46), channel_id=1, source_target_pairs={{0,192},{8,200},{16,208},{24,216},{32,224},{40,232},{48,240},{56,2... | collective-permute-start | bytes 196616 | tf_op jit(solution)/shard_map/ppermute | solution.py:555
  32.8 4.9 %collective-permute-done.7.three_ref = bf16[2,128,128]{2,1,0:T(8,128)(2,1)S(1)} collective-permute-done((bf16[2,128,128]{2,1,0:T(8,128)(2,1)S(1)}, bf16[2,128,128]{2,1,0:T(8,128)(2,1)S(1)}, u32[]{:S(2)}, u32[]{:S(2)}) %collective-permute-start.7) | collective-permute-done | bytes 65568 | tf_op jit(solution)/shard_map/ppermute | solution.py:555
  37.7 0.8 %collective-permute-done.5.one_ref = bf16[2,128,256]{2,1,0:T(8,128)(2,1)S(1)} collective-permute-done((bf16[2,128,256]{2,1,0:T(8,128)(2,1)S(1)}, bf16[2,128,256]{2,1,0:T(8,128)(2,1)S(1)}, u32[]{:S(2)}, u32[]{:S(2)}) %collective-permute-start.5) | collective-permute-done | bytes 131104 | tf_op jit(solution)/shard_map/ppermute | solution.py:553
  38.5 0.0 collective-permute-done.6.two_ref
  38.5 0.6 %shard_map.124 = (bf16[2,128,128]{2,1,0:T(8,128)(2,1)S(1)}, bf16[2,128,128]{2,1,0:T(8,128)(2,1)S(1)}) custom-call(bf16[2,128,256]{2,1,0:T(8,128)(2,1)S(1)} %get-tuple-element.45.own_ref, bf16[2,128,256]{2,1,0:T(8,128)(2,1)S(1)} %collective-permute-done.5.one_ref, bf16[2,128,256]{2,1,0:T(8,128)(2,1)S(1)} %collective-permute-done.6.two_ref, ...), custom_call_target="tpu_custom_call" | custom-call | flops 60000000 | bytes 1000000 | tf_op jit(solution)/shard_map/pallas_call | solution.py:483
  39.1 0.1 collective-permute-start.8
  39.2 1.2 %collective-permute-done.8.got_ref = bf16[2,128,128]{2,1,0:T(8,128)(2,1)S(1)} collective-permute-done((bf16[2,128,128]{2,1,0:T(8,128)(2,1)S(1)}, bf16[2,128,128]{2,1,0:T(8,128)(2,1)S(1)}, u32[]{:S(2)}, u32[]{:S(2)}) %collective-permute-start.8) | collective-permute-done | bytes 65568 | tf_op jit(solution)/shard_map/ppermute | solution.py:561
  40.5 0.0 collective-permute-done.11.behind_w_ref
  40.5 0.2 collective-permute-start.12
  40.6 0.0 copy-done.1
  40.6 0.0 copy-done.2
  40.6 0.4 shard_map.125
  41.1 0.1 collective-permute-start.9
  41.2 3.2 %collective-permute-start.10 = (bf16[64,512]{1,0:T(8,128)(2,1)S(1)}, bf16[64,512]{1,0:T(8,128)(2,1)S(1)}, u32[]{:S(2)}, u32[]{:S(2)}) collective-permute-start(bf16[64,512]{1,0:T(8,128)(2,1)S(1)} %get-tuple-element.52), channel_id=1, source_target_pairs={{0,7},{1,0},{2,1},{3,2},{4,3},{5,4},{6,5},{7,6},{8,9},{9,10},{10,1... | collective-permute-start | bytes 196616 | tf_op jit(solution)/shard_map/ppermute | solution.py:576
  44.4 0.5 shard_map.126.kept_ref
  44.9 1.4 %collective-permute-done.10.ahead_ref = bf16[64,512]{1,0:T(8,128)(2,1)S(1)} collective-permute-done((bf16[64,512]{1,0:T(8,128)(2,1)S(1)}, bf16[64,512]{1,0:T(8,128)(2,1)S(1)}, u32[]{:S(2)}, u32[]{:S(2)}) %collective-permute-start.10) | collective-permute-done | bytes 65568 | tf_op jit(solution)/shard_map/ppermute | solution.py:576
  46.3 1.4 %collective-permute-done.9.behind_ref = bf16[96,512]{1,0:T(8,128)(2,1)S(1)} collective-permute-done((bf16[96,512]{1,0:T(8,128)(2,1)S(1)}, bf16[96,512]{1,0:T(8,128)(2,1)S(1)}, u32[]{:S(2)}, u32[]{:S(2)}) %collective-permute-start.9) | collective-permute-done | bytes 98336 | tf_op jit(solution)/shard_map/ppermute | solution.py:575
  47.7 0.0 collective-permute-done.12.ahead_w_ref
  47.7 0.8 %shard_map.128 = (bf16[32,2048]{1,0:T(8,128)(2,1)S(1)}, bf16[32,2048]{1,0:T(8,128)(2,1)S(1)}) custom-call(f32[96,2048]{1,0:T(8,128)S(1)} %shard_map.126.kept_ref, bf16[96,512]{1,0:T(8,128)(2,1)S(1)} %collective-permute-done.9.behind_ref, bf16[64,512]{1,0:T(8,128)(2,1)S(1)} %collective-permute-done.10.ahead_ref, ...), custom_call_target="tpu_custom_call" | custom-call | flops 200000000 | bytes 4000000 | tf_op jit(solution)/shard_map/pallas_call | solution.py:483
  48.5 1.4 %collective-permute-start.13 = (bf16[32,2048]{1,0:T(8,128)(2,1)S(1)}, bf16[32,2048]{1,0:T(8,128)(2,1)S(1)}, u32[]{:S(2)}, u32[]{:S(2)}) collective-permute-start(bf16[32,2048]{1,0:T(8,128)(2,1)S(1)} %get-tuple-element.55), channel_id=1, source_target_pairs={{0,5},{1,6},{2,7},{3,0},{4,1},{5,2},{6,3},{7,4},{8,11},{9,12},{10,... | collective-permute-start | bytes 393224 | tf_op jit(solution)/shard_map/ppermute | solution.py:588
  49.9 3.2 %collective-permute-start.14 = (bf16[32,2048]{1,0:T(8,128)(2,1)S(1)}, bf16[32,2048]{1,0:T(8,128)(2,1)S(1)}, u32[]{:S(2)}, u32[]{:S(2)}) collective-permute-start(bf16[32,2048]{1,0:T(8,128)(2,1)S(1)} %get-tuple-element.56), channel_id=1, source_target_pairs={{0,2},{1,3},{2,4},{3,5},{4,6},{5,7},{6,0},{7,1},{8,14},{9,15},{10,... | collective-permute-start | bytes 393224 | tf_op jit(solution)/shard_map/ppermute | solution.py:589
  53.1 0.8 %shard_map.127.own_ref = f32[32,2048]{1,0:T(8,128)S(1)} custom-call(f32[96,2048]{1,0:T(8,128)S(1)} %shard_map.126.kept_ref, bf16[96,512]{1,0:T(8,128)(2,1)S(1)} %collective-permute-done.9.behind_ref, bf16[64,512]{1,0:T(8,128)(2,1)S(1)} %collective-permute-done.10.ahead_ref, bf16[512,2048]{1,0:T(8,128)(2,1)S(1)} %collective-permute-done.11.behind_w_ref, ...), custom_call_target="tpu_custom_call" | custom-call | flops 200000000 | bytes 4000000 | tf_op jit(solution)/shard_map/pallas_call | solution.py:483
  53.9 6.0 %collective-permute-done.13.one_ref = bf16[32,2048]{1,0:T(8,128)(2,1)S(1)} collective-permute-done((bf16[32,2048]{1,0:T(8,128)(2,1)S(1)}, bf16[32,2048]{1,0:T(8,128)(2,1)S(1)}, u32[]{:S(2)}, u32[]{:S(2)}) %collective-permute-start.13) | collective-permute-done | bytes 131104 | tf_op jit(solution)/shard_map/ppermute | solution.py:588
  59.9 0.0 collective-permute-done.14.two_ref
  59.9 0.7 %shard_map.129 = bf16[32,2048]{1,0:T(8,128)(2,1)} custom-call(f32[32,2048]{1,0:T(8,128)S(1)} %shard_map.127.own_ref, bf16[32,2048]{1,0:T(8,128)(2,1)S(1)} %collective-permute-done.13.one_ref, bf16[32,2048]{1,0:T(8,128)(2,1)S(1)} %collective-permute-done.14.two_ref), custom_call_target="tpu_custom_call" | custom-call | flops 1000000 | bytes 800000 | tf_op jit(solution)/shard_map/pallas_call | solution.py:483
  (2 shorter events, 0.0 us)
Async XLA Ops:
  0.0 7.1 %copy-start.4 = (bf16[256,256]{1,0:T(8,128)(2,1)S(1)}, bf16[256,256]{1,0:T(8,128)(2,1)}, u32[]{:S(2)}) copy-start(bf16[256,256]{1,0:T(8,128)(2,1)} %k_ref.3) | copy-start | bytes 393220
  0.0 7.1 %copy-start.3 = (bf16[256,512]{1,0:T(8,128)(2,1)S(1)}, bf16[256,512]{1,0:T(8,128)(2,1)}, u32[]{:S(2)}) copy-start(bf16[256,512]{1,0:T(8,128)(2,1)} %v_ref.3) | copy-start | bytes 786436
  0.0 1.7 %copy-start = (bf16[512,2048]{1,0:T(8,128)(2,1)S(1)}, bf16[512,2048]{1,0:T(8,128)(2,1)}, u32[]{:S(2)}) copy-start(bf16[512,2048]{1,0:T(8,128)(2,1)} %weight_ref.1) | copy-start | bytes 6291460
  0.0 7.1 %copy-start.11 = (s32[256]{0:T(256)S(1)}, s32[256]{0:T(256)}, u32[]{:S(2)}) copy-start(s32[256]{0:T(256)} %param.18) | copy-start | bytes 3076
  0.0 7.1 %copy-start.9 = (f32[4,256]{1,0:T(4,128)S(1)}, f32[4,256]{1,0:T(4,128)}, u32[]{:S(2)}) copy-start(f32[4,256]{1,0:T(4,128)} %decay_ref.3) | copy-start | bytes 12292
  0.0 7.1 %copy-start.7 = (f32[4,256]{1,0:T(4,128)S(1)}, f32[4,256]{1,0:T(4,128)}, u32[]{:S(2)}) copy-start(f32[4,256]{1,0:T(4,128)} %beta_ref.3) | copy-start | bytes 12292
  0.0 7.1 %copy-start.8 = (f32[4,256]{1,0:T(4,128)S(1)}, f32[4,256]{1,0:T(4,128)}, u32[]{:S(2)}) copy-start(f32[4,256]{1,0:T(4,128)} %wk_ref.3) | copy-start | bytes 12292
  0.0 7.1 %copy-start.6 = (f32[4,512]{1,0:T(4,128)S(1)}, f32[4,512]{1,0:T(4,128)}, u32[]{:S(2)}) copy-start(f32[4,512]{1,0:T(4,128)} %wv_ref.3) | copy-start | bytes 24580
  1.7 38.8 %collective-permute-start.11 = (bf16[512,2048]{1,0:T(8,128)(2,1)S(1)}, bf16[512,2048]{1,0:T(8,128)(2,1)S(1)}, u32[]{:S(2)}, u32[]{:S(2)}) collective-permute-start(bf16[512,2048]{1,0:T(8,128)(2,1)S(1)} %copy-done), channel_id=1, source_target_pairs={{0,1},{1,2},{2,3},{3,4},{4,5},{5,6},{6,7},{7,0},{8,15},{9,8},{10,9... | collective-permute-start | bytes 6291464 | tf_op jit(solution)/shard_map/ppermute | solution.py:511
  3.6 5.7 %collective-permute-start = (bf16[16,1024]{1,0:T(8,128)(2,1)}, bf16[16,1024]{1,0:T(8,128)(2,1)S(1)}, u32[]{:S(2)}, u32[]{:S(2)}) collective-permute-start(bf16[16,1024]{1,0:T(8,128)(2,1)} %shard_map.118), channel_id=1, source_target_pairs={{0,8},{8,16},{16,24},{24,32},{32,40},{40,48},{48,56},{56,64},{64,7... | collective-permute-start | bytes 98312 | tf_op jit(solution)/shard_map/ppermute | solution.py:514
  9.3 10.9 %copy-start.5 = (bf16[256,256]{1,0:T(8,128)(2,1)S(1)}, bf16[256,256]{1,0:T(8,128)(2,1)}, u32[]{:S(2)}) copy-start(bf16[256,256]{1,0:T(8,128)(2,1)} %q_ref.3) | copy-start | bytes 393220
  9.3 10.9 %copy-start.10 = (f32[4,256]{1,0:T(4,128)S(1)}, f32[4,256]{1,0:T(4,128)}, u32[]{:S(2)}) copy-start(f32[4,256]{1,0:T(4,128)} %wq_ref.1) | copy-start | bytes 12292
  12.2 1.4 %collective-permute-start.1 = (bf16[2,128,256]{2,1,0:T(8,128)(2,1)S(1)}, bf16[2,128,256]{2,1,0:T(8,128)(2,1)S(1)}, u32[]{:S(2)}, u32[]{:S(2)}) collective-permute-start(bf16[2,128,256]{2,1,0:T(8,128)(2,1)S(1)} %get-tuple-element.44), channel_id=1, source_target_pairs={{0,8},{8,0},{16,24},{24,16},{32,40},{40,32},{48,56},{56,48},{64,72... | collective-permute-start | bytes 393224 | tf_op jit(solution)/shard_map/ppermute | solution.py:536
  13.8 7.3 %collective-permute-start.2 = (bf16[2,128,256]{2,1,0:T(8,128)(2,1)S(1)}, bf16[2,128,256]{2,1,0:T(8,128)(2,1)S(1)}, u32[]{:S(2)}, u32[]{:S(2)}) collective-permute-start(bf16[2,128,256]{2,1,0:T(8,128)(2,1)S(1)} %shard_map.122.own_ref), channel_id=1, source_target_pairs={{0,16},{8,24},{16,0},{24,8},{32,48},{40,56},{48,32},{56,40},{64,80... | collective-permute-start | bytes 393224 | tf_op jit(solution)/shard_map/ppermute | solution.py:538
  14.5 12.2 %collective-permute-start.3 = (bf16[2,128,256]{2,1,0:T(8,128)(2,1)S(1)}, bf16[2,128,256]{2,1,0:T(8,128)(2,1)S(1)}, u32[]{:S(2)}, u32[]{:S(2)}) collective-permute-start(bf16[2,128,256]{2,1,0:T(8,128)(2,1)S(1)} %shard_map.122.own_ref), channel_id=1, source_target_pairs={{0,32},{8,40},{16,48},{24,56},{32,0},{40,8},{48,16},{56,24},{64,96... | collective-permute-start | bytes 393224 | tf_op jit(solution)/shard_map/ppermute | solution.py:538
  20.2 8.7 %collective-permute-start.4 = (bf16[2,128,256]{2,1,0:T(8,128)(2,1)S(1)}, bf16[2,128,256]{2,1,0:T(8,128)(2,1)S(1)}, u32[]{:S(2)}, u32[]{:S(2)}) collective-permute-start(bf16[2,128,256]{2,1,0:T(8,128)(2,1)S(1)} %shard_map.122.own_ref), channel_id=1, source_target_pairs={{0,48},{8,56},{16,32},{24,40},{32,16},{40,24},{48,0},{56,8},{64,11... | collective-permute-start | bytes 393224 | tf_op jit(solution)/shard_map/ppermute | solution.py:538
  20.3 20.4 %copy-start.1 = (bf16[256,512]{1,0:T(8,128)(2,1)S(1)}, bf16[256,512]{1,0:T(8,128)(2,1)}, u32[]{:S(2)}) copy-start(bf16[256,512]{1,0:T(8,128)(2,1)} %gate_ref.1) | copy-start | bytes 786436
  20.3 20.4 %copy-start.2 = (f32[128]{0:T(128)S(1)}, f32[128]{0:T(128)}, u32[]{:S(2)}) copy-start(f32[128]{0:T(128)} %param.22) | copy-start | bytes 1540
  29.5 9.0 %collective-permute-start.5 = (bf16[2,128,256]{2,1,0:T(8,128)(2,1)S(1)}, bf16[2,128,256]{2,1,0:T(8,128)(2,1)S(1)}, u32[]{:S(2)}, u32[]{:S(2)}) collective-permute-start(bf16[2,128,256]{2,1,0:T(8,128)(2,1)S(1)} %get-tuple-element.45.own_ref), channel_id=1, source_target_pairs={{0,64},{8,72},{16,80},{24,88},{32,96},{40,104},{48,112},{56,120},{... | collective-permute-start | bytes 393224 | tf_op jit(solution)/shard_map/ppermute | solution.py:553
  29.6 8.9 %collective-permute-start.6 = (bf16[2,128,256]{2,1,0:T(8,128)(2,1)S(1)}, bf16[2,128,256]{2,1,0:T(8,128)(2,1)S(1)}, u32[]{:S(2)}, u32[]{:S(2)}) collective-permute-start(bf16[2,128,256]{2,1,0:T(8,128)(2,1)S(1)} %get-tuple-element.45.own_ref), channel_id=1, source_target_pairs={{0,128},{8,136},{16,144},{24,152},{32,160},{40,168},{48,176},{56,1... | collective-permute-start | bytes 393224 | tf_op jit(solution)/shard_map/ppermute | solution.py:554
  31.8 5.9 %collective-permute-start.7 = (bf16[2,128,128]{2,1,0:T(8,128)(2,1)S(1)}, bf16[2,128,128]{2,1,0:T(8,128)(2,1)S(1)}, u32[]{:S(2)}, u32[]{:S(2)}) collective-permute-start(bf16[2,128,128]{2,1,0:T(8,128)(2,1)S(1)} %get-tuple-element.46), channel_id=1, source_target_pairs={{0,192},{8,200},{16,208},{24,216},{32,224},{40,232},{48,240},{56,2... | collective-permute-start | bytes 196616 | tf_op jit(solution)/shard_map/ppermute | solution.py:555
  39.1 1.3 %collective-permute-start.8 = (bf16[2,128,128]{2,1,0:T(8,128)(2,1)S(1)}, bf16[2,128,128]{2,1,0:T(8,128)(2,1)S(1)}, u32[]{:S(2)}, u32[]{:S(2)}) collective-permute-start(bf16[2,128,128]{2,1,0:T(8,128)(2,1)S(1)} %get-tuple-element.49), channel_id=1, source_target_pairs={{0,8},{8,0},{16,24},{24,16},{32,40},{40,32},{48,56},{56,48},{64,72... | collective-permute-start | bytes 196616 | tf_op jit(solution)/shard_map/ppermute | solution.py:561
  40.5 7.2 %collective-permute-start.12 = (bf16[512,2048]{1,0:T(8,128)(2,1)S(1)}, bf16[512,2048]{1,0:T(8,128)(2,1)S(1)}, u32[]{:S(2)}, u32[]{:S(2)}) collective-permute-start(bf16[512,2048]{1,0:T(8,128)(2,1)S(1)} %collective-permute-done.11.behind_w_ref), channel_id=1, source_target_pairs={{0,8},{8,0},{16,24},{24,16},{32,40},{40,32},{48,56},{56,48},{64,72... | collective-permute-start | bytes 6291464 | tf_op jit(solution)/shard_map/ppermute | solution.py:563
  41.1 6.6 %collective-permute-start.9 = (bf16[96,512]{1,0:T(8,128)(2,1)S(1)}, bf16[96,512]{1,0:T(8,128)(2,1)S(1)}, u32[]{:S(2)}, u32[]{:S(2)}) collective-permute-start(bf16[96,512]{1,0:T(8,128)(2,1)S(1)} %get-tuple-element.51), channel_id=1, source_target_pairs={{0,1},{1,2},{2,3},{3,4},{4,5},{5,6},{6,7},{7,0},{8,15},{9,8},{10,9... | collective-permute-start | bytes 294920 | tf_op jit(solution)/shard_map/ppermute | solution.py:575
  41.2 5.1 %collective-permute-start.10 = (bf16[64,512]{1,0:T(8,128)(2,1)S(1)}, bf16[64,512]{1,0:T(8,128)(2,1)S(1)}, u32[]{:S(2)}, u32[]{:S(2)}) collective-permute-start(bf16[64,512]{1,0:T(8,128)(2,1)S(1)} %get-tuple-element.52), channel_id=1, source_target_pairs={{0,7},{1,0},{2,1},{3,2},{4,3},{5,4},{6,5},{7,6},{8,9},{9,10},{10,1... | collective-permute-start | bytes 196616 | tf_op jit(solution)/shard_map/ppermute | solution.py:576
  48.5 11.4 %collective-permute-start.13 = (bf16[32,2048]{1,0:T(8,128)(2,1)S(1)}, bf16[32,2048]{1,0:T(8,128)(2,1)S(1)}, u32[]{:S(2)}, u32[]{:S(2)}) collective-permute-start(bf16[32,2048]{1,0:T(8,128)(2,1)S(1)} %get-tuple-element.55), channel_id=1, source_target_pairs={{0,5},{1,6},{2,7},{3,0},{4,1},{5,2},{6,3},{7,4},{8,11},{9,12},{10,... | collective-permute-start | bytes 393224 | tf_op jit(solution)/shard_map/ppermute | solution.py:588
  49.9 10.0 %collective-permute-start.14 = (bf16[32,2048]{1,0:T(8,128)(2,1)S(1)}, bf16[32,2048]{1,0:T(8,128)(2,1)S(1)}, u32[]{:S(2)}, u32[]{:S(2)}) collective-permute-start(bf16[32,2048]{1,0:T(8,128)(2,1)S(1)} %get-tuple-element.56), channel_id=1, source_target_pairs={{0,2},{1,3},{2,4},{3,5},{4,6},{5,7},{6,0},{7,1},{8,14},{9,15},{10,... | collective-permute-start | bytes 393224 | tf_op jit(solution)/shard_map/ppermute | solution.py:589

commit v11 on v10

--- a/solution.py
+++ b/solution.py
@@ -168,7 +168,7 @@
     return [fn(*items) for items in zip(*lists)]
 
 
-def unit_inverses(many, masks):
+def unit_inverses(many, masks, beside):
     row, col = rows_and_columns((8, HALF))
     eye = ((col & 7) == row).astype(F32)
     d = each(lambda a: gather_blocks(a, 8, False), many)
@@ -180,6 +180,7 @@
     for i, size in enumerate(LEVELS):
         e = each(lambda a: gather_blocks(a, size, True), many)
         y = each(lambda e, t: times(e, t, masks[2 * i]), e, t)
+        beside(i)
         z = each(lambda t, y: times(t, y, masks[2 * i + 1]), t, y)
         lane = lax.broadcasted_iota(jnp.int32, (size, HALF), 1)
         left = ((lane >> (size.bit_length() - 1)) & 1) == 0
@@ -215,14 +216,14 @@
 
 
 def early_kernel(
-    k_ref, v_ref, decay_ref, beta_ref, doc_ref, wk_ref, wv_ref,
-    key_ref, value_ref, factor_ref, carry_ref, last_ref, start_ref, head_ref, mask_ref, ext_ref,
+    k_ref, decay_ref, beta_ref, doc_ref, wk_ref,
+    key_ref, factor_ref, carry_ref, last_ref, start_ref, head_ref, mask_ref, ext_ref,
 ):
     row, col = rows_and_columns()
     lower = (col <= row).astype(BF16)
     eye = (col == row).astype(BF16)
     start = spread([local_start(doc_ref)], eye, 1)[0]
-    start_ref[...] = start[0:RIM]
+    start_ref[...] = start
     decay = decay_ref[...]
     beta = beta_ref[...]
     cum_row = sum(mm_t(piece, lower) for piece in parts(decay, 3))
@@ -239,10 +240,7 @@
     key_conv = short_conv(ext_ref, k_ref, jnp.zeros((8, 256), F32), wk_ref, valid)
     for g, key in enumerate(unit_keys(key_conv)):
         key_ref[g] = key.astype(BF16)
-    value_conv = short_conv(ext_ref, v_ref, jnp.zeros((8, 512), F32), wv_ref, valid)
-    value_ref[...] = value_conv.astype(BF16)
-    head_ref[:, 0:256] = k_ref[0:RIM, :]
-    head_ref[:, 256:768] = v_ref[0:RIM, :]
+    head_ref[...] = k_ref[0:RIM, :]
     for i, mask in enumerate(block_masks()):
         mask_ref[i] = mask
 
@@ -259,21 +257,31 @@
 
 
 def map_kernel(
-    rim_ref, head_ref, start_ref, key_ref, value_ref, factor_ref, carry_ref, last_ref, beta_ref,
-    wk_ref, wv_ref, mask_ref, wu_ref, kb_ref, own_ref, give_ref,
+    rim_ref, head_ref, start_ref, key_ref, v_ref, factor_ref, carry_ref, last_ref, beta_ref,
+    wk_ref, wv_ref, mask_ref, wu_ref, kb_ref, own_ref, give_ref, ext_ref,
 ):
     rim = rim_ref[...].astype(F32)[8:16]
     head = head_ref[...].astype(F32)[0:8]
-    start = start_ref[0:8]
-    first_keys = unit_keys(first_rows(rim[:, 0:256], head[:, 0:256], wk_ref, start))
-    first_values = first_rows(rim[:, 256:768], head[:, 256:768], wv_ref, start)
+    start = start_ref[...]
+    valid = tap_masks(start)
+    first_keys = unit_keys(first_rows(rim[:, 0:256], head, wk_ref, start[0:8]))
+    ext_ref[0:8] = rim[:, 256:768]
+
+    def convolved(h):
+        at = slice(h * DV, (h + 1) * DV)
+        own = v_ref[:, at].astype(F32)
+        ext_ref[8 : 8 + TOK, at] = own
+        total = own * wv_ref[0:1, at]
+        for tap in range(1, TAPS):
+            shifted = ext_ref[8 - tap : 8 - tap + TOK, at]
+            total = total + jnp.where(valid[tap - 1], shifted * wv_ref[tap : tap + 1, at], 0.0)
+        return (total * jax.nn.sigmoid(total)).astype(BF16)
 
     def patched(first, whole):
         whole = whole.astype(F32)
         return jnp.concatenate([first, whole[8:]], axis=0)
 
     keys = [patched(first_keys[g], key_ref[g]).astype(BF16) for g in range(GROUPS)]
-    values = patched(first_values, value_ref[...]).astype(BF16)
     beta = beta_ref[...]
     gram = [mm_t(k, k) for k in keys]
     flipped = [k.astype(F32).T for k in keys]
@@ -283,12 +291,17 @@
     heads = range(HEADS)
     masks = [mask_ref[i] for i in range(2 * len(LEVELS))]
     a = [factor_ref[h] * gram[h // 2] for h in heads]
-    inverses = unit_inverses([m[:HALF, :HALF] for m in a] + [m[HALF:, HALF:] for m in a], masks)
+    values = []
+    inverses = unit_inverses(
+        [m[:HALF, :HALF] for m in a] + [m[HALF:, HALF:] for m in a],
+        masks,
+        lambda level: values.append(convolved(level)),
+    )
     right = [
         jnp.concatenate(
             [
                 (carry_ref[h] * keys[h // 2].astype(F32)).astype(BF16),
-                values[:, h * DV : (h + 1) * DV],
+                values[h],
             ],
             axis=1,
         )
@@ -314,7 +327,8 @@
 
 
 def output_kernel(
-    q_ref, rim_ref, decay_ref, doc_ref, wq_ref, kb_ref, wu_ref, out_ref, reach_ref, ext_ref
+    q_ref, rim_ref, decay_ref, doc_ref, wq_ref, kb_ref, wu_ref, gate_ref, gain_ref,
+    out_ref, reach_ref, factor_ref, ext_ref,
 ):
     row, col = rows_and_columns()
     lower = (col <= row).astype(BF16)
@@ -338,6 +352,8 @@
         reach = carry * query_conv[:, g * DK : (g + 1) * DK] - both[:, :DK]
         reach_ref[h] = reach.astype(BF16)
         out_ref[h] = both[:, DK:]
+        gate = gate_ref[:, h * DV : (h + 1) * DV].astype(F32)
+        factor_ref[h] = gain_ref[...] * (gate * jax.nn.sigmoid(gate))
 
 
 def joined(first, later):
@@ -412,7 +428,7 @@
 
 
 def norm_kernel(
-    local_ref, reach_ref, mine_ref, got_ref, gate_ref, gain_ref, keep_ref, ahead_ref, behind_ref, normed_ref
+    local_ref, reach_ref, mine_ref, got_ref, factor_ref, keep_ref, ahead_ref, behind_ref, normed_ref
 ):
     core = lax.axis_index("ctx") % CORES
     place = lax.axis_index("head")
@@ -420,9 +436,7 @@
         state = jnp.where(core == h // 2, mine_ref[h % 2], got_ref[h % 2])
         heads = local_ref[h] + mm(reach_ref[h], state)
         inv = lax.rsqrt(jnp.mean(heads * heads, axis=-1, keepdims=True) + EPS)
-        gate = gate_ref[:, h * DV : (h + 1) * DV].astype(F32)
-        gate = gate * jax.nn.sigmoid(gate)
-        normed_ref[:, h * DV : (h + 1) * DV] = (heads * inv * gain_ref[...] * gate).astype(BF16)
+        normed_ref[:, h * DV : (h + 1) * DV] = (heads * inv * factor_ref[h]).astype(BF16)
     rows = TOK // 8
     sign = 1 - 2 * core
     for steps, ref in ((KEPT, keep_ref), (TO_AHEAD, ahead_ref), (TO_BEHIND, behind_ref)):
@@ -516,30 +530,29 @@
     early = call(
         early_kernel,
         [
-            ((GROUPS, TOK, DK), BF16), ((TOK, HEADS * DV), BF16), ((HEADS, TOK, TOK), F32),
-            ((HEADS, TOK, 128), F32), ((HEADS, TOK), F32), ((RIM, 128), F32), ((RIM, 768), BF16),
+            ((GROUPS, TOK, DK), BF16), ((HEADS, TOK, TOK), F32),
+            ((HEADS, TOK, 128), F32), ((HEADS, TOK), F32), ((TOK, 128), F32), ((RIM, 256), BF16),
             ((2 * len(LEVELS), HALF, HALF), BF16),
         ],
-        [key_in, value_in, log_decay, beta_gate, doc_row, conv_key, conv_value],
-        [
-            pltpu.VMEM((8 + TOK, 512), F32),
-        ],
+        [key_in, log_decay, beta_gate, doc_row, conv_key],
+        [pltpu.VMEM((8 + TOK, 256), F32)],
         flops=500_000_000, moved=0, limit=48, blocked=True,
     )
-    keys, values, factor, carry, final, start, head, masks = early
+    keys, factor, carry, final, start, head, masks = early
     solved, keys, own, give = call(
         map_kernel,
         [((HEADS, TOK, DK + DV), BF16), ((GROUPS, TOK, DK), BF16), (wide, BF16), (wide, BF16)],
-        [rim, head, start, keys, values, factor, carry, final, beta_gate, conv_key, conv_value, masks],
+        [rim, head, start, keys, value_in, factor, carry, final, beta_gate, conv_key, conv_value, masks],
+        [pltpu.VMEM((8 + TOK, HEADS * DV), F32)],
         flops=4_000_000_000, moved=2_000_000,
     )
     other = lax.ppermute(give, "ctx", core_swap())
     (pair,) = call(pair_kernel, [(wide, BF16)], [own, other], flops=20_000_000, moved=400_000)
     near = [lax.ppermute(pair, "ctx", pairs_x(k)) for k in (1, 2, 3)]
-    local, reach = call(
+    local, reach, factor = call(
         output_kernel,
-        [((HEADS, TOK, DV), F32), ((HEADS, TOK, DK), BF16)],
-        [query_in, rim, log_decay, doc_row, conv_query, keys, solved],
+        [((HEADS, TOK, DV), F32), ((HEADS, TOK, DK), BF16), ((HEADS, TOK, DV), F32)],
+        [query_in, rim, log_decay, doc_row, conv_query, keys, solved, out_gate, gain_row],
         [pltpu.VMEM((8 + TOK, 256), F32)],
         flops=2_000_000_000, moved=2_000_000,
     )
@@ -568,7 +581,7 @@
 
     keep, to_ahead, to_behind = call(
         norm_kernel, [normed_rows(KEPT), normed_rows(TO_AHEAD), normed_rows(TO_BEHIND)],
-        [local, reach, mine, got, out_gate, gain_row],
+        [local, reach, mine, got, factor],
         [pltpu.VMEM((TOK, HEADS * DV), BF16)],
         flops=100_000_000, moved=1_500_000,
     )

time: 60.7 us -> 59.4 us (0.979)
  the two profiles are of different devices: /device:TPU:6 before, /device:TPU:64 now
where the time goes in v11:
time: 59.4 us; the launch traced here: 59.3 us
  waiting for transfers between devices  29.4 us (49%)
  starting transfers between devices  18.7 us (31%)
  Pallas kernels  10.9 us (18%)
    pallas_call x11, Pallas kernels, call(): pl.pallas_call(kernel, grid=(1,) if blocked else (), out_shape=[jax.Shape...  9.37 us
    ppermute x1, waiting for transfers between devices, on_device(): far_part = lax.ppermute(far_part, ('ctx', 'head'), mirrored(-3))  8.36 us
    ppermute x1, waiting for transfers between devices, on_device(): rim = lax.ppermute(edge, 'ctx', [(i, (i + 1) % CTX) for i in range(CTX)])  6 us
    ppermute x3, waiting for transfers between devices, on_device(): near = [lax.ppermute(pair, 'ctx', pairs_x(k)) for k in (1, 2, 3)]  5.12 us
    ppermute x3, starting transfers between devices, on_device(): near = [lax.ppermute(pair, 'ctx', pairs_x(k)) for k in (1, 2, 3)]  4.17 us
    ppermute x1, waiting for transfers between devices, on_device(): from_ahead = lax.ppermute(to_behind, ('ctx', 'head'), mirrored(-1))  3.8 us
    ppermute x1, starting transfers between devices, on_device(): far_part = lax.ppermute(far_part, ('ctx', 'head'), mirrored(-3))  3.66 us
    ppermute x1, starting transfers between devices, on_device(): from_behind = lax.ppermute(to_ahead, ('ctx', 'head'), mirrored(1))  3.2 us
  transfers between devices with their start and end apart: 15, of which 10 were waited for; matrix products, arithmetic and copies ran while one was open for 0% of the time, Pallas kernels for 13%

profile of v11, /device:TPU:64, one launch (start us, length us, event | category | flops | bytes accessed | tf_op | source)
XLA Modules:
  0.0 59.3 jit_solution(15954553288080717300)
XLA Ops:
  0.0 0.0 copy-start.1
  0.0 0.0 copy-start.3
  0.0 0.0 copy-start
  0.0 0.0 copy-start.7
  0.0 0.0 copy-start.6
  0.0 0.0 copy-start.8
  0.0 0.0 copy-start.10
  0.0 0.0 copy-start.5
  0.1 1.5 %shard_map.118 = bf16[16,1024]{1,0:T(8,128)(2,1)} custom-call(bf16[256,256]{1,0:T(8,128)(2,1)} %k_ref.3, bf16[256,512]{1,0:T(8,128)(2,1)} %v_ref.3, bf16[256,256]{1,0:T(8,128)(2,1)} %q_ref.3), custom_call_target="tpu_custom_call" | custom-call | flops 5000000000 | tf_op jit(solution)/shard_map/pallas_call | solution.py:517
  1.5 0.1 copy-done
  1.7 1.9 %collective-permute-start.11 = (bf16[512,2048]{1,0:T(8,128)(2,1)S(1)}, bf16[512,2048]{1,0:T(8,128)(2,1)S(1)}, u32[]{:S(2)}, u32[]{:S(2)}) collective-permute-start(bf16[512,2048]{1,0:T(8,128)(2,1)S(1)} %copy-done), channel_id=1, source_target_pairs={{0,1},{1,2},{2,3},{3,4},{4,5},{5,6},{6,7},{7,0},{8,15},{9,8},{10,9... | collective-permute-start | bytes 6291464 | tf_op jit(solution)/shard_map/ppermute | solution.py:525
  3.6 0.0 collective-permute-start
  3.6 0.0 copy-done.3
  3.6 0.0 copy-done.7
  3.6 0.0 copy-done.6
  3.6 0.0 copy-done.8
  3.6 0.0 copy-done.10
  3.6 0.8 %shard_map.119 = (bf16[2,256,128]{2,1,0:T(8,128)(2,1)S(1)}, f32[4,256,256]{2,1,0:T(8,128)S(1)}, f32[4,256,128]{2,1,0:T(8,128)S(1)}, f32[4,256]{1,0:T(4,128)S(1)}...) custom-call(bf16[256,256]{1,0:T(8,128)(2,1)S(1)} %copy-done.3, ...), custom_call_target="tpu_custom_call" | custom-call | flops 500000000 | tf_op jit(solution)/shard_map/pallas_call | solution.py:497
  4.4 6.0 %collective-permute-done.rim_ref = bf16[16,1024]{1,0:T(8,128)(2,1)S(1)} collective-permute-done((bf16[16,1024]{1,0:T(8,128)(2,1)}, bf16[16,1024]{1,0:T(8,128)(2,1)S(1)}, u32[]{:S(2)}, u32[]{:S(2)}) %collective-permute-start) | collective-permute-done | bytes 32800 | tf_op jit(solution)/shard_map/ppermute | solution.py:528
  10.4 0.0 copy-done.1
  10.4 0.0 copy-done.5
  10.5 0.0 copy-start.9
  10.5 0.0 copy-start.11
  10.5 3.0 %shard_map.120 = (bf16[4,256,256]{2,1,0:T(8,128)(2,1)S(1)}, bf16[2,256,128]{2,1,0:T(8,128)(2,1)S(1)}, bf16[2,128,256]{2,1,0:T(8,128)(2,1)S(1)}, bf16[2,128,256]{2,1,0:T(8,128)(2,1)S(1)}) custom-call(bf16[16,1024]{1,0:T(8,128)(2,1)S(1)} %collective-permute-done.rim_ref, bf16[16,256]{1,0:T(8,128)(2,1)S(1)} %get-tuple-element.31.head_ref, ...), custom_call_target="tpu_custom_call" | custom-call | flops 4000000000 | bytes 2000000 | tf_op jit(solution)/shard_map/pallas_call | solution.py:497
  13.5 0.1 collective-permute-start.1
  13.6 1.3 %collective-permute-done.1.got_ref.other_ref = bf16[2,128,256]{2,1,0:T(8,128)(2,1)S(1)} collective-permute-done((bf16[2,128,256]{2,1,0:T(8,128)(2,1)S(1)}, bf16[2,128,256]{2,1,0:T(8,128)(2,1)S(1)}, u32[]{:S(2)}, u32[]{:S(2)}) %collective-permute-start.1) | collective-permute-done | bytes 131104 | tf_op jit(solution)/shard_map/ppermute | solution.py:549
  15.0 0.2 shard_map.122.own_ref
  15.2 0.1 collective-permute-start.4
  15.3 0.2 collective-permute-start.3
  15.5 3.9 %collective-permute-start.2 = (bf16[2,128,256]{2,1,0:T(8,128)(2,1)S(1)}, bf16[2,128,256]{2,1,0:T(8,128)(2,1)S(1)}, u32[]{:S(2)}, u32[]{:S(2)}) collective-permute-start(bf16[2,128,256]{2,1,0:T(8,128)(2,1)S(1)} %shard_map.122.own_ref), channel_id=1, source_target_pairs={{0,16},{8,24},{16,0},{24,8},{32,48},{40,56},{48,32},{56,40},{64,80... | collective-permute-start | bytes 393224 | tf_op jit(solution)/shard_map/ppermute | solution.py:551
  19.3 0.0 copy-done.2
  19.4 0.0 copy-done.4
  19.4 0.0 copy-done.9
  19.4 0.0 copy-done.11
  19.4 0.9 %shard_map.121 = (f32[4,256,128]{2,1,0:T(8,128)S(1)}, bf16[4,256,128]{2,1,0:T(8,128)(2,1)S(1)}, f32[4,256,128]{2,1,0:T(8,128)S(1)}) custom-call(bf16[256,256]{1,0:T(8,128)(2,1)S(1)} %copy-done.4, bf16[16,1024]{1,0:T(8,128)(2,1)S(1)} %collective-permute-done.rim_ref, f32[4,256]{1,0:T(4,128)S(1)} %copy-done.8, s32[1,256]{1,0:T(1,128)S(1)} %bitcast.3, ...), custom_call_target="tpu_custom_call" | custom-call | flops 2000000000 | bytes 2000000 | tf_op jit(solution)/shard_map/pallas_call | solution.py:497
  20.3 4.5 %collective-permute-done.4.three_ref = bf16[2,128,256]{2,1,0:T(8,128)(2,1)S(1)} collective-permute-done((bf16[2,128,256]{2,1,0:T(8,128)(2,1)S(1)}, bf16[2,128,256]{2,1,0:T(8,128)(2,1)S(1)}, u32[]{:S(2)}, u32[]{:S(2)}) %collective-permute-start.4) | collective-permute-done | bytes 131104 | tf_op jit(solution)/shard_map/ppermute | solution.py:551
  24.8 0.0 collective-permute-done.3.two_ref
  24.8 0.6 collective-permute-done.2.one_ref
  25.4 0.6 shard_map.123
  26.0 2.1 %collective-permute-start.6 = (bf16[2,128,256]{2,1,0:T(8,128)(2,1)S(1)}, bf16[2,128,256]{2,1,0:T(8,128)(2,1)S(1)}, u32[]{:S(2)}, u32[]{:S(2)}) collective-permute-start(bf16[2,128,256]{2,1,0:T(8,128)(2,1)S(1)} %get-tuple-element.44.own_ref), channel_id=1, source_target_pairs={{0,128},{8,136},{16,144},{24,152},{32,160},{40,168},{48,176},{56,1... | collective-permute-start | bytes 393224 | tf_op jit(solution)/shard_map/ppermute | solution.py:567
  28.1 0.7 %collective-permute-start.5 = (bf16[2,128,256]{2,1,0:T(8,128)(2,1)S(1)}, bf16[2,128,256]{2,1,0:T(8,128)(2,1)S(1)}, u32[]{:S(2)}, u32[]{:S(2)}) collective-permute-start(bf16[2,128,256]{2,1,0:T(8,128)(2,1)S(1)} %get-tuple-element.44.own_ref), channel_id=1, source_target_pairs={{0,64},{8,72},{16,80},{24,88},{32,96},{40,104},{48,112},{56,120},{... | collective-permute-start | bytes 393224 | tf_op jit(solution)/shard_map/ppermute | solution.py:566
  28.8 2.6 %collective-permute-start.7 = (bf16[2,128,128]{2,1,0:T(8,128)(2,1)S(1)}, bf16[2,128,128]{2,1,0:T(8,128)(2,1)S(1)}, u32[]{:S(2)}, u32[]{:S(2)}) collective-permute-start(bf16[2,128,128]{2,1,0:T(8,128)(2,1)S(1)} %get-tuple-element.45), channel_id=1, source_target_pairs={{0,192},{8,200},{16,208},{24,216},{32,224},{40,232},{48,240},{56,2... | collective-permute-start | bytes 196616 | tf_op jit(solution)/shard_map/ppermute | solution.py:568
  31.3 1.9 %collective-permute-done.7.three_ref = bf16[2,128,128]{2,1,0:T(8,128)(2,1)S(1)} collective-permute-done((bf16[2,128,128]{2,1,0:T(8,128)(2,1)S(1)}, bf16[2,128,128]{2,1,0:T(8,128)(2,1)S(1)}, u32[]{:S(2)}, u32[]{:S(2)}) %collective-permute-start.7) | collective-permute-done | bytes 65568 | tf_op jit(solution)/shard_map/ppermute | solution.py:568
  33.2 0.3 collective-permute-done.6.two_ref
  33.5 1.3 %collective-permute-done.5.one_ref = bf16[2,128,256]{2,1,0:T(8,128)(2,1)S(1)} collective-permute-done((bf16[2,128,256]{2,1,0:T(8,128)(2,1)S(1)}, bf16[2,128,256]{2,1,0:T(8,128)(2,1)S(1)}, u32[]{:S(2)}, u32[]{:S(2)}) %collective-permute-start.5) | collective-permute-done | bytes 131104 | tf_op jit(solution)/shard_map/ppermute | solution.py:566
  34.9 0.6 %shard_map.124 = (bf16[2,128,128]{2,1,0:T(8,128)(2,1)S(1)}, bf16[2,128,128]{2,1,0:T(8,128)(2,1)S(1)}) custom-call(bf16[2,128,256]{2,1,0:T(8,128)(2,1)S(1)} %get-tuple-element.44.own_ref, bf16[2,128,256]{2,1,0:T(8,128)(2,1)S(1)} %collective-permute-done.5.one_ref, bf16[2,128,256]{2,1,0:T(8,128)(2,1)S(1)} %collective-permute-done.6.two_ref, ...), custom_call_target="tpu_custom_call" | custom-call | flops 60000000 | bytes 1000000 | tf_op jit(solution)/shard_map/pallas_call | solution.py:497
  35.5 0.1 collective-permute-start.8
  35.6 1.2 %collective-permute-done.8.got_ref = bf16[2,128,128]{2,1,0:T(8,128)(2,1)S(1)} collective-permute-done((bf16[2,128,128]{2,1,0:T(8,128)(2,1)S(1)}, bf16[2,128,128]{2,1,0:T(8,128)(2,1)S(1)}, u32[]{:S(2)}, u32[]{:S(2)}) %collective-permute-start.8) | collective-permute-done | bytes 65568 | tf_op jit(solution)/shard_map/ppermute | solution.py:574
  36.8 0.0 collective-permute-done.11.behind_w_ref
  36.8 0.2 collective-permute-start.12
  37.0 0.4 shard_map.125
  37.4 3.2 %collective-permute-start.9 = (bf16[96,512]{1,0:T(8,128)(2,1)S(1)}, bf16[96,512]{1,0:T(8,128)(2,1)S(1)}, u32[]{:S(2)}, u32[]{:S(2)}) collective-permute-start(bf16[96,512]{1,0:T(8,128)(2,1)S(1)} %get-tuple-element.51), channel_id=1, source_target_pairs={{0,1},{1,2},{2,3},{3,4},{4,5},{5,6},{6,7},{7,0},{8,15},{9,8},{10,9... | collective-permute-start | bytes 294920 | tf_op jit(solution)/shard_map/ppermute | solution.py:588
  40.6 0.0 collective-permute-start.10
  40.6 0.5 shard_map.126.kept_ref
  41.1 3.8 %collective-permute-done.10.ahead_ref = bf16[64,512]{1,0:T(8,128)(2,1)S(1)} collective-permute-done((bf16[64,512]{1,0:T(8,128)(2,1)S(1)}, bf16[64,512]{1,0:T(8,128)(2,1)S(1)}, u32[]{:S(2)}, u32[]{:S(2)}) %collective-permute-start.10) | collective-permute-done | bytes 65568 | tf_op jit(solution)/shard_map/ppermute | solution.py:589
  44.9 0.0 collective-permute-done.9.behind_ref
  44.9 0.0 collective-permute-done.12.ahead_w_ref
  44.9 0.8 %shard_map.128 = (bf16[32,2048]{1,0:T(8,128)(2,1)S(1)}, bf16[32,2048]{1,0:T(8,128)(2,1)S(1)}) custom-call(f32[96,2048]{1,0:T(8,128)S(1)} %shard_map.126.kept_ref, bf16[96,512]{1,0:T(8,128)(2,1)S(1)} %collective-permute-done.9.behind_ref, bf16[64,512]{1,0:T(8,128)(2,1)S(1)} %collective-permute-done.10.ahead_ref, ...), custom_call_target="tpu_custom_call" | custom-call | flops 200000000 | bytes 4000000 | tf_op jit(solution)/shard_map/pallas_call | solution.py:497
  45.7 3.7 %collective-permute-start.13 = (bf16[32,2048]{1,0:T(8,128)(2,1)S(1)}, bf16[32,2048]{1,0:T(8,128)(2,1)S(1)}, u32[]{:S(2)}, u32[]{:S(2)}) collective-permute-start(bf16[32,2048]{1,0:T(8,128)(2,1)S(1)} %get-tuple-element.55), channel_id=1, source_target_pairs={{0,5},{1,6},{2,7},{3,0},{4,1},{5,2},{6,3},{7,4},{8,11},{9,12},{10,... | collective-permute-start | bytes 393224 | tf_op jit(solution)/shard_map/ppermute | solution.py:601
  49.4 0.0 collective-permute-start.14
  49.4 0.8 %shard_map.127.own_ref = f32[32,2048]{1,0:T(8,128)S(1)} custom-call(f32[96,2048]{1,0:T(8,128)S(1)} %shard_map.126.kept_ref, bf16[96,512]{1,0:T(8,128)(2,1)S(1)} %collective-permute-done.9.behind_ref, bf16[64,512]{1,0:T(8,128)(2,1)S(1)} %collective-permute-done.10.ahead_ref, bf16[512,2048]{1,0:T(8,128)(2,1)S(1)} %collective-permute-done.11.behind_w_ref, ...), custom_call_target="tpu_custom_call" | custom-call | flops 200000000 | bytes 4000000 | tf_op jit(solution)/shard_map/pallas_call | solution.py:497
  50.2 8.4 %collective-permute-done.13.one_ref = bf16[32,2048]{1,0:T(8,128)(2,1)S(1)} collective-permute-done((bf16[32,2048]{1,0:T(8,128)(2,1)S(1)}, bf16[32,2048]{1,0:T(8,128)(2,1)S(1)}, u32[]{:S(2)}, u32[]{:S(2)}) %collective-permute-start.13) | collective-permute-done | bytes 131104 | tf_op jit(solution)/shard_map/ppermute | solution.py:601
  58.6 0.0 collective-permute-done.14.two_ref
  58.6 0.7 %shard_map.129 = bf16[32,2048]{1,0:T(8,128)(2,1)} custom-call(f32[32,2048]{1,0:T(8,128)S(1)} %shard_map.127.own_ref, bf16[32,2048]{1,0:T(8,128)(2,1)S(1)} %collective-permute-done.13.one_ref, bf16[32,2048]{1,0:T(8,128)(2,1)S(1)} %collective-permute-done.14.two_ref), custom_call_target="tpu_custom_call" | custom-call | flops 1000000 | bytes 800000 | tf_op jit(solution)/shard_map/pallas_call | solution.py:497
  (2 shorter events, 0.0 us)
Async XLA Ops:
  0.0 10.4 %copy-start.1 = (bf16[256,512]{1,0:T(8,128)(2,1)S(1)}, bf16[256,512]{1,0:T(8,128)(2,1)}, u32[]{:S(2)}) copy-start(bf16[256,512]{1,0:T(8,128)(2,1)} %v_ref.3) | copy-start | bytes 786436
  0.0 3.6 %copy-start.3 = (bf16[256,256]{1,0:T(8,128)(2,1)S(1)}, bf16[256,256]{1,0:T(8,128)(2,1)}, u32[]{:S(2)}) copy-start(bf16[256,256]{1,0:T(8,128)(2,1)} %k_ref.3) | copy-start | bytes 393220
  0.0 1.7 %copy-start = (bf16[512,2048]{1,0:T(8,128)(2,1)S(1)}, bf16[512,2048]{1,0:T(8,128)(2,1)}, u32[]{:S(2)}) copy-start(bf16[512,2048]{1,0:T(8,128)(2,1)} %weight_ref.1) | copy-start | bytes 6291460
  0.0 3.6 %copy-start.7 = (f32[4,256]{1,0:T(4,128)S(1)}, f32[4,256]{1,0:T(4,128)}, u32[]{:S(2)}) copy-start(f32[4,256]{1,0:T(4,128)} %wk_ref.3) | copy-start | bytes 12292
  0.0 3.6 %copy-start.6 = (f32[4,256]{1,0:T(4,128)S(1)}, f32[4,256]{1,0:T(4,128)}, u32[]{:S(2)}) copy-start(f32[4,256]{1,0:T(4,128)} %beta_ref.3) | copy-start | bytes 12292
  0.0 3.6 %copy-start.8 = (f32[4,256]{1,0:T(4,128)S(1)}, f32[4,256]{1,0:T(4,128)}, u32[]{:S(2)}) copy-start(f32[4,256]{1,0:T(4,128)} %decay_ref.3) | copy-start | bytes 12292
  0.0 3.6 %copy-start.10 = (s32[256]{0:T(256)S(1)}, s32[256]{0:T(256)}, u32[]{:S(2)}) copy-start(s32[256]{0:T(256)} %param.18) | copy-start | bytes 3076
  0.0 10.4 %copy-start.5 = (f32[4,512]{1,0:T(4,128)S(1)}, f32[4,512]{1,0:T(4,128)}, u32[]{:S(2)}) copy-start(f32[4,512]{1,0:T(4,128)} %wv_ref.1) | copy-start | bytes 24580
  1.7 35.2 %collective-permute-start.11 = (bf16[512,2048]{1,0:T(8,128)(2,1)S(1)}, bf16[512,2048]{1,0:T(8,128)(2,1)S(1)}, u32[]{:S(2)}, u32[]{:S(2)}) collective-permute-start(bf16[512,2048]{1,0:T(8,128)(2,1)S(1)} %copy-done), channel_id=1, source_target_pairs={{0,1},{1,2},{2,3},{3,4},{4,5},{5,6},{6,7},{7,0},{8,15},{9,8},{10,9... | collective-permute-start | bytes 6291464 | tf_op jit(solution)/shard_map/ppermute | solution.py:525
  3.6 6.9 %collective-permute-start = (bf16[16,1024]{1,0:T(8,128)(2,1)}, bf16[16,1024]{1,0:T(8,128)(2,1)S(1)}, u32[]{:S(2)}, u32[]{:S(2)}) collective-permute-start(bf16[16,1024]{1,0:T(8,128)(2,1)} %shard_map.118), channel_id=1, source_target_pairs={{0,8},{8,16},{16,24},{24,32},{32,40},{40,48},{48,56},{56,64},{64,7... | collective-permute-start | bytes 98312 | tf_op jit(solution)/shard_map/ppermute | solution.py:528
  10.5 8.9 %copy-start.2 = (bf16[256,512]{1,0:T(8,128)(2,1)S(1)}, bf16[256,512]{1,0:T(8,128)(2,1)}, u32[]{:S(2)}) copy-start(bf16[256,512]{1,0:T(8,128)(2,1)} %gate_ref.1) | copy-start | bytes 786436
  10.5 8.9 %copy-start.4 = (bf16[256,256]{1,0:T(8,128)(2,1)S(1)}, bf16[256,256]{1,0:T(8,128)(2,1)}, u32[]{:S(2)}) copy-start(bf16[256,256]{1,0:T(8,128)(2,1)} %q_ref.3) | copy-start | bytes 393220
  10.5 8.9 %copy-start.9 = (f32[4,256]{1,0:T(4,128)S(1)}, f32[4,256]{1,0:T(4,128)}, u32[]{:S(2)}) copy-start(f32[4,256]{1,0:T(4,128)} %wq_ref.1) | copy-start | bytes 12292
  10.5 8.9 %copy-start.11 = (f32[128]{0:T(128)S(1)}, f32[128]{0:T(128)}, u32[]{:S(2)}) copy-start(f32[128]{0:T(128)} %param.22) | copy-start | bytes 1540
  13.5 1.4 %collective-permute-start.1 = (bf16[2,128,256]{2,1,0:T(8,128)(2,1)S(1)}, bf16[2,128,256]{2,1,0:T(8,128)(2,1)S(1)}, u32[]{:S(2)}, u32[]{:S(2)}) collective-permute-start(bf16[2,128,256]{2,1,0:T(8,128)(2,1)S(1)} %get-tuple-element.43), channel_id=1, source_target_pairs={{0,8},{8,0},{16,24},{24,16},{32,40},{40,32},{48,56},{56,48},{64,72... | collective-permute-start | bytes 393224 | tf_op jit(solution)/shard_map/ppermute | solution.py:549
  15.2 9.7 %collective-permute-start.4 = (bf16[2,128,256]{2,1,0:T(8,128)(2,1)S(1)}, bf16[2,128,256]{2,1,0:T(8,128)(2,1)S(1)}, u32[]{:S(2)}, u32[]{:S(2)}) collective-permute-start(bf16[2,128,256]{2,1,0:T(8,128)(2,1)S(1)} %shard_map.122.own_ref), channel_id=1, source_target_pairs={{0,48},{8,56},{16,32},{24,40},{32,16},{40,24},{48,0},{56,8},{64,11... | collective-permute-start | bytes 393224 | tf_op jit(solution)/shard_map/ppermute | solution.py:551
  15.3 9.6 %collective-permute-start.3 = (bf16[2,128,256]{2,1,0:T(8,128)(2,1)S(1)}, bf16[2,128,256]{2,1,0:T(8,128)(2,1)S(1)}, u32[]{:S(2)}, u32[]{:S(2)}) collective-permute-start(bf16[2,128,256]{2,1,0:T(8,128)(2,1)S(1)} %shard_map.122.own_ref), channel_id=1, source_target_pairs={{0,32},{8,40},{16,48},{24,56},{32,0},{40,8},{48,16},{56,24},{64,96... | collective-permute-start | bytes 393224 | tf_op jit(solution)/shard_map/ppermute | solution.py:551
  15.5 9.9 %collective-permute-start.2 = (bf16[2,128,256]{2,1,0:T(8,128)(2,1)S(1)}, bf16[2,128,256]{2,1,0:T(8,128)(2,1)S(1)}, u32[]{:S(2)}, u32[]{:S(2)}) collective-permute-start(bf16[2,128,256]{2,1,0:T(8,128)(2,1)S(1)} %shard_map.122.own_ref), channel_id=1, source_target_pairs={{0,16},{8,24},{16,0},{24,8},{32,48},{40,56},{48,32},{56,40},{64,80... | collective-permute-start | bytes 393224 | tf_op jit(solution)/shard_map/ppermute | solution.py:551
  26.0 7.6 %collective-permute-start.6 = (bf16[2,128,256]{2,1,0:T(8,128)(2,1)S(1)}, bf16[2,128,256]{2,1,0:T(8,128)(2,1)S(1)}, u32[]{:S(2)}, u32[]{:S(2)}) collective-permute-start(bf16[2,128,256]{2,1,0:T(8,128)(2,1)S(1)} %get-tuple-element.44.own_ref), channel_id=1, source_target_pairs={{0,128},{8,136},{16,144},{24,152},{32,160},{40,168},{48,176},{56,1... | collective-permute-start | bytes 393224 | tf_op jit(solution)/shard_map/ppermute | solution.py:567
  28.1 6.8 %collective-permute-start.5 = (bf16[2,128,256]{2,1,0:T(8,128)(2,1)S(1)}, bf16[2,128,256]{2,1,0:T(8,128)(2,1)S(1)}, u32[]{:S(2)}, u32[]{:S(2)}) collective-permute-start(bf16[2,128,256]{2,1,0:T(8,128)(2,1)S(1)} %get-tuple-element.44.own_ref), channel_id=1, source_target_pairs={{0,64},{8,72},{16,80},{24,88},{32,96},{40,104},{48,112},{56,120},{... | collective-permute-start | bytes 393224 | tf_op jit(solution)/shard_map/ppermute | solution.py:566
  28.8 4.5 %collective-permute-start.7 = (bf16[2,128,128]{2,1,0:T(8,128)(2,1)S(1)}, bf16[2,128,128]{2,1,0:T(8,128)(2,1)S(1)}, u32[]{:S(2)}, u32[]{:S(2)}) collective-permute-start(bf16[2,128,128]{2,1,0:T(8,128)(2,1)S(1)} %get-tuple-element.45), channel_id=1, source_target_pairs={{0,192},{8,200},{16,208},{24,216},{32,224},{40,232},{48,240},{56,2... | collective-permute-start | bytes 196616 | tf_op jit(solution)/shard_map/ppermute | solution.py:568
  35.5 1.3 %collective-permute-start.8 = (bf16[2,128,128]{2,1,0:T(8,128)(2,1)S(1)}, bf16[2,128,128]{2,1,0:T(8,128)(2,1)S(1)}, u32[]{:S(2)}, u32[]{:S(2)}) collective-permute-start(bf16[2,128,128]{2,1,0:T(8,128)(2,1)S(1)} %get-tuple-element.48), channel_id=1, source_target_pairs={{0,8},{8,0},{16,24},{24,16},{32,40},{40,32},{48,56},{56,48},{64,72... | collective-permute-start | bytes 196616 | tf_op jit(solution)/shard_map/ppermute | solution.py:574
  36.8 8.0 %collective-permute-start.12 = (bf16[512,2048]{1,0:T(8,128)(2,1)S(1)}, bf16[512,2048]{1,0:T(8,128)(2,1)S(1)}, u32[]{:S(2)}, u32[]{:S(2)}) collective-permute-start(bf16[512,2048]{1,0:T(8,128)(2,1)S(1)} %collective-permute-done.11.behind_w_ref), channel_id=1, source_target_pairs={{0,8},{8,0},{16,24},{24,16},{32,40},{40,32},{48,56},{56,48},{64,72... | collective-permute-start | bytes 6291464 | tf_op jit(solution)/shard_map/ppermute | solution.py:576
  37.4 7.5 %collective-permute-start.9 = (bf16[96,512]{1,0:T(8,128)(2,1)S(1)}, bf16[96,512]{1,0:T(8,128)(2,1)S(1)}, u32[]{:S(2)}, u32[]{:S(2)}) collective-permute-start(bf16[96,512]{1,0:T(8,128)(2,1)S(1)} %get-tuple-element.51), channel_id=1, source_target_pairs={{0,1},{1,2},{2,3},{3,4},{4,5},{5,6},{6,7},{7,0},{8,15},{9,8},{10,9... | collective-permute-start | bytes 294920 | tf_op jit(solution)/shard_map/ppermute | solution.py:588
  40.6 4.3 %collective-permute-start.10 = (bf16[64,512]{1,0:T(8,128)(2,1)S(1)}, bf16[64,512]{1,0:T(8,128)(2,1)S(1)}, u32[]{:S(2)}, u32[]{:S(2)}) collective-permute-start(bf16[64,512]{1,0:T(8,128)(2,1)S(1)} %get-tuple-element.52), channel_id=1, source_target_pairs={{0,7},{1,0},{2,1},{3,2},{4,3},{5,4},{6,5},{7,6},{8,9},{9,10},{10,1... | collective-permute-start | bytes 196616 | tf_op jit(solution)/shard_map/ppermute | solution.py:589
  45.7 12.9 %collective-permute-start.13 = (bf16[32,2048]{1,0:T(8,128)(2,1)S(1)}, bf16[32,2048]{1,0:T(8,128)(2,1)S(1)}, u32[]{:S(2)}, u32[]{:S(2)}) collective-permute-start(bf16[32,2048]{1,0:T(8,128)(2,1)S(1)} %get-tuple-element.55), channel_id=1, source_target_pairs={{0,5},{1,6},{2,7},{3,0},{4,1},{5,2},{6,3},{7,4},{8,11},{9,12},{10,... | collective-permute-start | bytes 393224 | tf_op jit(solution)/shard_map/ppermute | solution.py:601
  49.4 9.2 %collective-permute-start.14 = (bf16[32,2048]{1,0:T(8,128)(2,1)S(1)}, bf16[32,2048]{1,0:T(8,128)(2,1)S(1)}, u32[]{:S(2)}, u32[]{:S(2)}) collective-permute-start(bf16[32,2048]{1,0:T(8,128)(2,1)S(1)} %get-tuple-element.56), channel_id=1, source_target_pairs={{0,2},{1,3},{2,4},{3,5},{4,6},{5,7},{6,0},{7,1},{8,14},{9,15},{10,... | collective-permute-start | bytes 393224 | tf_op jit(solution)/shard_map/ppermute | solution.py:602
